TPU v7x, 32 devices: a whole 2x2x4 slice. The times are simulated.
32 devices in a mesh: slab: 8 (over z, x), cross: 4 (over y, core).
Axes of the slice: x: 2, y: 2, z: 4, core: 2. Of those that a mesh axis runs over, the one named last changes fastest.
Arguments:
- velocity: float32 [3, 128, 256, 256], P(None, 'slab', 'cross'), may hold values from -6 to 6
- shape_weight: float32 [32, 384], replicated, may hold values from -6 to 6
- w_in: bfloat16 [384, 1024], replicated, may hold values from -0.3125 to 0.3125
- w_out: bfloat16 [1024, 4096], replicated, may hold values from -0.1875 to 0.1875
- decay: float32 [1024], replicated, may hold values from 0.1 to 2
- rotor_states: float32 [32, 1024], P('slab'), may hold values from -6 to 6
- slot_of_rotor: int32 [32], replicated, may hold values from 0 to 31, each once
- entry_rotor: int32 [32768, 1], P(('slab', 'cross')), may hold values from 0 to 31; in each aligned block of 1024 rows (0 to 1023, 1024 to 2047, ...) at most 64 rows name the same one
- entry_tile: int32 [32768], P(('slab', 'cross')), may hold values from 0 to 2047
- entry_sub: int32 [32768], P(('slab', 'cross')), may hold values from 0 to 31
Outputs:
- advanced: float32 [3, 128, 256, 256], P(None, 'slab', 'cross')
- new_states: float32 [32, 1024], P('slab')
Inputs may be any that keep to these rules, and one draw needn't show every extreme that they name: `entry_rotor`: in the rows of one device no rotor is named more than 64 times, a bound that some block reaches; every rotor is named by some entry. Each slot once; rotor r is owned by slab slot_of_rotor[r] // 4.
All inputs are finite; a program needn't handle non-finite values.
Results may differ from a plain program's by a relative error of at most 0.0026.
Values may be sent and summed in bfloat16 or wider, within the bound.
No kernel may reach another device: no remote copies, remote signals or barrier semaphores. Data moves between devices by JAX's collectives and lax.ppermute only.
A program may use at most 64 MiB of HBM per device.

v0:
```python
import jax
import jax.numpy as jnp
from jax import lax
from jax.sharding import PartitionSpec as P

TILE = 128
R = 32
NSUB = 32


time_step = 0.1
viscosity = 0.3
pool_scale = 1.0 / 64.0
state_step = 0.5
force_scale = 0.5


def extended(cells, sides, width):
    for axis, dim in sides:
        count = lax.axis_size(axis)
        ends = count - 1
        head = lax.slice_in_dim(cells, 0, width, axis=dim)
        tail = lax.slice_in_dim(cells, cells.shape[dim] - width, cells.shape[dim], axis=dim)
        cells = jnp.concatenate(
            [
                lax.ppermute(tail, axis, [(i, (i + 1) % count) for i in range(ends)]),
                cells,
                lax.ppermute(head, axis, [((i + 1) % count, i) for i in range(ends)]),
            ],
            axis=dim,
        )
    return cells


def combine_terms(velocity, east, west, north, south, upper, lower):
    laplace = east + west + north + south + upper + lower - 6.0 * velocity
    advect = (
        velocity[0:1] * ((east - west) * 0.5)
        + velocity[1:2] * ((north - south) * 0.5)
        + velocity[2:3] * ((upper - lower) * 0.5)
    )
    return velocity + time_step * (viscosity * laplace - advect)


def on_device(
    velocity,
    shape_weight,
    w_in,
    w_out,
    decay,
    rotor_states,
    slot_of_rotor,
    entry_rotor,
    entry_tile,
    entry_sub,
):
    local_x, local_y, local_z = (velocity.shape[1], velocity.shape[2], velocity.shape[3])
    tile_count = local_x * local_y * local_z // TILE
    entry_count = entry_tile.shape[0]
    rotor_hot = (entry_rotor == jnp.arange(R, dtype=jnp.int32)[None, :]).astype(jnp.int32)
    slots = jnp.sum(rotor_hot * slot_of_rotor[None, :], axis=1)
    flat_cells = velocity.reshape(3, tile_count, TILE)
    picked = jnp.take(flat_cells, entry_tile, axis=1)
    payload = jnp.transpose(picked, (1, 0, 2)).reshape(entry_count, 3 * TILE).astype(jnp.bfloat16)
    sub_range = jnp.arange(NSUB, dtype=jnp.int32)
    sub_hot = (entry_sub[:, None] == sub_range[None, :]).astype(jnp.float32)
    gains = jnp.dot(sub_hot, shape_weight, precision=lax.Precision.HIGHEST)
    weighted = gains * payload.astype(jnp.float32)
    slot_hot = (slots[:, None] == jnp.arange(R, dtype=jnp.int32)[None, :]).astype(jnp.float32)
    per_rotor = jnp.dot(slot_hot.T, weighted, precision=lax.Precision.HIGHEST)
    partial_value = lax.psum_scatter(per_rotor, "slab", scatter_dimension=0, tiled=True)
    pooled = lax.psum(partial_value, "cross")
    pooled_b = (pooled * pool_scale).astype(jnp.bfloat16)
    drive = jnp.dot(pooled_b, w_in, preferred_element_type=jnp.float32)
    new_states = rotor_states + state_step * (drive - decay[None, :] * rotor_states)
    own_sources = jnp.dot(
        new_states.astype(jnp.bfloat16), w_out, preferred_element_type=jnp.float32
    ).astype(jnp.bfloat16)
    all_sources = lax.all_gather(own_sources, "slab", axis=0, tiled=True)
    rows = all_sources.reshape(R * NSUB, TILE)[slots * NSUB + entry_sub].astype(jnp.float32)
    forcing = jnp.zeros((tile_count, TILE), jnp.float32).at[entry_tile].add(rows)
    vertical = jnp.pad(velocity, ((0, 0), (0, 0), (0, 0), (1, 1)))
    upper = vertical[:, :, :, 2:]
    lower = vertical[:, :, :, :-2]
    padded = extended(velocity.astype(jnp.bfloat16), (("slab", 1), ("cross", 2)), 1).astype(
        velocity.dtype
    )
    east = padded[:, 2:, 1:-1, :]
    west = padded[:, :-2, 1:-1, :]
    north = padded[:, 1:-1, 2:, :]
    south = padded[:, 1:-1, :-2, :]
    advanced = combine_terms(velocity, east, west, north, south, upper, lower)
    advanced = advanced.at[0].add(-force_scale * forcing.reshape(local_x, local_y, local_z))
    return (advanced, new_states)


def solution(mesh):
    in_specs = (
        P(None, "slab", "cross", None),
        P(),
        P(),
        P(),
        P(),
        P("slab", None),
        P(),
        P(("slab", "cross"), None),
        P(("slab", "cross")),
        P(("slab", "cross")),
    )
    out_specs = (P(None, "slab", "cross", None), P("slab", None))
    return jax.shard_map(
        on_device, mesh=mesh, in_specs=in_specs, out_specs=out_specs, check_vma=False
    )
```

profile of v0, /device:TPU:0, one launch (start us, length us, event | category | flops | bytes accessed | tf_op | source)
XLA Modules:
  0.0 148.5 jit_solution(3841347414742956193)
XLA Ops:
  0.6 2.2 %convert_element_type.37 = bf16[3,16,64,256]{3,2,1,0:T(8,128)(2,1)S(1)} convert(f32[3,16,64,256]{3,2,1,0:T(8,128)} %param.12) | non-fusion elementwise | flops 786432 | bytes 4718592 | tf_op jit(solution)/shard_map/convert_element_type | solution.py:85
  2.8 0.7 fusion.19
  3.5 4.8 %collective-permute-start = (bf16[3,1,64,256]{3,2,1,0:T(8,128)(2,1)}, bf16[3,1,64,256]{3,2,1,0:T(8,128)(2,1)S(1)}, u32[]{:S(2)}, u32[]{:S(2)}) collective-permute-start(bf16[3,1,64,256]{3,2,1,0:T(8,128)(2,1)} %get-tuple-element.19), channel_id=1, source_target_pairs={{0,4},{4,8},{8,12},{12,16},{16,20},{20,24},{24,28},{1,5},{5,9},{9,... | collective-permute-start | bytes 294920 | tf_op jit(solution)/shard_map/ppermute | solution.py:26
  8.4 1.3 collective-permute-start.1
  9.7 4.0 %reshape.75 = bf16[3,2048,128]{2,1,0:T(8,128)(2,1)} reshape(f32[3,16,64,256]{3,2,1,0:T(8,128)} %param.12) | data formatting | bytes 4718592 | tf_op jit(solution)/shard_map/reshape | solution.py:62
  13.7 4.2 %copy.22 = bf16[3,2048,128]{2,0,1:T(4,128)(2,1)} copy(bf16[3,2048,128]{2,1,0:T(8,128)(2,1)} %reshape.75) | data formatting | bytes 3145728 | tf_op jit(solution)/shard_map/reshape | solution.py:62
  17.9 5.1 %gather_fusion = bf16[1024,3,128]{2,1,0:T(4,128)(2,1)S(1)} fusion(bf16[3,2048,128]{2,0,1:T(4,128)(2,1)} %copy.22, s32[1024]{0:T(1024)S(1)} %get-tuple-element.21), kind=kCustom, calls=%fused_computation | custom fusion | bytes 1576960 | tf_op jit(solution)/shard_map/jit(_take)/gather | solution.py:63
  23.0 1.3 fusion.7
  24.4 3.1 %copy.24 = f32[1024,3,128]{0,2,1:T(8,128)} copy(f32[1024,3,128]{2,0,1:T(8,128)} %fusion.7) | data formatting | bytes 3145728 | tf_op jit(solution)/shard_map/convert_element_type | solution.py:68
  27.4 3.0 %copy.25 = f32[1024,384]{1,0:T(8,128)} copy(f32[1024,384]{0,1:T(8,128)} %bitcast.16) | data formatting | bytes 3145728 | tf_op jit(solution)/shard_map/convert_element_type | solution.py:68
  30.6 0.8 fusion.11
  31.4 2.3 %fusion.2 = f32[32,384]{1,0:T(8,128)S(1)} fusion(f32[1024,384]{1,0:T(8,128)S(1)} %fusion.11, f32[1024,384]{1,0:T(8,128)} %copy.25, s32[1024]{0:T(1024)S(1)} %select_reduce_fusion), kind=kOutput, calls=%fused_computation.11 | convolution fusion | flops 151420928 | bytes 3198976 | tf_op jit(solution)/shard_map/dot_general | solution.py:70
  33.7 39.6 %all-reduce.1 = f32[32,384]{1,0:T(8,128)S(1)} all-reduce(f32[32,384]{1,0:T(8,128)S(1)} %fusion.2), channel_id=2, replica_groups=mesh['slab'=8,'cross'=4] {'slab'}, use_global_device_ids=true, to_apply=%region_1.2.clone | all-reduce | flops 12288 | bytes 98304
  73.4 0.6 dynamic-slice.8
  74.6 5.8 %psum.7 = f32[4,384]{1,0:T(4,128)S(1)} all-reduce(f32[4,384]{1,0:T(4,128)S(1)} %constant_dynamic-slice_fusion), channel_id=1, replica_groups=mesh['slab'=8,'cross'=4] {'cross'}, use_global_device_ids=true, to_apply=%region_2.3 | all-reduce | flops 1536 | bytes 12288 | tf_op jit(solution)/shard_map/psum | solution.py:72
  80.4 0.2 fusion.5
  80.6 4.6 %fusion = bf16[1,4,4096]{2,1,0:T(4,128)(2,1)S(1)} fusion(bf16[1024,4096]{1,0:T(8,128)(2,1)} %param.15, f32[4,1024]{1,0:T(4,128)S(1)} %fusion.5), kind=kOutput, calls=%fused_computation.6 | convolution fusion | flops 33574912 | bytes 8437760 | tf_op jit(solution)/shard_map/dot_general | solution.py:76
  85.2 30.8 %all-gather = bf16[8,4,4096]{2,1,0:T(4,128)(2,1)S(1)} all-gather(bf16[1,4,4096]{2,1,0:T(4,128)(2,1)S(1)} %fusion), channel_id=1, replica_groups=mesh['slab'=8,'cross'=4] {'slab'}, dimensions={0}, use_global_device_ids=true | all-gather | bytes 294912 | tf_op jit(solution)/shard_map/all_gather | solution.py:79
  116.0 1.0 reshape.76
  117.0 12.7 %scatter_custom_fusion = f32[2048,128]{1,0:T(8,128)S(1)} fusion(s32[1024]{0:T(1024)S(1)} %get-tuple-element.22, f32[]{:T(128)} %constant.53.clone.1, bf16[1024,128]{1,0:T(8,128)(2,1)} %reshape.76, s32[1024]{0:T(1024)S(1)} %fusion.15), kind=kCustom, calls=%fused_computation.23 | custom fusion | flops 262144 | bytes 1314820 | tf_op jit(solution)/shard_map/scatter-add | solution.py:81
  129.7 1.0 broadcast_multiply_fusion
  130.8 1.7 %pad_maximum_fusion.2 = (bf16[3,18,1,256]{3,2,1,0:T(2,128)(2,1)}, bf16[3,18,1,256]{3,2,1,0:T(2,128)(2,1)}) fusion(bf16[3,1,64,256]{3,2,1,0:T(8,128)(2,1)} %collective-permute-done.1, bf16[3,16,64,256]{3,2,1,0:T(8,128)(2,1)S(1)} %convert_element_type.37, bf16[3,1,64,256]{3,2,1,0:T(8,128)(2,1)S(1)} %collective-permute-done), kind=kLoop, calls=%fused_computation.35 | loop fusion | flops 165888 | bytes 1824768 | tf_op jit(solution)/shard_map/slice | solution.py:23
  132.5 1.9 %collective-permute-start.2 = (bf16[3,18,1,256]{3,2,1,0:T(2,128)(2,1)}, bf16[3,18,1,256]{3,2,1,0:T(2,128)(2,1)}, u32[]{:S(2)}, u32[]{:S(2)}) collective-permute-start(bf16[3,18,1,256]{3,2,1,0:T(2,128)(2,1)} %get-tuple-element.17), channel_id=1, source_target_pairs={{0,1},{1,2},{2,3},{4,5},{5,6},{6,7},{8,9},{9,10},{10,11},{12,13},{... | collective-permute-start | bytes 82952 | tf_op jit(solution)/shard_map/ppermute | solution.py:26
  134.4 1.5 collective-permute-start.3
  135.9 1.8 %multiply_bitcast_fusion.2 = (f32[16,64,256]{2,1,0:T(8,128)}, f32[16,64,256]{2,1,0:T(8,128)}, f32[16,64,256]{2,1,0:T(8,128)}) fusion(f32[3,16,64,256]{3,2,1,0:T(8,128)S(1)} %copy-done.1), kind=kLoop, calls=%fused_computation.20 | loop fusion | flops 786432 | bytes 6291456 | tf_op jit(solution)/shard_map/mul | solution.py:38
  137.6 1.5 %mul.142 = f32[1,16,64,256]{3,2,1,0:T(8,128)S(1)} reshape(f32[2048,128]{1,0:T(8,128)} %broadcast_multiply_fusion) | data formatting | bytes 2097152 | tf_op jit(solution)/shard_map/mul | solution.py:93
  139.2 1.8 %maximum_convert_fusion = f32[3,18,66,256]{3,2,1,0:T(8,128)S(1)} fusion(bf16[3,18,1,256]{3,2,1,0:T(2,128)(2,1)} %collective-permute-done.3, bf16[3,1,64,256]{3,2,1,0:T(8,128)(2,1)} %collective-permute-done.1, bf16[3,16,64,256]{3,2,1,0:T(8,128)(2,1)S(1)} %convert_element_type.37, bf16[3,1,64,256]{3,2,1,0:T(8,128)(2,1)S(1)} %collective-permute-done, ...), kind=kLoop, calls=%fused_computation.8 | loop fusion | flops 9123840 | bytes 5474304 | tf_op jit(solution)/shard_map/convert_element_type | solution.py:85
  141.2 0.3 copy-done.4
  141.5 0.3 copy-done.5
  141.8 4.8 %multiply_add_fusion = f32[3,16,64,256]{3,2,1,0:T(8,128)S(1)} fusion(f32[3,16,64,256]{3,2,1,0:T(8,128)S(1)} %copy-done.2, f32[3,18,66,256]{3,2,1,0:T(8,128)S(1)} %maximum_convert_fusion, f32[16,64,256]{2,1,0:T(8,128)S(1)} %copy-done.5, f32[16,64,256]{2,1,0:T(8,128)} %get-tuple-element.16, f32[16,64,256]{2,1,0:T(8,128)S(1)} %copy-done.4), kind=kLoop, calls=%fused_computation.7 | loop fusion | flops 14942208 | bytes 22020096 | tf_op jit(solution)/shard_map/add | solution.py:42
  146.6 0.3 fusion.6
  146.9 1.7 %copy-done.3 = f32[3,16,64,256]{3,2,1,0:T(8,128)} copy-done((f32[3,16,64,256]{3,2,1,0:T(8,128)}, f32[3,16,64,256]{3,2,1,0:T(8,128)S(1)}, u32[]{:S(2)}) %copy-start.3) | copy-done | bytes 3145752
  (36 shorter events, 0.3 us)
Async XLA Ops:
  0.6 79.7 %copy-start = (bf16[384,1024]{1,0:T(8,128)(2,1)S(1)}, bf16[384,1024]{1,0:T(8,128)(2,1)}, u32[]{:S(2)}) copy-start(bf16[384,1024]{1,0:T(8,128)(2,1)} %param.14) | copy-start | bytes 2359300
  2.8 10.8 %copy-start.10 = (s32[1024]{0:T(1024)S(1)}, s32[1024]{0:T(1024)}, u32[]{:S(2)}) copy-start(s32[1024]{0:T(1024)} %param.20) | copy-start | bytes 12292
  3.5 127.2 %collective-permute-start = (bf16[3,1,64,256]{3,2,1,0:T(8,128)(2,1)}, bf16[3,1,64,256]{3,2,1,0:T(8,128)(2,1)S(1)}, u32[]{:S(2)}, u32[]{:S(2)}) collective-permute-start(bf16[3,1,64,256]{3,2,1,0:T(8,128)(2,1)} %get-tuple-element.19), channel_id=1, source_target_pairs={{0,4},{4,8},{8,12},{12,16},{16,20},{20,24},{24,28},{1,5},{5,9},{9,... | collective-permute-start | bytes 294920 | tf_op jit(solution)/shard_map/ppermute | solution.py:26
  8.4 122.4 %collective-permute-start.1 = (bf16[3,1,64,256]{3,2,1,0:T(8,128)(2,1)}, bf16[3,1,64,256]{3,2,1,0:T(8,128)(2,1)}, u32[]{:S(2)}, u32[]{:S(2)}) collective-permute-start(bf16[3,1,64,256]{3,2,1,0:T(8,128)(2,1)} %get-tuple-element.20), channel_id=1, source_target_pairs={{4,0},{8,4},{12,8},{16,12},{20,16},{24,20},{28,24},{5,1},{9,5},{13... | collective-permute-start | bytes 294920 | tf_op jit(solution)/shard_map/ppermute | solution.py:28
  24.4 6.1 %copy-start.12 = (s32[1024,1]{0,1:T(1,128)S(1)}, s32[1024,1]{0,1:T(1,128)}, u32[]{:S(2)}) copy-start(s32[1024,1]{0,1:T(1,128)} %param.19) | copy-start | bytes 12292
  24.4 6.1 %copy-start.13 = (s32[32]{0:T(128)S(1)}, s32[32]{0:T(128)}, u32[]{:S(2)}) copy-start(s32[32]{0:T(128)} %param.18) | copy-start | bytes 388
  24.4 6.2 %copy-start.7 = (f32[32,384]{1,0:T(8,128)S(1)}, f32[32,384]{1,0:T(8,128)}, u32[]{:S(2)}) copy-start(f32[32,384]{1,0:T(8,128)} %param.13) | copy-start | bytes 147460
  24.4 6.2 %copy-start.8 = (s32[1024]{0:T(1024)S(1)}, s32[1024]{0:T(1024)}, u32[]{:S(2)}) copy-start(s32[1024]{0:T(1024)} %param.21) | copy-start | bytes 12292
  30.5 42.9 %copy-start.14 = (u32[32]{0:T(128)S(1)}, u32[32]{0:T(128)}, u32[]{:S(2)}) copy-start(u32[32]{0:T(128)} %constant.71) | copy-start | bytes 388
  30.5 49.9 %copy-start.9 = (f32[4,1024]{1,0:T(4,128)S(1)}, f32[4,1024]{1,0:T(4,128)}, u32[]{:S(2)}) copy-start(f32[4,1024]{1,0:T(4,128)} %param.17) | copy-start | bytes 49156
  30.5 49.9 %copy-start.11 = (f32[1024]{0:T(1024)S(1)}, f32[1024]{0:T(1024)}, u32[]{:S(2)}) copy-start(f32[1024]{0:T(1024)} %param.16) | copy-start | bytes 12292
  80.6 4.6 %copy-start.6 = (f32[4,1024]{1,0:T(4,128)}, f32[4,1024]{1,0:T(4,128)S(1)}, u32[]{:S(2)}) copy-start(f32[4,1024]{1,0:T(4,128)S(1)} %fusion.5) | copy-start | bytes 49156
  129.7 6.1 %copy-start.1 = (f32[3,16,64,256]{3,2,1,0:T(8,128)S(1)}, f32[3,16,64,256]{3,2,1,0:T(8,128)}, u32[]{:S(2)}) copy-start(f32[3,16,64,256]{3,2,1,0:T(8,128)} %param.12) | copy-start | bytes 9437188
  132.5 6.7 %collective-permute-start.2 = (bf16[3,18,1,256]{3,2,1,0:T(2,128)(2,1)}, bf16[3,18,1,256]{3,2,1,0:T(2,128)(2,1)}, u32[]{:S(2)}, u32[]{:S(2)}) collective-permute-start(bf16[3,18,1,256]{3,2,1,0:T(2,128)(2,1)} %get-tuple-element.17), channel_id=1, source_target_pairs={{0,1},{1,2},{2,3},{4,5},{5,6},{6,7},{8,9},{9,10},{10,11},{12,13},{... | collective-permute-start | bytes 82952 | tf_op jit(solution)/shard_map/ppermute | solution.py:26
  134.4 4.9 %collective-permute-start.3 = (bf16[3,18,1,256]{3,2,1,0:T(2,128)(2,1)}, bf16[3,18,1,256]{3,2,1,0:T(2,128)(2,1)}, u32[]{:S(2)}, u32[]{:S(2)}) collective-permute-start(bf16[3,18,1,256]{3,2,1,0:T(2,128)(2,1)} %get-tuple-element.18), channel_id=1, source_target_pairs={{1,0},{2,1},{3,2},{5,4},{6,5},{7,6},{9,8},{10,9},{11,10},{13,12},{... | collective-permute-start | bytes 82952 | tf_op jit(solution)/shard_map/ppermute | solution.py:28
  139.2 2.0 %copy-start.2 = (f32[3,16,64,256]{3,2,1,0:T(8,128)S(1)}, f32[3,16,64,256]{3,2,1,0:T(8,128)}, u32[]{:S(2)}) copy-start(f32[3,16,64,256]{3,2,1,0:T(8,128)} %param.12) | copy-start | bytes 9437188
  139.2 2.3 %copy-start.4 = (f32[16,64,256]{2,1,0:T(8,128)S(1)}, f32[16,64,256]{2,1,0:T(8,128)}, u32[]{:S(2)}) copy-start(f32[16,64,256]{2,1,0:T(8,128)} %get-tuple-element.14) | copy-start | bytes 3145732
  139.2 2.6 %copy-start.5 = (f32[16,64,256]{2,1,0:T(8,128)S(1)}, f32[16,64,256]{2,1,0:T(8,128)}, u32[]{:S(2)}) copy-start(f32[16,64,256]{2,1,0:T(8,128)} %get-tuple-element.15) | copy-start | bytes 3145732
  146.9 1.7 %copy-start.3 = (f32[3,16,64,256]{3,2,1,0:T(8,128)}, f32[3,16,64,256]{3,2,1,0:T(8,128)S(1)}, u32[]{:S(2)}) copy-start(f32[3,16,64,256]{3,2,1,0:T(8,128)S(1)} %fusion.6) | copy-start | bytes 9437188
where the time goes:
time: 151 us; the launch traced here: 149 us
  blocking collectives  76.1 us (50%)
  other arithmetic  27.8 us (18%)
  local copies, waits for them, and re-layouts  25.6 us (17%)
  starting transfers between devices  9.49 us (6%)
  matrix products  7.92 us (5%)
  between operations  1.58 us (1%)
    unnamed x1, blocking collectives  39.6 us
    all_gather x1, blocking collectives, on_device(): all_sources = lax.all_gather(own_sources, 'slab', axis=0, tiled=True)  30.8 us
    scatter-add x1, other arithmetic, on_device(): jnp.zeros((tile_count, TILE), jnp.float32).at[entry_tile].add(rows)  12.7 us
    reshape x2, local copies, waits for them, and re-layouts, on_device(): flat_cells = velocity.reshape(3, tile_count, TILE)  8.15 us
    ppermute x2, starting transfers between devices, extended(): lax.ppermute(tail, axis, [(i, (i + 1) % count) for i in range(ends)])  6.73 us
    convert_element_type x2, local copies, waits for them, and re-layouts, on_device(): weighted = gains * payload.astype(jnp.float32)  6.1 us
    psum x1, blocking collectives, on_device(): pooled = lax.psum(partial_value, 'cross')  5.76 us
    gather x1, local copies, waits for them, and re-layouts, on_device(): picked = jnp.take(flat_cells, entry_tile, axis=1)  5.14 us
  transfers between devices with their start and end apart: 4, of which 0 were waited for; matrix products, arithmetic and copies ran while one was open for 32% of the time, Pallas kernels for 0%

commit v1 on v0

v1 whole, which is shorter than its diff:
```python
import functools

import jax
import jax.numpy as jnp
from jax import lax
from jax.experimental import pallas as pl
from jax.experimental.pallas import tpu as pltpu
from jax.sharding import PartitionSpec as P

TILE = 128

time_step = 0.1
viscosity = 0.3
pool_scale = 1.0 / 64.0
state_step = 0.5
force_scale = 0.5

BOTH = ("slab", "cross")
F32 = jnp.float32
BF16 = jnp.bfloat16


def lanes(rows):
    return lax.broadcasted_iota(jnp.int32, (rows, TILE), 1)


def sublanes(rows):
    return lax.broadcasted_iota(jnp.int32, (rows, TILE), 0)


def as_column(row):
    return jnp.transpose(jnp.broadcast_to(row, (TILE, TILE)))


def hot(mask):
    return jnp.where(mask, 1.0, 0.0).astype(BF16)


def slots_of(rotor_ref, slot_ref):
    rotors = rotor_ref[...]
    slots = jnp.zeros_like(rotors)
    for rotor in range(slot_ref.shape[0]):
        slots = jnp.where(rotors == rotor, slot_ref[rotor], slots)
    return slots


def pool_kernel(
    tile_ref,
    rotor_ref,
    sub_ref,
    slot_ref,
    weight_ref,
    velocity_ref,
    part_ref,
    west_ref,
    east_ref,
    south_ref,
    north_ref,
    cells,
    place_hot,
    gains,
    half_column,
    sems,
):
    parts, size_x, size_y, size_z = velocity_ref.shape
    columns = size_x * size_y
    halves = size_z // TILE
    groups = tile_ref.shape[0]
    entries = groups * TILE
    rotors = slot_ref.shape[0]
    subs = weight_ref.shape[0]
    copies = [
        pltpu.make_async_copy(velocity_ref.at[c], cells.at[c], sems.at[c]) for c in range(parts)
    ]
    for copy in copies:
        copy.start()
    weight = weight_ref[...]
    high = weight.astype(BF16)
    rest = weight - high.astype(F32)
    middle = rest.astype(BF16)
    low = (rest - middle.astype(F32)).astype(BF16)
    weight_parts = jnp.concatenate([high, middle, low], axis=0)
    sub_hot = []
    place_rows = tile_ref[...] // halves
    half_rows = tile_ref[...] % halves
    for group in range(groups):
        half_column[pl.ds(group * TILE, TILE), :] = as_column(half_rows[group : group + 1, :])
        place = as_column(place_rows[group : group + 1, :])
        for block in range(columns // TILE):
            place_hot[pl.ds(group * TILE, TILE), pl.ds(block * TILE, TILE)] = hot(
                place == lanes(TILE) + block * TILE
            )
        sub = as_column(sub_ref[group : group + 1, :])
        wide = jnp.concatenate([sub[:, :subs]] * 3, axis=1)
        index = lax.broadcasted_iota(jnp.int32, (TILE, subs), 1)
        sub_hot.append(hot(wide == jnp.concatenate([index] * 3, axis=1)))
    gains[...] = jnp.dot(
        jnp.concatenate(sub_hot, axis=0), weight_parts, preferred_element_type=F32
    )
    slots = slots_of(rotor_ref, slot_ref)
    slot_hot = jnp.concatenate(
        [hot(slots[g : g + 1, :] == sublanes(rotors)) for g in range(groups)], axis=1
    )
    half = half_column[...]
    for c in range(parts):
        copies[c].wait()
        flat = cells[c].reshape(columns, size_z).astype(BF16)
        found = jnp.dot(place_hot[...], flat, preferred_element_type=F32)
        sample = found[:, :TILE]
        for h in range(1, halves):
            sample = jnp.where(half == h, found[:, h * TILE : (h + 1) * TILE], sample)
        weighted = sample * gains[:, c * TILE : (c + 1) * TILE]
        high = weighted.astype(BF16)
        rest = weighted - high.astype(F32)
        middle = rest.astype(BF16)
        low = (rest - middle.astype(F32)).astype(BF16)
        sums = jnp.dot(
            slot_hot, jnp.concatenate([high, middle, low], axis=1), preferred_element_type=F32
        )
        part_ref[:, c * TILE : (c + 1) * TILE] = (
            sums[:, 2 * TILE :] + sums[:, TILE : 2 * TILE] + sums[:, :TILE]
        )
        west_ref[c] = cells[c, 0].astype(BF16)
        east_ref[c] = cells[c, size_x - 1].astype(BF16)
        south_ref[c] = cells[c, :, 0, :].astype(BF16)
        north_ref[c] = cells[c, :, size_y - 1, :].astype(BF16)


def stencil_kernel(velocity_ref, west_ref, east_ref, south_ref, north_ref, out_ref, cells, result, sems, out_sems):
    parts, size_x, size_y, size_z = velocity_ref.shape
    chunks = sems.shape[0]
    depth = size_x // chunks

    def load(chunk):
        at = pl.ds(chunk * depth, depth)
        return pltpu.make_async_copy(velocity_ref.at[:, at], cells.at[:, at], sems.at[chunk])

    def store(chunk):
        at = pl.ds(chunk * depth, depth)
        return pltpu.make_async_copy(result.at[:, at], out_ref.at[:, at], out_sems.at[chunk])

    for chunk in range(chunks):
        load(chunk).start()
    row = lax.broadcasted_iota(jnp.int32, (size_y, size_z), 0)
    lane = lax.broadcasted_iota(jnp.int32, (size_y, size_z), 1)
    load(0).wait()
    for chunk in range(chunks):
        if chunk + 1 < chunks:
            load(chunk + 1).wait()
        for x in range(chunk * depth, (chunk + 1) * depth):
            wind = [cells[c, x] for c in range(parts)]
            for c in range(parts):
                here = wind[c]
                west = cells[c, x - 1] if x > 0 else west_ref[c].astype(F32)
                east = cells[c, x + 1] if x + 1 < size_x else east_ref[c].astype(F32)
                south = jnp.where(
                    row == 0, south_ref[c, x : x + 1, :].astype(F32), pltpu.roll(here, 1, 0)
                )
                north = jnp.where(
                    row == size_y - 1,
                    north_ref[c, x : x + 1, :].astype(F32),
                    pltpu.roll(here, size_y - 1, 0),
                )
                lower = jnp.where(lane == 0, 0.0, pltpu.roll(here, 1, 1))
                upper = jnp.where(lane == size_z - 1, 0.0, pltpu.roll(here, size_z - 1, 1))
                laplace = east + west + north + south + upper + lower - 6.0 * here
                advect = (
                    wind[0] * ((east - west) * 0.5)
                    + wind[1] * ((north - south) * 0.5)
                    + wind[2] * ((upper - lower) * 0.5)
                )
                result[c, x] = here + time_step * (viscosity * laplace - advect)
        store(chunk).start()
    for chunk in range(chunks):
        store(chunk).wait()


def rotor_kernel(
    index_ref,
    slot_ref,
    tile_ref,
    rotor_ref,
    sub_ref,
    pooled_ref,
    w_in_ref,
    w_out_ref,
    decay_ref,
    states_ref,
    field_ref,
    out_ref,
    new_ref,
    wind,
    states,
    by_slab,
    source_rows,
    key_hot,
    place_hot,
    sems,
):
    slabs, rows, width = states_ref.shape
    rotors = slabs * rows
    _, size_x, size_y, size_z = field_ref.shape
    columns = size_x * size_y
    halves = size_z // TILE
    groups = tile_ref.shape[0]
    subs = w_out_ref.shape[1] // TILE
    me = index_ref[0]
    load = pltpu.make_async_copy(field_ref.at[0], wind, sems.at[0])
    load.start()
    slots = slots_of(rotor_ref, slot_ref)
    for j in range(slabs):
        states[j * rows : (j + 1) * rows, :] = states_ref[me ^ j]
    pooled = (pooled_ref[...] * pool_scale).astype(BF16)
    drive = jnp.dot(pooled, w_in_ref[...], preferred_element_type=F32)
    old = states[...]
    new = old + state_step * (drive - decay_ref[...] * old)
    for j in range(slabs):
        by_slab[j] = new[j * rows : (j + 1) * rows, :]
    new_ref[...] = by_slab[me]
    new_b = new.astype(BF16)
    keys = sub_ref[...] * rotors + slots
    tiles = tile_ref[...]
    place_rows = tiles // halves
    half_rows = tiles % halves
    for group in range(groups):
        key = as_column(keys[group : group + 1, :])
        at = pl.ds(group * TILE, TILE)
        for block in range(subs * rotors // TILE):
            key_hot[at, pl.ds(block * TILE, TILE)] = hot(key == lanes(TILE) + block * TILE)
        for block in range(columns // TILE):
            place_hot[pl.ds(block * TILE, TILE), at] = hot(
                place_rows[group : group + 1, :] == sublanes(TILE) + block * TILE
            )
    sources = jnp.dot(new_b, w_out_ref[...], preferred_element_type=F32).astype(BF16)
    for sub in range(subs):
        source_rows[sub * rotors : (sub + 1) * rotors, :] = sources[:, sub * TILE : (sub + 1) * TILE]
    taken = jnp.dot(key_hot[...], source_rows[...], preferred_element_type=F32).astype(BF16)
    half = jnp.concatenate([as_column(half_rows[g : g + 1, :]) for g in range(groups)], axis=0)
    spread = jnp.concatenate(
        [jnp.where(half == h, taken.astype(F32), 0.0).astype(BF16) for h in range(halves)], axis=1
    )
    forcing = jnp.dot(place_hot[...], spread, preferred_element_type=F32)
    load.wait()
    wind[...] = wind[...] - force_scale * forcing.reshape(size_x, size_y, size_z)
    store = pltpu.make_async_copy(wind, out_ref.at[0], sems.at[1])
    store.start()
    store.wait()


def xor_groups(bits):
    first = bits % 2
    groups = [(0,)] if first else []
    return groups + [(b, b + 1) for b in range(first, bits, 2)]


def offsets_of(group):
    found = [0]
    for bit in group:
        found = found + [offset | (1 << bit) for offset in found]
    return found[1:]


def exchange(value, axis, count, offset):
    return lax.ppermute(value, axis, [(i, i ^ offset) for i in range(count)])


def sum_all(value, axis, count):
    for group in xor_groups(count.bit_length() - 1):
        received = [exchange(value, axis, count, offset) for offset in offsets_of(group)]
        for other in received:
            value = value + other
    return value


def gather_xor(value, axis, count):
    blocks = value[None]
    for bit in range(count.bit_length() - 1):
        blocks = jnp.concatenate([blocks, exchange(blocks, axis, count, 1 << bit)], axis=0)
    return blocks


def vmem(count):
    return [pl.BlockSpec(memory_space=pltpu.VMEM)] * count


SMEM = pl.BlockSpec(memory_space=pltpu.SMEM)
ANY = pl.BlockSpec(memory_space=pl.ANY)


def on_device(
    slabs,
    crosses,
    velocity,
    shape_weight,
    w_in,
    w_out,
    decay,
    rotor_states,
    slot_of_rotor,
    entry_rotor,
    entry_tile,
    entry_sub,
):
    parts, size_x, size_y, size_z = velocity.shape
    columns = size_x * size_y
    entries = entry_tile.shape[0]
    groups = entries // TILE
    rotors = slot_of_rotor.shape[0]
    subs = shape_weight.shape[0]
    width = w_in.shape[1]
    rows = rotor_states.shape[0]
    tile = entry_tile.reshape(groups, TILE)
    rotor = entry_rotor.reshape(groups, TILE)
    sub = entry_sub.reshape(groups, TILE)

    gathered = gather_xor(rotor_states, "slab", slabs)
    part, west, east, south, north = pl.pallas_call(
        pool_kernel,
        out_shape=(
            jax.ShapeDtypeStruct((rotors, parts * TILE), F32),
            jax.ShapeDtypeStruct((parts, size_y, size_z), BF16),
            jax.ShapeDtypeStruct((parts, size_y, size_z), BF16),
            jax.ShapeDtypeStruct((parts, size_x, size_z), BF16),
            jax.ShapeDtypeStruct((parts, size_x, size_z), BF16),
        ),
        in_specs=vmem(3) + [SMEM] + vmem(1) + [ANY],
        out_specs=tuple(vmem(5)),
        scratch_shapes=[
            pltpu.VMEM(velocity.shape, F32),
            pltpu.VMEM((entries, columns), BF16),
            pltpu.VMEM((entries, parts * TILE), F32),
            pltpu.VMEM((entries, TILE), jnp.int32),
            pltpu.SemaphoreType.DMA((parts,)),
        ],
        compiler_params=pltpu.CompilerParams(vmem_limit_bytes=24 << 20),
        cost_estimate=pl.CostEstimate(
            flops=2 * entries * columns * parts * size_z,
            bytes_accessed=velocity.size * 4,
            transcendentals=0,
        ),
        name="pool",
    )(tile, rotor, sub, slot_of_rotor, shape_weight, velocity)

    pooled = sum_all(part, BOTH, slabs * crosses)

    up = lambda count: [(i, i + 1) for i in range(count - 1)]
    down = lambda count: [(i + 1, i) for i in range(count - 1)]
    from_west = lax.ppermute(east, "slab", up(slabs))
    from_east = lax.ppermute(west, "slab", down(slabs))
    from_south = lax.ppermute(north, "cross", up(crosses))
    from_north = lax.ppermute(south, "cross", down(crosses))
    chunks = 4
    field = pl.pallas_call(
        stencil_kernel,
        out_shape=jax.ShapeDtypeStruct(velocity.shape, F32),
        in_specs=[ANY] + vmem(4),
        out_specs=ANY,
        scratch_shapes=[
            pltpu.VMEM(velocity.shape, F32),
            pltpu.VMEM(velocity.shape, F32),
            pltpu.SemaphoreType.DMA((chunks,)),
            pltpu.SemaphoreType.DMA((chunks,)),
        ],
        compiler_params=pltpu.CompilerParams(vmem_limit_bytes=16 << 20),
        cost_estimate=pl.CostEstimate(
            flops=30 * velocity.size, bytes_accessed=velocity.size * 8, transcendentals=0
        ),
        name="stencil",
    )(velocity, from_west, from_east, from_south, from_north)

    index = lax.axis_index("slab").astype(jnp.int32).reshape(1)
    return pl.pallas_call(
        rotor_kernel,
        out_shape=(
            jax.ShapeDtypeStruct(velocity.shape, F32),
            jax.ShapeDtypeStruct(rotor_states.shape, F32),
        ),
        in_specs=[SMEM, SMEM] + vmem(8) + [ANY],
        out_specs=(ANY, pl.BlockSpec(memory_space=pltpu.VMEM)),
        scratch_shapes=[
            pltpu.VMEM((size_x, size_y, size_z), F32),
            pltpu.VMEM((rotors, width), F32),
            pltpu.VMEM((slabs, rows, width), F32),
            pltpu.VMEM((subs * rotors, TILE), BF16),
            pltpu.VMEM((entries, subs * rotors), BF16),
            pltpu.VMEM((columns, entries), BF16),
            pltpu.SemaphoreType.DMA((2,)),
        ],
        input_output_aliases={10: 0},
        compiler_params=pltpu.CompilerParams(vmem_limit_bytes=32 << 20),
        cost_estimate=pl.CostEstimate(
            flops=4 * entries * columns * size_z, bytes_accessed=w_out.size * 2, transcendentals=0
        ),
        name="rotors",
    )(index, slot_of_rotor, tile, rotor, sub, pooled, w_in, w_out, decay[None, :], gathered, field)


def solution(mesh):
    slabs, crosses = mesh.shape["slab"], mesh.shape["cross"]
    in_specs = (
        P(None, "slab", "cross", None),
        P(),
        P(),
        P(),
        P(),
        P("slab", None),
        P(),
        P(("slab", "cross"), None),
        P(("slab", "cross")),
        P(("slab", "cross")),
    )
    out_specs = (P(None, "slab", "cross", None), P("slab", None))
    return jax.shard_map(
        functools.partial(on_device, slabs, crosses),
        mesh=mesh,
        in_specs=in_specs,
        out_specs=out_specs,
        check_vma=False,
    )
```

time: 151 us -> 56.6 us (0.37); the launches traced: 149 us -> 56.1 us
  blocking collectives: 76.1 us -> 0 us
  other arithmetic: 27.8 us -> 1.51 us
  starting transfers between devices: 9.49 us -> 27 us
  Pallas kernels: 0 us -> 16.9 us
  local copies, waits for them, and re-layouts: 25.6 us -> 8.82 us
  matrix products: 7.92 us -> 0 us
    unnamed x1 -> x0, blocking collectives: 39.6 us -> none
    all_gather x1 -> x0, blocking collectives: 30.8 us -> none  [on_device(): all_sources = lax.all_gather(own_sources, 'slab', axis=0, tiled=True)]
    ppermute x4 -> x14, starting transfers between devices: 9.49 us -> 27 us  [the longest x10 19.1 us: exchange(): return lax.ppermute(value, axis, [(i, i ^ offset) for i in range(count)])]
    pallas_call x0 -> x3, Pallas kernels: none -> 16.9 us  [the longest x1 6.35 us: on_device(): pl.pallas_call(rotor_kernel, out_shape=(jax.ShapeDtypeStruct(velocity.sha...]
    scatter-add x2 -> x0, other arithmetic: 13 us -> none  [the longest x1 12.7 us: on_device(): jnp.zeros((tile_count, TILE), jnp.float32).at[entry_tile].add(rows)]
    reshape x3 -> x0, local copies, waits for them, and re-layouts: 9.14 us -> none  [the longest x2 8.15 us: on_device(): flat_cells = velocity.reshape(3, tile_count, TILE)]
    dot_general x4 -> x0, matrix products: 7.92 us -> none  [the longest x1 4.58 us: on_device(): jnp.dot(new_states.astype(jnp.bfloat16), w_out, preferred_element_type=jn...]
    convert_element_type x2 -> x0, local copies, waits for them, and re-layouts: 6.1 us -> none  [on_device(): weighted = gains * payload.astype(jnp.float32)]
  transfers between devices with their start and end apart: 4 -> 14, of which waited for: 0 -> 2; matrix products, arithmetic and copies ran while one was open for 32% -> 3% of each run, Pallas kernels for 0% -> 19%
where the time goes in v1:
time: 56.6 us; the launch traced here: 56.1 us
  starting transfers between devices  27 us (48%)
  Pallas kernels  16.9 us (30%)
  local copies, waits for them, and re-layouts  8.82 us (16%)
  other arithmetic  1.51 us (3%)
  waiting for transfers between devices  0.98 us (2%)
  between operations  0.89 us (2%)
    ppermute x10, starting transfers between devices, exchange(): return lax.ppermute(value, axis, [(i, i ^ offset) for i in range(count)])  19.1 us
    unnamed x30, local copies, waits for them, and re-layouts  8.82 us
    pallas_call x1, Pallas kernels, on_device(): pl.pallas_call(rotor_kernel, out_shape=(jax.ShapeDtypeStruct(velocity.sha...  6.35 us
    pallas_call x1, Pallas kernels, on_device(): pl.pallas_call(pool_kernel, out_shape=(jax.ShapeDtypeStruct((rotors, part...  5.85 us
    pallas_call x1, Pallas kernels, on_device(): pl.pallas_call(stencil_kernel, out_shape=jax.ShapeDtypeStruct(velocity.sh...  4.65 us
    ppermute x1, starting transfers between devices, on_device(): from_west = lax.ppermute(east, 'slab', up(slabs))  3.24 us
    ppermute x1, starting transfers between devices, on_device(): from_south = lax.ppermute(north, 'cross', up(crosses))  2.09 us
    ppermute x1, starting transfers between devices, on_device(): from_north = lax.ppermute(south, 'cross', down(crosses))  1.29 us
  transfers between devices with their start and end apart: 14, of which 2 were waited for; matrix products, arithmetic and copies ran while one was open for 3% of the time, Pallas kernels for 19%

profile of v1, /device:TPU:0, one launch (start us, length us, event | category | flops | bytes accessed | tf_op | source)
XLA Modules:
  0.0 56.1 jit_solution(14989466124284550273)
XLA Ops:
  0.6 3.0 %collective-permute-start.7 = (f32[1,4,1024]{2,1,0:T(4,128)}, f32[1,4,1024]{2,1,0:T(4,128)S(1)}, u32[]{:S(2)}, u32[]{:S(2)}) collective-permute-start(f32[1,4,1024]{2,1,0:T(4,128)} %bitcast.13), channel_id=1, source_target_pairs={{0,4},{4,0},{8,12},{12,8},{16,20},{20,16},{24,28},{28,24},{1,5},{5... | collective-permute-start | bytes 49160 | tf_op jit(solution)/shard_map/ppermute | solution.py:264
  3.6 1.9 %copy-done.1 = f32[3,16,64,256]{3,2,1,0:T(8,128)S(1)} copy-done((f32[3,16,64,256]{3,2,1,0:T(8,128)S(1)}, f32[3,16,64,256]{3,2,1,0:T(8,128)}, u32[]{:S(2)}) %copy-start.1) | copy-done | bytes 3145752
  5.5 0.7 %copy-done.4 = s32[1024]{0:T(1024)S(1)} copy-done((s32[1024]{0:T(1024)S(1)}, s32[1024]{0:T(1024)}, u32[]{:S(2)}) %copy-start.4) | copy-done | bytes 4120
  6.2 0.7 %copy-done.6 = s32[1024,1]{0,1:T(1,128)S(1)} copy-done((s32[1024,1]{0,1:T(1,128)S(1)}, s32[1024,1]{0,1:T(1,128)}, u32[]{:S(2)}) %copy-start.6) | copy-done | bytes 4120
  6.9 0.7 %copy-done.8 = s32[1024]{0:T(1024)S(1)} copy-done((s32[1024]{0:T(1024)S(1)}, s32[1024]{0:T(1024)}, u32[]{:S(2)}) %copy-start.8) | copy-done | bytes 4120
  7.6 0.7 %copy-done.11 = s32[32]{0:T(128)S(1)} copy-done((s32[32]{0:T(128)S(1)}, s32[32]{0:T(128)}, u32[]{:S(2)}) %copy-start.11) | copy-done | bytes 152
  8.2 0.8 %copy-done.13 = f32[32,384]{1,0:T(8,128)S(1)} copy-done((f32[32,384]{1,0:T(8,128)S(1)}, f32[32,384]{1,0:T(8,128)}, u32[]{:S(2)}) %copy-start.13) | copy-done | bytes 49176
  9.0 5.9 %pool.1 = (f32[32,384]{1,0:T(8,128)S(1)}, bf16[3,64,256]{2,1,0:T(8,128)(2,1)S(1)}, bf16[3,64,256]{2,1,0:T(8,128)(2,1)S(1)}, bf16[3,16,256]{2,1,0:T(8,128)(2,1)S(1)}, bf16[3,16,256]{2,1,0:T(8,128)(2,1)S(1)}) custom-call(s32[8,128]{1,0:T(8,128)S(1)} %bitcast.6, s32[8,128]{1,0:T(8,128)S(1)} %bitcast.8, s32[8,128]{1,0:T(8,128)S(1)} %bitcast.10, ...), custom_call_target="tpu_custom_call" | custom-call | flops 1610612736 | bytes 3145728 | tf_op jit(solution)/shard_map/pool/pallas_call | solution.py:317
  14.9 0.1 collective-permute-start
  15.0 0.6 %pad_maximum_fusion.2 = f32[2,4,1024]{2,1,0:T(4,128)} fusion(f32[1,4,1024]{2,1,0:T(4,128)S(1)} %collective-permute-done.7, f32[1,4,1024]{2,1,0:T(4,128)S(1)} %bitcast.14), kind=kLoop, calls=%fused_computation.4 | loop fusion | flops 8192 | bytes 65536 | tf_op jit(solution)/shard_map/concatenate | solution.py:278
  15.6 1.6 %collective-permute-start.8 = (f32[2,4,1024]{2,1,0:T(4,128)}, f32[2,4,1024]{2,1,0:T(4,128)S(1)}, u32[]{:S(2)}, u32[]{:S(2)}) collective-permute-start(f32[2,4,1024]{2,1,0:T(4,128)} %pad_maximum_fusion.2), channel_id=1, source_target_pairs={{0,8},{4,12},{8,0},{12,4},{16,24},{20,28},{24,16},{28,20},{1,9},{5... | collective-permute-start | bytes 98312 | tf_op jit(solution)/shard_map/ppermute | solution.py:264
  17.2 2.1 %collective-permute-start.12 = (bf16[3,16,256]{2,1,0:T(8,128)(2,1)S(1)}, bf16[3,16,256]{2,1,0:T(8,128)(2,1)S(1)}, u32[]{:S(2)}, u32[]{:S(2)}) collective-permute-start(bf16[3,16,256]{2,1,0:T(8,128)(2,1)S(1)} %get-tuple-element.10), channel_id=1, source_target_pairs={{0,1},{1,2},{2,3},{4,5},{5,6},{6,7},{8,9},{9,10},{10,11},{12,13},{... | collective-permute-start | bytes 73736 | tf_op jit(solution)/shard_map/ppermute | solution.py:350
  19.3 1.3 %collective-permute-start.13 = (bf16[3,16,256]{2,1,0:T(8,128)(2,1)S(1)}, bf16[3,16,256]{2,1,0:T(8,128)(2,1)S(1)}, u32[]{:S(2)}, u32[]{:S(2)}) collective-permute-start(bf16[3,16,256]{2,1,0:T(8,128)(2,1)S(1)} %get-tuple-element.11), channel_id=1, source_target_pairs={{1,0},{2,1},{3,2},{5,4},{6,5},{7,6},{9,8},{10,9},{11,10},{13,12},{... | collective-permute-start | bytes 73736 | tf_op jit(solution)/shard_map/ppermute | solution.py:351
  20.6 0.8 %add.21 = f32[32,384]{1,0:T(8,128)S(1)} add(f32[32,384]{1,0:T(8,128)S(1)} %get-tuple-element.7, f32[32,384]{1,0:T(8,128)} %collective-permute-done) | non-fusion elementwise | flops 12288 | bytes 147456 | tf_op jit(solution)/shard_map/add | solution.py:271
  21.4 3.7 %collective-permute-start.3 = (f32[32,384]{1,0:T(8,128)S(1)}, f32[32,384]{1,0:T(8,128)S(1)}, u32[]{:S(2)}, u32[]{:S(2)}) collective-permute-start(f32[32,384]{1,0:T(8,128)S(1)} %add.21), channel_id=1, source_target_pairs={{0,6},{1,7},{2,4},{3,5},{4,2},{5,3},{6,0},{7,1},{8,14},{9,15},{10,... | collective-permute-start | bytes 147464 | tf_op jit(solution)/shard_map/ppermute | solution.py:264
  25.1 1.5 %collective-permute-start.2 = (f32[32,384]{1,0:T(8,128)S(1)}, f32[32,384]{1,0:T(8,128)S(1)}, u32[]{:S(2)}, u32[]{:S(2)}) collective-permute-start(f32[32,384]{1,0:T(8,128)S(1)} %add.21), channel_id=1, source_target_pairs={{0,4},{1,5},{2,6},{3,7},{4,0},{5,1},{6,2},{7,3},{8,12},{9,13},{10,... | collective-permute-start | bytes 147464 | tf_op jit(solution)/shard_map/ppermute | solution.py:264
  26.6 0.8 %collective-permute-done.3 = f32[32,384]{1,0:T(8,128)S(1)} collective-permute-done((f32[32,384]{1,0:T(8,128)S(1)}, f32[32,384]{1,0:T(8,128)S(1)}, u32[]{:S(2)}, u32[]{:S(2)}) %collective-permute-start.3) | collective-permute-done | bytes 49184 | tf_op jit(solution)/shard_map/ppermute | solution.py:264
  27.4 3.2 %collective-permute-start.10 = (bf16[3,64,256]{2,1,0:T(8,128)(2,1)S(1)}, bf16[3,64,256]{2,1,0:T(8,128)(2,1)S(1)}, u32[]{:S(2)}, u32[]{:S(2)}) collective-permute-start(bf16[3,64,256]{2,1,0:T(8,128)(2,1)S(1)} %get-tuple-element.8), channel_id=1, source_target_pairs={{0,4},{4,8},{8,12},{12,16},{16,20},{20,24},{24,28},{1,5},{5,9},{9,... | collective-permute-start | bytes 294920 | tf_op jit(solution)/shard_map/ppermute | solution.py:348
  30.7 1.3 %collective-permute-start.11 = (bf16[3,64,256]{2,1,0:T(8,128)(2,1)S(1)}, bf16[3,64,256]{2,1,0:T(8,128)(2,1)S(1)}, u32[]{:S(2)}, u32[]{:S(2)}) collective-permute-start(bf16[3,64,256]{2,1,0:T(8,128)(2,1)S(1)} %get-tuple-element.9), channel_id=1, source_target_pairs={{4,0},{8,4},{12,8},{16,12},{20,16},{24,20},{28,24},{5,1},{9,5},{13... | collective-permute-start | bytes 294920 | tf_op jit(solution)/shard_map/ppermute | solution.py:349
  32.0 4.8 %collective-permute-start.9 = (f32[4,4,1024]{2,1,0:T(4,128)S(1)}, f32[4,4,1024]{2,1,0:T(4,128)S(1)}, u32[]{:S(2)}, u32[]{:S(2)}) collective-permute-start(f32[4,4,1024]{2,1,0:T(4,128)S(1)} %pad_maximum_fusion.1), channel_id=1, source_target_pairs={{0,16},{4,20},{8,24},{12,28},{16,0},{20,4},{24,8},{28,12},{1,17},{... | collective-permute-start | bytes 196616 | tf_op jit(solution)/shard_map/ppermute | solution.py:264
  36.8 0.0 copy-start.3
  36.9 0.0 copy-start.5
  36.9 0.0 copy-start.7
  36.9 0.0 copy-start.9
  36.9 0.0 copy-start.12
  36.9 0.3 collective-permute-start.6
  37.2 1.7 %collective-permute-start.5 = (f32[32,384]{1,0:T(8,128)S(1)}, f32[32,384]{1,0:T(8,128)S(1)}, u32[]{:S(2)}, u32[]{:S(2)}) collective-permute-start(f32[32,384]{1,0:T(8,128)S(1)} %add_add_fusion.1), channel_id=1, source_target_pairs={{0,16},{1,17},{2,18},{3,19},{4,20},{5,21},{6,22},{7,23},{8,24},{9,... | collective-permute-start | bytes 147464 | tf_op jit(solution)/shard_map/ppermute | solution.py:264
  38.9 2.5 %collective-permute-start.4 = (f32[32,384]{1,0:T(8,128)S(1)}, f32[32,384]{1,0:T(8,128)S(1)}, u32[]{:S(2)}, u32[]{:S(2)}) collective-permute-start(f32[32,384]{1,0:T(8,128)S(1)} %add_add_fusion.1), channel_id=1, source_target_pairs={{0,8},{1,9},{2,10},{3,11},{4,12},{5,13},{6,14},{7,15},{8,0},{9,1},... | collective-permute-start | bytes 147464 | tf_op jit(solution)/shard_map/ppermute | solution.py:264
  41.4 4.7 %stencil.1.field_ref = f32[3,16,64,256]{3,2,1,0:T(8,128)} custom-call(f32[3,16,64,256]{3,2,1,0:T(8,128)S(1)} %copy-done.2, bf16[3,64,256]{2,1,0:T(8,128)(2,1)S(1)} %collective-permute-done.10.west_ref, bf16[3,64,256]{2,1,0:T(8,128)(2,1)S(1)} %collective-permute-done.11.east_ref, bf16[3,16,256]{2,1,0:T(8,128)(2,1)S(1)} %collective-permute-done.12.south_ref, ...), custom_call_target="tpu_custom_call" | custom-call | flops 23592960 | bytes 6291456 | tf_op jit(solution)/shard_map/stencil/pallas_call | solution.py:353
  46.1 0.1 collective-permute-done.5
  46.4 3.4 %copy-done = bf16[1024,4096]{1,0:T(8,128)(2,1)S(1)} copy-done((bf16[1024,4096]{1,0:T(8,128)(2,1)S(1)}, bf16[1024,4096]{1,0:T(8,128)(2,1)}, u32[]{:S(2)}) %copy-start) | copy-done | bytes 8388632
  49.7 6.3 %rotors.1 = (f32[3,16,64,256]{3,2,1,0:T(8,128)}, f32[4,1024]{1,0:T(4,128)}) custom-call(s32[1]{0:T(128)} %bitcast.index_ref, s32[32]{0:T(128)S(1)} %copy-done.12, s32[8,128]{1,0:T(8,128)S(1)} %bitcast.7, s32[8,128]{1,0:T(8,128)S(1)} %bitcast.9, s32[8,128]{1,0:T(8,128)S(1)} %bitcast.11, ...), custom_call_target="tpu_custom_call", output_to_operand_aliasing={{0}: (10, {})} | custom-call | flops 1073741824 | bytes 8388608 | tf_op jit(solution)/shard_map/rotors/pallas_call | solution.py:372
  (35 shorter events, 0.2 us)
Async XLA Ops:
  0.6 14.4 %collective-permute-start.7 = (f32[1,4,1024]{2,1,0:T(4,128)}, f32[1,4,1024]{2,1,0:T(4,128)S(1)}, u32[]{:S(2)}, u32[]{:S(2)}) collective-permute-start(f32[1,4,1024]{2,1,0:T(4,128)} %bitcast.13), channel_id=1, source_target_pairs={{0,4},{4,0},{8,12},{12,8},{16,20},{20,16},{24,28},{28,24},{1,5},{5... | collective-permute-start | bytes 49160 | tf_op jit(solution)/shard_map/ppermute | solution.py:264
  3.6 1.9 %copy-start.1 = (f32[3,16,64,256]{3,2,1,0:T(8,128)S(1)}, f32[3,16,64,256]{3,2,1,0:T(8,128)}, u32[]{:S(2)}) copy-start(f32[3,16,64,256]{3,2,1,0:T(8,128)} %velocity_ref.3) | copy-start | bytes 9437188
  5.5 0.7 %copy-start.4 = (s32[1024]{0:T(1024)S(1)}, s32[1024]{0:T(1024)}, u32[]{:S(2)}) copy-start(s32[1024]{0:T(1024)} %param.18) | copy-start | bytes 12292
  6.2 0.7 %copy-start.6 = (s32[1024,1]{0,1:T(1,128)S(1)}, s32[1024,1]{0,1:T(1,128)}, u32[]{:S(2)}) copy-start(s32[1024,1]{0,1:T(1,128)} %param.17) | copy-start | bytes 12292
  6.9 0.7 %copy-start.8 = (s32[1024]{0:T(1024)S(1)}, s32[1024]{0:T(1024)}, u32[]{:S(2)}) copy-start(s32[1024]{0:T(1024)} %param.19) | copy-start | bytes 12292
  7.6 0.7 %copy-start.11 = (s32[32]{0:T(128)S(1)}, s32[32]{0:T(128)}, u32[]{:S(2)}) copy-start(s32[32]{0:T(128)} %slot_ref.3) | copy-start | bytes 388
  8.2 0.8 %copy-start.13 = (f32[32,384]{1,0:T(8,128)S(1)}, f32[32,384]{1,0:T(8,128)}, u32[]{:S(2)}) copy-start(f32[32,384]{1,0:T(8,128)} %weight_ref.1) | copy-start | bytes 147460
  9.0 6.0 %copy-start.14 = (f32[4,1024]{1,0:T(4,128)S(1)}, f32[4,1024]{1,0:T(4,128)}, u32[]{:S(2)}) copy-start(f32[4,1024]{1,0:T(4,128)} %param.15) | copy-start | bytes 49156
  9.0 32.3 %copy-start.2 = (f32[3,16,64,256]{3,2,1,0:T(8,128)S(1)}, f32[3,16,64,256]{3,2,1,0:T(8,128)}, u32[]{:S(2)}) copy-start(f32[3,16,64,256]{3,2,1,0:T(8,128)} %velocity_ref.3) | copy-start | bytes 9437188
  14.9 5.7 %collective-permute-start = (f32[32,384]{1,0:T(8,128)S(1)}, f32[32,384]{1,0:T(8,128)}, u32[]{:S(2)}, u32[]{:S(2)}) collective-permute-start(f32[32,384]{1,0:T(8,128)S(1)} %get-tuple-element.7), channel_id=1, source_target_pairs={{0,1},{1,0},{2,3},{3,2},{4,5},{5,4},{6,7},{7,6},{8,9},{9,8},{10,11... | collective-permute-start | bytes 147464 | tf_op jit(solution)/shard_map/ppermute | solution.py:264
  15.6 11.0 %collective-permute-start.8 = (f32[2,4,1024]{2,1,0:T(4,128)}, f32[2,4,1024]{2,1,0:T(4,128)S(1)}, u32[]{:S(2)}, u32[]{:S(2)}) collective-permute-start(f32[2,4,1024]{2,1,0:T(4,128)} %pad_maximum_fusion.2), channel_id=1, source_target_pairs={{0,8},{4,12},{8,0},{12,4},{16,24},{20,28},{24,16},{28,20},{1,9},{5... | collective-permute-start | bytes 98312 | tf_op jit(solution)/shard_map/ppermute | solution.py:264
  17.2 19.7 %collective-permute-start.12 = (bf16[3,16,256]{2,1,0:T(8,128)(2,1)S(1)}, bf16[3,16,256]{2,1,0:T(8,128)(2,1)S(1)}, u32[]{:S(2)}, u32[]{:S(2)}) collective-permute-start(bf16[3,16,256]{2,1,0:T(8,128)(2,1)S(1)} %get-tuple-element.10), channel_id=1, source_target_pairs={{0,1},{1,2},{2,3},{4,5},{5,6},{6,7},{8,9},{9,10},{10,11},{12,13},{... | collective-permute-start | bytes 73736 | tf_op jit(solution)/shard_map/ppermute | solution.py:350
  19.3 17.9 %collective-permute-start.13 = (bf16[3,16,256]{2,1,0:T(8,128)(2,1)S(1)}, bf16[3,16,256]{2,1,0:T(8,128)(2,1)S(1)}, u32[]{:S(2)}, u32[]{:S(2)}) collective-permute-start(bf16[3,16,256]{2,1,0:T(8,128)(2,1)S(1)} %get-tuple-element.11), channel_id=1, source_target_pairs={{1,0},{2,1},{3,2},{5,4},{6,5},{7,6},{9,8},{10,9},{11,10},{13,12},{... | collective-permute-start | bytes 73736 | tf_op jit(solution)/shard_map/ppermute | solution.py:351
  21.4 6.0 %collective-permute-start.3 = (f32[32,384]{1,0:T(8,128)S(1)}, f32[32,384]{1,0:T(8,128)S(1)}, u32[]{:S(2)}, u32[]{:S(2)}) collective-permute-start(f32[32,384]{1,0:T(8,128)S(1)} %add.21), channel_id=1, source_target_pairs={{0,6},{1,7},{2,4},{3,5},{4,2},{5,3},{6,0},{7,1},{8,14},{9,15},{10,... | collective-permute-start | bytes 147464 | tf_op jit(solution)/shard_map/ppermute | solution.py:264
  25.1 5.6 %collective-permute-start.2 = (f32[32,384]{1,0:T(8,128)S(1)}, f32[32,384]{1,0:T(8,128)S(1)}, u32[]{:S(2)}, u32[]{:S(2)}) collective-permute-start(f32[32,384]{1,0:T(8,128)S(1)} %add.21), channel_id=1, source_target_pairs={{0,4},{1,5},{2,6},{3,7},{4,0},{5,1},{6,2},{7,3},{8,12},{9,13},{10,... | collective-permute-start | bytes 147464 | tf_op jit(solution)/shard_map/ppermute | solution.py:264
  26.6 5.4 %collective-permute-start.1 = (f32[32,384]{1,0:T(8,128)S(1)}, f32[32,384]{1,0:T(8,128)S(1)}, u32[]{:S(2)}, u32[]{:S(2)}) collective-permute-start(f32[32,384]{1,0:T(8,128)S(1)} %add.21), channel_id=1, source_target_pairs={{0,2},{1,3},{2,0},{3,1},{4,6},{5,7},{6,4},{7,5},{8,10},{9,11},{10,... | collective-permute-start | bytes 147464 | tf_op jit(solution)/shard_map/ppermute | solution.py:264
  27.4 11.5 %collective-permute-start.10 = (bf16[3,64,256]{2,1,0:T(8,128)(2,1)S(1)}, bf16[3,64,256]{2,1,0:T(8,128)(2,1)S(1)}, u32[]{:S(2)}, u32[]{:S(2)}) collective-permute-start(bf16[3,64,256]{2,1,0:T(8,128)(2,1)S(1)} %get-tuple-element.8), channel_id=1, source_target_pairs={{0,4},{4,8},{8,12},{12,16},{16,20},{20,24},{24,28},{1,5},{5,9},{9,... | collective-permute-start | bytes 294920 | tf_op jit(solution)/shard_map/ppermute | solution.py:348
  30.7 10.7 %collective-permute-start.11 = (bf16[3,64,256]{2,1,0:T(8,128)(2,1)S(1)}, bf16[3,64,256]{2,1,0:T(8,128)(2,1)S(1)}, u32[]{:S(2)}, u32[]{:S(2)}) collective-permute-start(bf16[3,64,256]{2,1,0:T(8,128)(2,1)S(1)} %get-tuple-element.9), channel_id=1, source_target_pairs={{4,0},{8,4},{12,8},{16,12},{20,16},{24,20},{28,24},{5,1},{9,5},{13... | collective-permute-start | bytes 294920 | tf_op jit(solution)/shard_map/ppermute | solution.py:349
  32.0 14.1 %collective-permute-start.9 = (f32[4,4,1024]{2,1,0:T(4,128)S(1)}, f32[4,4,1024]{2,1,0:T(4,128)S(1)}, u32[]{:S(2)}, u32[]{:S(2)}) collective-permute-start(f32[4,4,1024]{2,1,0:T(4,128)S(1)} %pad_maximum_fusion.1), channel_id=1, source_target_pairs={{0,16},{4,20},{8,24},{12,28},{16,0},{20,4},{24,8},{28,12},{1,17},{... | collective-permute-start | bytes 196616 | tf_op jit(solution)/shard_map/ppermute | solution.py:264
  36.8 9.4 %copy-start.3 = (bf16[384,1024]{1,0:T(8,128)(2,1)S(1)}, bf16[384,1024]{1,0:T(8,128)(2,1)}, u32[]{:S(2)}) copy-start(bf16[384,1024]{1,0:T(8,128)(2,1)} %w_in_ref.1) | copy-start | bytes 2359300
  36.9 9.4 %copy-start.5 = (s32[1024]{0:T(1024)S(1)}, s32[1024]{0:T(1024)}, u32[]{:S(2)}) copy-start(s32[1024]{0:T(1024)} %param.18) | copy-start | bytes 12292
  36.9 9.4 %copy-start.7 = (s32[1024,1]{0,1:T(1,128)S(1)}, s32[1024,1]{0,1:T(1,128)}, u32[]{:S(2)}) copy-start(s32[1024,1]{0,1:T(1,128)} %param.17) | copy-start | bytes 12292
  36.9 9.4 %copy-start.9 = (s32[1024]{0:T(1024)S(1)}, s32[1024]{0:T(1024)}, u32[]{:S(2)}) copy-start(s32[1024]{0:T(1024)} %param.19) | copy-start | bytes 12292
  36.9 9.4 %copy-start.10 = (f32[1024]{0:T(1024)S(1)}, f32[1024]{0:T(1024)}, u32[]{:S(2)}) copy-start(f32[1024]{0:T(1024)} %param.14) | copy-start | bytes 12292
  36.9 9.4 %copy-start.12 = (s32[32]{0:T(128)S(1)}, s32[32]{0:T(128)}, u32[]{:S(2)}) copy-start(s32[32]{0:T(128)} %slot_ref.3) | copy-start | bytes 388
  36.9 9.2 %collective-permute-start.6 = (f32[32,384]{1,0:T(8,128)S(1)}, f32[32,384]{1,0:T(8,128)S(1)}, u32[]{:S(2)}, u32[]{:S(2)}) collective-permute-start(f32[32,384]{1,0:T(8,128)S(1)} %add_add_fusion.1), channel_id=1, source_target_pairs={{0,24},{1,25},{2,26},{3,27},{4,28},{5,29},{6,30},{7,31},{8,16},{9,... | collective-permute-start | bytes 147464 | tf_op jit(solution)/shard_map/ppermute | solution.py:264
  37.2 9.0 %collective-permute-start.5 = (f32[32,384]{1,0:T(8,128)S(1)}, f32[32,384]{1,0:T(8,128)S(1)}, u32[]{:S(2)}, u32[]{:S(2)}) collective-permute-start(f32[32,384]{1,0:T(8,128)S(1)} %add_add_fusion.1), channel_id=1, source_target_pairs={{0,16},{1,17},{2,18},{3,19},{4,20},{5,21},{6,22},{7,23},{8,24},{9,... | collective-permute-start | bytes 147464 | tf_op jit(solution)/shard_map/ppermute | solution.py:264
  38.9 7.3 %collective-permute-start.4 = (f32[32,384]{1,0:T(8,128)S(1)}, f32[32,384]{1,0:T(8,128)S(1)}, u32[]{:S(2)}, u32[]{:S(2)}) collective-permute-start(f32[32,384]{1,0:T(8,128)S(1)} %add_add_fusion.1), channel_id=1, source_target_pairs={{0,8},{1,9},{2,10},{3,11},{4,12},{5,13},{6,14},{7,15},{8,0},{9,1},... | collective-permute-start | bytes 147464 | tf_op jit(solution)/shard_map/ppermute | solution.py:264
  46.3 3.4 %copy-start = (bf16[1024,4096]{1,0:T(8,128)(2,1)S(1)}, bf16[1024,4096]{1,0:T(8,128)(2,1)}, u32[]{:S(2)}) copy-start(bf16[1024,4096]{1,0:T(8,128)(2,1)} %w_out_ref.1) | copy-start | bytes 25165828

commit v2 on v1

--- a/solution.py
+++ b/solution.py
@@ -36,8 +36,7 @@
     return jnp.where(mask, 1.0, 0.0).astype(BF16)
 
 
-def slots_of(rotor_ref, slot_ref):
-    rotors = rotor_ref[...]
+def slots_of(rotors, slot_ref):
     slots = jnp.zeros_like(rotors)
     for rotor in range(slot_ref.shape[0]):
         slots = jnp.where(rotors == rotor, slot_ref[rotor], slots)
@@ -57,10 +56,16 @@
     south_ref,
     north_ref,
     cells,
+    tiles,
+    rotor_rows,
+    sub_rows,
+    slot_table,
+    weights,
     place_hot,
     gains,
     half_column,
     sems,
+    small_sems,
 ):
     parts, size_x, size_y, size_z = velocity_ref.shape
     columns = size_x * size_y
@@ -69,20 +74,34 @@
     entries = groups * TILE
     rotors = slot_ref.shape[0]
     subs = weight_ref.shape[0]
+    small = [
+        pltpu.make_async_copy(source, target, small_sems.at[i])
+        for i, (source, target) in enumerate(
+            (
+                (tile_ref, tiles),
+                (sub_ref, sub_rows),
+                (weight_ref, weights),
+                (rotor_ref, rotor_rows),
+                (slot_ref, slot_table),
+            )
+        )
+    ]
     copies = [
         pltpu.make_async_copy(velocity_ref.at[c], cells.at[c], sems.at[c]) for c in range(parts)
     ]
-    for copy in copies:
+    for copy in small + copies:
         copy.start()
-    weight = weight_ref[...]
+    for copy in small:
+        copy.wait()
+    weight = weights[...]
     high = weight.astype(BF16)
     rest = weight - high.astype(F32)
     middle = rest.astype(BF16)
     low = (rest - middle.astype(F32)).astype(BF16)
     weight_parts = jnp.concatenate([high, middle, low], axis=0)
     sub_hot = []
-    place_rows = tile_ref[...] // halves
-    half_rows = tile_ref[...] % halves
+    place_rows = tiles[...] // halves
+    half_rows = tiles[...] % halves
     for group in range(groups):
         half_column[pl.ds(group * TILE, TILE), :] = as_column(half_rows[group : group + 1, :])
         place = as_column(place_rows[group : group + 1, :])
@@ -90,14 +109,14 @@
             place_hot[pl.ds(group * TILE, TILE), pl.ds(block * TILE, TILE)] = hot(
                 place == lanes(TILE) + block * TILE
             )
-        sub = as_column(sub_ref[group : group + 1, :])
+        sub = as_column(sub_rows[group : group + 1, :])
         wide = jnp.concatenate([sub[:, :subs]] * 3, axis=1)
         index = lax.broadcasted_iota(jnp.int32, (TILE, subs), 1)
         sub_hot.append(hot(wide == jnp.concatenate([index] * 3, axis=1)))
     gains[...] = jnp.dot(
         jnp.concatenate(sub_hot, axis=0), weight_parts, preferred_element_type=F32
     )
-    slots = slots_of(rotor_ref, slot_ref)
+    slots = slots_of(rotor_rows[...], slot_table)
     slot_hot = jnp.concatenate(
         [hot(slots[g : g + 1, :] == sublanes(rotors)) for g in range(groups)], axis=1
     )
@@ -126,33 +145,50 @@
         north_ref[c] = cells[c, :, size_y - 1, :].astype(BF16)
 
 
-def stencil_kernel(velocity_ref, west_ref, east_ref, south_ref, north_ref, out_ref, cells, result, sems, out_sems):
+def stencil_kernel(
+    slot_ref,
+    tile_ref,
+    rotor_ref,
+    sub_ref,
+    velocity_ref,
+    west_ref,
+    east_ref,
+    south_ref,
+    north_ref,
+    w_out_ref,
+    out_ref,
+    wind_ref,
+    key_ref,
+    place_ref,
+    w_out_here,
+    result,
+    w_sem,
+    out_sems,
+):
     parts, size_x, size_y, size_z = velocity_ref.shape
-    chunks = sems.shape[0]
+    columns = size_x * size_y
+    halves = size_z // TILE
+    groups = tile_ref.shape[0]
+    rotors = slot_ref.shape[0]
+    keys_size = key_ref.shape[1]
+    chunks = out_sems.shape[0]
     depth = size_x // chunks
-
-    def load(chunk):
-        at = pl.ds(chunk * depth, depth)
-        return pltpu.make_async_copy(velocity_ref.at[:, at], cells.at[:, at], sems.at[chunk])
+    bring = pltpu.make_async_copy(w_out_ref, w_out_here, w_sem)
+    bring.start()
 
     def store(chunk):
         at = pl.ds(chunk * depth, depth)
-        return pltpu.make_async_copy(result.at[:, at], out_ref.at[:, at], out_sems.at[chunk])
-
-    for chunk in range(chunks):
-        load(chunk).start()
+        return pltpu.make_async_copy(result.at[:, at], out_ref.at[1:, at], out_sems.at[chunk])
+
     row = lax.broadcasted_iota(jnp.int32, (size_y, size_z), 0)
     lane = lax.broadcasted_iota(jnp.int32, (size_y, size_z), 1)
-    load(0).wait()
     for chunk in range(chunks):
-        if chunk + 1 < chunks:
-            load(chunk + 1).wait()
         for x in range(chunk * depth, (chunk + 1) * depth):
-            wind = [cells[c, x] for c in range(parts)]
+            wind = [velocity_ref[c, x] for c in range(parts)]
             for c in range(parts):
                 here = wind[c]
-                west = cells[c, x - 1] if x > 0 else west_ref[c].astype(F32)
-                east = cells[c, x + 1] if x + 1 < size_x else east_ref[c].astype(F32)
+                west = velocity_ref[c, x - 1] if x > 0 else west_ref[c].astype(F32)
+                east = velocity_ref[c, x + 1] if x + 1 < size_x else east_ref[c].astype(F32)
                 south = jnp.where(
                     row == 0, south_ref[c, x : x + 1, :].astype(F32), pltpu.roll(here, 1, 0)
                 )
@@ -169,45 +205,56 @@
                     + wind[1] * ((north - south) * 0.5)
                     + wind[2] * ((upper - lower) * 0.5)
                 )
-                result[c, x] = here + time_step * (viscosity * laplace - advect)
+                value = here + time_step * (viscosity * laplace - advect)
+                if c == 0:
+                    wind_ref[x] = value
+                else:
+                    result[c - 1, x] = value
         store(chunk).start()
+    slots = slots_of(rotor_ref[...], slot_ref)
+    keys = sub_ref[...] * rotors + slots
+    places = tile_ref[...] // halves
+    for group in range(groups):
+        key = as_column(keys[group : group + 1, :])
+        at = pl.ds(group * TILE, TILE)
+        for block in range(keys_size // TILE):
+            key_ref[at, pl.ds(block * TILE, TILE)] = hot(key == lanes(TILE) + block * TILE)
+        for block in range(columns // TILE):
+            place_ref[pl.ds(block * TILE, TILE), at] = hot(
+                places[group : group + 1, :] == sublanes(TILE) + block * TILE
+            )
     for chunk in range(chunks):
         store(chunk).wait()
+    bring.wait()
 
 
 def rotor_kernel(
     index_ref,
-    slot_ref,
     tile_ref,
-    rotor_ref,
-    sub_ref,
     pooled_ref,
     w_in_ref,
     w_out_ref,
     decay_ref,
     states_ref,
+    wind_ref,
+    key_ref,
+    place_ref,
     field_ref,
     out_ref,
     new_ref,
-    wind,
     states,
     by_slab,
     source_rows,
-    key_hot,
-    place_hot,
+    wind,
     sems,
 ):
     slabs, rows, width = states_ref.shape
     rotors = slabs * rows
-    _, size_x, size_y, size_z = field_ref.shape
-    columns = size_x * size_y
+    size_x, size_y, size_z = wind_ref.shape
     halves = size_z // TILE
     groups = tile_ref.shape[0]
     subs = w_out_ref.shape[1] // TILE
     me = index_ref[0]
-    load = pltpu.make_async_copy(field_ref.at[0], wind, sems.at[0])
-    load.start()
-    slots = slots_of(rotor_ref, slot_ref)
     for j in range(slabs):
         states[j * rows : (j + 1) * rows, :] = states_ref[me ^ j]
     pooled = (pooled_ref[...] * pool_scale).astype(BF16)
@@ -218,33 +265,30 @@
         by_slab[j] = new[j * rows : (j + 1) * rows, :]
     new_ref[...] = by_slab[me]
     new_b = new.astype(BF16)
-    keys = sub_ref[...] * rotors + slots
-    tiles = tile_ref[...]
-    place_rows = tiles // halves
-    half_rows = tiles % halves
-    for group in range(groups):
-        key = as_column(keys[group : group + 1, :])
-        at = pl.ds(group * TILE, TILE)
-        for block in range(subs * rotors // TILE):
-            key_hot[at, pl.ds(block * TILE, TILE)] = hot(key == lanes(TILE) + block * TILE)
-        for block in range(columns // TILE):
-            place_hot[pl.ds(block * TILE, TILE), at] = hot(
-                place_rows[group : group + 1, :] == sublanes(TILE) + block * TILE
-            )
+    half_rows = tile_ref[...] % halves
     sources = jnp.dot(new_b, w_out_ref[...], preferred_element_type=F32).astype(BF16)
     for sub in range(subs):
         source_rows[sub * rotors : (sub + 1) * rotors, :] = sources[:, sub * TILE : (sub + 1) * TILE]
-    taken = jnp.dot(key_hot[...], source_rows[...], preferred_element_type=F32).astype(BF16)
+    taken = jnp.dot(key_ref[...], source_rows[...], preferred_element_type=F32)
     half = jnp.concatenate([as_column(half_rows[g : g + 1, :]) for g in range(groups)], axis=0)
     spread = jnp.concatenate(
-        [jnp.where(half == h, taken.astype(F32), 0.0).astype(BF16) for h in range(halves)], axis=1
-    )
-    forcing = jnp.dot(place_hot[...], spread, preferred_element_type=F32)
-    load.wait()
-    wind[...] = wind[...] - force_scale * forcing.reshape(size_x, size_y, size_z)
-    store = pltpu.make_async_copy(wind, out_ref.at[0], sems.at[1])
-    store.start()
-    store.wait()
+        [jnp.where(half == h, taken, 0.0).astype(BF16) for h in range(halves)], axis=1
+    )
+    chunks = sems.shape[0]
+    depth = size_x // chunks
+    stores = []
+    for chunk in range(chunks):
+        at = pl.ds(chunk * depth, depth)
+        forcing = jnp.dot(
+            place_ref[pl.ds(chunk * depth * size_y, depth * size_y), :],
+            spread,
+            preferred_element_type=F32,
+        )
+        wind[at] = wind_ref[at] - force_scale * forcing.reshape(depth, size_y, size_z)
+        stores.append(pltpu.make_async_copy(wind.at[at], out_ref.at[0, at], sems.at[chunk]))
+        stores[-1].start()
+    for store in stores:
+        store.wait()
 
 
 def xor_groups(bits):
@@ -283,8 +327,12 @@
     return [pl.BlockSpec(memory_space=pltpu.VMEM)] * count
 
 
+def in_hbm(value):
+    return pltpu.with_memory_space_constraint(value, pltpu.HBM)
+
+
 SMEM = pl.BlockSpec(memory_space=pltpu.SMEM)
-ANY = pl.BlockSpec(memory_space=pl.ANY)
+HBM = pl.BlockSpec(memory_space=pltpu.HBM)
 
 
 def on_device(
@@ -314,7 +362,7 @@
     sub = entry_sub.reshape(groups, TILE)
 
     gathered = gather_xor(rotor_states, "slab", slabs)
-    part, west, east, south, north = pl.pallas_call(
+    part, west, east, south, north, cells = pl.pallas_call(
         pool_kernel,
         out_shape=(
             jax.ShapeDtypeStruct((rotors, parts * TILE), F32),
@@ -322,24 +370,30 @@
             jax.ShapeDtypeStruct((parts, size_y, size_z), BF16),
             jax.ShapeDtypeStruct((parts, size_x, size_z), BF16),
             jax.ShapeDtypeStruct((parts, size_x, size_z), BF16),
-        ),
-        in_specs=vmem(3) + [SMEM] + vmem(1) + [ANY],
-        out_specs=tuple(vmem(5)),
+            jax.ShapeDtypeStruct(velocity.shape, F32),
+        ),
+        in_specs=[HBM] * 6,
+        out_specs=tuple(vmem(6)),
         scratch_shapes=[
-            pltpu.VMEM(velocity.shape, F32),
+            pltpu.VMEM((groups, TILE), jnp.int32),
+            pltpu.VMEM((groups, TILE), jnp.int32),
+            pltpu.VMEM((groups, TILE), jnp.int32),
+            pltpu.SMEM((rotors,), jnp.int32),
+            pltpu.VMEM(shape_weight.shape, F32),
             pltpu.VMEM((entries, columns), BF16),
             pltpu.VMEM((entries, parts * TILE), F32),
             pltpu.VMEM((entries, TILE), jnp.int32),
             pltpu.SemaphoreType.DMA((parts,)),
+            pltpu.SemaphoreType.DMA((5,)),
         ],
-        compiler_params=pltpu.CompilerParams(vmem_limit_bytes=24 << 20),
+        compiler_params=pltpu.CompilerParams(vmem_limit_bytes=20 << 20),
         cost_estimate=pl.CostEstimate(
             flops=2 * entries * columns * parts * size_z,
             bytes_accessed=velocity.size * 4,
             transcendentals=0,
         ),
         name="pool",
-    )(tile, rotor, sub, slot_of_rotor, shape_weight, velocity)
+    )(*(in_hbm(value) for value in (tile, rotor, sub, slot_of_rotor, shape_weight, velocity)))
 
     pooled = sum_all(part, BOTH, slabs * crosses)
 
@@ -350,23 +404,29 @@
     from_south = lax.ppermute(north, "cross", up(crosses))
     from_north = lax.ppermute(south, "cross", down(crosses))
     chunks = 4
-    field = pl.pallas_call(
+    keys = subs * rotors
+    field, wind, key_hot, place_hot, w_out_here = pl.pallas_call(
         stencil_kernel,
-        out_shape=jax.ShapeDtypeStruct(velocity.shape, F32),
-        in_specs=[ANY] + vmem(4),
-        out_specs=ANY,
+        out_shape=(
+            jax.ShapeDtypeStruct(velocity.shape, F32),
+            jax.ShapeDtypeStruct(velocity.shape[1:], F32),
+            jax.ShapeDtypeStruct((entries, keys), BF16),
+            jax.ShapeDtypeStruct((columns, entries), BF16),
+            jax.ShapeDtypeStruct(w_out.shape, BF16),
+        ),
+        in_specs=[SMEM] + vmem(8) + [HBM],
+        out_specs=(HBM, *vmem(4)),
         scratch_shapes=[
-            pltpu.VMEM(velocity.shape, F32),
-            pltpu.VMEM(velocity.shape, F32),
-            pltpu.SemaphoreType.DMA((chunks,)),
+            pltpu.VMEM((parts - 1, size_x, size_y, size_z), F32),
+            pltpu.SemaphoreType.DMA,
             pltpu.SemaphoreType.DMA((chunks,)),
         ],
-        compiler_params=pltpu.CompilerParams(vmem_limit_bytes=16 << 20),
+        compiler_params=pltpu.CompilerParams(vmem_limit_bytes=24 << 20),
         cost_estimate=pl.CostEstimate(
             flops=30 * velocity.size, bytes_accessed=velocity.size * 8, transcendentals=0
         ),
         name="stencil",
-    )(velocity, from_west, from_east, from_south, from_north)
+    )(slot_of_rotor, tile, rotor, sub, cells, from_west, from_east, from_south, from_north, in_hbm(w_out))
 
     index = lax.axis_index("slab").astype(jnp.int32).reshape(1)
     return pl.pallas_call(
@@ -375,24 +435,34 @@
             jax.ShapeDtypeStruct(velocity.shape, F32),
             jax.ShapeDtypeStruct(rotor_states.shape, F32),
         ),
-        in_specs=[SMEM, SMEM] + vmem(8) + [ANY],
-        out_specs=(ANY, pl.BlockSpec(memory_space=pltpu.VMEM)),
+        in_specs=[SMEM] + vmem(9) + [HBM],
+        out_specs=(HBM, pl.BlockSpec(memory_space=pltpu.VMEM)),
         scratch_shapes=[
-            pltpu.VMEM((size_x, size_y, size_z), F32),
             pltpu.VMEM((rotors, width), F32),
             pltpu.VMEM((slabs, rows, width), F32),
-            pltpu.VMEM((subs * rotors, TILE), BF16),
-            pltpu.VMEM((entries, subs * rotors), BF16),
-            pltpu.VMEM((columns, entries), BF16),
-            pltpu.SemaphoreType.DMA((2,)),
+            pltpu.VMEM((keys, TILE), BF16),
+            pltpu.VMEM((size_x, size_y, size_z), F32),
+            pltpu.SemaphoreType.DMA((chunks,)),
         ],
         input_output_aliases={10: 0},
-        compiler_params=pltpu.CompilerParams(vmem_limit_bytes=32 << 20),
+        compiler_params=pltpu.CompilerParams(vmem_limit_bytes=24 << 20),
         cost_estimate=pl.CostEstimate(
             flops=4 * entries * columns * size_z, bytes_accessed=w_out.size * 2, transcendentals=0
         ),
         name="rotors",
-    )(index, slot_of_rotor, tile, rotor, sub, pooled, w_in, w_out, decay[None, :], gathered, field)
+    )(
+        index,
+        tile,
+        pooled,
+        w_in,
+        w_out_here,
+        decay[None, :],
+        gathered,
+        wind,
+        key_hot,
+        place_hot,
+        field,
+    )
 
 
 def solution(mesh):

time: 56.6 us -> 51.1 us (0.903)
  local copies, waits for them, and re-layouts: 8.82 us -> 0.05 us
  Pallas kernels: 16.9 us -> 20.3 us
  other arithmetic: 1.51 us -> 3.03 us
  starting transfers between devices: 27 us -> 25.9 us
    unnamed x30 -> x20, local copies, waits for them, and re-layouts: 8.82 us -> 0.05 us
    pallas_call x1, Pallas kernels: 4.65 us -> 8.15 us  [on_device(): pl.pallas_call(stencil_kernel, out_shape=(jax.ShapeDtypeStruct(velocity.s...]
    concatenate x3, other arithmetic: 0.67 us -> 2.2 us  [gather_xor(): jnp.concatenate([blocks, exchange(blocks, axis, count, 1 << bit)], axis=0)]
    pallas_call x1, Pallas kernels: 6.35 us -> 5.2 us  [on_device(): pl.pallas_call(rotor_kernel, out_shape=(jax.ShapeDtypeStruct(velocity.sha...]
    pallas_call x1, Pallas kernels: 5.85 us -> 6.96 us  [on_device(): pl.pallas_call(pool_kernel, out_shape=(jax.ShapeDtypeStruct((rotors, part...]
    ppermute x10, starting transfers between devices: 19.1 us -> 18.3 us  [exchange(): return lax.ppermute(value, axis, [(i, i ^ offset) for i in range(count)])]
    ppermute x1, starting transfers between devices: 3.24 us -> 2.43 us  [on_device(): from_west = lax.ppermute(east, 'slab', up(slabs))]
  transfers between devices with their start and end apart: 14 -> 14, of which waited for: 2 -> 1; matrix products, arithmetic and copies ran while one was open for 3% -> 6% of each run, Pallas kernels for 19% -> 30%
where the time goes in v2:
time: 51.1 us; the launch traced here: 50.6 us
  starting transfers between devices  25.9 us (51%)
  Pallas kernels  20.3 us (40%)
  other arithmetic  3.03 us (6%)
  between operations  0.9 us (2%)
    ppermute x10, starting transfers between devices, exchange(): return lax.ppermute(value, axis, [(i, i ^ offset) for i in range(count)])  18.3 us
    pallas_call x1, Pallas kernels, on_device(): pl.pallas_call(stencil_kernel, out_shape=(jax.ShapeDtypeStruct(velocity.s...  8.15 us
    pallas_call x1, Pallas kernels, on_device(): pl.pallas_call(pool_kernel, out_shape=(jax.ShapeDtypeStruct((rotors, part...  6.96 us
    pallas_call x1, Pallas kernels, on_device(): pl.pallas_call(rotor_kernel, out_shape=(jax.ShapeDtypeStruct(velocity.sha...  5.2 us
    ppermute x1, starting transfers between devices, on_device(): from_south = lax.ppermute(north, 'cross', up(crosses))  2.63 us
    ppermute x1, starting transfers between devices, on_device(): from_west = lax.ppermute(east, 'slab', up(slabs))  2.43 us
    concatenate x3, other arithmetic, gather_xor(): jnp.concatenate([blocks, exchange(blocks, axis, count, 1 << bit)], axis=0)  2.2 us
    ppermute x1, starting transfers between devices, on_device(): from_east = lax.ppermute(west, 'slab', down(slabs))  1.29 us
  transfers between devices with their start and end apart: 14, of which 1 were waited for; matrix products, arithmetic and copies ran while one was open for 6% of the time, Pallas kernels for 30%

profile of v2, /device:TPU:0, one launch (start us, length us, event | category | flops | bytes accessed | tf_op | source)
XLA Modules:
  0.0 50.6 jit_solution(17075114615409327810)
XLA Ops:
  0.6 0.0 copy-start.6
  0.6 3.0 %collective-permute-start.11 = (f32[1,4,1024]{2,1,0:T(4,128)}, f32[1,4,1024]{2,1,0:T(4,128)S(1)}, u32[]{:S(2)}, u32[]{:S(2)}) collective-permute-start(f32[1,4,1024]{2,1,0:T(4,128)} %bitcast.14), channel_id=1, source_target_pairs={{0,4},{4,0},{8,12},{12,8},{16,20},{20,16},{24,28},{28,24},{1,5},{5... | collective-permute-start | bytes 49160 | tf_op jit(solution)/shard_map/ppermute | solution.py:308
  3.7 7.0 %pool.1 = (f32[32,384]{1,0:T(8,128)S(1)}, bf16[3,64,256]{2,1,0:T(8,128)(2,1)S(1)}, bf16[3,64,256]{2,1,0:T(8,128)(2,1)}, bf16[3,16,256]{2,1,0:T(8,128)(2,1)S(1)},...) custom-call(s32[8,128]{1,0:T(8,128)} %bitcast.6, s32[8,128]{1,0:T(8,128)} %bitcast.9, s32[8,128]{1,0:T(8,128)} %bitcast.11, ...), custom_call_target="tpu_custom_call" | custom-call | flops 1610612736 | bytes 3145728 | tf_op jit(solution)/shard_map/pool/pallas_call | solution.py:365
  10.6 0.1 collective-permute-start
  10.7 0.0 collective-permute-done.11
  10.7 0.0 copy-start.8
  10.7 0.6 %pad_maximum_fusion.2 = f32[2,4,1024]{2,1,0:T(4,128)} fusion(f32[1,4,1024]{2,1,0:T(4,128)S(1)} %collective-permute-done.11, f32[1,4,1024]{2,1,0:T(4,128)S(1)} %bitcast.16), kind=kLoop, calls=%fused_computation.4 | loop fusion | flops 8192 | bytes 65536 | tf_op jit(solution)/shard_map/concatenate | solution.py:322
  11.4 1.6 %collective-permute-start.12 = (f32[2,4,1024]{2,1,0:T(4,128)}, f32[2,4,1024]{2,1,0:T(4,128)}, u32[]{:S(2)}, u32[]{:S(2)}) collective-permute-start(f32[2,4,1024]{2,1,0:T(4,128)} %pad_maximum_fusion.2), channel_id=1, source_target_pairs={{0,8},{4,12},{8,0},{12,4},{16,24},{20,28},{24,16},{28,20},{1,9},{5... | collective-permute-start | bytes 98312 | tf_op jit(solution)/shard_map/ppermute | solution.py:308
  12.9 2.4 %collective-permute-start.7 = (bf16[3,64,256]{2,1,0:T(8,128)(2,1)}, bf16[3,64,256]{2,1,0:T(8,128)(2,1)S(1)}, u32[]{:S(2)}, u32[]{:S(2)}) collective-permute-start(bf16[3,64,256]{2,1,0:T(8,128)(2,1)} %get-tuple-element.15), channel_id=1, source_target_pairs={{0,4},{4,8},{8,12},{12,16},{16,20},{20,24},{24,28},{1,5},{5,9},{9,... | collective-permute-start | bytes 294920 | tf_op jit(solution)/shard_map/ppermute | solution.py:402
  15.4 1.3 %collective-permute-start.8 = (bf16[3,64,256]{2,1,0:T(8,128)(2,1)S(1)}, bf16[3,64,256]{2,1,0:T(8,128)(2,1)S(1)}, u32[]{:S(2)}, u32[]{:S(2)}) collective-permute-start(bf16[3,64,256]{2,1,0:T(8,128)(2,1)S(1)} %get-tuple-element.16), channel_id=1, source_target_pairs={{4,0},{8,4},{12,8},{16,12},{20,16},{24,20},{28,24},{5,1},{9,5},{13... | collective-permute-start | bytes 294920 | tf_op jit(solution)/shard_map/ppermute | solution.py:403
  16.7 0.0 collective-permute-done
  16.7 0.8 %add.21 = f32[32,384]{1,0:T(8,128)S(1)} add(f32[32,384]{1,0:T(8,128)S(1)} %get-tuple-element.13, f32[32,384]{1,0:T(8,128)} %collective-permute-done) | non-fusion elementwise | flops 12288 | bytes 147456 | tf_op jit(solution)/shard_map/add | solution.py:315
  17.5 1.5 %collective-permute-start.1 = (f32[32,384]{1,0:T(8,128)S(1)}, f32[32,384]{1,0:T(8,128)S(1)}, u32[]{:S(2)}, u32[]{:S(2)}) collective-permute-start(f32[32,384]{1,0:T(8,128)S(1)} %add.21), channel_id=1, source_target_pairs={{0,2},{1,3},{2,0},{3,1},{4,6},{5,7},{6,4},{7,5},{8,10},{9,11},{10,... | collective-permute-start | bytes 147464 | tf_op jit(solution)/shard_map/ppermute | solution.py:308
  19.0 2.6 %collective-permute-start.2 = (f32[32,384]{1,0:T(8,128)S(1)}, f32[32,384]{1,0:T(8,128)S(1)}, u32[]{:S(2)}, u32[]{:S(2)}) collective-permute-start(f32[32,384]{1,0:T(8,128)S(1)} %add.21), channel_id=1, source_target_pairs={{0,4},{1,5},{2,6},{3,7},{4,0},{5,1},{6,2},{7,3},{8,12},{9,13},{10,... | collective-permute-start | bytes 147464 | tf_op jit(solution)/shard_map/ppermute | solution.py:308
  21.7 0.8 %pad_maximum_fusion.1 = f32[4,4,1024]{2,1,0:T(4,128)S(1)} fusion(f32[2,4,1024]{2,1,0:T(4,128)} %collective-permute-done.12, f32[1,4,1024]{2,1,0:T(4,128)} %copy-done.8, f32[1,4,1024]{2,1,0:T(4,128)} %bitcast.15), kind=kLoop, calls=%fused_computation.1 | loop fusion | flops 32768 | bytes 131072 | tf_op jit(solution)/shard_map/concatenate | solution.py:322
  22.5 0.0 collective-permute-done.1
  22.5 1.3 %collective-permute-start.10 = (bf16[3,16,256]{2,1,0:T(8,128)(2,1)S(1)}, bf16[3,16,256]{2,1,0:T(8,128)(2,1)S(1)}, u32[]{:S(2)}, u32[]{:S(2)}) collective-permute-start(bf16[3,16,256]{2,1,0:T(8,128)(2,1)S(1)} %get-tuple-element.18), channel_id=1, source_target_pairs={{1,0},{2,1},{3,2},{5,4},{6,5},{7,6},{9,8},{10,9},{11,10},{13,12},{... | collective-permute-start | bytes 73736 | tf_op jit(solution)/shard_map/ppermute | solution.py:405
  23.8 0.4 collective-permute-done.2
  24.2 2.6 %collective-permute-start.9 = (bf16[3,16,256]{2,1,0:T(8,128)(2,1)S(1)}, bf16[3,16,256]{2,1,0:T(8,128)(2,1)S(1)}, u32[]{:S(2)}, u32[]{:S(2)}) collective-permute-start(bf16[3,16,256]{2,1,0:T(8,128)(2,1)S(1)} %get-tuple-element.17), channel_id=1, source_target_pairs={{0,1},{1,2},{2,3},{4,5},{5,6},{6,7},{8,9},{9,10},{10,11},{12,13},{... | collective-permute-start | bytes 73736 | tf_op jit(solution)/shard_map/ppermute | solution.py:404
  26.8 5.0 %collective-permute-start.13 = (f32[4,4,1024]{2,1,0:T(4,128)S(1)}, f32[4,4,1024]{2,1,0:T(4,128)S(1)}, u32[]{:S(2)}, u32[]{:S(2)}) collective-permute-start(f32[4,4,1024]{2,1,0:T(4,128)S(1)} %pad_maximum_fusion.1), channel_id=1, source_target_pairs={{0,16},{4,20},{8,24},{12,28},{16,0},{20,4},{24,8},{28,12},{1,17},{... | collective-permute-start | bytes 196616 | tf_op jit(solution)/shard_map/ppermute | solution.py:308
  31.8 0.0 collective-permute-done.10.north_ref
  31.8 0.5 %collective-permute-start.4 = (f32[32,384]{1,0:T(8,128)S(1)}, f32[32,384]{1,0:T(8,128)S(1)}, u32[]{:S(2)}, u32[]{:S(2)}) collective-permute-start(f32[32,384]{1,0:T(8,128)S(1)} %add_add_fusion.1), channel_id=1, source_target_pairs={{0,8},{1,9},{2,10},{3,11},{4,12},{5,13},{6,14},{7,15},{8,0},{9,1},... | collective-permute-start | bytes 147464 | tf_op jit(solution)/shard_map/ppermute | solution.py:308
  32.4 0.3 collective-permute-start.5
  32.7 0.0 collective-permute-done.7.west_ref
  32.7 3.6 %collective-permute-start.6 = (f32[32,384]{1,0:T(8,128)S(1)}, f32[32,384]{1,0:T(8,128)S(1)}, u32[]{:S(2)}, u32[]{:S(2)}) collective-permute-start(f32[32,384]{1,0:T(8,128)S(1)} %add_add_fusion.1), channel_id=1, source_target_pairs={{0,24},{1,25},{2,26},{3,27},{4,28},{5,29},{6,30},{7,31},{8,16},{9,... | collective-permute-start | bytes 147464 | tf_op jit(solution)/shard_map/ppermute | solution.py:308
  36.3 0.0 copy-start.7
  36.3 0.0 copy-start.9
  36.4 0.0 copy-start
  36.4 0.0 copy-start.4
  36.4 8.2 %stencil.1 = (f32[3,16,64,256]{3,2,1,0:T(8,128)}, f32[16,64,256]{2,1,0:T(8,128)S(1)}, bf16[1024,1024]{1,0:T(8,128)(2,1)S(1)}, bf16[1024,1024]{1,0:T(8,128)(2,1)S(1)}, bf16[1024,4096]{1,0:T(8,128)(2,1)S(1)}) custom-call(s32[32]{0:T(128)S(1)} %copy-done.5, s32[8,128]{1,0:T(8,128)S(1)} %bitcast.7, s32[8,128]{1,0:T(8,128)S(1)} %bitcast.10, ...), custom_call_target="tpu_custom_call" | custom-call | flops 23592960 | bytes 6291456 | tf_op jit(solution)/shard_map/stencil/pallas_call | solution.py:408
  44.6 0.8 %pad_maximum_fusion.states_ref = f32[8,4,1024]{2,1,0:T(4,128)S(1)} fusion(f32[4,4,1024]{2,1,0:T(4,128)S(1)} %collective-permute-done.13, f32[2,4,1024]{2,1,0:T(4,128)} %collective-permute-done.12, f32[1,4,1024]{2,1,0:T(4,128)S(1)} %copy-done.9, f32[1,4,1024]{2,1,0:T(4,128)S(1)} %bitcast.17), kind=kLoop, calls=%fused_computation | loop fusion | flops 98304 | bytes 262144 | tf_op jit(solution)/shard_map/concatenate | solution.py:322
  45.4 5.2 %rotors.1 = (f32[3,16,64,256]{3,2,1,0:T(8,128)}, f32[4,1024]{1,0:T(4,128)}) custom-call(s32[1]{0:T(128)} %bitcast.index_ref, s32[8,128]{1,0:T(8,128)S(1)} %bitcast.8, f32[32,384]{1,0:T(8,128)S(1)} %add_add_fusion.pooled_ref, bf16[384,1024]{1,0:T(8,128)(2,1)S(1)} %copy-done, ...), custom_call_target="tpu_custom_call", output_to_operand_aliasing={{0}: (10, {})} | custom-call | flops 1073741824 | bytes 8388608 | tf_op jit(solution)/shard_map/rotors/pallas_call | solution.py:432
  (25 shorter events, 0.1 us)
Async XLA Ops:
  0.6 10.1 %copy-start.6 = (f32[4,1024]{1,0:T(4,128)S(1)}, f32[4,1024]{1,0:T(4,128)}, u32[]{:S(2)}) copy-start(f32[4,1024]{1,0:T(4,128)} %param.15) | copy-start | bytes 49156
  0.6 10.1 %collective-permute-start.11 = (f32[1,4,1024]{2,1,0:T(4,128)}, f32[1,4,1024]{2,1,0:T(4,128)S(1)}, u32[]{:S(2)}, u32[]{:S(2)}) collective-permute-start(f32[1,4,1024]{2,1,0:T(4,128)} %bitcast.14), channel_id=1, source_target_pairs={{0,4},{4,0},{8,12},{12,8},{16,20},{20,16},{24,28},{28,24},{1,5},{5... | collective-permute-start | bytes 49160 | tf_op jit(solution)/shard_map/ppermute | solution.py:308
  3.6 32.7 %copy-start.1 = (s32[1024]{0:T(1024)S(1)}, s32[1024]{0:T(1024)}, u32[]{:S(2)}) copy-start(s32[1024]{0:T(1024)} %param.18) | copy-start | bytes 12292
  3.6 32.7 %copy-start.2 = (s32[1024,1]{0,1:T(1,128)S(1)}, s32[1024,1]{0,1:T(1,128)}, u32[]{:S(2)}) copy-start(s32[1024,1]{0,1:T(1,128)} %param.17) | copy-start | bytes 12292
  3.7 32.7 %copy-start.3 = (s32[1024]{0:T(1024)S(1)}, s32[1024]{0:T(1024)}, u32[]{:S(2)}) copy-start(s32[1024]{0:T(1024)} %param.19) | copy-start | bytes 12292
  3.7 32.7 %copy-start.5 = (s32[32]{0:T(128)S(1)}, s32[32]{0:T(128)}, u32[]{:S(2)}) copy-start(s32[32]{0:T(128)} %slot_ref.3) | copy-start | bytes 388
  10.6 6.1 %collective-permute-start = (f32[32,384]{1,0:T(8,128)S(1)}, f32[32,384]{1,0:T(8,128)}, u32[]{:S(2)}, u32[]{:S(2)}) collective-permute-start(f32[32,384]{1,0:T(8,128)S(1)} %get-tuple-element.13), channel_id=1, source_target_pairs={{0,1},{1,0},{2,3},{3,2},{4,5},{5,4},{6,7},{7,6},{8,9},{9,8},{10,11... | collective-permute-start | bytes 147464 | tf_op jit(solution)/shard_map/ppermute | solution.py:308
  10.7 2.2 %copy-start.8 = (f32[1,4,1024]{2,1,0:T(4,128)}, f32[1,4,1024]{2,1,0:T(4,128)S(1)}, u32[]{:S(2)}) copy-start(f32[1,4,1024]{2,1,0:T(4,128)S(1)} %collective-permute-done.11) | copy-start | bytes 49156
  11.4 10.3 %collective-permute-start.12 = (f32[2,4,1024]{2,1,0:T(4,128)}, f32[2,4,1024]{2,1,0:T(4,128)}, u32[]{:S(2)}, u32[]{:S(2)}) collective-permute-start(f32[2,4,1024]{2,1,0:T(4,128)} %pad_maximum_fusion.2), channel_id=1, source_target_pairs={{0,8},{4,12},{8,0},{12,4},{16,24},{20,28},{24,16},{28,20},{1,9},{5... | collective-permute-start | bytes 98312 | tf_op jit(solution)/shard_map/ppermute | solution.py:308
  12.9 19.8 %collective-permute-start.7 = (bf16[3,64,256]{2,1,0:T(8,128)(2,1)}, bf16[3,64,256]{2,1,0:T(8,128)(2,1)S(1)}, u32[]{:S(2)}, u32[]{:S(2)}) collective-permute-start(bf16[3,64,256]{2,1,0:T(8,128)(2,1)} %get-tuple-element.15), channel_id=1, source_target_pairs={{0,4},{4,8},{8,12},{12,16},{16,20},{20,24},{24,28},{1,5},{5,9},{9,... | collective-permute-start | bytes 294920 | tf_op jit(solution)/shard_map/ppermute | solution.py:402
  15.4 20.9 %collective-permute-start.8 = (bf16[3,64,256]{2,1,0:T(8,128)(2,1)S(1)}, bf16[3,64,256]{2,1,0:T(8,128)(2,1)S(1)}, u32[]{:S(2)}, u32[]{:S(2)}) collective-permute-start(bf16[3,64,256]{2,1,0:T(8,128)(2,1)S(1)} %get-tuple-element.16), channel_id=1, source_target_pairs={{4,0},{8,4},{12,8},{16,12},{20,16},{24,20},{28,24},{5,1},{9,5},{13... | collective-permute-start | bytes 294920 | tf_op jit(solution)/shard_map/ppermute | solution.py:403
  17.5 5.0 %collective-permute-start.1 = (f32[32,384]{1,0:T(8,128)S(1)}, f32[32,384]{1,0:T(8,128)S(1)}, u32[]{:S(2)}, u32[]{:S(2)}) collective-permute-start(f32[32,384]{1,0:T(8,128)S(1)} %add.21), channel_id=1, source_target_pairs={{0,2},{1,3},{2,0},{3,1},{4,6},{5,7},{6,4},{7,5},{8,10},{9,11},{10,... | collective-permute-start | bytes 147464 | tf_op jit(solution)/shard_map/ppermute | solution.py:308
  19.0 5.2 %collective-permute-start.2 = (f32[32,384]{1,0:T(8,128)S(1)}, f32[32,384]{1,0:T(8,128)S(1)}, u32[]{:S(2)}, u32[]{:S(2)}) collective-permute-start(f32[32,384]{1,0:T(8,128)S(1)} %add.21), channel_id=1, source_target_pairs={{0,4},{1,5},{2,6},{3,7},{4,0},{5,1},{6,2},{7,3},{8,12},{9,13},{10,... | collective-permute-start | bytes 147464 | tf_op jit(solution)/shard_map/ppermute | solution.py:308
  21.7 5.2 %collective-permute-start.3 = (f32[32,384]{1,0:T(8,128)S(1)}, f32[32,384]{1,0:T(8,128)S(1)}, u32[]{:S(2)}, u32[]{:S(2)}) collective-permute-start(f32[32,384]{1,0:T(8,128)S(1)} %add.21), channel_id=1, source_target_pairs={{0,6},{1,7},{2,4},{3,5},{4,2},{5,3},{6,0},{7,1},{8,14},{9,15},{10,... | collective-permute-start | bytes 147464 | tf_op jit(solution)/shard_map/ppermute | solution.py:308
  22.5 9.4 %collective-permute-start.10 = (bf16[3,16,256]{2,1,0:T(8,128)(2,1)S(1)}, bf16[3,16,256]{2,1,0:T(8,128)(2,1)S(1)}, u32[]{:S(2)}, u32[]{:S(2)}) collective-permute-start(bf16[3,16,256]{2,1,0:T(8,128)(2,1)S(1)} %get-tuple-element.18), channel_id=1, source_target_pairs={{1,0},{2,1},{3,2},{5,4},{6,5},{7,6},{9,8},{10,9},{11,10},{13,12},{... | collective-permute-start | bytes 73736 | tf_op jit(solution)/shard_map/ppermute | solution.py:405
  24.2 8.2 %collective-permute-start.9 = (bf16[3,16,256]{2,1,0:T(8,128)(2,1)S(1)}, bf16[3,16,256]{2,1,0:T(8,128)(2,1)S(1)}, u32[]{:S(2)}, u32[]{:S(2)}) collective-permute-start(bf16[3,16,256]{2,1,0:T(8,128)(2,1)S(1)} %get-tuple-element.17), channel_id=1, source_target_pairs={{0,1},{1,2},{2,3},{4,5},{5,6},{6,7},{8,9},{9,10},{10,11},{12,13},{... | collective-permute-start | bytes 73736 | tf_op jit(solution)/shard_map/ppermute | solution.py:404
  26.8 17.7 %collective-permute-start.13 = (f32[4,4,1024]{2,1,0:T(4,128)S(1)}, f32[4,4,1024]{2,1,0:T(4,128)S(1)}, u32[]{:S(2)}, u32[]{:S(2)}) collective-permute-start(f32[4,4,1024]{2,1,0:T(4,128)S(1)} %pad_maximum_fusion.1), channel_id=1, source_target_pairs={{0,16},{4,20},{8,24},{12,28},{16,0},{20,4},{24,8},{28,12},{1,17},{... | collective-permute-start | bytes 196616 | tf_op jit(solution)/shard_map/ppermute | solution.py:308
  31.8 13.5 %collective-permute-start.4 = (f32[32,384]{1,0:T(8,128)S(1)}, f32[32,384]{1,0:T(8,128)S(1)}, u32[]{:S(2)}, u32[]{:S(2)}) collective-permute-start(f32[32,384]{1,0:T(8,128)S(1)} %add_add_fusion.1), channel_id=1, source_target_pairs={{0,8},{1,9},{2,10},{3,11},{4,12},{5,13},{6,14},{7,15},{8,0},{9,1},... | collective-permute-start | bytes 147464 | tf_op jit(solution)/shard_map/ppermute | solution.py:308
  32.4 13.0 %collective-permute-start.5 = (f32[32,384]{1,0:T(8,128)S(1)}, f32[32,384]{1,0:T(8,128)S(1)}, u32[]{:S(2)}, u32[]{:S(2)}) collective-permute-start(f32[32,384]{1,0:T(8,128)S(1)} %add_add_fusion.1), channel_id=1, source_target_pairs={{0,16},{1,17},{2,18},{3,19},{4,20},{5,21},{6,22},{7,23},{8,24},{9,... | collective-permute-start | bytes 147464 | tf_op jit(solution)/shard_map/ppermute | solution.py:308
  32.7 12.7 %collective-permute-start.6 = (f32[32,384]{1,0:T(8,128)S(1)}, f32[32,384]{1,0:T(8,128)S(1)}, u32[]{:S(2)}, u32[]{:S(2)}) collective-permute-start(f32[32,384]{1,0:T(8,128)S(1)} %add_add_fusion.1), channel_id=1, source_target_pairs={{0,24},{1,25},{2,26},{3,27},{4,28},{5,29},{6,30},{7,31},{8,16},{9,... | collective-permute-start | bytes 147464 | tf_op jit(solution)/shard_map/ppermute | solution.py:308
  36.3 8.2 %copy-start.7 = (f32[4,1024]{1,0:T(4,128)S(1)}, f32[4,1024]{1,0:T(4,128)}, u32[]{:S(2)}) copy-start(f32[4,1024]{1,0:T(4,128)} %param.15) | copy-start | bytes 49156
  36.3 8.2 %copy-start.9 = (f32[1,4,1024]{2,1,0:T(4,128)S(1)}, f32[1,4,1024]{2,1,0:T(4,128)}, u32[]{:S(2)}) copy-start(f32[1,4,1024]{2,1,0:T(4,128)} %copy-done.8) | copy-start | bytes 49156
  36.4 9.1 %copy-start = (bf16[384,1024]{1,0:T(8,128)(2,1)S(1)}, bf16[384,1024]{1,0:T(8,128)(2,1)}, u32[]{:S(2)}) copy-start(bf16[384,1024]{1,0:T(8,128)(2,1)} %w_in_ref.1) | copy-start | bytes 2359300
  36.4 9.1 %copy-start.4 = (f32[1024]{0:T(1024)S(1)}, f32[1024]{0:T(1024)}, u32[]{:S(2)}) copy-start(f32[1024]{0:T(1024)} %param.14) | copy-start | bytes 12292

commit v3 on v2

v3 whole, which is shorter than its diff:
```python
import functools

import jax
import jax.numpy as jnp
from jax import lax
from jax.experimental import pallas as pl
from jax.experimental.pallas import tpu as pltpu
from jax.sharding import PartitionSpec as P

TILE = 128

time_step = 0.1
viscosity = 0.3
pool_scale = 1.0 / 64.0
state_step = 0.5
force_scale = 0.5

BOTH = ("slab", "cross")
F32 = jnp.float32
BF16 = jnp.bfloat16


def lanes(rows):
    return lax.broadcasted_iota(jnp.int32, (rows, TILE), 1)


def sublanes(rows):
    return lax.broadcasted_iota(jnp.int32, (rows, TILE), 0)


def as_column(row):
    return jnp.transpose(jnp.broadcast_to(row, (TILE, TILE)))


def hot(mask):
    return jnp.where(mask, 1.0, 0.0).astype(BF16)


def slots_of(rotors, slot_ref):
    slots = jnp.zeros_like(rotors)
    for rotor in range(slot_ref.shape[0]):
        slots = jnp.where(rotors == rotor, slot_ref[rotor], slots)
    return slots


def pool_kernel(
    tile_ref,
    rotor_ref,
    sub_ref,
    slot_ref,
    weight_ref,
    velocity_ref,
    part_ref,
    x_even_ref,
    x_odd_ref,
    y_even_ref,
    y_odd_ref,
    cells,
    tiles,
    rotor_rows,
    sub_rows,
    slot_table,
    weights,
    place_hot,
    gains,
    half_column,
    sems,
    small_sems,
):
    parts, size_x, size_y, size_z = velocity_ref.shape
    columns = size_x * size_y
    halves = size_z // TILE
    groups = tile_ref.shape[0]
    entries = groups * TILE
    rotors = slot_ref.shape[0]
    subs = weight_ref.shape[0]
    small = [
        pltpu.make_async_copy(source, target, small_sems.at[i])
        for i, (source, target) in enumerate(
            (
                (tile_ref, tiles),
                (sub_ref, sub_rows),
                (weight_ref, weights),
                (rotor_ref, rotor_rows),
                (slot_ref, slot_table),
            )
        )
    ]
    copies = [
        pltpu.make_async_copy(velocity_ref.at[c], cells.at[c], sems.at[c]) for c in range(parts)
    ]
    for copy in small + copies:
        copy.start()
    for copy in small:
        copy.wait()
    weight = weights[...]
    high = weight.astype(BF16)
    rest = weight - high.astype(F32)
    middle = rest.astype(BF16)
    low = (rest - middle.astype(F32)).astype(BF16)
    weight_parts = jnp.concatenate([high, middle, low], axis=0)
    sub_hot = []
    place_rows = tiles[...] // halves
    half_rows = tiles[...] % halves
    for group in range(groups):
        half_column[pl.ds(group * TILE, TILE), :] = as_column(half_rows[group : group + 1, :])
        place = as_column(place_rows[group : group + 1, :])
        for block in range(columns // TILE):
            place_hot[pl.ds(group * TILE, TILE), pl.ds(block * TILE, TILE)] = hot(
                place == lanes(TILE) + block * TILE
            )
        sub = as_column(sub_rows[group : group + 1, :])
        wide = jnp.concatenate([sub[:, :subs]] * 3, axis=1)
        index = lax.broadcasted_iota(jnp.int32, (TILE, subs), 1)
        sub_hot.append(hot(wide == jnp.concatenate([index] * 3, axis=1)))
    gains[...] = jnp.dot(
        jnp.concatenate(sub_hot, axis=0), weight_parts, preferred_element_type=F32
    )
    slots = slots_of(rotor_rows[...], slot_table)
    slot_hot = jnp.concatenate(
        [hot(slots[g : g + 1, :] == sublanes(rotors)) for g in range(groups)], axis=1
    )
    half = half_column[...]
    even_x = lax.axis_index("slab") % 2 == 0
    even_y = lax.axis_index("cross") % 2 == 0
    for c in range(parts):
        copies[c].wait()
        flat = cells[c].reshape(columns, size_z).astype(BF16)
        found = jnp.dot(place_hot[...], flat, preferred_element_type=F32)
        sample = found[:, :TILE]
        for h in range(1, halves):
            sample = jnp.where(half == h, found[:, h * TILE : (h + 1) * TILE], sample)
        weighted = sample * gains[:, c * TILE : (c + 1) * TILE]
        high = weighted.astype(BF16)
        rest = weighted - high.astype(F32)
        middle = rest.astype(BF16)
        low = (rest - middle.astype(F32)).astype(BF16)
        sums = jnp.dot(
            slot_hot, jnp.concatenate([high, middle, low], axis=1), preferred_element_type=F32
        )
        part_ref[c * rotors : (c + 1) * rotors, :] = (
            sums[:, 2 * TILE :] + sums[:, TILE : 2 * TILE] + sums[:, :TILE]
        )
        first, last = cells[c, 0].astype(BF16), cells[c, size_x - 1].astype(BF16)
        x_even_ref[c] = jnp.where(even_x, last, first)
        x_odd_ref[c] = jnp.where(even_x, first, last)
        first, last = cells[c, :, 0, :].astype(BF16), cells[c, :, size_y - 1, :].astype(BF16)
        y_even_ref[c] = jnp.where(even_y, last, first)
        y_odd_ref[c] = jnp.where(even_y, first, last)


def pack_rows(target_ref, start, blocks):
    rows, width = blocks[0].shape
    count = rows * len(blocks)
    for j in range(width // TILE):
        for k, block in enumerate(blocks):
            at = start + j * count + k * rows
            target_ref[at : at + rows, :] = block[:, j * TILE : (j + 1) * TILE]


def unpack_rows(source_ref, start, width):
    count = (source_ref.shape[0] - start) // (width // TILE)
    return jnp.concatenate(
        [source_ref[start + j * count : start + (j + 1) * count, :] for j in range(width // TILE)],
        axis=1,
    )


def stencil_kernel(begin, depth, fences, *refs):
    velocity_ref, out_ref = refs[fences], refs[-1]
    parts, size_x, size_y, size_z = velocity_ref.shape
    row = lax.broadcasted_iota(jnp.int32, (size_y, size_z), 0)
    lane = lax.broadcasted_iota(jnp.int32, (size_y, size_z), 1)
    zero = jnp.zeros((size_y, size_z), F32)
    for x in range(begin, begin + depth):
        wind = [velocity_ref[c, x] for c in range(parts)]
        for c in range(parts):
            here = wind[c]
            west = velocity_ref[c, x - 1] if x > 0 else zero
            east = velocity_ref[c, x + 1] if x + 1 < size_x else zero
            south = jnp.where(row == 0, 0.0, pltpu.roll(here, 1, 0))
            north = jnp.where(row == size_y - 1, 0.0, pltpu.roll(here, size_y - 1, 0))
            lower = jnp.where(lane == 0, 0.0, pltpu.roll(here, 1, 1))
            upper = jnp.where(lane == size_z - 1, 0.0, pltpu.roll(here, size_z - 1, 1))
            laplace = east + west + north + south + upper + lower - 6.0 * here
            advect = (
                wind[0] * ((east - west) * 0.5)
                + wind[1] * ((north - south) * 0.5)
                + wind[2] * ((upper - lower) * 0.5)
            )
            out_ref[c, x - begin] = here + time_step * (viscosity * laplace - advect)


def join_kernel(fences, *refs):
    refs, out_ref = refs[fences:-1], refs[-1]
    pooled_refs, state_refs = refs[:-2], refs[-2:]
    rows = pooled_refs[0].shape[0]
    total = pooled_refs[0][...]
    for other in pooled_refs[1:]:
        total = total + other[...]
    out_ref[:rows, :] = total
    even = lax.axis_index("slab") % 2 == 0
    mine, other = state_refs[0][...], state_refs[1][...]
    pack_rows(out_ref, rows, [jnp.where(even, mine, other), jnp.where(even, other, mine)])


def merge_kernel(shift, pooled_rows, width, *refs):
    packed, out_ref = refs[:-1], refs[-1]
    total = packed[0][:pooled_rows, :]
    for other in packed[1:]:
        total = total + other[:pooled_rows, :]
    out_ref[:pooled_rows, :] = total
    pack_rows(out_ref, pooled_rows, in_order(packed, shift, pooled_rows, width))


def in_order(packed, shift, pooled_rows, width):
    count = len(packed)
    mine = (lax.axis_index("slab") >> shift) % count
    blocks = [unpack_rows(ref, pooled_rows, width) for ref in packed]
    ordered = []
    for place in range(count):
        block = blocks[0]
        for k in range(1, count):
            block = jnp.where((mine ^ k) == place, blocks[k], block)
        ordered.append(block)
    return ordered


def add_halo(field, wind, halo, sign):
    return field + halo.astype(F32) * (time_step * (viscosity - sign * 0.5 * wind))


def rotor_kernel(
    packs,
    planes,
    shift,
    slot_ref,
    tile_ref,
    rotor_ref,
    sub_ref,
    w_in_ref,
    w_out_ref,
    decay_ref,
    cells_ref,
    x_even_ref,
    x_odd_ref,
    y_even_ref,
    y_odd_ref,
    *rest,
):
    packed, rest = rest[:packs], rest[packs:]
    field_refs, rest = rest[:planes], rest[planes:]
    out_ref, new_ref, by_slab, source_rows, key_hot, place_hot, field, sems = rest
    slabs, rows, width = by_slab.shape
    rotors = slabs * rows
    parts, size_x, size_y, size_z = cells_ref.shape
    columns = size_x * size_y
    halves = size_z // TILE
    groups = tile_ref.shape[0]
    subs = w_out_ref.shape[1] // TILE
    pooled = packed[0][: parts * rotors, :]
    for other in packed[1:]:
        pooled = pooled + other[: parts * rotors, :]
    pooled = (pooled * pool_scale).astype(BF16)
    pooled = jnp.concatenate([pooled[c * rotors : (c + 1) * rotors] for c in range(parts)], axis=1)
    old = jnp.concatenate(in_order(packed, shift, parts * rotors, width), axis=0)
    drive = jnp.dot(pooled, w_in_ref[...], preferred_element_type=F32)
    new = old + state_step * (drive - decay_ref[...] * old)
    for j in range(slabs):
        by_slab[j] = new[j * rows : (j + 1) * rows, :]
    new_ref[...] = by_slab[lax.axis_index("slab")]
    new_b = new.astype(BF16)

    depth = size_x // planes
    even_x = lax.axis_index("slab") % 2 == 0
    even_y = lax.axis_index("cross") % 2 == 0
    stores = []
    for c in range(parts - 1, -1, -1):
        for k in range(planes):
            field[c, k * depth : (k + 1) * depth] = field_refs[k][c]
        near, far = x_even_ref[c], x_odd_ref[c]
        west, east = jnp.where(even_x, far, near), jnp.where(even_x, near, far)
        wind = cells_ref[0, 0]
        field[c, 0] = add_halo(field[c, 0], wind, west, -1)
        wind = cells_ref[0, size_x - 1]
        field[c, size_x - 1] = add_halo(field[c, size_x - 1], wind, east, 1)
        near, far = y_even_ref[c], y_odd_ref[c]
        south, north = jnp.where(even_y, far, near), jnp.where(even_y, near, far)
        wind = cells_ref[1, :, 0, :]
        field[c, :, 0, :] = add_halo(field[c, :, 0, :], wind, south, -1)
        wind = cells_ref[1, :, size_y - 1, :]
        field[c, :, size_y - 1, :] = add_halo(field[c, :, size_y - 1, :], wind, north, 1)
        if c > 0:
            stores.append(pltpu.make_async_copy(field.at[c], out_ref.at[c], sems.at[c]))
            stores[-1].start()

    slots = slots_of(rotor_ref[...], slot_ref)
    keys = sub_ref[...] * rotors + slots
    places = tile_ref[...] // halves
    half_rows = tile_ref[...] % halves
    for group in range(groups):
        key = as_column(keys[group : group + 1, :])
        at = pl.ds(group * TILE, TILE)
        for block in range(subs * rotors // TILE):
            key_hot[at, pl.ds(block * TILE, TILE)] = hot(key == lanes(TILE) + block * TILE)
        for block in range(columns // TILE):
            place_hot[pl.ds(block * TILE, TILE), at] = hot(
                places[group : group + 1, :] == sublanes(TILE) + block * TILE
            )
    sources = jnp.dot(new_b, w_out_ref[...], preferred_element_type=F32).astype(BF16)
    for sub in range(subs):
        source_rows[sub * rotors : (sub + 1) * rotors, :] = sources[:, sub * TILE : (sub + 1) * TILE]
    taken = jnp.dot(key_hot[...], source_rows[...], preferred_element_type=F32)
    half = jnp.concatenate([as_column(half_rows[g : g + 1, :]) for g in range(groups)], axis=0)
    spread = jnp.concatenate(
        [jnp.where(half == h, taken, 0.0).astype(BF16) for h in range(halves)], axis=1
    )
    chunks = sems.shape[0] - parts
    depth = size_x // chunks
    for chunk in range(chunks):
        at = pl.ds(chunk * depth, depth)
        forcing = jnp.dot(
            place_hot[pl.ds(chunk * depth * size_y, depth * size_y), :],
            spread,
            preferred_element_type=F32,
        )
        field[0, at] = field[0, at] - force_scale * forcing.reshape(depth, size_y, size_z)
        stores.append(
            pltpu.make_async_copy(field.at[0, at], out_ref.at[0, at], sems.at[parts + chunk])
        )
        stores[-1].start()
    for store in stores:
        store.wait()


def bit_groups(bits):
    first = bits % 2
    return ([(0,)] if first else []) + [(b, b + 1) for b in range(first, bits, 2)]


def offsets_of(group):
    found = [0]
    for bit in group:
        found = found + [offset | (1 << bit) for offset in found]
    return found[1:]


def swap(value, axis, count, offset):
    return lax.ppermute(value, axis, [(i, i ^ offset) for i in range(count)])


def swap_pairs(value, axis, count, first):
    pairs = [(i, i + 1) for i in range(first, count - 1, 2)]
    return lax.ppermute(value, axis, pairs + [(j, i) for i, j in pairs])


def vmem(count):
    return [pl.BlockSpec(memory_space=pltpu.VMEM)] * count


def in_hbm(value):
    return pltpu.with_memory_space_constraint(value, pltpu.HBM)


SMEM = pl.BlockSpec(memory_space=pltpu.SMEM)
HBM = pl.BlockSpec(memory_space=pltpu.HBM)
ANY = pl.BlockSpec(memory_space=pl.ANY)


def pool(tile, rotor, sub, slot_of_rotor, shape_weight, velocity):
    parts, size_x, size_y, size_z = velocity.shape
    columns = size_x * size_y
    groups = tile.shape[0]
    entries = groups * TILE
    rotors = slot_of_rotor.shape[0]
    return pl.pallas_call(
        pool_kernel,
        out_shape=(
            jax.ShapeDtypeStruct((parts * rotors, TILE), F32),
            jax.ShapeDtypeStruct((parts, size_y, size_z), BF16),
            jax.ShapeDtypeStruct((parts, size_y, size_z), BF16),
            jax.ShapeDtypeStruct((parts, size_x, size_z), BF16),
            jax.ShapeDtypeStruct((parts, size_x, size_z), BF16),
            jax.ShapeDtypeStruct(velocity.shape, F32),
        ),
        in_specs=[HBM] * 6,
        out_specs=tuple(vmem(6)),
        scratch_shapes=[
            pltpu.VMEM((groups, TILE), jnp.int32),
            pltpu.VMEM((groups, TILE), jnp.int32),
            pltpu.VMEM((groups, TILE), jnp.int32),
            pltpu.SMEM((rotors,), jnp.int32),
            pltpu.VMEM(shape_weight.shape, F32),
            pltpu.VMEM((entries, columns), BF16),
            pltpu.VMEM((entries, parts * TILE), F32),
            pltpu.VMEM((entries, TILE), jnp.int32),
            pltpu.SemaphoreType.DMA((parts,)),
            pltpu.SemaphoreType.DMA((5,)),
        ],
        compiler_params=pltpu.CompilerParams(vmem_limit_bytes=12 << 20),
        cost_estimate=pl.CostEstimate(
            flops=2 * entries * columns * parts * size_z,
            bytes_accessed=velocity.size * 4,
            transcendentals=0,
        ),
        name="pool",
    )(*(in_hbm(value) for value in (tile, rotor, sub, slot_of_rotor, shape_weight, velocity)))


def stencil(begin, depth, fences, velocity):
    parts, size_x, size_y, size_z = velocity.shape
    return pl.pallas_call(
        functools.partial(stencil_kernel, begin, depth, len(fences)),
        out_shape=jax.ShapeDtypeStruct((parts, depth, size_y, size_z), F32),
        in_specs=[ANY] * len(fences) + vmem(1),
        out_specs=vmem(1)[0],
        compiler_params=pltpu.CompilerParams(vmem_limit_bytes=4 << 20),
        cost_estimate=pl.CostEstimate(
            flops=1000 * velocity.size * depth // size_x,
            bytes_accessed=8 * velocity.size * depth // size_x,
            transcendentals=0,
        ),
        name="stencil",
    )(*fences, velocity)


def join(fences, pooled, states):
    rows = pooled[0].shape[0] + 2 * states[0].size // TILE
    return pl.pallas_call(
        functools.partial(join_kernel, len(fences)),
        out_shape=jax.ShapeDtypeStruct((rows, TILE), F32),
        in_specs=[ANY] * len(fences) + vmem(len(pooled) + 2),
        out_specs=vmem(1)[0],
        compiler_params=pltpu.CompilerParams(vmem_limit_bytes=4 << 20),
        name="join",
    )(*fences, *pooled, *states)


def merge(shift, pooled_rows, width, packed):
    rows = pooled_rows + len(packed) * (packed[0].shape[0] - pooled_rows)
    return pl.pallas_call(
        functools.partial(merge_kernel, shift, pooled_rows, width),
        out_shape=jax.ShapeDtypeStruct((rows, TILE), F32),
        in_specs=vmem(len(packed)),
        out_specs=vmem(1)[0],
        compiler_params=pltpu.CompilerParams(vmem_limit_bytes=4 << 20),
        name="merge",
    )(*packed)


def rotors_step(
    slabs, shift, slot_of_rotor, tile, rotor, sub, w_in, w_out, decay, velocity, halos, packed, fields
):
    width = w_in.shape[1]
    rows = slot_of_rotor.shape[0] // slabs
    parts, size_x, size_y, size_z = velocity.shape
    columns = size_x * size_y
    entries = tile.shape[0] * TILE
    keys = w_out.shape[1] // TILE * slabs * rows
    chunks = 4
    return pl.pallas_call(
        functools.partial(rotor_kernel, len(packed), len(fields), shift),
        out_shape=(
            jax.ShapeDtypeStruct(velocity.shape, F32),
            jax.ShapeDtypeStruct((rows, width), F32),
        ),
        in_specs=[SMEM] + vmem(11 + len(packed) + len(fields)),
        out_specs=(HBM, vmem(1)[0]),
        scratch_shapes=[
            pltpu.VMEM((slabs, rows, width), F32),
            pltpu.VMEM((keys, TILE), BF16),
            pltpu.VMEM((entries, keys), BF16),
            pltpu.VMEM((columns, entries), BF16),
            pltpu.VMEM(velocity.shape, F32),
            pltpu.SemaphoreType.DMA((parts + chunks,)),
        ],
        compiler_params=pltpu.CompilerParams(vmem_limit_bytes=16 << 20),
        cost_estimate=pl.CostEstimate(
            flops=4 * entries * columns * size_z, bytes_accessed=w_out.size * 2, transcendentals=0
        ),
        name="rotors",
    )(slot_of_rotor, tile, rotor, sub, w_in, w_out, decay, velocity, *halos, *packed, *fields)


def on_device(
    slabs,
    crosses,
    velocity,
    shape_weight,
    w_in,
    w_out,
    decay,
    rotor_states,
    slot_of_rotor,
    entry_rotor,
    entry_tile,
    entry_sub,
):
    entries = entry_tile.shape[0]
    width = w_in.shape[1]
    count = slabs * crosses
    tile = entry_tile.reshape(entries // TILE, TILE)
    rotor = entry_rotor.reshape(entries // TILE, TILE)
    sub = entry_sub.reshape(entries // TILE, TILE)

    states = [rotor_states, swap(rotor_states, "slab", slabs, 1)]
    part, x_even, x_odd, y_even, y_odd, cells = pool(
        tile, rotor, sub, slot_of_rotor, shape_weight, velocity
    )
    pooled_rows = part.shape[0]
    groups = bit_groups(count.bit_length() - 1)
    cross_bits = crosses.bit_length() - 1
    planes = 2
    depth = velocity.shape[1] // planes

    def exchanged(value, group):
        return [value] + [swap(value, BOTH, count, offset) for offset in offsets_of(group)]

    y_even = swap_pairs(y_even, "cross", crosses, 0)
    pooled = exchanged(part, groups[0])
    total = pooled[0] + pooled[1]
    x_even = swap_pairs(x_even, "slab", slabs, 0)
    pooled = exchanged(total, groups[1])
    fields = [stencil(0, depth, (total, x_even, y_even, states[1]), cells)]
    packed = join(fields, pooled, states)
    for group in groups[2:-1]:
        packed = merge(group[0] - cross_bits, pooled_rows, width, exchanged(packed, group))
    y_odd = swap_pairs(y_odd, "cross", crosses, 1)
    x_odd = swap_pairs(x_odd, "slab", slabs, 1)
    fields.append(stencil(depth, depth, (packed,), cells))
    packed = exchanged(packed, groups[-1])

    return rotors_step(
        slabs,
        groups[-1][0] - cross_bits,
        slot_of_rotor,
        tile,
        rotor,
        sub,
        w_in,
        w_out,
        decay[None, :],
        cells,
        (x_even, x_odd, y_even, y_odd),
        packed,
        fields,
    )


def solution(mesh):
    slabs, crosses = mesh.shape["slab"], mesh.shape["cross"]
    in_specs = (
        P(None, "slab", "cross", None),
        P(),
        P(),
        P(),
        P(),
        P("slab", None),
        P(),
        P(("slab", "cross"), None),
        P(("slab", "cross")),
        P(("slab", "cross")),
    )
    out_specs = (P(None, "slab", "cross", None), P("slab", None))
    return jax.shard_map(
        functools.partial(on_device, slabs, crosses),
        mesh=mesh,
        in_specs=in_specs,
        out_specs=out_specs,
        check_vma=False,
    )
```

time: 51.1 us -> 37.2 us (0.73)
  starting transfers between devices: 25.9 us -> 14.8 us
  waiting for transfers between devices: 0.44 us -> 5.1 us
  Pallas kernels: 20.3 us -> 16.2 us
  other arithmetic: 3.03 us -> 0.01 us
    ppermute x14 -> x12, starting transfers between devices: 25.9 us -> 14.8 us  [the longest x8 10.2 us: swap(): return lax.ppermute(value, axis, [(i, i ^ offset) for i in range(count)])]
    ppermute x14 -> x12, waiting for transfers between devices: 0.44 us -> 5.1 us  [the longest x8 5.09 us: swap(): return lax.ppermute(value, axis, [(i, i ^ offset) for i in range(count)])]
    pallas_call x3 -> x5, Pallas kernels: 20.3 us -> 16.2 us  [the longest x1 6.47 us: rotors_step(): pl.pallas_call(functools.partial(rotor_kernel, len(packed), len(fields),...]
    concatenate x3 -> x0, other arithmetic: 2.2 us -> none  [gather_xor(): jnp.concatenate([blocks, exchange(blocks, axis, count, 1 << bit)], axis=0)]
    add x3 -> x1, other arithmetic: 0.83 us -> 0.01 us  [on_device(): total = pooled[0] + pooled[1]]
  transfers between devices with their start and end apart: 14 -> 12, of which waited for: 1 -> 4; matrix products, arithmetic and copies ran while one was open for 6% -> 0% of each run, Pallas kernels for 30% -> 9%
where the time goes in v3:
time: 37.2 us; the launch traced here: 37.1 us
  Pallas kernels  16.2 us (44%)
  starting transfers between devices  14.8 us (40%)
  waiting for transfers between devices  5.1 us (14%)
  between operations  0.85 us (2%)
    ppermute x8, starting transfers between devices, swap(): return lax.ppermute(value, axis, [(i, i ^ offset) for i in range(count)])  10.2 us
    pallas_call x1, Pallas kernels, rotors_step(): pl.pallas_call(functools.partial(rotor_kernel, len(packed), len(fields),...  6.47 us
    pallas_call x1, Pallas kernels, pool(): pl.pallas_call(pool_kernel, out_shape=(jax.ShapeDtypeStruct((parts * roto...  6.43 us
    ppermute x8, waiting for transfers between devices, swap(): return lax.ppermute(value, axis, [(i, i ^ offset) for i in range(count)])  5.09 us
    ppermute x4, starting transfers between devices, swap_pairs(): return lax.ppermute(value, axis, pairs + [(j, i) for i, j in pairs])  4.66 us
    pallas_call x2, Pallas kernels, stencil(): pl.pallas_call(functools.partial(stencil_kernel, begin, depth, len(fences...  3.28 us
  transfers between devices with their start and end apart: 12, of which 4 were waited for; matrix products, arithmetic and copies ran while one was open for 0% of the time, Pallas kernels for 9%

profile of v3, /device:TPU:0, one launch (start us, length us, event | category | flops | bytes accessed | tf_op | source)
XLA Modules:
  0.0 37.1 jit_solution(12144486332785887869)
XLA Ops:
  0.6 0.0 slice-start
  0.7 6.4 %pool.1 = (f32[96,128]{1,0:T(8,128)S(1)}, bf16[3,64,256]{2,1,0:T(8,128)(2,1)S(1)}, bf16[3,64,256]{2,1,0:T(8,128)(2,1)S(1)}, bf16[3,16,256]{2,1,0:T(8,128)(2,1)S(...) custom-call(s32[8,128]{1,0:T(8,128)} %bitcast.6, s32[8,128]{1,0:T(8,128)} %bitcast.8, ...), custom_call_target="tpu_custom_call" | custom-call | flops 1610612736 | bytes 3145728 | tf_op jit(solution)/shard_map/pool/pallas_call | solution.py:376
  7.1 3.0 %collective-permute-start = (bf16[3,64,256]{2,1,0:T(8,128)(2,1)S(1)}, bf16[3,64,256]{2,1,0:T(8,128)(2,1)S(1)}, u32[]{:S(2)}, u32[]{:S(2)}) collective-permute-start(bf16[3,64,256]{2,1,0:T(8,128)(2,1)S(1)} %get-tuple-element.9), channel_id=1, source_target_pairs={{0,4},{8,12},{16,20},{24,28},{4,0},{12,8},{20,16},{28,24},{1,5},{9... | collective-permute-start | bytes 294920 | tf_op jit(solution)/shard_map/ppermute | solution.py:354
  10.1 0.2 collective-permute-start.5
  10.3 0.3 collective-permute-start.2
  10.6 0.7 %collective-permute-done.4 = f32[96,128]{1,0:T(8,128)S(1)} collective-permute-done((f32[96,128]{1,0:T(8,128)S(1)}, f32[96,128]{1,0:T(8,128)S(1)}, u32[]{:S(2)}, u32[]{:S(2)}) %collective-permute-start.4) | collective-permute-done | bytes 49184 | tf_op jit(solution)/shard_map/ppermute | solution.py:349
  11.3 2.1 %collective-permute-start.8 = (f32[96,128]{1,0:T(8,128)S(1)}, f32[96,128]{1,0:T(8,128)S(1)}, u32[]{:S(2)}, u32[]{:S(2)}) collective-permute-start(f32[96,128]{1,0:T(8,128)S(1)} %add.3.refs_0_.refs_1_), channel_id=1, source_target_pairs={{0,6},{1,7},{2,4},{3,5},{4,2},{5,3},{6,0},{7,1},{8,14},{9,15},{10,... | collective-permute-start | bytes 147464 | tf_op jit(solution)/shard_map/ppermute | solution.py:349
  13.4 1.0 %collective-permute-start.7 = (f32[96,128]{1,0:T(8,128)S(1)}, f32[96,128]{1,0:T(8,128)S(1)}, u32[]{:S(2)}, u32[]{:S(2)}) collective-permute-start(f32[96,128]{1,0:T(8,128)S(1)} %add.3.refs_0_.refs_1_), channel_id=1, source_target_pairs={{0,4},{1,5},{2,6},{3,7},{4,0},{5,1},{6,2},{7,3},{8,12},{9,13},{10,... | collective-permute-start | bytes 147464 | tf_op jit(solution)/shard_map/ppermute | solution.py:349
  14.4 0.0 collective-permute-done.5.refs_3_.refs_6_
  14.4 1.0 %collective-permute-start.6 = (f32[96,128]{1,0:T(8,128)S(1)}, f32[96,128]{1,0:T(8,128)S(1)}, u32[]{:S(2)}, u32[]{:S(2)}) collective-permute-start(f32[96,128]{1,0:T(8,128)S(1)} %add.3.refs_0_.refs_1_), channel_id=1, source_target_pairs={{0,2},{1,3},{2,0},{3,1},{4,6},{5,7},{6,4},{7,5},{8,10},{9,11},{10,... | collective-permute-start | bytes 147464 | tf_op jit(solution)/shard_map/ppermute | solution.py:349
  15.4 0.0 collective-permute-done.2.refs_2_.y_even_ref
  15.4 0.7 %collective-permute-start.1 = (bf16[3,64,256]{2,1,0:T(8,128)(2,1)S(1)}, bf16[3,64,256]{2,1,0:T(8,128)(2,1)S(1)}, u32[]{:S(2)}, u32[]{:S(2)}) collective-permute-start(bf16[3,64,256]{2,1,0:T(8,128)(2,1)S(1)} %get-tuple-element.10), channel_id=1, source_target_pairs={{4,8},{12,16},{20,24},{8,4},{16,12},{24,20},{5,9},{13,17},{21,25},... | collective-permute-start | bytes 294920 | tf_op jit(solution)/shard_map/ppermute | solution.py:354
  16.0 0.0 collective-permute-done.refs_1_.x_even_ref
  16.0 0.0 slice-start.1
  16.1 1.6 %stencil.2.refs_0_.rest_4_ = f32[3,8,64,256]{3,2,1,0:T(8,128)S(1)} custom-call(f32[96,128]{1,0:T(8,128)S(1)} %add.3.refs_0_.refs_1_, bf16[3,64,256]{2,1,0:T(8,128)(2,1)S(1)} %collective-permute-done.refs_1_.x_even_ref, bf16[3,16,256]{2,1,0:T(8,128)(2,1)S(1)} %collective-permute-done.2.refs_2_.y_even_ref, ...), custom_call_target="tpu_custom_call" | custom-call | flops 393216000 | bytes 3145728 | tf_op jit(solution)/shard_map/stencil/pallas_call | solution.py:412
  17.7 0.0 copy-start
  17.7 0.0 copy-start.2
  17.7 0.0 copy-start.3
  17.7 0.0 copy-start.4
  17.7 0.0 copy-start.5
  17.8 0.0 copy-start.6
  17.8 0.0 collective-permute-done.8.refs_4_
  17.8 0.0 collective-permute-done.7.refs_3_
  17.8 0.7 %collective-permute-done.6.refs_2_ = f32[96,128]{1,0:T(8,128)S(1)} collective-permute-done((f32[96,128]{1,0:T(8,128)S(1)}, f32[96,128]{1,0:T(8,128)S(1)}, u32[]{:S(2)}, u32[]{:S(2)}) %collective-permute-start.6) | collective-permute-done | bytes 49184 | tf_op jit(solution)/shard_map/ppermute | solution.py:349
  18.5 5.4 %collective-permute-start.11 = (f32[160,128]{1,0:T(8,128)S(1)}, f32[160,128]{1,0:T(8,128)S(1)}, u32[]{:S(2)}, u32[]{:S(2)}) collective-permute-start(f32[160,128]{1,0:T(8,128)S(1)} %join.1.refs_0_.rest_0_), channel_id=1, source_target_pairs={{0,24},{1,25},{2,26},{3,27},{4,28},{5,29},{6,30},{7,31},{8,16},{9,... | collective-permute-start | bytes 245768 | tf_op jit(solution)/shard_map/ppermute | solution.py:349
  23.9 0.0 collective-permute-start.10
  23.9 0.6 %collective-permute-start.9 = (f32[160,128]{1,0:T(8,128)S(1)}, f32[160,128]{1,0:T(8,128)S(1)}, u32[]{:S(2)}, u32[]{:S(2)}) collective-permute-start(f32[160,128]{1,0:T(8,128)S(1)} %join.1.refs_0_.rest_0_), channel_id=1, source_target_pairs={{0,8},{1,9},{2,10},{3,11},{4,12},{5,13},{6,14},{7,15},{8,0},{9,1},... | collective-permute-start | bytes 245768 | tf_op jit(solution)/shard_map/ppermute | solution.py:349
  24.5 0.7 %collective-permute-start.3 = (bf16[3,16,256]{2,1,0:T(8,128)(2,1)S(1)}, bf16[3,16,256]{2,1,0:T(8,128)(2,1)S(1)}, u32[]{:S(2)}, u32[]{:S(2)}) collective-permute-start(bf16[3,16,256]{2,1,0:T(8,128)(2,1)S(1)} %get-tuple-element.12), channel_id=1, source_target_pairs={{1,2},{2,1},{5,6},{6,5},{9,10},{10,9},{13,14},{14,13},{17,18},{18,... | collective-permute-start | bytes 73736 | tf_op jit(solution)/shard_map/ppermute | solution.py:354
  25.2 1.6 %stencil.3.rest_5_ = f32[3,8,64,256]{3,2,1,0:T(8,128)S(1)} custom-call(f32[160,128]{1,0:T(8,128)S(1)} %join.1.refs_0_.rest_0_, f32[3,16,64,256]{3,2,1,0:T(8,128)S(1)} %get-tuple-element.8.refs_4_.refs_1_.cells_ref), custom_call_target="tpu_custom_call" | custom-call | flops 393216000 | bytes 3145728 | tf_op jit(solution)/shard_map/stencil/pallas_call | solution.py:412
  26.8 0.2 collective-permute-done.11.rest_3_
  27.0 3.5 %collective-permute-done.10.rest_2_ = f32[160,128]{1,0:T(8,128)S(1)} collective-permute-done((f32[160,128]{1,0:T(8,128)S(1)}, f32[160,128]{1,0:T(8,128)S(1)}, u32[]{:S(2)}, u32[]{:S(2)}) %collective-permute-start.10) | collective-permute-done | bytes 81952 | tf_op jit(solution)/shard_map/ppermute | solution.py:349
  30.6 6.5 %rotors.1 = (f32[3,16,64,256]{3,2,1,0:T(8,128)}, f32[4,1024]{1,0:T(4,128)}) custom-call(s32[32]{0:T(128)S(1)} %copy-done.6, s32[8,128]{1,0:T(8,128)S(1)} %bitcast.7, s32[8,128]{1,0:T(8,128)S(1)} %bitcast.9, s32[8,128]{1,0:T(8,128)S(1)} %bitcast.11, bf16[384,1024]{1,0:T(8,128)(2,1)S(1)} %copy-done, bf16[1024,4096]{1,0:T(8,128)(2,1)S(1)} %bitcast.5, ...), custom_call_target="tpu_custom_call" | custom-call | flops 1073741824 | bytes 8388608 | tf_op jit(solution)/shard_map/rotors/pallas_call | solution.py:461
  (17 shorter events, 0.1 us)
Async XLA Ops:
  0.6 9.5 %copy-start.1 = (f32[4,1024]{1,0:T(4,128)S(1)}, f32[4,1024]{1,0:T(4,128)}, u32[]{:S(2)}) copy-start(f32[4,1024]{1,0:T(4,128)} %refs_5_.1) | copy-start | bytes 49156
  0.6 29.9 %slice-start = ((s8[8388608]{0:T(1024)(128)(4,1)}), s8[4194304]{0:T(1024)(128)(4,1)S(1)}, s32[]{:S(2)}) async-start(s8[8388608]{0:T(1024)(128)(4,1)} %bitcast.4), calls=%async_computation | async-start | bytes 8388608
  7.1 8.9 %collective-permute-start = (bf16[3,64,256]{2,1,0:T(8,128)(2,1)S(1)}, bf16[3,64,256]{2,1,0:T(8,128)(2,1)S(1)}, u32[]{:S(2)}, u32[]{:S(2)}) collective-permute-start(bf16[3,64,256]{2,1,0:T(8,128)(2,1)S(1)} %get-tuple-element.9), channel_id=1, source_target_pairs={{0,4},{8,12},{16,20},{24,28},{4,0},{12,8},{20,16},{28,24},{1,5},{9... | collective-permute-start | bytes 294920 | tf_op jit(solution)/shard_map/ppermute | solution.py:354
  10.1 1.2 %collective-permute-start.4 = (f32[96,128]{1,0:T(8,128)S(1)}, f32[96,128]{1,0:T(8,128)S(1)}, u32[]{:S(2)}, u32[]{:S(2)}) collective-permute-start(f32[96,128]{1,0:T(8,128)S(1)} %get-tuple-element.13), channel_id=1, source_target_pairs={{0,1},{1,0},{2,3},{3,2},{4,5},{5,4},{6,7},{7,6},{8,9},{9,8},{10,11... | collective-permute-start | bytes 147464 | tf_op jit(solution)/shard_map/ppermute | solution.py:349
  10.1 4.3 %collective-permute-start.5 = (f32[4,1024]{1,0:T(4,128)S(1)}, f32[4,1024]{1,0:T(4,128)S(1)}, u32[]{:S(2)}, u32[]{:S(2)}) collective-permute-start(f32[4,1024]{1,0:T(4,128)S(1)} %copy-done.1), channel_id=1, source_target_pairs={{0,4},{4,0},{8,12},{12,8},{16,20},{20,16},{24,28},{28,24},{1,5},{5... | collective-permute-start | bytes 49160 | tf_op jit(solution)/shard_map/ppermute | solution.py:349
  10.3 5.1 %collective-permute-start.2 = (bf16[3,16,256]{2,1,0:T(8,128)(2,1)S(1)}, bf16[3,16,256]{2,1,0:T(8,128)(2,1)S(1)}, u32[]{:S(2)}, u32[]{:S(2)}) collective-permute-start(bf16[3,16,256]{2,1,0:T(8,128)(2,1)S(1)} %get-tuple-element.11), channel_id=1, source_target_pairs={{0,1},{2,3},{1,0},{3,2},{4,5},{6,7},{5,4},{7,6},{8,9},{10,11},{9,8... | collective-permute-start | bytes 73736 | tf_op jit(solution)/shard_map/ppermute | solution.py:354
  11.3 6.4 %collective-permute-start.8 = (f32[96,128]{1,0:T(8,128)S(1)}, f32[96,128]{1,0:T(8,128)S(1)}, u32[]{:S(2)}, u32[]{:S(2)}) collective-permute-start(f32[96,128]{1,0:T(8,128)S(1)} %add.3.refs_0_.refs_1_), channel_id=1, source_target_pairs={{0,6},{1,7},{2,4},{3,5},{4,2},{5,3},{6,0},{7,1},{8,14},{9,15},{10,... | collective-permute-start | bytes 147464 | tf_op jit(solution)/shard_map/ppermute | solution.py:349
  13.4 4.4 %collective-permute-start.7 = (f32[96,128]{1,0:T(8,128)S(1)}, f32[96,128]{1,0:T(8,128)S(1)}, u32[]{:S(2)}, u32[]{:S(2)}) collective-permute-start(f32[96,128]{1,0:T(8,128)S(1)} %add.3.refs_0_.refs_1_), channel_id=1, source_target_pairs={{0,4},{1,5},{2,6},{3,7},{4,0},{5,1},{6,2},{7,3},{8,12},{9,13},{10,... | collective-permute-start | bytes 147464 | tf_op jit(solution)/shard_map/ppermute | solution.py:349
  14.4 4.1 %collective-permute-start.6 = (f32[96,128]{1,0:T(8,128)S(1)}, f32[96,128]{1,0:T(8,128)S(1)}, u32[]{:S(2)}, u32[]{:S(2)}) collective-permute-start(f32[96,128]{1,0:T(8,128)S(1)} %add.3.refs_0_.refs_1_), channel_id=1, source_target_pairs={{0,2},{1,3},{2,0},{3,1},{4,6},{5,7},{6,4},{7,5},{8,10},{9,11},{10,... | collective-permute-start | bytes 147464 | tf_op jit(solution)/shard_map/ppermute | solution.py:349
  15.4 11.5 %collective-permute-start.1 = (bf16[3,64,256]{2,1,0:T(8,128)(2,1)S(1)}, bf16[3,64,256]{2,1,0:T(8,128)(2,1)S(1)}, u32[]{:S(2)}, u32[]{:S(2)}) collective-permute-start(bf16[3,64,256]{2,1,0:T(8,128)(2,1)S(1)} %get-tuple-element.10), channel_id=1, source_target_pairs={{4,8},{12,16},{20,24},{8,4},{16,12},{24,20},{5,9},{13,17},{21,25},... | collective-permute-start | bytes 294920 | tf_op jit(solution)/shard_map/ppermute | solution.py:354
  16.0 14.5 %slice-start.1 = ((s8[8388608]{0:T(1024)(128)(4,1)}), s8[4194304]{0:T(1024)(128)(4,1)S(1)}, s32[]{:S(2)}) async-start(s8[8388608]{0:T(1024)(128)(4,1)} %bitcast.4), calls=%async_computation.1 | async-start | bytes 8388608
  17.7 12.8 %copy-start = (bf16[384,1024]{1,0:T(8,128)(2,1)S(1)}, bf16[384,1024]{1,0:T(8,128)(2,1)}, u32[]{:S(2)}) copy-start(bf16[384,1024]{1,0:T(8,128)(2,1)} %w_in_ref.1) | copy-start | bytes 2359300
  17.7 12.8 %copy-start.2 = (s32[1024]{0:T(1024)S(1)}, s32[1024]{0:T(1024)}, u32[]{:S(2)}) copy-start(s32[1024]{0:T(1024)} %param.18) | copy-start | bytes 12292
  17.7 12.8 %copy-start.3 = (s32[1024,1]{0,1:T(1,128)S(1)}, s32[1024,1]{0,1:T(1,128)}, u32[]{:S(2)}) copy-start(s32[1024,1]{0,1:T(1,128)} %param.17) | copy-start | bytes 12292
  17.7 12.8 %copy-start.4 = (s32[1024]{0:T(1024)S(1)}, s32[1024]{0:T(1024)}, u32[]{:S(2)}) copy-start(s32[1024]{0:T(1024)} %param.19) | copy-start | bytes 12292
  17.7 12.8 %copy-start.5 = (f32[1024]{0:T(1024)S(1)}, f32[1024]{0:T(1024)}, u32[]{:S(2)}) copy-start(f32[1024]{0:T(1024)} %param.14) | copy-start | bytes 12292
  17.8 12.8 %copy-start.6 = (s32[32]{0:T(128)S(1)}, s32[32]{0:T(128)}, u32[]{:S(2)}) copy-start(s32[32]{0:T(128)} %slot_ref.3) | copy-start | bytes 388
  18.5 8.5 %collective-permute-start.11 = (f32[160,128]{1,0:T(8,128)S(1)}, f32[160,128]{1,0:T(8,128)S(1)}, u32[]{:S(2)}, u32[]{:S(2)}) collective-permute-start(f32[160,128]{1,0:T(8,128)S(1)} %join.1.refs_0_.rest_0_), channel_id=1, source_target_pairs={{0,24},{1,25},{2,26},{3,27},{4,28},{5,29},{6,30},{7,31},{8,16},{9,... | collective-permute-start | bytes 245768 | tf_op jit(solution)/shard_map/ppermute | solution.py:349
  23.9 6.7 %collective-permute-start.10 = (f32[160,128]{1,0:T(8,128)S(1)}, f32[160,128]{1,0:T(8,128)S(1)}, u32[]{:S(2)}, u32[]{:S(2)}) collective-permute-start(f32[160,128]{1,0:T(8,128)S(1)} %join.1.refs_0_.rest_0_), channel_id=1, source_target_pairs={{0,16},{1,17},{2,18},{3,19},{4,20},{5,21},{6,22},{7,23},{8,24},{9,... | collective-permute-start | bytes 245768 | tf_op jit(solution)/shard_map/ppermute | solution.py:349
  23.9 6.7 %collective-permute-start.9 = (f32[160,128]{1,0:T(8,128)S(1)}, f32[160,128]{1,0:T(8,128)S(1)}, u32[]{:S(2)}, u32[]{:S(2)}) collective-permute-start(f32[160,128]{1,0:T(8,128)S(1)} %join.1.refs_0_.rest_0_), channel_id=1, source_target_pairs={{0,8},{1,9},{2,10},{3,11},{4,12},{5,13},{6,14},{7,15},{8,0},{9,1},... | collective-permute-start | bytes 245768 | tf_op jit(solution)/shard_map/ppermute | solution.py:349
  24.5 2.3 %collective-permute-start.3 = (bf16[3,16,256]{2,1,0:T(8,128)(2,1)S(1)}, bf16[3,16,256]{2,1,0:T(8,128)(2,1)S(1)}, u32[]{:S(2)}, u32[]{:S(2)}) collective-permute-start(bf16[3,16,256]{2,1,0:T(8,128)(2,1)S(1)} %get-tuple-element.12), channel_id=1, source_target_pairs={{1,2},{2,1},{5,6},{6,5},{9,10},{10,9},{13,14},{14,13},{17,18},{18,... | collective-permute-start | bytes 73736 | tf_op jit(solution)/shard_map/ppermute | solution.py:354

commit v4 on v3

v4 whole, which is shorter than its diff:
```python
import functools

import jax
import jax.numpy as jnp
from jax import lax
from jax.experimental import pallas as pl
from jax.experimental.pallas import tpu as pltpu
from jax.sharding import PartitionSpec as P

TILE = 128

time_step = 0.1
viscosity = 0.3
pool_scale = 1.0 / 64.0
state_step = 0.5
force_scale = 0.5

BOTH = ("slab", "cross")
F32 = jnp.float32
BF16 = jnp.bfloat16


def lanes(rows):
    return lax.broadcasted_iota(jnp.int32, (rows, TILE), 1)


def sublanes(rows):
    return lax.broadcasted_iota(jnp.int32, (rows, TILE), 0)


def as_column(row):
    return jnp.transpose(jnp.broadcast_to(row, (TILE, TILE)))


def hot(mask):
    return jnp.where(mask, 1.0, 0.0).astype(BF16)


def slots_of(rotors, slot_ref):
    slots = jnp.zeros_like(rotors)
    for rotor in range(slot_ref.shape[0]):
        slots = jnp.where(rotors == rotor, slot_ref[rotor], slots)
    return slots


def load_kernel(
    tile_ref,
    rotor_ref,
    sub_ref,
    slot_ref,
    weight_ref,
    velocity_ref,
    x_odd_ref,
    cells,
    place_hot,
    gains,
    half_column,
    slot_hot,
    tiles,
    rotor_rows,
    sub_rows,
    slot_table,
    weights,
    sems,
    small_sems,
):
    parts, size_x, size_y, size_z = velocity_ref.shape
    columns = size_x * size_y
    halves = size_z // TILE
    groups = tile_ref.shape[0]
    rotors = slot_ref.shape[0]
    subs = weight_ref.shape[0]
    small = [
        pltpu.make_async_copy(source, target, small_sems.at[i])
        for i, (source, target) in enumerate(
            (
                (tile_ref, tiles),
                (sub_ref, sub_rows),
                (weight_ref, weights),
                (rotor_ref, rotor_rows),
                (slot_ref, slot_table),
            )
        )
    ]
    copies = [
        pltpu.make_async_copy(velocity_ref.at[c], cells.at[c], sems.at[c]) for c in range(parts)
    ]
    for copy in small + copies:
        copy.start()
    for copy in small:
        copy.wait()
    weight = weights[...]
    high = weight.astype(BF16)
    rest = weight - high.astype(F32)
    middle = rest.astype(BF16)
    low = (rest - middle.astype(F32)).astype(BF16)
    weight_parts = jnp.concatenate([high, middle, low], axis=0)
    sub_hot = []
    place_rows = tiles[...] // halves
    half_rows = tiles[...] % halves
    for group in range(groups):
        half_column[pl.ds(group * TILE, TILE), :] = as_column(half_rows[group : group + 1, :])
        place = as_column(place_rows[group : group + 1, :])
        for block in range(columns // TILE):
            place_hot[pl.ds(group * TILE, TILE), pl.ds(block * TILE, TILE)] = hot(
                place == lanes(TILE) + block * TILE
            )
        sub = as_column(sub_rows[group : group + 1, :])
        wide = jnp.concatenate([sub[:, :subs]] * 3, axis=1)
        index = lax.broadcasted_iota(jnp.int32, (TILE, subs), 1)
        sub_hot.append(hot(wide == jnp.concatenate([index] * 3, axis=1)))
    gains[...] = jnp.dot(
        jnp.concatenate(sub_hot, axis=0), weight_parts, preferred_element_type=F32
    )
    slots = slots_of(rotor_rows[...], slot_table)
    slot_hot[...] = jnp.concatenate(
        [hot(slots[g : g + 1, :] == sublanes(rotors)) for g in range(groups)], axis=1
    )
    even_x = lax.axis_index("slab") % 2 == 0
    for c in range(parts):
        copies[c].wait()
        first, last = cells[c, 0], cells[c, size_x - 1]
        x_odd_ref[c] = jnp.where(even_x, first, last).astype(BF16)


def first_half(bits):
    index = lax.axis_index("slab") * lax.axis_size("cross") + lax.axis_index("cross")
    parity = index
    for bit in range(1, bits):
        parity = parity ^ (index >> bit)
    return parity % 2 == 0


def pool_kernel(
    bits,
    cells,
    place_hot,
    gains,
    half_column,
    slot_hot,
    keep_ref,
    send_ref,
    y_even_ref,
    y_odd_ref,
    total,
):
    parts, size_x, size_y, size_z = cells.shape
    columns = size_x * size_y
    halves = size_z // TILE
    rotors = slot_hot.shape[0]
    half = half_column[...]
    even_y = lax.axis_index("cross") % 2 == 0
    for c in range(parts):
        flat = cells[c].reshape(columns, size_z).astype(BF16)
        found = jnp.dot(place_hot[...], flat, preferred_element_type=F32)
        sample = found[:, :TILE]
        for h in range(1, halves):
            sample = jnp.where(half == h, found[:, h * TILE : (h + 1) * TILE], sample)
        weighted = sample * gains[:, c * TILE : (c + 1) * TILE]
        high = weighted.astype(BF16)
        rest = weighted - high.astype(F32)
        middle = rest.astype(BF16)
        low = (rest - middle.astype(F32)).astype(BF16)
        sums = jnp.dot(
            slot_hot[...],
            jnp.concatenate([high, middle, low], axis=1),
            preferred_element_type=F32,
        )
        total[c * rotors : (c + 1) * rotors, :] = (
            sums[:, 2 * TILE :] + sums[:, TILE : 2 * TILE] + sums[:, :TILE]
        )
        first, last = cells[c, :, 0, :], cells[c, :, size_y - 1, :]
        y_even_ref[c] = jnp.where(even_y, last, first).astype(BF16)
        y_odd_ref[c] = jnp.where(even_y, first, last).astype(BF16)
    rows = keep_ref.shape[0]
    first, second = total[:rows, :], total[rows:, :]
    keep_ref[...] = jnp.where(first_half(bits), first, second)
    send_ref[...] = jnp.where(first_half(bits), second, first)


def pack_rows(target_ref, start, blocks):
    rows, width = blocks[0].shape
    count = rows * len(blocks)
    for j in range(width // TILE):
        for k, block in enumerate(blocks):
            at = start + j * count + k * rows
            target_ref[at : at + rows, :] = block[:, j * TILE : (j + 1) * TILE]


def unpack_rows(source_ref, start, width):
    count = (source_ref.shape[0] - start) // (width // TILE)
    return jnp.concatenate(
        [source_ref[start + j * count : start + (j + 1) * count, :] for j in range(width // TILE)],
        axis=1,
    )


def stencil_kernel(begin, depth, fences, slabs, crosses, *refs):
    refs, out_ref = refs[fences:-1], refs[-1]
    velocity_ref, x_even_ref, x_odd_ref, y_even_ref, y_odd_ref = refs
    parts, size_x, size_y, size_z = velocity_ref.shape
    row = lax.broadcasted_iota(jnp.int32, (size_y, size_z), 0)
    lane = lax.broadcasted_iota(jnp.int32, (size_y, size_z), 1)
    slab, cross = lax.axis_index("slab"), lax.axis_index("cross")
    even_x, even_y = slab % 2 == 0, cross % 2 == 0
    inner_x = jnp.logical_and(slab > 0, slab < slabs - 1)
    inner_y = jnp.logical_and(cross > 0, cross < crosses - 1)
    for c in range(parts):
        near = y_even_ref[c].astype(F32)
        far = jnp.where(inner_y, y_odd_ref[c].astype(F32), 0.0)
        souths, norths = jnp.where(even_y, far, near), jnp.where(even_y, near, far)
        for x in range(begin, begin + depth):
            wind = [velocity_ref[d, x] for d in range(parts)]
            here = wind[c]
            if x > 0:
                west = velocity_ref[c, x - 1]
            else:
                far_x = jnp.where(inner_x, x_odd_ref[c].astype(F32), 0.0)
                west = jnp.where(even_x, far_x, x_even_ref[c].astype(F32))
            if x + 1 < size_x:
                east = velocity_ref[c, x + 1]
            else:
                far_x = jnp.where(inner_x, x_odd_ref[c].astype(F32), 0.0)
                east = jnp.where(even_x, x_even_ref[c].astype(F32), far_x)
            south = jnp.where(row == 0, souths[x : x + 1, :], pltpu.roll(here, 1, 0))
            north = jnp.where(
                row == size_y - 1, norths[x : x + 1, :], pltpu.roll(here, size_y - 1, 0)
            )
            lower = jnp.where(lane == 0, 0.0, pltpu.roll(here, 1, 1))
            upper = jnp.where(lane == size_z - 1, 0.0, pltpu.roll(here, size_z - 1, 1))
            laplace = east + west + north + south + upper + lower - 6.0 * here
            advect = (
                wind[0] * ((east - west) * 0.5)
                + wind[1] * ((north - south) * 0.5)
                + wind[2] * ((upper - lower) * 0.5)
            )
            out_ref[c, x - begin] = here + time_step * (viscosity * laplace - advect)


def key_kernel(fence_ref, cells, slot_ref, rotor_ref, sub_ref, key_ref, x_even_ref):
    del fence_ref
    even_x = lax.axis_index("slab") % 2 == 0
    for c in range(cells.shape[0]):
        face = jnp.where(even_x, cells[c, cells.shape[1] - 1], cells[c, 0])
        x_even_ref[c] = face.astype(BF16)
    rotors = slot_ref.shape[0]
    keys = sub_ref[...] * rotors + slots_of(rotor_ref[...], slot_ref)
    for group in range(keys.shape[0]):
        key = as_column(keys[group : group + 1, :])
        for block in range(key_ref.shape[1] // TILE):
            key_ref[pl.ds(group * TILE, TILE), pl.ds(block * TILE, TILE)] = hot(
                key == lanes(TILE) + block * TILE
            )


def place_kernel(halves, fence_ref, tile_ref, place_ref):
    del fence_ref
    places = tile_ref[...] // halves
    for group in range(places.shape[0]):
        for block in range(place_ref.shape[0] // TILE):
            place_ref[pl.ds(block * TILE, TILE), pl.ds(group * TILE, TILE)] = hot(
                places[group : group + 1, :] == sublanes(TILE) + block * TILE
            )


def join_kernel(bits, fences, *refs):
    keep_ref, other_ref, states_ref, out_ref = refs[fences:]
    rows = keep_ref.shape[0]
    out_ref[:rows, :] = keep_ref[...] + other_ref[...]
    half = states_ref.shape[1] // 2
    pack_rows(
        out_ref, rows, [jnp.where(first_half(bits), states_ref[:, :half], states_ref[:, half:])]
    )


def merge_kernel(fences, shift, rows, width, pooled_rows, *refs):
    mine_ref, other_ref, out_ref = refs[fences:]
    out_ref[:pooled_rows, :] = mine_ref[:pooled_rows, :] + other_ref[:pooled_rows, :]
    if shift is None:
        out_ref[pooled_rows:, :] = mine_ref[pooled_rows:, :]
        return
    first = (lax.axis_index("slab") >> shift) % 2 == 0
    mine, other = [unpack_rows(ref, pooled_rows, width) for ref in (mine_ref, other_ref)]
    low, high = jnp.where(first, mine, other), jnp.where(first, other, mine)
    pieces = []
    for at in range(0, low.shape[0], rows):
        pieces += [low[at : at + rows], high[at : at + rows]]
    pack_rows(out_ref, pooled_rows, pieces)


def rotor_kernel(
    bits,
    planes,
    tile_ref,
    w_in_ref,
    w_out_ref,
    decay_ref,
    key_hot,
    place_hot,
    keep_ref,
    other_ref,
    *rest,
):
    field_refs, rest = rest[:planes], rest[planes:]
    out_ref, new_ref, by_slab, source_rows, wind, sems = rest
    slabs, rows, width = by_slab.shape
    rotors = slabs * rows
    size_x, size_y, size_z = wind.shape
    parts = w_in_ref.shape[0] // TILE
    halves = size_z // TILE
    groups = tile_ref.shape[0]
    subs = w_out_ref.shape[1] // TILE
    depth = size_x // planes
    stores = []
    for k in range(planes):
        for c in range(1, parts):
            stores.append(
                pltpu.make_async_copy(
                    field_refs[k].at[c],
                    out_ref.at[c, pl.ds(k * depth, depth)],
                    sems.at[k * (parts - 1) + c - 1],
                )
            )
            stores[-1].start()
    split = parts * rotors // 2
    first = first_half(bits)
    keep, other = keep_ref[:split, :], other_ref[:split, :]
    pooled = jnp.concatenate(
        [jnp.where(first, keep, other), jnp.where(first, other, keep)], axis=0
    )
    pooled = (pooled * pool_scale).astype(BF16)
    pooled = jnp.concatenate([pooled[c * rotors : (c + 1) * rotors] for c in range(parts)], axis=1)
    keep, other = [unpack_rows(ref, split, width // 2) for ref in (keep_ref, other_ref)]
    old = jnp.concatenate(
        [jnp.where(first, keep, other), jnp.where(first, other, keep)], axis=1
    )
    drive = jnp.dot(pooled, w_in_ref[...], preferred_element_type=F32)
    new = old + state_step * (drive - decay_ref[...] * old)
    for j in range(slabs):
        by_slab[j] = new[j * rows : (j + 1) * rows, :]
    new_ref[...] = by_slab[lax.axis_index("slab")]
    new_b = new.astype(BF16)

    half_rows = tile_ref[...] % halves
    sources = jnp.dot(new_b, w_out_ref[...], preferred_element_type=F32).astype(BF16)
    for sub in range(subs):
        source_rows[sub * rotors : (sub + 1) * rotors, :] = sources[:, sub * TILE : (sub + 1) * TILE]
    taken = jnp.dot(key_hot[...], source_rows[...], preferred_element_type=F32)
    half = jnp.concatenate([as_column(half_rows[g : g + 1, :]) for g in range(groups)], axis=0)
    spread = jnp.concatenate(
        [jnp.where(half == h, taken, 0.0).astype(BF16) for h in range(halves)], axis=1
    )
    for k in range(planes):
        forcing = jnp.dot(
            place_hot[pl.ds(k * depth * size_y, depth * size_y), :],
            spread,
            preferred_element_type=F32,
        )
        at = pl.ds(k * depth, depth)
        wind[at] = field_refs[k][0] - force_scale * forcing.reshape(depth, size_y, size_z)
        stores.append(
            pltpu.make_async_copy(wind.at[at], out_ref.at[0, at], sems.at[planes * (parts - 1) + k])
        )
        stores[-1].start()
    for store in stores:
        store.wait()


def swap(value, axis, count, offset):
    return lax.ppermute(value, axis, [(i, i ^ offset) for i in range(count)])


def swap_pairs(value, axis, count, first):
    pairs = [(i, (i + 1) % count) for i in range(first, count, 2)]
    return lax.ppermute(value, axis, pairs + [(j, i) for i, j in pairs])


def vmem(count):
    return [pl.BlockSpec(memory_space=pltpu.VMEM)] * count


def in_hbm(value):
    return pltpu.with_memory_space_constraint(value, pltpu.HBM)


SMEM = pl.BlockSpec(memory_space=pltpu.SMEM)
HBM = pl.BlockSpec(memory_space=pltpu.HBM)
ANY = pl.BlockSpec(memory_space=pl.ANY)


def load(tile, rotor, sub, slot_of_rotor, shape_weight, velocity):
    parts, size_x, size_y, size_z = velocity.shape
    columns = size_x * size_y
    groups = tile.shape[0]
    entries = groups * TILE
    rotors = slot_of_rotor.shape[0]
    return pl.pallas_call(
        load_kernel,
        out_shape=(
            jax.ShapeDtypeStruct((parts, size_y, size_z), BF16),
            jax.ShapeDtypeStruct(velocity.shape, F32),
            jax.ShapeDtypeStruct((entries, columns), BF16),
            jax.ShapeDtypeStruct((entries, parts * TILE), F32),
            jax.ShapeDtypeStruct((entries, TILE), jnp.int32),
            jax.ShapeDtypeStruct((rotors, entries), BF16),
        ),
        in_specs=[HBM] * 6,
        out_specs=tuple(vmem(6)),
        scratch_shapes=[
            pltpu.VMEM((groups, TILE), jnp.int32),
            pltpu.VMEM((groups, TILE), jnp.int32),
            pltpu.VMEM((groups, TILE), jnp.int32),
            pltpu.SMEM((rotors,), jnp.int32),
            pltpu.VMEM(shape_weight.shape, F32),
            pltpu.SemaphoreType.DMA((parts,)),
            pltpu.SemaphoreType.DMA((5,)),
        ],
        compiler_params=pltpu.CompilerParams(vmem_limit_bytes=8 << 20),
        cost_estimate=pl.CostEstimate(
            flops=2 * entries * columns * size_z,
            bytes_accessed=velocity.size * 4,
            transcendentals=0,
        ),
        name="load",
    )(*(in_hbm(value) for value in (tile, rotor, sub, slot_of_rotor, shape_weight, velocity)))


def pool(bits, cells, place_hot, gains, half_column, slot_hot):
    parts, size_x, size_y, size_z = cells.shape
    rows = parts * slot_hot.shape[0]
    part = jax.ShapeDtypeStruct((rows // 2, TILE), F32)
    return pl.pallas_call(
        functools.partial(pool_kernel, bits),
        out_shape=(
            part,
            part,
            jax.ShapeDtypeStruct((parts, size_x, size_z), BF16),
            jax.ShapeDtypeStruct((parts, size_x, size_z), BF16),
        ),
        in_specs=vmem(5),
        out_specs=tuple(vmem(4)),
        scratch_shapes=[pltpu.VMEM((rows, TILE), F32)],
        compiler_params=pltpu.CompilerParams(vmem_limit_bytes=8 << 20),
        cost_estimate=pl.CostEstimate(
            flops=2 * place_hot.size * parts * size_z, bytes_accessed=cells.size * 4, transcendentals=0
        ),
        name="pool",
    )(cells, place_hot, gains, half_column, slot_hot)


def stencil(begin, depth, fences, slabs, crosses, velocity, halos):
    parts, size_x, size_y, size_z = velocity.shape
    return pl.pallas_call(
        functools.partial(stencil_kernel, begin, depth, len(fences), slabs, crosses),
        out_shape=jax.ShapeDtypeStruct((parts, depth, size_y, size_z), F32),
        in_specs=[ANY] * len(fences) + vmem(5),
        out_specs=vmem(1)[0],
        compiler_params=pltpu.CompilerParams(vmem_limit_bytes=4 << 20),
        cost_estimate=pl.CostEstimate(
            flops=1000 * velocity.size * depth // size_x,
            bytes_accessed=8 * velocity.size * depth // size_x,
            transcendentals=0,
        ),
        name="stencil",
    )(*fences, velocity, *halos)


def key_matrix(fence, cells, slot_of_rotor, rotor, sub, keys):
    parts, _, size_y, size_z = cells.shape
    entries = rotor.shape[0] * TILE
    return pl.pallas_call(
        key_kernel,
        out_shape=(
            jax.ShapeDtypeStruct((entries, keys), BF16),
            jax.ShapeDtypeStruct((parts, size_y, size_z), BF16),
        ),
        in_specs=[ANY] + vmem(1) + [SMEM] + vmem(2),
        out_specs=tuple(vmem(2)),
        compiler_params=pltpu.CompilerParams(vmem_limit_bytes=4 << 20),
        cost_estimate=pl.CostEstimate(
            flops=1000 * entries * keys, bytes_accessed=2 * entries * keys, transcendentals=0
        ),
        name="keys",
    )(fence, cells, slot_of_rotor, rotor, sub)


def place_matrix(fence, tile, columns, halves):
    entries = tile.shape[0] * TILE
    return pl.pallas_call(
        functools.partial(place_kernel, halves),
        out_shape=jax.ShapeDtypeStruct((columns, entries), BF16),
        in_specs=[ANY] + vmem(1),
        out_specs=vmem(1)[0],
        compiler_params=pltpu.CompilerParams(vmem_limit_bytes=4 << 20),
        cost_estimate=pl.CostEstimate(
            flops=1000 * entries * columns, bytes_accessed=2 * entries * columns, transcendentals=0
        ),
        name="places",
    )(fence, tile)


def join(bits, fences, keep, other, states):
    rows = keep.shape[0] + states.size // 2 // TILE
    return pl.pallas_call(
        functools.partial(join_kernel, bits, len(fences)),
        out_shape=jax.ShapeDtypeStruct((rows, TILE), F32),
        in_specs=[ANY] * len(fences) + vmem(3),
        out_specs=vmem(1)[0],
        compiler_params=pltpu.CompilerParams(vmem_limit_bytes=4 << 20),
        name="join",
    )(*fences, keep, other, states)


def merge(fences, shift, rows, width, pooled_rows, mine, other):
    total = mine.shape[0] + (other.shape[0] - pooled_rows if shift is not None else 0)
    return pl.pallas_call(
        functools.partial(merge_kernel, len(fences), shift, rows, width, pooled_rows),
        out_shape=jax.ShapeDtypeStruct((total, TILE), F32),
        in_specs=[ANY] * len(fences) + vmem(2),
        out_specs=vmem(1)[0],
        compiler_params=pltpu.CompilerParams(vmem_limit_bytes=4 << 20),
        name="merge",
    )(*fences, mine, other)


def rotors_step(slabs, bits, tile, w_in, w_out, decay, key_hot, place_hot, keep, other, fields):
    width = w_in.shape[1]
    planes = len(fields)
    parts, depth, size_y, size_z = fields[0].shape
    size_x = planes * depth
    entries, keys = key_hot.shape
    rows = keys // (w_out.shape[1] // TILE) // slabs
    return pl.pallas_call(
        functools.partial(rotor_kernel, bits, planes),
        out_shape=(
            jax.ShapeDtypeStruct((parts, size_x, size_y, size_z), F32),
            jax.ShapeDtypeStruct((rows, width), F32),
        ),
        in_specs=vmem(8 + planes),
        out_specs=(HBM, vmem(1)[0]),
        scratch_shapes=[
            pltpu.VMEM((slabs, rows, width), F32),
            pltpu.VMEM((keys, TILE), BF16),
            pltpu.VMEM((size_x, size_y, size_z), F32),
            pltpu.SemaphoreType.DMA((planes * parts,)),
        ],
        compiler_params=pltpu.CompilerParams(vmem_limit_bytes=10 << 20),
        cost_estimate=pl.CostEstimate(
            flops=4 * place_hot.size * size_z, bytes_accessed=w_out.size * 2, transcendentals=0
        ),
        name="rotors",
    )(tile, w_in, w_out, decay, key_hot, place_hot, keep, other, *fields)


def on_device(
    slabs,
    crosses,
    velocity,
    shape_weight,
    w_in,
    w_out,
    decay,
    rotor_states,
    slot_of_rotor,
    entry_rotor,
    entry_tile,
    entry_sub,
):
    size_x, size_y, size_z = velocity.shape[1:]
    entries = entry_tile.shape[0]
    width = w_in.shape[1]
    count = slabs * crosses
    tile = entry_tile.reshape(entries // TILE, TILE)
    rotor = entry_rotor.reshape(entries // TILE, TILE)
    sub = entry_sub.reshape(entries // TILE, TILE)

    bits = count.bit_length() - 1
    x_odd, cells, *loaded = load(tile, rotor, sub, slot_of_rotor, shape_weight, velocity)
    x_odd = swap_pairs(x_odd, "slab", slabs, 1)
    keep, send, y_even, y_odd = pool(bits, cells, *loaded)
    y_even = swap_pairs(y_even, "cross", crosses, 0)
    y_odd = swap_pairs(y_odd, "cross", crosses, 1)
    pooled_rows = keep.shape[0]

    planes = 2
    depth = size_x // planes
    halos = [None, x_odd, y_even, y_odd]

    def make_keys(fence):
        made, face = key_matrix(
            fence,
            cells,
            slot_of_rotor,
            rotor,
            sub,
            w_out.shape[1] // TILE * slot_of_rotor.shape[0],
        )
        halos[0] = swap_pairs(face, "slab", slabs, 0)
        return made

    def make_places(fence):
        return place_matrix(fence, tile, size_x * size_y, size_z // TILE)

    def make_field(k, fence):
        return stencil(k * depth, depth, (fence,), slabs, crosses, cells, halos)

    work = [make_keys, make_places] + [functools.partial(make_field, k) for k in range(planes)]
    done = []
    packed = join(bits, (x_odd,), keep, swap(send, BOTH, count, 1), rotor_states)
    steps = range(bits - 1, 0, -1)
    for bit in steps:
        beside = 1 if bit > steps[-1] else len(work) - len(done)
        made = [item(packed) for item in work[len(done) : len(done) + beside]]
        done += made
        if 1 << bit >= crosses:
            other, shift = packed, bit - (crosses.bit_length() - 1)
        else:
            other, shift = packed[:pooled_rows], None
        other = swap(other, BOTH, count, 1 << bit | 1)
        packed = merge(made, shift, rotor_states.shape[0], width // 2, pooled_rows, packed, other)
    other = swap(packed, BOTH, count, 1)
    key_hot, place_hot, *fields = done
    return rotors_step(
        slabs, bits, tile, w_in, w_out, decay[None, :], key_hot, place_hot, packed, other, fields
    )


def solution(mesh):
    slabs, crosses = mesh.shape["slab"], mesh.shape["cross"]
    in_specs = (
        P(None, "slab", "cross", None),
        P(),
        P(),
        P(),
        P(),
        P("slab", None),
        P(),
        P(("slab", "cross"), None),
        P(("slab", "cross")),
        P(("slab", "cross")),
    )
    out_specs = (P(None, "slab", "cross", None), P("slab", None))
    return jax.shard_map(
        functools.partial(on_device, slabs, crosses),
        mesh=mesh,
        in_specs=in_specs,
        out_specs=out_specs,
        check_vma=False,
    )
```

time: 37.2 us -> 36.2 us (0.973)
  starting transfers between devices: 14.8 us -> 11 us
  waiting for transfers between devices: 5.1 us -> 8.01 us
    ppermute x8 -> x6, starting transfers between devices: 10.2 us -> 2.08 us  [swap(): return lax.ppermute(value, axis, [(i, i ^ offset) for i in range(count)])]
    ppermute x4, starting transfers between devices: 4.66 us -> 8.92 us  [swap_pairs(): return lax.ppermute(value, axis, pairs + [(j, i) for i, j in pairs])]
    ppermute x8 -> x6, waiting for transfers between devices: 5.09 us -> 8 us  [swap(): return lax.ppermute(value, axis, [(i, i ^ offset) for i in range(count)])]
    pallas_call x3 -> x10, Pallas kernels: 12.9 us -> 12.8 us  [the longest x1 5.3 us: rotors_step(): pl.pallas_call(functools.partial(rotor_kernel, bits, planes), out_shape=(...]
  transfers between devices with their start and end apart: 12 -> 10, of which waited for: 4 -> 5; matrix products, arithmetic and copies ran while one was open for 0% -> 0% of each run, Pallas kernels for 9% -> 24%
where the time goes in v4:
time: 36.2 us; the launch traced here: 36 us
  Pallas kernels  16.1 us (44%)
  starting transfers between devices  11 us (30%)
  waiting for transfers between devices  8.01 us (22%)
  between operations  0.85 us (2%)
    ppermute x4, starting transfers between devices, swap_pairs(): return lax.ppermute(value, axis, pairs + [(j, i) for i, j in pairs])  8.92 us
    ppermute x6, waiting for transfers between devices, swap(): return lax.ppermute(value, axis, [(i, i ^ offset) for i in range(count)])  8 us
    pallas_call x1, Pallas kernels, rotors_step(): pl.pallas_call(functools.partial(rotor_kernel, bits, planes), out_shape=(...  5.3 us
    pallas_call x1, Pallas kernels, pool(): pl.pallas_call(functools.partial(pool_kernel, bits), out_shape=(part, par...  3.69 us
    pallas_call x2, Pallas kernels, stencil(): pl.pallas_call(functools.partial(stencil_kernel, begin, depth, len(fences...  3.22 us
    pallas_call x1, Pallas kernels, load(): pl.pallas_call(load_kernel, out_shape=(jax.ShapeDtypeStruct((parts, size_...  2.13 us
    ppermute x6, starting transfers between devices, swap(): return lax.ppermute(value, axis, [(i, i ^ offset) for i in range(count)])  2.08 us
    pallas_call x1, Pallas kernels, key_matrix(): pl.pallas_call(key_kernel, out_shape=(jax.ShapeDtypeStruct((entries, keys...  1.05 us
  transfers between devices with their start and end apart: 10, of which 5 were waited for; matrix products, arithmetic and copies ran while one was open for 0% of the time, Pallas kernels for 24%

profile of v4, /device:TPU:0, one launch (start us, length us, event | category | flops | bytes accessed | tf_op | source)
XLA Modules:
  0.0 36.0 jit_solution(3010040000818974258)
XLA Ops:
  0.6 2.1 %load.1 = (bf16[3,64,256]{2,1,0:T(8,128)(2,1)S(1)}, f32[3,16,64,256]{3,2,1,0:T(8,128)S(1)}, bf16[1024,1024]{1,0:T(8,128)(2,1)S(1)}, f32[1024,384]{1,0:T(8,128)S(...) custom-call(s32[8,128]{1,0:T(8,128)} %bitcast.6, s32[8,128]{1,0:T(8,128)} %bitcast.9, s32[8,128]{1,0:T(8,128)} %bitcast.11, ...), custom_call_target="tpu_custom_call" | custom-call | flops 536870912 | bytes 3145728 | tf_op jit(solution)/shard_map/load/pallas_call | solution.py:397
  2.8 6.0 %collective-permute-start = (bf16[3,64,256]{2,1,0:T(8,128)(2,1)S(1)}, bf16[3,64,256]{2,1,0:T(8,128)(2,1)S(1)}, u32[]{:S(2)}, u32[]{:S(2)}) collective-permute-start(bf16[3,64,256]{2,1,0:T(8,128)(2,1)S(1)} %get-tuple-element.14), channel_id=1, source_target_pairs={{4,8},{12,16},{20,24},{28,0},{8,4},{16,12},{24,20},{0,28},{5,9},{1... | collective-permute-start | bytes 294920 | tf_op jit(solution)/shard_map/ppermute | solution.py:375
  8.8 3.7 %pool.1 = (f32[48,128]{1,0:T(8,128)S(1)}, f32[48,128]{1,0:T(8,128)S(1)}, bf16[3,16,256]{2,1,0:T(8,128)(2,1)S(1)}, bf16[3,16,256]{2,1,0:T(8,128)(2,1)S(1)}) custom-call(f32[3,16,64,256]{3,2,1,0:T(8,128)S(1)} %get-tuple-element.15.cells.refs_1_, bf16[1024,1024]{1,0:T(8,128)(2,1)S(1)} %get-tuple-element.16.place_hot, f32[1024,384]{1,0:T(8,128)S(1)} %get-tuple-element.17.gains, ...), custom_call_target="tpu_custom_call" | custom-call | flops 1610612736 | bytes 3145728 | tf_op jit(solution)/shard_map/pool/pallas_call | solution.py:432
  12.5 0.1 collective-permute-start.1
  12.6 0.5 %collective-permute-start.5 = (bf16[3,16,256]{2,1,0:T(8,128)(2,1)S(1)}, bf16[3,16,256]{2,1,0:T(8,128)(2,1)S(1)}, u32[]{:S(2)}, u32[]{:S(2)}) collective-permute-start(bf16[3,16,256]{2,1,0:T(8,128)(2,1)S(1)} %get-tuple-element.24), channel_id=1, source_target_pairs={{0,1},{2,3},{1,0},{3,2},{4,5},{6,7},{5,4},{7,6},{8,9},{10,11},{9,8... | collective-permute-start | bytes 73736 | tf_op jit(solution)/shard_map/ppermute | solution.py:375
  13.1 1.2 %collective-permute-start.6 = (bf16[3,16,256]{2,1,0:T(8,128)(2,1)S(1)}, bf16[3,16,256]{2,1,0:T(8,128)(2,1)S(1)}, u32[]{:S(2)}, u32[]{:S(2)}) collective-permute-start(bf16[3,16,256]{2,1,0:T(8,128)(2,1)S(1)} %get-tuple-element.25), channel_id=1, source_target_pairs={{1,2},{3,0},{2,1},{0,3},{5,6},{7,4},{6,5},{4,7},{9,10},{11,8},{10,... | collective-permute-start | bytes 73736 | tf_op jit(solution)/shard_map/ppermute | solution.py:375
  14.3 0.0 collective-permute-done.1.refs_2_
  14.3 0.0 collective-permute-done.refs_0_.refs_3_
  14.3 0.0 copy-done.2
  14.3 0.0 copy-start.1
  14.4 0.1 collective-permute-start.2
  14.5 1.0 %keys.1 = (bf16[1024,1024]{1,0:T(8,128)(2,1)S(1)}, bf16[3,64,256]{2,1,0:T(8,128)(2,1)S(1)}) custom-call(f32[64,128]{1,0:T(8,128)S(1)} %join.1.fence_ref.refs_1_, f32[3,16,64,256]{3,2,1,0:T(8,128)S(1)} %get-tuple-element.15.cells.refs_1_, s32[32]{0:T(128)S(1)} %copy-done.6, s32[8,128]{1,0:T(8,128)S(1)} %bitcast.10, s32[8,128]{1,0:T(8,128)S(1)} %bitcast.12), custom_call_target="tpu_custom_call" | custom-call | flops 1048576000 | bytes 2097152 | tf_op jit(solution)/shard_map/keys/pallas_call | solution.py:471
  15.5 1.2 %collective-permute-start.4 = (bf16[3,64,256]{2,1,0:T(8,128)(2,1)S(1)}, bf16[3,64,256]{2,1,0:T(8,128)(2,1)S(1)}, u32[]{:S(2)}, u32[]{:S(2)}) collective-permute-start(bf16[3,64,256]{2,1,0:T(8,128)(2,1)S(1)} %get-tuple-element.23), channel_id=1, source_target_pairs={{0,4},{8,12},{16,20},{24,28},{4,0},{12,8},{20,16},{28,24},{1,5},{9... | collective-permute-start | bytes 294920 | tf_op jit(solution)/shard_map/ppermute | solution.py:375
  16.7 2.0 %collective-permute-done.2.refs_2_ = f32[64,128]{1,0:T(8,128)S(1)} collective-permute-done((f32[64,128]{1,0:T(8,128)S(1)}, f32[64,128]{1,0:T(8,128)S(1)}, u32[]{:S(2)}, u32[]{:S(2)}) %collective-permute-start.2) | collective-permute-done | bytes 32800 | tf_op jit(solution)/shard_map/ppermute | solution.py:370
  18.7 0.1 collective-permute-start.3
  18.8 0.6 %places.1.refs_0_.place_hot = bf16[1024,1024]{1,0:T(8,128)(2,1)S(1)} custom-call(f32[80,128]{1,0:T(8,128)S(1)} %merge.4.fence_ref.refs_1_, s32[8,128]{1,0:T(8,128)S(1)} %bitcast.7), custom_call_target="tpu_custom_call" | custom-call | flops 1048576000 | bytes 2097152 | tf_op jit(solution)/shard_map/places/pallas_call | solution.py:489
  19.4 2.8 %collective-permute-done.3.refs_2_ = f32[80,128]{1,0:T(8,128)S(1)} collective-permute-done((f32[80,128]{1,0:T(8,128)S(1)}, f32[80,128]{1,0:T(8,128)S(1)}, u32[]{:S(2)}, u32[]{:S(2)}) %collective-permute-start.3) | collective-permute-done | bytes 40992 | tf_op jit(solution)/shard_map/ppermute | solution.py:370
  22.2 0.1 collective-permute-start.7
  22.3 0.0 collective-permute-done.5.refs_4_
  22.3 0.0 collective-permute-done.6.refs_5_
  22.3 0.0 collective-permute-done.4.refs_2_
  22.3 1.6 %stencil.2.refs_0_.rest_0_ = f32[3,8,64,256]{3,2,1,0:T(8,128)S(1)} custom-call(f32[112,128]{1,0:T(8,128)S(1)} %merge.5.refs_0_.refs_1_, f32[3,16,64,256]{3,2,1,0:T(8,128)S(1)} %get-tuple-element.15.cells.refs_1_, bf16[3,64,256]{2,1,0:T(8,128)(2,1)S(1)} %collective-permute-done.4.refs_2_, bf16[3,64,256]{2,1,0:T(8,128)(2,1)S(1)} %collective-permute-done.refs_0_.refs_3_, ...), custom_call_target="tpu_custom_call" | custom-call | flops 393216000 | bytes 3145728 | tf_op jit(solution)/shard_map/stencil/pallas_call | solution.py:453
  23.9 0.0 slice-start.1
  23.9 1.9 %collective-permute-done.7.refs_2_ = f32[112,128]{1,0:T(8,128)S(1)} collective-permute-done((f32[112,128]{1,0:T(8,128)S(1)}, f32[112,128]{1,0:T(8,128)S(1)}, u32[]{:S(2)}, u32[]{:S(2)}) %collective-permute-start.7) | collective-permute-done | bytes 57376 | tf_op jit(solution)/shard_map/ppermute | solution.py:370
  25.9 0.0 copy-start.5
  25.9 1.3 %collective-permute-start.8 = (f32[48,128]{1,0:T(8,128)S(1)}, f32[48,128]{1,0:T(8,128)S(1)}, u32[]{:S(2)}, u32[]{:S(2)}) collective-permute-start(f32[48,128]{1,0:T(8,128)S(1)} %slice.4), channel_id=1, source_target_pairs={{0,3},{1,2},{2,1},{3,0},{4,7},{5,6},{6,5},{7,4},{8,11},{9,10},{10,... | collective-permute-start | bytes 73736 | tf_op jit(solution)/shard_map/ppermute | solution.py:370
  27.2 1.6 %stencil.3.refs_0_.rest_1_ = f32[3,8,64,256]{3,2,1,0:T(8,128)S(1)} custom-call(f32[176,128]{1,0:T(8,128)S(1)} %merge.6.refs_0_.refs_1_, f32[3,16,64,256]{3,2,1,0:T(8,128)S(1)} %get-tuple-element.15.cells.refs_1_, bf16[3,64,256]{2,1,0:T(8,128)(2,1)S(1)} %collective-permute-done.4.refs_2_, bf16[3,64,256]{2,1,0:T(8,128)(2,1)S(1)} %collective-permute-done.refs_0_.refs_3_, ...), custom_call_target="tpu_custom_call" | custom-call | flops 393216000 | bytes 3145728 | tf_op jit(solution)/shard_map/stencil/pallas_call | solution.py:453
  28.8 0.0 copy-start
  28.8 0.4 %collective-permute-done.8.refs_2_ = f32[48,128]{1,0:T(8,128)S(1)} collective-permute-done((f32[48,128]{1,0:T(8,128)S(1)}, f32[48,128]{1,0:T(8,128)S(1)}, u32[]{:S(2)}, u32[]{:S(2)}) %collective-permute-start.8) | collective-permute-done | bytes 24608 | tf_op jit(solution)/shard_map/ppermute | solution.py:370
  29.2 0.5 %collective-permute-start.9 = (f32[176,128]{1,0:T(8,128)S(1)}, f32[176,128]{1,0:T(8,128)S(1)}, u32[]{:S(2)}, u32[]{:S(2)}) collective-permute-start(f32[176,128]{1,0:T(8,128)S(1)} %merge.7.keep_ref), channel_id=1, source_target_pairs={{0,1},{1,0},{2,3},{3,2},{4,5},{5,4},{6,7},{7,6},{8,9},{9,8},{10,11... | collective-permute-start | bytes 270344 | tf_op jit(solution)/shard_map/ppermute | solution.py:370
  29.7 0.9 %collective-permute-done.9.other_ref = f32[176,128]{1,0:T(8,128)S(1)} collective-permute-done((f32[176,128]{1,0:T(8,128)S(1)}, f32[176,128]{1,0:T(8,128)S(1)}, u32[]{:S(2)}, u32[]{:S(2)}) %collective-permute-start.9) | collective-permute-done | bytes 90144 | tf_op jit(solution)/shard_map/ppermute | solution.py:370
  30.7 5.3 %rotors.1 = (f32[3,16,64,256]{3,2,1,0:T(8,128)}, f32[4,1024]{1,0:T(4,128)}) custom-call(s32[8,128]{1,0:T(8,128)S(1)} %bitcast.8, bf16[384,1024]{1,0:T(8,128)(2,1)S(1)} %copy-done, bf16[1024,4096]{1,0:T(8,128)(2,1)S(1)} %bitcast.5, f32[1,1024]{1,0:T(1,128)S(1)} %bitcast.13, bf16[1024,1024]{1,0:T(8,128)(2,1)S(1)} %get-tuple-element.22.refs_0_.key_hot, ...), custom_call_target="tpu_custom_call" | custom-call | flops 1073741824 | bytes 8388608 | tf_op jit(solution)/shard_map/rotors/pallas_call | solution.py:533
  (20 shorter events, 0.1 us)
Async XLA Ops:
  2.8 11.5 %collective-permute-start = (bf16[3,64,256]{2,1,0:T(8,128)(2,1)S(1)}, bf16[3,64,256]{2,1,0:T(8,128)(2,1)S(1)}, u32[]{:S(2)}, u32[]{:S(2)}) collective-permute-start(bf16[3,64,256]{2,1,0:T(8,128)(2,1)S(1)} %get-tuple-element.14), channel_id=1, source_target_pairs={{4,8},{12,16},{20,24},{28,0},{8,4},{16,12},{24,20},{0,28},{5,9},{1... | collective-permute-start | bytes 294920 | tf_op jit(solution)/shard_map/ppermute | solution.py:375
  8.8 5.5 %copy-start.2 = (f32[4,1024]{1,0:T(4,128)S(1)}, f32[4,1024]{1,0:T(4,128)}, u32[]{:S(2)}) copy-start(f32[4,1024]{1,0:T(4,128)} %refs_3_.1) | copy-start | bytes 49156
  8.8 5.6 %copy-start.3 = (s32[1024,1]{0,1:T(1,128)S(1)}, s32[1024,1]{0,1:T(1,128)}, u32[]{:S(2)}) copy-start(s32[1024,1]{0,1:T(1,128)} %param.17) | copy-start | bytes 12292
  8.8 5.6 %copy-start.4 = (s32[1024]{0:T(1024)S(1)}, s32[1024]{0:T(1024)}, u32[]{:S(2)}) copy-start(s32[1024]{0:T(1024)} %param.19) | copy-start | bytes 12292
  8.8 5.6 %copy-start.6 = (s32[32]{0:T(128)S(1)}, s32[32]{0:T(128)}, u32[]{:S(2)}) copy-start(s32[32]{0:T(128)} %slot_ref.3) | copy-start | bytes 388
  12.5 1.8 %collective-permute-start.1 = (f32[48,128]{1,0:T(8,128)S(1)}, f32[48,128]{1,0:T(8,128)S(1)}, u32[]{:S(2)}, u32[]{:S(2)}) collective-permute-start(f32[48,128]{1,0:T(8,128)S(1)} %get-tuple-element.21), channel_id=1, source_target_pairs={{0,1},{1,0},{2,3},{3,2},{4,5},{5,4},{6,7},{7,6},{8,9},{9,8},{10,11... | collective-permute-start | bytes 73736 | tf_op jit(solution)/shard_map/ppermute | solution.py:370
  12.6 9.7 %collective-permute-start.5 = (bf16[3,16,256]{2,1,0:T(8,128)(2,1)S(1)}, bf16[3,16,256]{2,1,0:T(8,128)(2,1)S(1)}, u32[]{:S(2)}, u32[]{:S(2)}) collective-permute-start(bf16[3,16,256]{2,1,0:T(8,128)(2,1)S(1)} %get-tuple-element.24), channel_id=1, source_target_pairs={{0,1},{2,3},{1,0},{3,2},{4,5},{6,7},{5,4},{7,6},{8,9},{10,11},{9,8... | collective-permute-start | bytes 73736 | tf_op jit(solution)/shard_map/ppermute | solution.py:375
  13.1 9.2 %collective-permute-start.6 = (bf16[3,16,256]{2,1,0:T(8,128)(2,1)S(1)}, bf16[3,16,256]{2,1,0:T(8,128)(2,1)S(1)}, u32[]{:S(2)}, u32[]{:S(2)}) collective-permute-start(bf16[3,16,256]{2,1,0:T(8,128)(2,1)S(1)} %get-tuple-element.25), channel_id=1, source_target_pairs={{1,2},{3,0},{2,1},{0,3},{5,6},{7,4},{6,5},{4,7},{9,10},{11,8},{10,... | collective-permute-start | bytes 73736 | tf_op jit(solution)/shard_map/ppermute | solution.py:375
  14.3 4.4 %copy-start.1 = (s32[1024]{0:T(1024)S(1)}, s32[1024]{0:T(1024)}, u32[]{:S(2)}) copy-start(s32[1024]{0:T(1024)} %param.18) | copy-start | bytes 12292
  14.4 4.3 %collective-permute-start.2 = (f32[64,128]{1,0:T(8,128)S(1)}, f32[64,128]{1,0:T(8,128)S(1)}, u32[]{:S(2)}, u32[]{:S(2)}) collective-permute-start(f32[64,128]{1,0:T(8,128)S(1)} %join.1.fence_ref.refs_1_), channel_id=1, source_target_pairs={{0,17},{1,16},{2,19},{3,18},{4,21},{5,20},{6,23},{7,22},{8,25},{9,... | collective-permute-start | bytes 98312 | tf_op jit(solution)/shard_map/ppermute | solution.py:370
  15.5 6.8 %collective-permute-start.4 = (bf16[3,64,256]{2,1,0:T(8,128)(2,1)S(1)}, bf16[3,64,256]{2,1,0:T(8,128)(2,1)S(1)}, u32[]{:S(2)}, u32[]{:S(2)}) collective-permute-start(bf16[3,64,256]{2,1,0:T(8,128)(2,1)S(1)} %get-tuple-element.23), channel_id=1, source_target_pairs={{0,4},{8,12},{16,20},{24,28},{4,0},{12,8},{20,16},{28,24},{1,5},{9... | collective-permute-start | bytes 294920 | tf_op jit(solution)/shard_map/ppermute | solution.py:375
  18.7 3.5 %collective-permute-start.3 = (f32[80,128]{1,0:T(8,128)S(1)}, f32[80,128]{1,0:T(8,128)S(1)}, u32[]{:S(2)}, u32[]{:S(2)}) collective-permute-start(f32[80,128]{1,0:T(8,128)S(1)} %merge.4.fence_ref.refs_1_), channel_id=1, source_target_pairs={{0,9},{1,8},{2,11},{3,10},{4,13},{5,12},{6,15},{7,14},{8,1},{9,0},... | collective-permute-start | bytes 122888 | tf_op jit(solution)/shard_map/ppermute | solution.py:370
  22.2 8.5 %slice-start = ((s8[8388608]{0:T(1024)(128)(4,1)}), s8[4194304]{0:T(1024)(128)(4,1)S(1)}, s32[]{:S(2)}) async-start(s8[8388608]{0:T(1024)(128)(4,1)} %bitcast.4), calls=%async_computation | async-start | bytes 8388608
  22.2 3.7 %collective-permute-start.7 = (f32[112,128]{1,0:T(8,128)S(1)}, f32[112,128]{1,0:T(8,128)S(1)}, u32[]{:S(2)}, u32[]{:S(2)}) collective-permute-start(f32[112,128]{1,0:T(8,128)S(1)} %merge.5.refs_0_.refs_1_), channel_id=1, source_target_pairs={{0,5},{1,4},{2,7},{3,6},{4,1},{5,0},{6,3},{7,2},{8,13},{9,12},{10,... | collective-permute-start | bytes 172040 | tf_op jit(solution)/shard_map/ppermute | solution.py:370
  23.9 6.8 %slice-start.1 = ((s8[8388608]{0:T(1024)(128)(4,1)}), s8[4194304]{0:T(1024)(128)(4,1)S(1)}, s32[]{:S(2)}) async-start(s8[8388608]{0:T(1024)(128)(4,1)} %bitcast.4), calls=%async_computation.1 | async-start | bytes 8388608
  25.9 4.8 %copy-start.5 = (f32[1024]{0:T(1024)S(1)}, f32[1024]{0:T(1024)}, u32[]{:S(2)}) copy-start(f32[1024]{0:T(1024)} %param.14) | copy-start | bytes 12292
  25.9 3.3 %collective-permute-start.8 = (f32[48,128]{1,0:T(8,128)S(1)}, f32[48,128]{1,0:T(8,128)S(1)}, u32[]{:S(2)}, u32[]{:S(2)}) collective-permute-start(f32[48,128]{1,0:T(8,128)S(1)} %slice.4), channel_id=1, source_target_pairs={{0,3},{1,2},{2,1},{3,0},{4,7},{5,6},{6,5},{7,4},{8,11},{9,10},{10,... | collective-permute-start | bytes 73736 | tf_op jit(solution)/shard_map/ppermute | solution.py:370
  28.8 1.9 %copy-start = (bf16[384,1024]{1,0:T(8,128)(2,1)S(1)}, bf16[384,1024]{1,0:T(8,128)(2,1)}, u32[]{:S(2)}) copy-start(bf16[384,1024]{1,0:T(8,128)(2,1)} %w_in_ref.1) | copy-start | bytes 2359300
  29.2 1.4 %collective-permute-start.9 = (f32[176,128]{1,0:T(8,128)S(1)}, f32[176,128]{1,0:T(8,128)S(1)}, u32[]{:S(2)}, u32[]{:S(2)}) collective-permute-start(f32[176,128]{1,0:T(8,128)S(1)} %merge.7.keep_ref), channel_id=1, source_target_pairs={{0,1},{1,0},{2,3},{3,2},{4,5},{5,4},{6,7},{7,6},{8,9},{9,8},{10,11... | collective-permute-start | bytes 270344 | tf_op jit(solution)/shard_map/ppermute | solution.py:370

commit v5 on v4

--- a/solution.py
+++ b/solution.py
@@ -150,25 +150,22 @@
     rotors = slot_hot.shape[0]
     half = half_column[...]
     even_y = lax.axis_index("cross") % 2 == 0
+    flat = jnp.concatenate(
+        [cells[c].reshape(columns, size_z).astype(BF16) for c in range(parts)], axis=1
+    )
+    found = jnp.dot(place_hot[...], flat, preferred_element_type=F32)
     for c in range(parts):
-        flat = cells[c].reshape(columns, size_z).astype(BF16)
-        found = jnp.dot(place_hot[...], flat, preferred_element_type=F32)
-        sample = found[:, :TILE]
+        sample = found[:, c * size_z : c * size_z + TILE]
         for h in range(1, halves):
-            sample = jnp.where(half == h, found[:, h * TILE : (h + 1) * TILE], sample)
+            at = c * size_z + h * TILE
+            sample = jnp.where(half == h, found[:, at : at + TILE], sample)
         weighted = sample * gains[:, c * TILE : (c + 1) * TILE]
         high = weighted.astype(BF16)
-        rest = weighted - high.astype(F32)
-        middle = rest.astype(BF16)
-        low = (rest - middle.astype(F32)).astype(BF16)
+        low = (weighted - high.astype(F32)).astype(BF16)
         sums = jnp.dot(
-            slot_hot[...],
-            jnp.concatenate([high, middle, low], axis=1),
-            preferred_element_type=F32,
+            slot_hot[...], jnp.concatenate([high, low], axis=1), preferred_element_type=F32
         )
-        total[c * rotors : (c + 1) * rotors, :] = (
-            sums[:, 2 * TILE :] + sums[:, TILE : 2 * TILE] + sums[:, :TILE]
-        )
+        total[c * rotors : (c + 1) * rotors, :] = sums[:, TILE:] + sums[:, :TILE]
         first, last = cells[c, :, 0, :], cells[c, :, size_y - 1, :]
         y_even_ref[c] = jnp.where(even_y, last, first).astype(BF16)
         y_odd_ref[c] = jnp.where(even_y, first, last).astype(BF16)
@@ -205,13 +202,21 @@
     even_x, even_y = slab % 2 == 0, cross % 2 == 0
     inner_x = jnp.logical_and(slab > 0, slab < slabs - 1)
     inner_y = jnp.logical_and(cross > 0, cross < crosses - 1)
+    souths, norths = [], []
     for c in range(parts):
         near = y_even_ref[c].astype(F32)
         far = jnp.where(inner_y, y_odd_ref[c].astype(F32), 0.0)
-        souths, norths = jnp.where(even_y, far, near), jnp.where(even_y, near, far)
-        for x in range(begin, begin + depth):
-            wind = [velocity_ref[d, x] for d in range(parts)]
-            here = wind[c]
+        souths.append(jnp.where(even_y, far, near))
+        norths.append(jnp.where(even_y, near, far))
+    spread = time_step * viscosity
+    for x in range(begin, begin + depth):
+        drift = [(0.5 * time_step) * velocity_ref[d, x] for d in range(parts)]
+        to_east, to_west = spread - drift[0], spread + drift[0]
+        to_north, to_south = spread - drift[1], spread + drift[1]
+        to_upper = jnp.where(lane == size_z - 1, 0.0, spread - drift[2])
+        to_lower = jnp.where(lane == 0, 0.0, spread + drift[2])
+        for c in range(parts):
+            here = velocity_ref[c, x]
             if x > 0:
                 west = velocity_ref[c, x - 1]
             else:
@@ -222,29 +227,26 @@
             else:
                 far_x = jnp.where(inner_x, x_odd_ref[c].astype(F32), 0.0)
                 east = jnp.where(even_x, x_even_ref[c].astype(F32), far_x)
-            south = jnp.where(row == 0, souths[x : x + 1, :], pltpu.roll(here, 1, 0))
+            south = jnp.where(row == 0, souths[c][x : x + 1, :], pltpu.roll(here, 1, 0))
             north = jnp.where(
-                row == size_y - 1, norths[x : x + 1, :], pltpu.roll(here, size_y - 1, 0)
+                row == size_y - 1, norths[c][x : x + 1, :], pltpu.roll(here, size_y - 1, 0)
             )
-            lower = jnp.where(lane == 0, 0.0, pltpu.roll(here, 1, 1))
-            upper = jnp.where(lane == size_z - 1, 0.0, pltpu.roll(here, size_z - 1, 1))
-            laplace = east + west + north + south + upper + lower - 6.0 * here
-            advect = (
-                wind[0] * ((east - west) * 0.5)
-                + wind[1] * ((north - south) * 0.5)
-                + wind[2] * ((upper - lower) * 0.5)
+            out_ref[c, x - begin] = (
+                (1.0 - 6.0 * spread) * here
+                + (to_east * east + to_west * west)
+                + (to_north * north + to_south * south)
+                + (to_upper * pltpu.roll(here, size_z - 1, 1) + to_lower * pltpu.roll(here, 1, 1))
             )
-            out_ref[c, x - begin] = here + time_step * (viscosity * laplace - advect)
-
-
-def key_kernel(fence_ref, cells, slot_ref, rotor_ref, sub_ref, key_ref, x_even_ref):
-    del fence_ref
+
+
+def key_kernel(fences, *refs):
+    cells, slot_ref, rotor_ref, sub_ref, key_ref, x_even_ref = refs[fences:]
     even_x = lax.axis_index("slab") % 2 == 0
     for c in range(cells.shape[0]):
         face = jnp.where(even_x, cells[c, cells.shape[1] - 1], cells[c, 0])
         x_even_ref[c] = face.astype(BF16)
     rotors = slot_ref.shape[0]
-    keys = sub_ref[...] * rotors + slots_of(rotor_ref[...], slot_ref)
+    keys = sub_ref[...] // 2 * rotors + slots_of(rotor_ref[...], slot_ref)
     for group in range(keys.shape[0]):
         key = as_column(keys[group : group + 1, :])
         for block in range(key_ref.shape[1] // TILE):
@@ -292,6 +294,7 @@
     bits,
     planes,
     tile_ref,
+    sub_ref,
     w_in_ref,
     w_out_ref,
     decay_ref,
@@ -302,7 +305,7 @@
     *rest,
 ):
     field_refs, rest = rest[:planes], rest[planes:]
-    out_ref, new_ref, by_slab, source_rows, wind, sems = rest
+    out_ref, new_ref, by_slab, source_rows, wind, sems, new_sem = rest
     slabs, rows, width = by_slab.shape
     rotors = slabs * rows
     size_x, size_y, size_z = wind.shape
@@ -338,26 +341,37 @@
     new = old + state_step * (drive - decay_ref[...] * old)
     for j in range(slabs):
         by_slab[j] = new[j * rows : (j + 1) * rows, :]
-    new_ref[...] = by_slab[lax.axis_index("slab")]
+    own = pltpu.make_async_copy(by_slab.at[lax.axis_index("slab")], new_ref, new_sem)
+    own.start()
+    stores.append(own)
     new_b = new.astype(BF16)
 
     half_rows = tile_ref[...] % halves
     sources = jnp.dot(new_b, w_out_ref[...], preferred_element_type=F32).astype(BF16)
-    for sub in range(subs):
-        source_rows[sub * rotors : (sub + 1) * rotors, :] = sources[:, sub * TILE : (sub + 1) * TILE]
+    for pair in range(subs // 2):
+        source_rows[pair * rotors : (pair + 1) * rotors, :] = sources[
+            :, pair * 2 * TILE : (pair + 1) * 2 * TILE
+        ]
     taken = jnp.dot(key_hot[...], source_rows[...], preferred_element_type=F32)
+    second = jnp.concatenate(
+        [as_column(sub_ref[g : g + 1, :] % 2) for g in range(groups)], axis=0
+    )
+    taken = jnp.where(second == 1, taken[:, TILE:], taken[:, :TILE])
     half = jnp.concatenate([as_column(half_rows[g : g + 1, :]) for g in range(groups)], axis=0)
     spread = jnp.concatenate(
         [jnp.where(half == h, taken, 0.0).astype(BF16) for h in range(halves)], axis=1
     )
-    for k in range(planes):
+    chunks = sems.shape[0] - planes * (parts - 1)
+    step = size_x // chunks
+    for k in range(chunks):
         forcing = jnp.dot(
-            place_hot[pl.ds(k * depth * size_y, depth * size_y), :],
+            place_hot[pl.ds(k * step * size_y, step * size_y), :],
             spread,
             preferred_element_type=F32,
         )
-        at = pl.ds(k * depth, depth)
-        wind[at] = field_refs[k][0] - force_scale * forcing.reshape(depth, size_y, size_z)
+        at = pl.ds(k * step, step)
+        field = field_refs[k * step // depth][0, pl.ds(k * step % depth, step)]
+        wind[at] = field - force_scale * forcing.reshape(step, size_y, size_z)
         stores.append(
             pltpu.make_async_copy(wind.at[at], out_ref.at[0, at], sems.at[planes * (parts - 1) + k])
         )
@@ -370,9 +384,19 @@
     return lax.ppermute(value, axis, [(i, i ^ offset) for i in range(count)])
 
 
-def swap_pairs(value, axis, count, first):
-    pairs = [(i, (i + 1) % count) for i in range(first, count, 2)]
-    return lax.ppermute(value, axis, pairs + [(j, i) for i, j in pairs])
+def swap_pairs(value, axis, counts, first):
+    slabs, crosses = counts
+    if axis == "cross":
+        pairs = [(i, (i + 1) % crosses) for i in range(first, crosses, 2)]
+        return lax.ppermute(value, axis, pairs + [(j, i) for i, j in pairs])
+    partner = {i: i + 1 for i in range(first, slabs - 1, 2)}
+    partner.update({j: i for i, j in partner.items()})
+    pairs = []
+    for slab in range(slabs):
+        for cross in range(crosses):
+            to = (partner[slab], cross) if slab in partner else (slab, cross ^ 1)
+            pairs.append((slab * crosses + cross, to[0] * crosses + to[1]))
+    return lax.ppermute(value, BOTH, pairs)
 
 
 def vmem(count):
@@ -440,7 +464,7 @@
         in_specs=vmem(5),
         out_specs=tuple(vmem(4)),
         scratch_shapes=[pltpu.VMEM((rows, TILE), F32)],
-        compiler_params=pltpu.CompilerParams(vmem_limit_bytes=8 << 20),
+        compiler_params=pltpu.CompilerParams(vmem_limit_bytes=12 << 20),
         cost_estimate=pl.CostEstimate(
             flops=2 * place_hot.size * parts * size_z, bytes_accessed=cells.size * 4, transcendentals=0
         ),
@@ -465,23 +489,23 @@
     )(*fences, velocity, *halos)
 
 
-def key_matrix(fence, cells, slot_of_rotor, rotor, sub, keys):
+def key_matrix(fences, cells, slot_of_rotor, rotor, sub, keys):
     parts, _, size_y, size_z = cells.shape
     entries = rotor.shape[0] * TILE
     return pl.pallas_call(
-        key_kernel,
+        functools.partial(key_kernel, len(fences)),
         out_shape=(
             jax.ShapeDtypeStruct((entries, keys), BF16),
             jax.ShapeDtypeStruct((parts, size_y, size_z), BF16),
         ),
-        in_specs=[ANY] + vmem(1) + [SMEM] + vmem(2),
+        in_specs=[ANY] * len(fences) + vmem(1) + [SMEM] + vmem(2),
         out_specs=tuple(vmem(2)),
         compiler_params=pltpu.CompilerParams(vmem_limit_bytes=4 << 20),
         cost_estimate=pl.CostEstimate(
             flops=1000 * entries * keys, bytes_accessed=2 * entries * keys, transcendentals=0
         ),
         name="keys",
-    )(fence, cells, slot_of_rotor, rotor, sub)
+    )(*fences, cells, slot_of_rotor, rotor, sub)
 
 
 def place_matrix(fence, tile, columns, halves):
@@ -523,33 +547,37 @@
     )(*fences, mine, other)
 
 
-def rotors_step(slabs, bits, tile, w_in, w_out, decay, key_hot, place_hot, keep, other, fields):
+def rotors_step(
+    slabs, bits, tile, sub, w_in, w_out, decay, key_hot, place_hot, keep, other, fields
+):
     width = w_in.shape[1]
     planes = len(fields)
     parts, depth, size_y, size_z = fields[0].shape
     size_x = planes * depth
-    entries, keys = key_hot.shape
-    rows = keys // (w_out.shape[1] // TILE) // slabs
+    keys = key_hot.shape[1]
+    rows = keys // (w_out.shape[1] // (2 * TILE)) // slabs
+    chunks = 4
     return pl.pallas_call(
         functools.partial(rotor_kernel, bits, planes),
         out_shape=(
             jax.ShapeDtypeStruct((parts, size_x, size_y, size_z), F32),
             jax.ShapeDtypeStruct((rows, width), F32),
         ),
-        in_specs=vmem(8 + planes),
-        out_specs=(HBM, vmem(1)[0]),
+        in_specs=vmem(9 + planes),
+        out_specs=(HBM, HBM),
         scratch_shapes=[
             pltpu.VMEM((slabs, rows, width), F32),
-            pltpu.VMEM((keys, TILE), BF16),
+            pltpu.VMEM((keys, 2 * TILE), BF16),
             pltpu.VMEM((size_x, size_y, size_z), F32),
-            pltpu.SemaphoreType.DMA((planes * parts,)),
+            pltpu.SemaphoreType.DMA((planes * (parts - 1) + chunks,)),
+            pltpu.SemaphoreType.DMA,
         ],
         compiler_params=pltpu.CompilerParams(vmem_limit_bytes=10 << 20),
         cost_estimate=pl.CostEstimate(
             flops=4 * place_hot.size * size_z, bytes_accessed=w_out.size * 2, transcendentals=0
         ),
         name="rotors",
-    )(tile, w_in, w_out, decay, key_hot, place_hot, keep, other, *fields)
+    )(tile, sub, w_in, w_out, decay, key_hot, place_hot, keep, other, *fields)
 
 
 def on_device(
@@ -576,10 +604,10 @@
 
     bits = count.bit_length() - 1
     x_odd, cells, *loaded = load(tile, rotor, sub, slot_of_rotor, shape_weight, velocity)
-    x_odd = swap_pairs(x_odd, "slab", slabs, 1)
+    x_odd = swap_pairs(x_odd, "slab", (slabs, crosses), 1)
     keep, send, y_even, y_odd = pool(bits, cells, *loaded)
-    y_even = swap_pairs(y_even, "cross", crosses, 0)
-    y_odd = swap_pairs(y_odd, "cross", crosses, 1)
+    y_even = swap_pairs(y_even, "cross", (slabs, crosses), 0)
+    y_odd = swap_pairs(y_odd, "cross", (slabs, crosses), 1)
     pooled_rows = keep.shape[0]
 
     planes = 2
@@ -588,14 +616,14 @@
 
     def make_keys(fence):
         made, face = key_matrix(
-            fence,
+            (fence, x_odd),
             cells,
             slot_of_rotor,
             rotor,
             sub,
-            w_out.shape[1] // TILE * slot_of_rotor.shape[0],
+            w_out.shape[1] // (2 * TILE) * slot_of_rotor.shape[0],
         )
-        halos[0] = swap_pairs(face, "slab", slabs, 0)
+        halos[0] = swap_pairs(face, "slab", (slabs, crosses), 0)
         return made
 
     def make_places(fence):
@@ -606,7 +634,7 @@
 
     work = [make_keys, make_places] + [functools.partial(make_field, k) for k in range(planes)]
     done = []
-    packed = join(bits, (x_odd,), keep, swap(send, BOTH, count, 1), rotor_states)
+    packed = join(bits, (), keep, swap(send, BOTH, count, 1), rotor_states)
     steps = range(bits - 1, 0, -1)
     for bit in steps:
         beside = 1 if bit > steps[-1] else len(work) - len(done)
@@ -621,7 +649,7 @@
     other = swap(packed, BOTH, count, 1)
     key_hot, place_hot, *fields = done
     return rotors_step(
-        slabs, bits, tile, w_in, w_out, decay[None, :], key_hot, place_hot, packed, other, fields
+        slabs, bits, tile, sub, w_in, w_out, decay[None, :], key_hot, place_hot, packed, other, fields
     )
 
 

time: 36.2 us -> 31 us (0.86)
  Pallas kernels: 16.1 us -> 12.6 us
  waiting for transfers between devices: 8.01 us -> 5.06 us
  starting transfers between devices: 11 us -> 12.3 us
    ppermute x4 -> x2, starting transfers between devices: 8.92 us -> 3.1 us  [swap_pairs(): return lax.ppermute(value, axis, pairs + [(j, i) for i, j in pairs])]
    ppermute x6, starting transfers between devices: 2.08 us -> 7.03 us  [swap(): return lax.ppermute(value, axis, [(i, i ^ offset) for i in range(count)])]
    ppermute x6, waiting for transfers between devices: 8 us -> 3.7 us  [swap(): return lax.ppermute(value, axis, [(i, i ^ offset) for i in range(count)])]
    ppermute x0 -> x2, starting transfers between devices: none -> 2.18 us  [swap_pairs(): return lax.ppermute(value, BOTH, pairs)]
    pallas_call x1, Pallas kernels: 3.69 us -> 2.15 us  [pool(): pl.pallas_call(functools.partial(pool_kernel, bits), out_shape=(part, par...]
    pallas_call x1, Pallas kernels: 5.3 us -> 3.86 us  [rotors_step(): pl.pallas_call(functools.partial(rotor_kernel, bits, planes), out_shape=(...]
    ppermute x0 -> x2, waiting for transfers between devices: none -> 1.35 us  [swap_pairs(): return lax.ppermute(value, BOTH, pairs)]
  transfers between devices with their start and end apart: 10 -> 10, of which waited for: 5 -> 5; matrix products, arithmetic and copies ran while one was open for 0% -> 0% of each run, Pallas kernels for 24% -> 22%
where the time goes in v5:
time: 31 us; the launch traced here: 30.8 us
  Pallas kernels  12.6 us (41%)
  starting transfers between devices  12.3 us (40%)
  waiting for transfers between devices  5.06 us (16%)
  between operations  0.79 us (3%)
    ppermute x6, starting transfers between devices, swap(): return lax.ppermute(value, axis, [(i, i ^ offset) for i in range(count)])  7.03 us
    pallas_call x1, Pallas kernels, rotors_step(): pl.pallas_call(functools.partial(rotor_kernel, bits, planes), out_shape=(...  3.86 us
    ppermute x6, waiting for transfers between devices, swap(): return lax.ppermute(value, axis, [(i, i ^ offset) for i in range(count)])  3.7 us
    ppermute x2, starting transfers between devices, swap_pairs(): return lax.ppermute(value, axis, pairs + [(j, i) for i, j in pairs])  3.1 us
    pallas_call x2, Pallas kernels, stencil(): pl.pallas_call(functools.partial(stencil_kernel, begin, depth, len(fences...  2.96 us
    ppermute x2, starting transfers between devices, swap_pairs(): return lax.ppermute(value, BOTH, pairs)  2.18 us
    pallas_call x1, Pallas kernels, pool(): pl.pallas_call(functools.partial(pool_kernel, bits), out_shape=(part, par...  2.15 us
    pallas_call x1, Pallas kernels, load(): pl.pallas_call(load_kernel, out_shape=(jax.ShapeDtypeStruct((parts, size_...  2.13 us
  transfers between devices with their start and end apart: 10, of which 5 were waited for; matrix products, arithmetic and copies ran while one was open for 0% of the time, Pallas kernels for 22%

profile of v5, /device:TPU:0, one launch (start us, length us, event | category | flops | bytes accessed | tf_op | source)
XLA Modules:
  0.0 30.8 jit_solution(9029054858887981588)
XLA Ops:
  0.6 2.1 %load.1 = (bf16[3,64,256]{2,1,0:T(8,128)(2,1)S(1)}, f32[3,16,64,256]{3,2,1,0:T(8,128)S(1)}, bf16[1024,1024]{1,0:T(8,128)(2,1)S(1)}, f32[1024,384]{1,0:T(8,128)S(...) custom-call(s32[8,128]{1,0:T(8,128)} %bitcast.11, s32[8,128]{1,0:T(8,128)} %bitcast.9, s32[8,128]{1,0:T(8,128)} %bitcast.6, ...), custom_call_target="tpu_custom_call" | custom-call | flops 536870912 | bytes 3145728 | tf_op jit(solution)/shard_map/load/pallas_call | solution.py:421
  2.8 0.5 %collective-permute-start.1 = (bf16[3,64,256]{2,1,0:T(8,128)(2,1)S(1)}, bf16[3,64,256]{2,1,0:T(8,128)(2,1)S(1)}, u32[]{:S(2)}, u32[]{:S(2)}) collective-permute-start(bf16[3,64,256]{2,1,0:T(8,128)(2,1)S(1)} %get-tuple-element.21), channel_id=1, source_target_pairs={{0,1},{1,0},{2,3},{3,2},{4,8},{5,9},{6,10},{7,11},{8,4},{9,5},{10,... | collective-permute-start | bytes 294920 | tf_op jit(solution)/shard_map/ppermute | solution.py:399
  3.3 2.2 %pool.1 = (f32[48,128]{1,0:T(8,128)S(1)}, f32[48,128]{1,0:T(8,128)S(1)}, bf16[3,16,256]{2,1,0:T(8,128)(2,1)S(1)}, bf16[3,16,256]{2,1,0:T(8,128)(2,1)S(1)}) custom-call(f32[3,16,64,256]{3,2,1,0:T(8,128)S(1)} %get-tuple-element.14.cells.refs_2_.refs_1_, bf16[1024,1024]{1,0:T(8,128)(2,1)S(1)} %get-tuple-element.15.place_hot, ...), custom_call_target="tpu_custom_call" | custom-call | flops 1610612736 | bytes 3145728 | tf_op jit(solution)/shard_map/pool/pallas_call | solution.py:456
  5.4 0.1 collective-permute-start
  5.5 0.5 %collective-permute-start.5 = (bf16[3,16,256]{2,1,0:T(8,128)(2,1)S(1)}, bf16[3,16,256]{2,1,0:T(8,128)(2,1)S(1)}, u32[]{:S(2)}, u32[]{:S(2)}) collective-permute-start(bf16[3,16,256]{2,1,0:T(8,128)(2,1)S(1)} %get-tuple-element.24), channel_id=1, source_target_pairs={{0,1},{2,3},{1,0},{3,2},{4,5},{6,7},{5,4},{7,6},{8,9},{10,11},{9,8... | collective-permute-start | bytes 73736 | tf_op jit(solution)/shard_map/ppermute | solution.py:391
  6.0 2.6 %collective-permute-start.6 = (bf16[3,16,256]{2,1,0:T(8,128)(2,1)S(1)}, bf16[3,16,256]{2,1,0:T(8,128)(2,1)S(1)}, u32[]{:S(2)}, u32[]{:S(2)}) collective-permute-start(bf16[3,16,256]{2,1,0:T(8,128)(2,1)S(1)} %get-tuple-element.25), channel_id=1, source_target_pairs={{1,2},{3,0},{2,1},{0,3},{5,6},{7,4},{6,5},{4,7},{9,10},{11,8},{10,... | collective-permute-start | bytes 73736 | tf_op jit(solution)/shard_map/ppermute | solution.py:391
  8.6 0.0 collective-permute-done.refs_1_
  8.7 0.0 copy-start.3
  8.7 3.6 %collective-permute-start.2 = (f32[64,128]{1,0:T(8,128)S(1)}, f32[64,128]{1,0:T(8,128)S(1)}, u32[]{:S(2)}, u32[]{:S(2)}) collective-permute-start(f32[64,128]{1,0:T(8,128)S(1)} %join.1.refs_0_.refs_1_), channel_id=1, source_target_pairs={{0,17},{1,16},{2,19},{3,18},{4,21},{5,20},{6,23},{7,22},{8,25},{9,... | collective-permute-start | bytes 98312 | tf_op jit(solution)/shard_map/ppermute | solution.py:384
  12.3 0.0 collective-permute-done.1.refs_1_.refs_3_
  12.3 0.8 %keys.1 = (bf16[1024,512]{1,0:T(8,128)(2,1)S(1)}, bf16[3,64,256]{2,1,0:T(8,128)(2,1)S(1)}) custom-call(f32[64,128]{1,0:T(8,128)S(1)} %join.1.refs_0_.refs_1_, bf16[3,64,256]{2,1,0:T(8,128)(2,1)S(1)} %collective-permute-done.1.refs_1_.refs_3_, f32[3,16,64,256]{3,2,1,0:T(8,128)S(1)} %get-tuple-element.14.cells.refs_2_.refs_1_, s32[32]{0:T(128)S(1)} %copy-done.6, ...), custom_call_target="tpu_custom_call" | custom-call | flops 524288000 | bytes 1048576 | tf_op jit(solution)/shard_map/keys/pallas_call | solution.py:495
  13.2 0.8 %collective-permute-done.2.refs_2_ = f32[64,128]{1,0:T(8,128)S(1)} collective-permute-done((f32[64,128]{1,0:T(8,128)S(1)}, f32[64,128]{1,0:T(8,128)S(1)}, u32[]{:S(2)}, u32[]{:S(2)}) %collective-permute-start.2) | collective-permute-done | bytes 32800 | tf_op jit(solution)/shard_map/ppermute | solution.py:384
  14.0 1.6 %collective-permute-start.3 = (f32[80,128]{1,0:T(8,128)S(1)}, f32[80,128]{1,0:T(8,128)S(1)}, u32[]{:S(2)}, u32[]{:S(2)}) collective-permute-start(f32[80,128]{1,0:T(8,128)S(1)} %merge.4.fence_ref.refs_1_), channel_id=1, source_target_pairs={{0,9},{1,8},{2,11},{3,10},{4,13},{5,12},{6,15},{7,14},{8,1},{9,0},... | collective-permute-start | bytes 122888 | tf_op jit(solution)/shard_map/ppermute | solution.py:384
  15.6 1.7 %collective-permute-start.4 = (bf16[3,64,256]{2,1,0:T(8,128)(2,1)S(1)}, bf16[3,64,256]{2,1,0:T(8,128)(2,1)S(1)}, u32[]{:S(2)}, u32[]{:S(2)}) collective-permute-start(bf16[3,64,256]{2,1,0:T(8,128)(2,1)S(1)} %get-tuple-element.23), channel_id=1, source_target_pairs={{0,4},{1,5},{2,6},{3,7},{4,0},{5,1},{6,2},{7,3},{8,12},{9,13},{10,... | collective-permute-start | bytes 294920 | tf_op jit(solution)/shard_map/ppermute | solution.py:399
  17.3 0.6 %places.1.refs_0_.place_hot = bf16[1024,1024]{1,0:T(8,128)(2,1)S(1)} custom-call(f32[80,128]{1,0:T(8,128)S(1)} %merge.4.fence_ref.refs_1_, s32[8,128]{1,0:T(8,128)S(1)} %bitcast.12), custom_call_target="tpu_custom_call" | custom-call | flops 1048576000 | bytes 2097152 | tf_op jit(solution)/shard_map/places/pallas_call | solution.py:513
  17.9 0.0 collective-permute-done.3.refs_2_
  17.9 0.0 slice-start
  18.0 1.3 %collective-permute-start.7 = (f32[112,128]{1,0:T(8,128)S(1)}, f32[112,128]{1,0:T(8,128)S(1)}, u32[]{:S(2)}, u32[]{:S(2)}) collective-permute-start(f32[112,128]{1,0:T(8,128)S(1)} %merge.5.refs_0_.refs_1_), channel_id=1, source_target_pairs={{0,5},{1,4},{2,7},{3,6},{4,1},{5,0},{6,3},{7,2},{8,13},{9,12},{10,... | collective-permute-start | bytes 172040 | tf_op jit(solution)/shard_map/ppermute | solution.py:384
  19.2 0.0 collective-permute-done.5.refs_4_
  19.2 0.0 collective-permute-done.6.refs_5_
  19.2 1.3 %collective-permute-done.4.refs_2_ = bf16[3,64,256]{2,1,0:T(8,128)(2,1)S(1)} collective-permute-done((bf16[3,64,256]{2,1,0:T(8,128)(2,1)S(1)}, bf16[3,64,256]{2,1,0:T(8,128)(2,1)S(1)}, u32[]{:S(2)}, u32[]{:S(2)}) %collective-permute-start.4) | collective-permute-done | bytes 98336 | tf_op jit(solution)/shard_map/ppermute | solution.py:399
  20.6 1.5 %stencil.2.refs_0_.rest_0_ = f32[3,8,64,256]{3,2,1,0:T(8,128)S(1)} custom-call(f32[112,128]{1,0:T(8,128)S(1)} %merge.5.refs_0_.refs_1_, f32[3,16,64,256]{3,2,1,0:T(8,128)S(1)} %get-tuple-element.14.cells.refs_2_.refs_1_, bf16[3,64,256]{2,1,0:T(8,128)(2,1)S(1)} %collective-permute-done.4.refs_2_, ...), custom_call_target="tpu_custom_call" | custom-call | flops 393216000 | bytes 3145728 | tf_op jit(solution)/shard_map/stencil/pallas_call | solution.py:477
  22.0 0.0 slice-start.1
  22.1 0.2 collective-permute-done.7.refs_2_
  22.3 0.0 copy-start.5
  22.3 0.3 collective-permute-start.8
  22.5 1.5 %stencil.3.refs_0_.rest_1_ = f32[3,8,64,256]{3,2,1,0:T(8,128)S(1)} custom-call(f32[176,128]{1,0:T(8,128)S(1)} %merge.6.refs_0_.refs_1_, f32[3,16,64,256]{3,2,1,0:T(8,128)S(1)} %get-tuple-element.14.cells.refs_2_.refs_1_, bf16[3,64,256]{2,1,0:T(8,128)(2,1)S(1)} %collective-permute-done.4.refs_2_, ...), custom_call_target="tpu_custom_call" | custom-call | flops 393216000 | bytes 3145728 | tf_op jit(solution)/shard_map/stencil/pallas_call | solution.py:477
  24.0 0.0 copy-start
  24.0 1.6 %collective-permute-done.8.refs_2_ = f32[48,128]{1,0:T(8,128)S(1)} collective-permute-done((f32[48,128]{1,0:T(8,128)S(1)}, f32[48,128]{1,0:T(8,128)S(1)}, u32[]{:S(2)}, u32[]{:S(2)}) %collective-permute-start.8) | collective-permute-done | bytes 24608 | tf_op jit(solution)/shard_map/ppermute | solution.py:384
  25.6 0.2 collective-permute-start.9
  25.8 1.2 %collective-permute-done.9.other_ref = f32[176,128]{1,0:T(8,128)S(1)} collective-permute-done((f32[176,128]{1,0:T(8,128)S(1)}, f32[176,128]{1,0:T(8,128)S(1)}, u32[]{:S(2)}, u32[]{:S(2)}) %collective-permute-start.9) | collective-permute-done | bytes 90144 | tf_op jit(solution)/shard_map/ppermute | solution.py:384
  27.0 3.9 %rotors.1 = (f32[3,16,64,256]{3,2,1,0:T(8,128)}, f32[4,1024]{1,0:T(4,128)}) custom-call(s32[8,128]{1,0:T(8,128)S(1)} %bitcast.13, s32[8,128]{1,0:T(8,128)S(1)} %bitcast.8, bf16[384,1024]{1,0:T(8,128)(2,1)S(1)} %copy-done, bf16[1024,4096]{1,0:T(8,128)(2,1)S(1)} %bitcast.5, f32[1,1024]{1,0:T(1,128)S(1)} %bitcast.14, ...), custom_call_target="tpu_custom_call" | custom-call | flops 1073741824 | bytes 8388608 | tf_op jit(solution)/shard_map/rotors/pallas_call | solution.py:560
  (20 shorter events, 0.1 us)
Async XLA Ops:
  2.8 9.5 %collective-permute-start.1 = (bf16[3,64,256]{2,1,0:T(8,128)(2,1)S(1)}, bf16[3,64,256]{2,1,0:T(8,128)(2,1)S(1)}, u32[]{:S(2)}, u32[]{:S(2)}) collective-permute-start(bf16[3,64,256]{2,1,0:T(8,128)(2,1)S(1)} %get-tuple-element.21), channel_id=1, source_target_pairs={{0,1},{1,0},{2,3},{3,2},{4,8},{5,9},{6,10},{7,11},{8,4},{9,5},{10,... | collective-permute-start | bytes 294920 | tf_op jit(solution)/shard_map/ppermute | solution.py:399
  3.3 5.3 %copy-start.4 = (f32[4,1024]{1,0:T(4,128)S(1)}, f32[4,1024]{1,0:T(4,128)}, u32[]{:S(2)}) copy-start(f32[4,1024]{1,0:T(4,128)} %refs_2_.1) | copy-start | bytes 49156
  3.3 9.0 %copy-start.1 = (s32[1024]{0:T(1024)S(1)}, s32[1024]{0:T(1024)}, u32[]{:S(2)}) copy-start(s32[1024]{0:T(1024)} %param.19) | copy-start | bytes 12292
  3.3 9.0 %copy-start.2 = (s32[1024,1]{0,1:T(1,128)S(1)}, s32[1024,1]{0,1:T(1,128)}, u32[]{:S(2)}) copy-start(s32[1024,1]{0,1:T(1,128)} %param.17) | copy-start | bytes 12292
  3.3 9.0 %copy-start.6 = (s32[32]{0:T(128)S(1)}, s32[32]{0:T(128)}, u32[]{:S(2)}) copy-start(s32[32]{0:T(128)} %refs_3_.1) | copy-start | bytes 388
  5.4 3.2 %collective-permute-start = (f32[48,128]{1,0:T(8,128)S(1)}, f32[48,128]{1,0:T(8,128)S(1)}, u32[]{:S(2)}, u32[]{:S(2)}) collective-permute-start(f32[48,128]{1,0:T(8,128)S(1)} %get-tuple-element.20), channel_id=1, source_target_pairs={{0,1},{1,0},{2,3},{3,2},{4,5},{5,4},{6,7},{7,6},{8,9},{9,8},{10,11... | collective-permute-start | bytes 73736 | tf_op jit(solution)/shard_map/ppermute | solution.py:384
  5.5 13.7 %collective-permute-start.5 = (bf16[3,16,256]{2,1,0:T(8,128)(2,1)S(1)}, bf16[3,16,256]{2,1,0:T(8,128)(2,1)S(1)}, u32[]{:S(2)}, u32[]{:S(2)}) collective-permute-start(bf16[3,16,256]{2,1,0:T(8,128)(2,1)S(1)} %get-tuple-element.24), channel_id=1, source_target_pairs={{0,1},{2,3},{1,0},{3,2},{4,5},{6,7},{5,4},{7,6},{8,9},{10,11},{9,8... | collective-permute-start | bytes 73736 | tf_op jit(solution)/shard_map/ppermute | solution.py:391
  6.0 13.2 %collective-permute-start.6 = (bf16[3,16,256]{2,1,0:T(8,128)(2,1)S(1)}, bf16[3,16,256]{2,1,0:T(8,128)(2,1)S(1)}, u32[]{:S(2)}, u32[]{:S(2)}) collective-permute-start(bf16[3,16,256]{2,1,0:T(8,128)(2,1)S(1)} %get-tuple-element.25), channel_id=1, source_target_pairs={{1,2},{3,0},{2,1},{0,3},{5,6},{7,4},{6,5},{4,7},{9,10},{11,8},{10,... | collective-permute-start | bytes 73736 | tf_op jit(solution)/shard_map/ppermute | solution.py:391
  8.7 8.6 %copy-start.3 = (s32[1024]{0:T(1024)S(1)}, s32[1024]{0:T(1024)}, u32[]{:S(2)}) copy-start(s32[1024]{0:T(1024)} %param.18) | copy-start | bytes 12292
  8.7 5.3 %collective-permute-start.2 = (f32[64,128]{1,0:T(8,128)S(1)}, f32[64,128]{1,0:T(8,128)S(1)}, u32[]{:S(2)}, u32[]{:S(2)}) collective-permute-start(f32[64,128]{1,0:T(8,128)S(1)} %join.1.refs_0_.refs_1_), channel_id=1, source_target_pairs={{0,17},{1,16},{2,19},{3,18},{4,21},{5,20},{6,23},{7,22},{8,25},{9,... | collective-permute-start | bytes 98312 | tf_op jit(solution)/shard_map/ppermute | solution.py:384
  14.0 3.9 %collective-permute-start.3 = (f32[80,128]{1,0:T(8,128)S(1)}, f32[80,128]{1,0:T(8,128)S(1)}, u32[]{:S(2)}, u32[]{:S(2)}) collective-permute-start(f32[80,128]{1,0:T(8,128)S(1)} %merge.4.fence_ref.refs_1_), channel_id=1, source_target_pairs={{0,9},{1,8},{2,11},{3,10},{4,13},{5,12},{6,15},{7,14},{8,1},{9,0},... | collective-permute-start | bytes 122888 | tf_op jit(solution)/shard_map/ppermute | solution.py:384
  15.6 4.9 %collective-permute-start.4 = (bf16[3,64,256]{2,1,0:T(8,128)(2,1)S(1)}, bf16[3,64,256]{2,1,0:T(8,128)(2,1)S(1)}, u32[]{:S(2)}, u32[]{:S(2)}) collective-permute-start(bf16[3,64,256]{2,1,0:T(8,128)(2,1)S(1)} %get-tuple-element.23), channel_id=1, source_target_pairs={{0,4},{1,5},{2,6},{3,7},{4,0},{5,1},{6,2},{7,3},{8,12},{9,13},{10,... | collective-permute-start | bytes 294920 | tf_op jit(solution)/shard_map/ppermute | solution.py:399
  17.9 9.0 %slice-start = ((s8[8388608]{0:T(1024)(128)(4,1)}), s8[4194304]{0:T(1024)(128)(4,1)S(1)}, s32[]{:S(2)}) async-start(s8[8388608]{0:T(1024)(128)(4,1)} %bitcast.4), calls=%async_computation | async-start | bytes 8388608
  18.0 4.3 %collective-permute-start.7 = (f32[112,128]{1,0:T(8,128)S(1)}, f32[112,128]{1,0:T(8,128)S(1)}, u32[]{:S(2)}, u32[]{:S(2)}) collective-permute-start(f32[112,128]{1,0:T(8,128)S(1)} %merge.5.refs_0_.refs_1_), channel_id=1, source_target_pairs={{0,5},{1,4},{2,7},{3,6},{4,1},{5,0},{6,3},{7,2},{8,13},{9,12},{10,... | collective-permute-start | bytes 172040 | tf_op jit(solution)/shard_map/ppermute | solution.py:384
  22.0 4.9 %slice-start.1 = ((s8[8388608]{0:T(1024)(128)(4,1)}), s8[4194304]{0:T(1024)(128)(4,1)S(1)}, s32[]{:S(2)}) async-start(s8[8388608]{0:T(1024)(128)(4,1)} %bitcast.4), calls=%async_computation.1 | async-start | bytes 8388608
  22.3 4.7 %copy-start.5 = (f32[1024]{0:T(1024)S(1)}, f32[1024]{0:T(1024)}, u32[]{:S(2)}) copy-start(f32[1024]{0:T(1024)} %param.14) | copy-start | bytes 12292
  22.3 3.3 %collective-permute-start.8 = (f32[48,128]{1,0:T(8,128)S(1)}, f32[48,128]{1,0:T(8,128)S(1)}, u32[]{:S(2)}, u32[]{:S(2)}) collective-permute-start(f32[48,128]{1,0:T(8,128)S(1)} %slice.4), channel_id=1, source_target_pairs={{0,3},{1,2},{2,1},{3,0},{4,7},{5,6},{6,5},{7,4},{8,11},{9,10},{10,... | collective-permute-start | bytes 73736 | tf_op jit(solution)/shard_map/ppermute | solution.py:384
  24.0 2.9 %copy-start = (bf16[384,1024]{1,0:T(8,128)(2,1)S(1)}, bf16[384,1024]{1,0:T(8,128)(2,1)}, u32[]{:S(2)}) copy-start(bf16[384,1024]{1,0:T(8,128)(2,1)} %w_in_ref.1) | copy-start | bytes 2359300
  25.6 1.4 %collective-permute-start.9 = (f32[176,128]{1,0:T(8,128)S(1)}, f32[176,128]{1,0:T(8,128)S(1)}, u32[]{:S(2)}, u32[]{:S(2)}) collective-permute-start(f32[176,128]{1,0:T(8,128)S(1)} %merge.7.keep_ref), channel_id=1, source_target_pairs={{0,1},{1,0},{2,3},{3,2},{4,5},{5,4},{6,7},{7,6},{8,9},{9,8},{10,11... | collective-permute-start | bytes 270344 | tf_op jit(solution)/shard_map/ppermute | solution.py:384

commit v6 on v5

--- a/solution.py
+++ b/solution.py
@@ -192,9 +192,11 @@
     )
 
 
-def stencil_kernel(begin, depth, fences, slabs, crosses, *refs):
+def stencil_kernel(planes, edges, fences, slabs, crosses, *refs):
     refs, out_ref = refs[fences:-1], refs[-1]
-    velocity_ref, x_even_ref, x_odd_ref, y_even_ref, y_odd_ref = refs
+    velocity_ref, y_even_ref, y_odd_ref = refs[:3]
+    if edges:
+        x_even_ref, x_odd_ref = refs[3:]
     parts, size_x, size_y, size_z = velocity_ref.shape
     row = lax.broadcasted_iota(jnp.int32, (size_y, size_z), 0)
     lane = lax.broadcasted_iota(jnp.int32, (size_y, size_z), 1)
@@ -209,7 +211,7 @@
         souths.append(jnp.where(even_y, far, near))
         norths.append(jnp.where(even_y, near, far))
     spread = time_step * viscosity
-    for x in range(begin, begin + depth):
+    for at, x in enumerate(planes):
         drift = [(0.5 * time_step) * velocity_ref[d, x] for d in range(parts)]
         to_east, to_west = spread - drift[0], spread + drift[0]
         to_north, to_south = spread - drift[1], spread + drift[1]
@@ -231,7 +233,7 @@
             north = jnp.where(
                 row == size_y - 1, norths[c][x : x + 1, :], pltpu.roll(here, size_y - 1, 0)
             )
-            out_ref[c, x - begin] = (
+            out_ref[c, at] = (
                 (1.0 - 6.0 * spread) * here
                 + (to_east * east + to_west * west)
                 + (to_north * north + to_south * south)
@@ -240,11 +242,7 @@
 
 
 def key_kernel(fences, *refs):
-    cells, slot_ref, rotor_ref, sub_ref, key_ref, x_even_ref = refs[fences:]
-    even_x = lax.axis_index("slab") % 2 == 0
-    for c in range(cells.shape[0]):
-        face = jnp.where(even_x, cells[c, cells.shape[1] - 1], cells[c, 0])
-        x_even_ref[c] = face.astype(BF16)
+    slot_ref, rotor_ref, sub_ref, key_ref = refs[fences:]
     rotors = slot_ref.shape[0]
     keys = sub_ref[...] // 2 * rotors + slots_of(rotor_ref[...], slot_ref)
     for group in range(keys.shape[0]):
@@ -266,7 +264,11 @@
 
 
 def join_kernel(bits, fences, *refs):
-    keep_ref, other_ref, states_ref, out_ref = refs[fences:]
+    keep_ref, other_ref, states_ref, cells, out_ref, x_even_ref = refs[fences:]
+    even_x = lax.axis_index("slab") % 2 == 0
+    for c in range(cells.shape[0]):
+        face = jnp.where(even_x, cells[c, cells.shape[1] - 1], cells[c, 0])
+        x_even_ref[c] = face.astype(BF16)
     rows = keep_ref.shape[0]
     out_ref[:rows, :] = keep_ref[...] + other_ref[...]
     half = states_ref.shape[1] // 2
@@ -275,24 +277,29 @@
     )
 
 
-def merge_kernel(fences, shift, rows, width, pooled_rows, *refs):
-    mine_ref, other_ref, out_ref = refs[fences:]
-    out_ref[:pooled_rows, :] = mine_ref[:pooled_rows, :] + other_ref[:pooled_rows, :]
-    if shift is None:
-        out_ref[pooled_rows:, :] = mine_ref[pooled_rows:, :]
-        return
-    first = (lax.axis_index("slab") >> shift) % 2 == 0
-    mine, other = [unpack_rows(ref, pooled_rows, width) for ref in (mine_ref, other_ref)]
-    low, high = jnp.where(first, mine, other), jnp.where(first, other, mine)
+def merge_kernel(fences, packs, shift, rows, width, pooled_rows, *refs):
+    refs, out_ref = refs[fences:-1], refs[-1]
+    total = refs[0][:pooled_rows, :]
+    for other in refs[1:]:
+        total = total + other[:pooled_rows, :]
+    out_ref[:pooled_rows, :] = total
+    mine = (lax.axis_index("slab") >> shift) % packs
+    blocks = [unpack_rows(ref, pooled_rows, width) for ref in refs[:packs]]
+    ordered = []
+    for place in range(packs):
+        block = blocks[0]
+        for k in range(1, packs):
+            block = jnp.where((mine ^ k) == place, blocks[k], block)
+        ordered.append(block)
     pieces = []
-    for at in range(0, low.shape[0], rows):
-        pieces += [low[at : at + rows], high[at : at + rows]]
+    for at in range(0, blocks[0].shape[0], rows):
+        pieces += [block[at : at + rows] for block in ordered]
     pack_rows(out_ref, pooled_rows, pieces)
 
 
 def rotor_kernel(
     bits,
-    planes,
+    runs,
     tile_ref,
     sub_ref,
     w_in_ref,
@@ -304,7 +311,8 @@
     other_ref,
     *rest,
 ):
-    field_refs, rest = rest[:planes], rest[planes:]
+    count = 1 + max(run[2] for run in runs)
+    field_refs, rest = rest[:count], rest[count:]
     out_ref, new_ref, by_slab, source_rows, wind, sems, new_sem = rest
     slabs, rows, width = by_slab.shape
     rotors = slabs * rows
@@ -313,18 +321,16 @@
     halves = size_z // TILE
     groups = tile_ref.shape[0]
     subs = w_out_ref.shape[1] // TILE
-    depth = size_x // planes
     stores = []
-    for k in range(planes):
-        for c in range(1, parts):
-            stores.append(
-                pltpu.make_async_copy(
-                    field_refs[k].at[c],
-                    out_ref.at[c, pl.ds(k * depth, depth)],
-                    sems.at[k * (parts - 1) + c - 1],
-                )
+    for k, (first, number, which, at) in enumerate(runs):
+        stores.append(
+            pltpu.make_async_copy(
+                field_refs[which].at[1:, pl.ds(at, number)],
+                out_ref.at[1:, pl.ds(first, number)],
+                sems.at[k],
             )
-            stores[-1].start()
+        )
+        stores[-1].start()
     split = parts * rotors // 2
     first = first_half(bits)
     keep, other = keep_ref[:split, :], other_ref[:split, :]
@@ -361,19 +367,22 @@
     spread = jnp.concatenate(
         [jnp.where(half == h, taken, 0.0).astype(BF16) for h in range(halves)], axis=1
     )
-    chunks = sems.shape[0] - planes * (parts - 1)
+    chunks = sems.shape[0] - len(runs)
     step = size_x // chunks
     for k in range(chunks):
         forcing = jnp.dot(
             place_hot[pl.ds(k * step * size_y, step * size_y), :],
             spread,
             preferred_element_type=F32,
-        )
+        ).reshape(step, size_y, size_z)
+        for first, number, which, at in runs:
+            begin, end = max(first, k * step), min(first + number, (k + 1) * step)
+            if begin < end:
+                field = field_refs[which][0, at + begin - first : at + end - first]
+                wind[begin:end] = field - force_scale * forcing[begin - k * step : end - k * step]
         at = pl.ds(k * step, step)
-        field = field_refs[k * step // depth][0, pl.ds(k * step % depth, step)]
-        wind[at] = field - force_scale * forcing.reshape(step, size_y, size_z)
         stores.append(
-            pltpu.make_async_copy(wind.at[at], out_ref.at[0, at], sems.at[planes * (parts - 1) + k])
+            pltpu.make_async_copy(wind.at[at], out_ref.at[0, at], sems.at[len(runs) + k])
         )
         stores[-1].start()
     for store in stores:
@@ -472,40 +481,37 @@
     )(cells, place_hot, gains, half_column, slot_hot)
 
 
-def stencil(begin, depth, fences, slabs, crosses, velocity, halos):
+def stencil(planes, fences, slabs, crosses, velocity, halos):
     parts, size_x, size_y, size_z = velocity.shape
+    edges = len(halos) > 2
     return pl.pallas_call(
-        functools.partial(stencil_kernel, begin, depth, len(fences), slabs, crosses),
-        out_shape=jax.ShapeDtypeStruct((parts, depth, size_y, size_z), F32),
-        in_specs=[ANY] * len(fences) + vmem(5),
+        functools.partial(stencil_kernel, planes, edges, len(fences), slabs, crosses),
+        out_shape=jax.ShapeDtypeStruct((parts, len(planes), size_y, size_z), F32),
+        in_specs=[ANY] * len(fences) + vmem(1 + len(halos)),
         out_specs=vmem(1)[0],
         compiler_params=pltpu.CompilerParams(vmem_limit_bytes=4 << 20),
         cost_estimate=pl.CostEstimate(
-            flops=1000 * velocity.size * depth // size_x,
-            bytes_accessed=8 * velocity.size * depth // size_x,
+            flops=1000 * velocity.size * len(planes) // size_x,
+            bytes_accessed=8 * velocity.size * len(planes) // size_x,
             transcendentals=0,
         ),
         name="stencil",
     )(*fences, velocity, *halos)
 
 
-def key_matrix(fences, cells, slot_of_rotor, rotor, sub, keys):
-    parts, _, size_y, size_z = cells.shape
+def key_matrix(fences, slot_of_rotor, rotor, sub, keys):
     entries = rotor.shape[0] * TILE
     return pl.pallas_call(
         functools.partial(key_kernel, len(fences)),
-        out_shape=(
-            jax.ShapeDtypeStruct((entries, keys), BF16),
-            jax.ShapeDtypeStruct((parts, size_y, size_z), BF16),
-        ),
-        in_specs=[ANY] * len(fences) + vmem(1) + [SMEM] + vmem(2),
-        out_specs=tuple(vmem(2)),
+        out_shape=jax.ShapeDtypeStruct((entries, keys), BF16),
+        in_specs=[ANY] * len(fences) + [SMEM] + vmem(2),
+        out_specs=vmem(1)[0],
         compiler_params=pltpu.CompilerParams(vmem_limit_bytes=4 << 20),
         cost_estimate=pl.CostEstimate(
             flops=1000 * entries * keys, bytes_accessed=2 * entries * keys, transcendentals=0
         ),
         name="keys",
-    )(*fences, cells, slot_of_rotor, rotor, sub)
+    )(*fences, slot_of_rotor, rotor, sub)
 
 
 def place_matrix(fence, tile, columns, halves):
@@ -523,53 +529,58 @@
     )(fence, tile)
 
 
-def join(bits, fences, keep, other, states):
+def join(bits, fences, keep, other, states, cells):
+    parts, _, size_y, size_z = cells.shape
     rows = keep.shape[0] + states.size // 2 // TILE
     return pl.pallas_call(
         functools.partial(join_kernel, bits, len(fences)),
-        out_shape=jax.ShapeDtypeStruct((rows, TILE), F32),
-        in_specs=[ANY] * len(fences) + vmem(3),
-        out_specs=vmem(1)[0],
+        out_shape=(
+            jax.ShapeDtypeStruct((rows, TILE), F32),
+            jax.ShapeDtypeStruct((parts, size_y, size_z), BF16),
+        ),
+        in_specs=[ANY] * len(fences) + vmem(4),
+        out_specs=tuple(vmem(2)),
         compiler_params=pltpu.CompilerParams(vmem_limit_bytes=4 << 20),
         name="join",
-    )(*fences, keep, other, states)
-
-
-def merge(fences, shift, rows, width, pooled_rows, mine, other):
-    total = mine.shape[0] + (other.shape[0] - pooled_rows if shift is not None else 0)
+    )(*fences, keep, other, states, cells)
+
+
+def merge(fences, shift, rows, width, pooled_rows, packed, pooled):
+    total = pooled_rows + len(packed) * (packed[0].shape[0] - pooled_rows)
     return pl.pallas_call(
-        functools.partial(merge_kernel, len(fences), shift, rows, width, pooled_rows),
+        functools.partial(
+            merge_kernel, len(fences), len(packed), shift, rows, width, pooled_rows
+        ),
         out_shape=jax.ShapeDtypeStruct((total, TILE), F32),
-        in_specs=[ANY] * len(fences) + vmem(2),
+        in_specs=[ANY] * len(fences) + vmem(len(packed) + len(pooled)),
         out_specs=vmem(1)[0],
         compiler_params=pltpu.CompilerParams(vmem_limit_bytes=4 << 20),
         name="merge",
-    )(*fences, mine, other)
+    )(*fences, *packed, *pooled)
 
 
 def rotors_step(
-    slabs, bits, tile, sub, w_in, w_out, decay, key_hot, place_hot, keep, other, fields
+    slabs, bits, runs, tile, sub, w_in, w_out, decay, key_hot, place_hot, keep, other, fields
 ):
     width = w_in.shape[1]
-    planes = len(fields)
-    parts, depth, size_y, size_z = fields[0].shape
-    size_x = planes * depth
+    parts, _, size_y, size_z = fields[0].shape
+    size_x = sum(field.shape[1] for field in fields)
     keys = key_hot.shape[1]
     rows = keys // (w_out.shape[1] // (2 * TILE)) // slabs
-    chunks = 4
+    chunks = 2
     return pl.pallas_call(
-        functools.partial(rotor_kernel, bits, planes),
+        functools.partial(rotor_kernel, bits, runs),
         out_shape=(
             jax.ShapeDtypeStruct((parts, size_x, size_y, size_z), F32),
             jax.ShapeDtypeStruct((rows, width), F32),
         ),
-        in_specs=vmem(9 + planes),
+        in_specs=vmem(9 + len(fields)),
         out_specs=(HBM, HBM),
         scratch_shapes=[
             pltpu.VMEM((slabs, rows, width), F32),
             pltpu.VMEM((keys, 2 * TILE), BF16),
             pltpu.VMEM((size_x, size_y, size_z), F32),
-            pltpu.SemaphoreType.DMA((planes * (parts - 1) + chunks,)),
+            pltpu.SemaphoreType.DMA((len(runs) + chunks,)),
             pltpu.SemaphoreType.DMA,
         ],
         compiler_params=pltpu.CompilerParams(vmem_limit_bytes=10 << 20),
@@ -610,46 +621,59 @@
     y_odd = swap_pairs(y_odd, "cross", (slabs, crosses), 1)
     pooled_rows = keep.shape[0]
 
-    planes = 2
-    depth = size_x // planes
-    halos = [None, x_odd, y_even, y_odd]
-
-    def make_keys(fence):
-        made, face = key_matrix(
-            (fence, x_odd),
-            cells,
-            slot_of_rotor,
-            rotor,
-            sub,
-            w_out.shape[1] // (2 * TILE) * slot_of_rotor.shape[0],
+    middle = size_x // 2
+    inner, outer = tuple(range(1, middle)), (0,) + tuple(range(middle, size_x))
+    runs = ((1, middle - 1, 0, 0), (0, 1, 1, 0), (middle, size_x - middle, 1, 1))
+    packed, x_even = join(bits, (), keep, swap(send, BOTH, count, 1), rotor_states, cells)
+    x_even = swap_pairs(x_even, "slab", (slabs, crosses), 0)
+    slab_bit = crosses.bit_length() - 1
+    steps = [tuple(range(b, min(b + 2, bits))) for b in range(1, bits, 2)][::-1]
+    fields = []
+    for step in steps:
+        made = []
+        if step == steps[0]:
+            keys = w_out.shape[1] // (2 * TILE) * slot_of_rotor.shape[0]
+            key_hot = key_matrix((packed, x_odd), slot_of_rotor, rotor, sub, keys)
+            fields.append(stencil(inner, (packed,), slabs, crosses, cells, (y_even, y_odd)))
+            made += [key_hot, fields[-1]]
+        if step == steps[-1]:
+            place_hot = place_matrix(packed, tile, size_x * size_y, size_z // TILE)
+            halos = (y_even, y_odd, x_even, x_odd)
+            fields.append(stencil(outer, (packed,), slabs, crosses, cells, halos))
+            made += [place_hot, fields[-1]]
+        slab_bits = [b for b in step if b >= slab_bit]
+        across = [1 << b | 1 for b in slab_bits]
+        if len(slab_bits) == 2:
+            across.append(sum(1 << b for b in step))
+            within = []
+        else:
+            within = [1 << b | 1 for b in step if b < slab_bit]
+            within += [sum(1 << b for b in step)] if len(step) == 2 else []
+        sums = packed[:pooled_rows]
+        packed = merge(
+            made,
+            slab_bits[0] - slab_bit,
+            rotor_states.shape[0],
+            width // 2,
+            pooled_rows,
+            [packed] + [swap(packed, BOTH, count, offset) for offset in across],
+            [swap(sums, BOTH, count, offset) for offset in within],
         )
-        halos[0] = swap_pairs(face, "slab", (slabs, crosses), 0)
-        return made
-
-    def make_places(fence):
-        return place_matrix(fence, tile, size_x * size_y, size_z // TILE)
-
-    def make_field(k, fence):
-        return stencil(k * depth, depth, (fence,), slabs, crosses, cells, halos)
-
-    work = [make_keys, make_places] + [functools.partial(make_field, k) for k in range(planes)]
-    done = []
-    packed = join(bits, (), keep, swap(send, BOTH, count, 1), rotor_states)
-    steps = range(bits - 1, 0, -1)
-    for bit in steps:
-        beside = 1 if bit > steps[-1] else len(work) - len(done)
-        made = [item(packed) for item in work[len(done) : len(done) + beside]]
-        done += made
-        if 1 << bit >= crosses:
-            other, shift = packed, bit - (crosses.bit_length() - 1)
-        else:
-            other, shift = packed[:pooled_rows], None
-        other = swap(other, BOTH, count, 1 << bit | 1)
-        packed = merge(made, shift, rotor_states.shape[0], width // 2, pooled_rows, packed, other)
     other = swap(packed, BOTH, count, 1)
-    key_hot, place_hot, *fields = done
     return rotors_step(
-        slabs, bits, tile, sub, w_in, w_out, decay[None, :], key_hot, place_hot, packed, other, fields
+        slabs,
+        bits,
+        runs,
+        tile,
+        sub,
+        w_in,
+        w_out,
+        decay[None, :],
+        key_hot,
+        place_hot,
+        packed,
+        other,
+        fields,
     )
 
 

time: 31 us -> 29.2 us (0.942)
  waiting for transfers between devices: 5.06 us -> 1.17 us
  starting transfers between devices: 12.3 us -> 14.6 us
    ppermute x6 -> x8, waiting for transfers between devices: 3.7 us -> 1.16 us  [swap(): return lax.ppermute(value, axis, [(i, i ^ offset) for i in range(count)])]
    ppermute x6 -> x8, starting transfers between devices: 7.03 us -> 9.1 us  [swap(): return lax.ppermute(value, axis, [(i, i ^ offset) for i in range(count)])]
    ppermute x2, waiting for transfers between devices: 1.35 us -> 0.01 us  [swap_pairs(): return lax.ppermute(value, BOTH, pairs)]
    pallas_call x8 -> x6, Pallas kernels: 7.72 us -> 7.46 us  [the longest x1 3.61 us: rotors_step(): pl.pallas_call(functools.partial(rotor_kernel, bits, runs), out_shape=(ja...]
  transfers between devices with their start and end apart: 10 -> 12, of which waited for: 5 -> 2; matrix products, arithmetic and copies ran while one was open for 0% -> 0% of each run, Pallas kernels for 22% -> 23%
where the time goes in v6:
time: 29.2 us; the launch traced here: 29 us
  starting transfers between devices  14.6 us (50%)
  Pallas kernels  12.4 us (42%)
  waiting for transfers between devices  1.17 us (4%)
  between operations  0.84 us (3%)
    ppermute x8, starting transfers between devices, swap(): return lax.ppermute(value, axis, [(i, i ^ offset) for i in range(count)])  9.1 us
    pallas_call x1, Pallas kernels, rotors_step(): pl.pallas_call(functools.partial(rotor_kernel, bits, runs), out_shape=(ja...  3.61 us
    ppermute x2, starting transfers between devices, swap_pairs(): return lax.ppermute(value, axis, pairs + [(j, i) for i, j in pairs])  3.1 us
    pallas_call x2, Pallas kernels, stencil(): pl.pallas_call(functools.partial(stencil_kernel, planes, edges, len(fence...  2.96 us
    ppermute x2, starting transfers between devices, swap_pairs(): return lax.ppermute(value, BOTH, pairs)  2.39 us
    pallas_call x1, Pallas kernels, pool(): pl.pallas_call(functools.partial(pool_kernel, bits), out_shape=(part, par...  2.15 us
    pallas_call x1, Pallas kernels, load(): pl.pallas_call(load_kernel, out_shape=(jax.ShapeDtypeStruct((parts, size_...  2.13 us
    ppermute x8, waiting for transfers between devices, swap(): return lax.ppermute(value, axis, [(i, i ^ offset) for i in range(count)])  1.16 us
  transfers between devices with their start and end apart: 12, of which 2 were waited for; matrix products, arithmetic and copies ran while one was open for 0% of the time, Pallas kernels for 23%

profile of v6, /device:TPU:0, one launch (start us, length us, event | category | flops | bytes accessed | tf_op | source)
XLA Modules:
  0.0 29.0 jit_solution(9800858825000284222)
XLA Ops:
  0.6 2.1 %load.1 = (bf16[3,64,256]{2,1,0:T(8,128)(2,1)S(1)}, f32[3,16,64,256]{3,2,1,0:T(8,128)S(1)}, bf16[1024,1024]{1,0:T(8,128)(2,1)S(1)}, f32[1024,384]{1,0:T(8,128)S(...) custom-call(s32[8,128]{1,0:T(8,128)} %bitcast.6, s32[8,128]{1,0:T(8,128)} %bitcast.12, s32[8,128]{1,0:T(8,128)} %bitcast.9, ...), custom_call_target="tpu_custom_call" | custom-call | flops 536870912 | bytes 3145728 | tf_op jit(solution)/shard_map/load/pallas_call | solution.py:430
  2.8 0.5 %collective-permute-start.1 = (bf16[3,64,256]{2,1,0:T(8,128)(2,1)S(1)}, bf16[3,64,256]{2,1,0:T(8,128)(2,1)S(1)}, u32[]{:S(2)}, u32[]{:S(2)}) collective-permute-start(bf16[3,64,256]{2,1,0:T(8,128)(2,1)S(1)} %get-tuple-element.22), channel_id=1, source_target_pairs={{0,1},{1,0},{2,3},{3,2},{4,8},{5,9},{6,10},{7,11},{8,4},{9,5},{10,... | collective-permute-start | bytes 294920 | tf_op jit(solution)/shard_map/ppermute | solution.py:408
  3.3 2.2 %pool.1 = (f32[48,128]{1,0:T(8,128)S(1)}, f32[48,128]{1,0:T(8,128)S(1)}, bf16[3,16,256]{2,1,0:T(8,128)(2,1)S(1)}, bf16[3,16,256]{2,1,0:T(8,128)(2,1)S(1)}) custom-call(f32[3,16,64,256]{3,2,1,0:T(8,128)S(1)} %get-tuple-element.14.cells.refs_3_.refs_1_, bf16[1024,1024]{1,0:T(8,128)(2,1)S(1)} %get-tuple-element.15.place_hot, ...), custom_call_target="tpu_custom_call" | custom-call | flops 1610612736 | bytes 3145728 | tf_op jit(solution)/shard_map/pool/pallas_call | solution.py:465
  5.4 0.1 collective-permute-start
  5.5 0.5 %collective-permute-start.2 = (bf16[3,16,256]{2,1,0:T(8,128)(2,1)S(1)}, bf16[3,16,256]{2,1,0:T(8,128)(2,1)S(1)}, u32[]{:S(2)}, u32[]{:S(2)}) collective-permute-start(bf16[3,16,256]{2,1,0:T(8,128)(2,1)S(1)} %get-tuple-element.23), channel_id=1, source_target_pairs={{0,1},{2,3},{1,0},{3,2},{4,5},{6,7},{5,4},{7,6},{8,9},{10,11},{9,8... | collective-permute-start | bytes 73736 | tf_op jit(solution)/shard_map/ppermute | solution.py:400
  6.0 2.6 %collective-permute-start.3 = (bf16[3,16,256]{2,1,0:T(8,128)(2,1)S(1)}, bf16[3,16,256]{2,1,0:T(8,128)(2,1)S(1)}, u32[]{:S(2)}, u32[]{:S(2)}) collective-permute-start(bf16[3,16,256]{2,1,0:T(8,128)(2,1)S(1)} %get-tuple-element.24), channel_id=1, source_target_pairs={{1,2},{3,0},{2,1},{0,3},{5,6},{7,4},{6,5},{4,7},{9,10},{11,8},{10,... | collective-permute-start | bytes 73736 | tf_op jit(solution)/shard_map/ppermute | solution.py:400
  8.6 0.0 collective-permute-done.refs_1_
  8.7 4.6 %collective-permute-start.6 = (f32[64,128]{1,0:T(8,128)S(1)}, f32[64,128]{1,0:T(8,128)S(1)}, u32[]{:S(2)}, u32[]{:S(2)}) collective-permute-start(f32[64,128]{1,0:T(8,128)S(1)} %get-tuple-element.21.refs_0_.refs_2_), channel_id=1, source_target_pairs={{0,24},{1,25},{2,26},{3,27},{4,28},{5,29},{6,30},{7,31},{8,16},{9,... | collective-permute-start | bytes 98312 | tf_op jit(solution)/shard_map/ppermute | solution.py:393
  13.3 0.0 collective-permute-start.5
  13.3 0.4 %collective-permute-start.4 = (f32[64,128]{1,0:T(8,128)S(1)}, f32[64,128]{1,0:T(8,128)S(1)}, u32[]{:S(2)}, u32[]{:S(2)}) collective-permute-start(f32[64,128]{1,0:T(8,128)S(1)} %get-tuple-element.21.refs_0_.refs_2_), channel_id=1, source_target_pairs={{0,9},{1,8},{2,11},{3,10},{4,13},{5,12},{6,15},{7,14},{8,1},{9,0},... | collective-permute-start | bytes 98312 | tf_op jit(solution)/shard_map/ppermute | solution.py:393
  13.6 1.9 %collective-permute-start.7 = (bf16[3,64,256]{2,1,0:T(8,128)(2,1)S(1)}, bf16[3,64,256]{2,1,0:T(8,128)(2,1)S(1)}, u32[]{:S(2)}, u32[]{:S(2)}) collective-permute-start(bf16[3,64,256]{2,1,0:T(8,128)(2,1)S(1)} %get-tuple-element.25), channel_id=1, source_target_pairs={{0,4},{1,5},{2,6},{3,7},{4,0},{5,1},{6,2},{7,3},{8,12},{9,13},{10,... | collective-permute-start | bytes 294920 | tf_op jit(solution)/shard_map/ppermute | solution.py:408
  15.5 1.3 %stencil.2.refs_1_.rest_0_ = f32[3,7,64,256]{3,2,1,0:T(8,128)S(1)} custom-call(f32[64,128]{1,0:T(8,128)S(1)} %get-tuple-element.21.refs_0_.refs_2_, f32[3,16,64,256]{3,2,1,0:T(8,128)S(1)} %get-tuple-element.14.cells.refs_3_.refs_1_, bf16[3,16,256]{2,1,0:T(8,128)(2,1)S(1)} %collective-permute-done.2.refs_2_, ...), custom_call_target="tpu_custom_call" | custom-call | flops 344064000 | bytes 2752512 | tf_op jit(solution)/shard_map/stencil/pallas_call | solution.py:487
  16.8 0.0 copy-start.2
  16.8 0.8 %keys.1.refs_0_.key_hot = bf16[1024,512]{1,0:T(8,128)(2,1)S(1)} custom-call(f32[64,128]{1,0:T(8,128)S(1)} %get-tuple-element.21.refs_0_.refs_2_, bf16[3,64,256]{2,1,0:T(8,128)(2,1)S(1)} %collective-permute-done.1.refs_1_.refs_5_, s32[32]{0:T(128)S(1)} %copy-done.6, s32[8,128]{1,0:T(8,128)S(1)} %bitcast.13, s32[8,128]{1,0:T(8,128)S(1)} %bitcast.10), custom_call_target="tpu_custom_call" | custom-call | flops 524288000 | bytes 1048576 | tf_op jit(solution)/shard_map/keys/pallas_call | solution.py:504
  17.7 0.0 collective-permute-done.6.refs_5_
  17.7 0.0 collective-permute-done.5.refs_4_
  17.7 0.0 slice-start
  17.8 0.7 %collective-permute-start.10 = (f32[48,128]{1,0:T(8,128)S(1)}, f32[48,128]{1,0:T(8,128)S(1)}, u32[]{:S(2)}, u32[]{:S(2)}) collective-permute-start(f32[48,128]{1,0:T(8,128)S(1)} %slice.4), channel_id=1, source_target_pairs={{0,6},{1,7},{2,4},{3,5},{4,2},{5,3},{6,0},{7,1},{8,14},{9,15},{10,... | collective-permute-start | bytes 73736 | tf_op jit(solution)/shard_map/ppermute | solution.py:393
  18.5 1.6 %collective-permute-start.9 = (f32[48,128]{1,0:T(8,128)S(1)}, f32[48,128]{1,0:T(8,128)S(1)}, u32[]{:S(2)}, u32[]{:S(2)}) collective-permute-start(f32[48,128]{1,0:T(8,128)S(1)} %slice.4), channel_id=1, source_target_pairs={{0,3},{1,2},{2,1},{3,0},{4,7},{5,6},{6,5},{7,4},{8,11},{9,10},{10,... | collective-permute-start | bytes 73736 | tf_op jit(solution)/shard_map/ppermute | solution.py:393
  20.1 1.0 %collective-permute-start.8 = (f32[112,128]{1,0:T(8,128)S(1)}, f32[112,128]{1,0:T(8,128)S(1)}, u32[]{:S(2)}, u32[]{:S(2)}) collective-permute-start(f32[112,128]{1,0:T(8,128)S(1)} %merge.2.fence_ref.refs_0_.refs_2_), channel_id=1, source_target_pairs={{0,5},{1,4},{2,7},{3,6},{4,1},{5,0},{6,3},{7,2},{8,13},{9,12},{10,... | collective-permute-start | bytes 172040 | tf_op jit(solution)/shard_map/ppermute | solution.py:393
  21.1 0.6 %places.1.refs_0_.place_hot = bf16[1024,1024]{1,0:T(8,128)(2,1)S(1)} custom-call(f32[112,128]{1,0:T(8,128)S(1)} %merge.2.fence_ref.refs_0_.refs_2_, s32[8,128]{1,0:T(8,128)S(1)} %bitcast.7), custom_call_target="tpu_custom_call" | custom-call | flops 1048576000 | bytes 2097152 | tf_op jit(solution)/shard_map/places/pallas_call | solution.py:519
  21.7 0.0 slice-start.1
  21.7 0.0 collective-permute-done.7.refs_4_
  21.7 1.7 %stencil.3.refs_1_.rest_1_ = f32[3,9,64,256]{3,2,1,0:T(8,128)S(1)} custom-call(f32[112,128]{1,0:T(8,128)S(1)} %merge.2.fence_ref.refs_0_.refs_2_, f32[3,16,64,256]{3,2,1,0:T(8,128)S(1)} %get-tuple-element.14.cells.refs_3_.refs_1_, bf16[3,16,256]{2,1,0:T(8,128)(2,1)S(1)} %collective-permute-done.2.refs_2_, ...), custom_call_target="tpu_custom_call" | custom-call | flops 442368000 | bytes 3538944 | tf_op jit(solution)/shard_map/stencil/pallas_call | solution.py:487
  23.4 0.0 copy-start
  23.4 0.0 copy-start.5
  23.4 0.0 collective-permute-done.10.refs_5_
  23.4 0.0 collective-permute-done.9.refs_4_
  23.4 0.2 collective-permute-done.8.refs_3_
  23.7 0.8 %collective-permute-start.11 = (f32[176,128]{1,0:T(8,128)S(1)}, f32[176,128]{1,0:T(8,128)S(1)}, u32[]{:S(2)}, u32[]{:S(2)}) collective-permute-start(f32[176,128]{1,0:T(8,128)S(1)} %merge.3.keep_ref), channel_id=1, source_target_pairs={{0,1},{1,0},{2,3},{3,2},{4,5},{5,4},{6,7},{7,6},{8,9},{9,8},{10,11... | collective-permute-start | bytes 270344 | tf_op jit(solution)/shard_map/ppermute | solution.py:393
  24.5 0.9 %collective-permute-done.11.other_ref = f32[176,128]{1,0:T(8,128)S(1)} collective-permute-done((f32[176,128]{1,0:T(8,128)S(1)}, f32[176,128]{1,0:T(8,128)S(1)}, u32[]{:S(2)}, u32[]{:S(2)}) %collective-permute-start.11) | collective-permute-done | bytes 90144 | tf_op jit(solution)/shard_map/ppermute | solution.py:393
  25.4 3.6 %rotors.1 = (f32[3,16,64,256]{3,2,1,0:T(8,128)}, f32[4,1024]{1,0:T(4,128)}) custom-call(s32[8,128]{1,0:T(8,128)S(1)} %bitcast.8, s32[8,128]{1,0:T(8,128)S(1)} %bitcast.11, bf16[384,1024]{1,0:T(8,128)(2,1)S(1)} %copy-done, bf16[1024,4096]{1,0:T(8,128)(2,1)S(1)} %bitcast.5, f32[1,1024]{1,0:T(1,128)S(1)} %bitcast.14, ...), custom_call_target="tpu_custom_call" | custom-call | flops 1073741824 | bytes 8388608 | tf_op jit(solution)/shard_map/rotors/pallas_call | solution.py:571
  (22 shorter events, 0.1 us)
Async XLA Ops:
  2.8 14.0 %collective-permute-start.1 = (bf16[3,64,256]{2,1,0:T(8,128)(2,1)S(1)}, bf16[3,64,256]{2,1,0:T(8,128)(2,1)S(1)}, u32[]{:S(2)}, u32[]{:S(2)}) collective-permute-start(bf16[3,64,256]{2,1,0:T(8,128)(2,1)S(1)} %get-tuple-element.22), channel_id=1, source_target_pairs={{0,1},{1,0},{2,3},{3,2},{4,8},{5,9},{6,10},{7,11},{8,4},{9,5},{10,... | collective-permute-start | bytes 294920 | tf_op jit(solution)/shard_map/ppermute | solution.py:408
  3.3 5.3 %copy-start.1 = (f32[4,1024]{1,0:T(4,128)S(1)}, f32[4,1024]{1,0:T(4,128)}, u32[]{:S(2)}) copy-start(f32[4,1024]{1,0:T(4,128)} %refs_2_.2) | copy-start | bytes 49156
  5.4 3.2 %collective-permute-start = (f32[48,128]{1,0:T(8,128)S(1)}, f32[48,128]{1,0:T(8,128)S(1)}, u32[]{:S(2)}, u32[]{:S(2)}) collective-permute-start(f32[48,128]{1,0:T(8,128)S(1)} %get-tuple-element.20), channel_id=1, source_target_pairs={{0,1},{1,0},{2,3},{3,2},{4,5},{5,4},{6,7},{7,6},{8,9},{9,8},{10,11... | collective-permute-start | bytes 73736 | tf_op jit(solution)/shard_map/ppermute | solution.py:393
  5.5 7.7 %collective-permute-start.2 = (bf16[3,16,256]{2,1,0:T(8,128)(2,1)S(1)}, bf16[3,16,256]{2,1,0:T(8,128)(2,1)S(1)}, u32[]{:S(2)}, u32[]{:S(2)}) collective-permute-start(bf16[3,16,256]{2,1,0:T(8,128)(2,1)S(1)} %get-tuple-element.23), channel_id=1, source_target_pairs={{0,1},{2,3},{1,0},{3,2},{4,5},{6,7},{5,4},{7,6},{8,9},{10,11},{9,8... | collective-permute-start | bytes 73736 | tf_op jit(solution)/shard_map/ppermute | solution.py:400
  6.0 7.7 %collective-permute-start.3 = (bf16[3,16,256]{2,1,0:T(8,128)(2,1)S(1)}, bf16[3,16,256]{2,1,0:T(8,128)(2,1)S(1)}, u32[]{:S(2)}, u32[]{:S(2)}) collective-permute-start(bf16[3,16,256]{2,1,0:T(8,128)(2,1)S(1)} %get-tuple-element.24), channel_id=1, source_target_pairs={{1,2},{3,0},{2,1},{0,3},{5,6},{7,4},{6,5},{4,7},{9,10},{11,8},{10,... | collective-permute-start | bytes 73736 | tf_op jit(solution)/shard_map/ppermute | solution.py:400
  8.7 9.0 %collective-permute-start.6 = (f32[64,128]{1,0:T(8,128)S(1)}, f32[64,128]{1,0:T(8,128)S(1)}, u32[]{:S(2)}, u32[]{:S(2)}) collective-permute-start(f32[64,128]{1,0:T(8,128)S(1)} %get-tuple-element.21.refs_0_.refs_2_), channel_id=1, source_target_pairs={{0,24},{1,25},{2,26},{3,27},{4,28},{5,29},{6,30},{7,31},{8,16},{9,... | collective-permute-start | bytes 98312 | tf_op jit(solution)/shard_map/ppermute | solution.py:393
  13.3 4.4 %collective-permute-start.5 = (f32[64,128]{1,0:T(8,128)S(1)}, f32[64,128]{1,0:T(8,128)S(1)}, u32[]{:S(2)}, u32[]{:S(2)}) collective-permute-start(f32[64,128]{1,0:T(8,128)S(1)} %get-tuple-element.21.refs_0_.refs_2_), channel_id=1, source_target_pairs={{0,17},{1,16},{2,19},{3,18},{4,21},{5,20},{6,23},{7,22},{8,25},{9,... | collective-permute-start | bytes 98312 | tf_op jit(solution)/shard_map/ppermute | solution.py:393
  13.3 4.4 %collective-permute-start.4 = (f32[64,128]{1,0:T(8,128)S(1)}, f32[64,128]{1,0:T(8,128)S(1)}, u32[]{:S(2)}, u32[]{:S(2)}) collective-permute-start(f32[64,128]{1,0:T(8,128)S(1)} %get-tuple-element.21.refs_0_.refs_2_), channel_id=1, source_target_pairs={{0,9},{1,8},{2,11},{3,10},{4,13},{5,12},{6,15},{7,14},{8,1},{9,0},... | collective-permute-start | bytes 98312 | tf_op jit(solution)/shard_map/ppermute | solution.py:393
  13.6 3.2 %copy-start.3 = (s32[1024]{0:T(1024)S(1)}, s32[1024]{0:T(1024)}, u32[]{:S(2)}) copy-start(s32[1024]{0:T(1024)} %param.19) | copy-start | bytes 12292
  13.6 3.2 %copy-start.4 = (s32[1024,1]{0,1:T(1,128)S(1)}, s32[1024,1]{0,1:T(1,128)}, u32[]{:S(2)}) copy-start(s32[1024,1]{0,1:T(1,128)} %param.17) | copy-start | bytes 12292
  13.6 3.2 %copy-start.6 = (s32[32]{0:T(128)S(1)}, s32[32]{0:T(128)}, u32[]{:S(2)}) copy-start(s32[32]{0:T(128)} %refs_2_.3) | copy-start | bytes 388
  13.6 8.1 %collective-permute-start.7 = (bf16[3,64,256]{2,1,0:T(8,128)(2,1)S(1)}, bf16[3,64,256]{2,1,0:T(8,128)(2,1)S(1)}, u32[]{:S(2)}, u32[]{:S(2)}) collective-permute-start(bf16[3,64,256]{2,1,0:T(8,128)(2,1)S(1)} %get-tuple-element.25), channel_id=1, source_target_pairs={{0,4},{1,5},{2,6},{3,7},{4,0},{5,1},{6,2},{7,3},{8,12},{9,13},{10,... | collective-permute-start | bytes 294920 | tf_op jit(solution)/shard_map/ppermute | solution.py:408
  16.8 4.3 %copy-start.2 = (s32[1024]{0:T(1024)S(1)}, s32[1024]{0:T(1024)}, u32[]{:S(2)}) copy-start(s32[1024]{0:T(1024)} %param.18) | copy-start | bytes 12292
  17.7 7.7 %slice-start = ((s8[8388608]{0:T(1024)(128)(4,1)}), s8[4194304]{0:T(1024)(128)(4,1)S(1)}, s32[]{:S(2)}) async-start(s8[8388608]{0:T(1024)(128)(4,1)} %bitcast.4), calls=%async_computation | async-start | bytes 8388608
  17.8 5.6 %collective-permute-start.10 = (f32[48,128]{1,0:T(8,128)S(1)}, f32[48,128]{1,0:T(8,128)S(1)}, u32[]{:S(2)}, u32[]{:S(2)}) collective-permute-start(f32[48,128]{1,0:T(8,128)S(1)} %slice.4), channel_id=1, source_target_pairs={{0,6},{1,7},{2,4},{3,5},{4,2},{5,3},{6,0},{7,1},{8,14},{9,15},{10,... | collective-permute-start | bytes 73736 | tf_op jit(solution)/shard_map/ppermute | solution.py:393
  18.5 4.9 %collective-permute-start.9 = (f32[48,128]{1,0:T(8,128)S(1)}, f32[48,128]{1,0:T(8,128)S(1)}, u32[]{:S(2)}, u32[]{:S(2)}) collective-permute-start(f32[48,128]{1,0:T(8,128)S(1)} %slice.4), channel_id=1, source_target_pairs={{0,3},{1,2},{2,1},{3,0},{4,7},{5,6},{6,5},{7,4},{8,11},{9,10},{10,... | collective-permute-start | bytes 73736 | tf_op jit(solution)/shard_map/ppermute | solution.py:393
  20.1 3.6 %collective-permute-start.8 = (f32[112,128]{1,0:T(8,128)S(1)}, f32[112,128]{1,0:T(8,128)S(1)}, u32[]{:S(2)}, u32[]{:S(2)}) collective-permute-start(f32[112,128]{1,0:T(8,128)S(1)} %merge.2.fence_ref.refs_0_.refs_2_), channel_id=1, source_target_pairs={{0,5},{1,4},{2,7},{3,6},{4,1},{5,0},{6,3},{7,2},{8,13},{9,12},{10,... | collective-permute-start | bytes 172040 | tf_op jit(solution)/shard_map/ppermute | solution.py:393
  21.7 3.7 %slice-start.1 = ((s8[8388608]{0:T(1024)(128)(4,1)}), s8[4194304]{0:T(1024)(128)(4,1)S(1)}, s32[]{:S(2)}) async-start(s8[8388608]{0:T(1024)(128)(4,1)} %bitcast.4), calls=%async_computation.1 | async-start | bytes 8388608
  23.4 2.0 %copy-start = (bf16[384,1024]{1,0:T(8,128)(2,1)S(1)}, bf16[384,1024]{1,0:T(8,128)(2,1)}, u32[]{:S(2)}) copy-start(bf16[384,1024]{1,0:T(8,128)(2,1)} %w_in_ref.1) | copy-start | bytes 2359300
  23.4 2.0 %copy-start.5 = (f32[1024]{0:T(1024)S(1)}, f32[1024]{0:T(1024)}, u32[]{:S(2)}) copy-start(f32[1024]{0:T(1024)} %param.14) | copy-start | bytes 12292
  23.7 1.7 %collective-permute-start.11 = (f32[176,128]{1,0:T(8,128)S(1)}, f32[176,128]{1,0:T(8,128)S(1)}, u32[]{:S(2)}, u32[]{:S(2)}) collective-permute-start(f32[176,128]{1,0:T(8,128)S(1)} %merge.3.keep_ref), channel_id=1, source_target_pairs={{0,1},{1,0},{2,3},{3,2},{4,5},{5,4},{6,7},{7,6},{8,9},{9,8},{10,11... | collective-permute-start | bytes 270344 | tf_op jit(solution)/shard_map/ppermute | solution.py:393

commit v7 on v6

--- a/solution.py
+++ b/solution.py
@@ -353,7 +353,8 @@
     new_b = new.astype(BF16)
 
     half_rows = tile_ref[...] % halves
-    sources = jnp.dot(new_b, w_out_ref[...], preferred_element_type=F32).astype(BF16)
+    new_b = jnp.concatenate([new_b, jnp.zeros((max(TILE - rotors, 0), width), BF16)], axis=0)
+    sources = jnp.dot(new_b, w_out_ref[...], preferred_element_type=F32)[:rotors].astype(BF16)
     for pair in range(subs // 2):
         source_rows[pair * rotors : (pair + 1) * rotors, :] = sources[
             :, pair * 2 * TILE : (pair + 1) * 2 * TILE

time: 29.2 us -> 28.9 us (0.990)
  Pallas kernels: 12.4 us -> 12 us
    pallas_call x1, Pallas kernels: 3.61 us -> 3.27 us  [rotors_step(): pl.pallas_call(functools.partial(rotor_kernel, bits, runs), out_shape=(ja...]
where the time goes in v7:
time: 28.9 us; the launch traced here: 28.7 us
  starting transfers between devices  14.6 us (51%)
  Pallas kernels  12 us (42%)
  waiting for transfers between devices  1.17 us (4%)
  between operations  0.84 us (3%)
    ppermute x8, starting transfers between devices, swap(): return lax.ppermute(value, axis, [(i, i ^ offset) for i in range(count)])  9.1 us
    pallas_call x1, Pallas kernels, rotors_step(): pl.pallas_call(functools.partial(rotor_kernel, bits, runs), out_shape=(ja...  3.27 us
    ppermute x2, starting transfers between devices, swap_pairs(): return lax.ppermute(value, axis, pairs + [(j, i) for i, j in pairs])  3.1 us
    pallas_call x2, Pallas kernels, stencil(): pl.pallas_call(functools.partial(stencil_kernel, planes, edges, len(fence...  2.96 us
    ppermute x2, starting transfers between devices, swap_pairs(): return lax.ppermute(value, BOTH, pairs)  2.39 us
    pallas_call x1, Pallas kernels, pool(): pl.pallas_call(functools.partial(pool_kernel, bits), out_shape=(part, par...  2.15 us
    pallas_call x1, Pallas kernels, load(): pl.pallas_call(load_kernel, out_shape=(jax.ShapeDtypeStruct((parts, size_...  2.13 us
    ppermute x8, waiting for transfers between devices, swap(): return lax.ppermute(value, axis, [(i, i ^ offset) for i in range(count)])  1.16 us
  transfers between devices with their start and end apart: 12, of which 2 were waited for; matrix products, arithmetic and copies ran while one was open for 0% of the time, Pallas kernels for 23%

profile of v7, /device:TPU:0, one launch (start us, length us, event | category | flops | bytes accessed | tf_op | source)
XLA Modules:
  0.0 28.7 jit_solution(4780079896164809927)
XLA Ops:
  0.6 2.1 %load.1 = (bf16[3,64,256]{2,1,0:T(8,128)(2,1)S(1)}, f32[3,16,64,256]{3,2,1,0:T(8,128)S(1)}, bf16[1024,1024]{1,0:T(8,128)(2,1)S(1)}, f32[1024,384]{1,0:T(8,128)S(...) custom-call(s32[8,128]{1,0:T(8,128)} %bitcast.6, s32[8,128]{1,0:T(8,128)} %bitcast.12, s32[8,128]{1,0:T(8,128)} %bitcast.9, ...), custom_call_target="tpu_custom_call" | custom-call | flops 536870912 | bytes 3145728 | tf_op jit(solution)/shard_map/load/pallas_call | solution.py:431
  2.8 0.5 %collective-permute-start.1 = (bf16[3,64,256]{2,1,0:T(8,128)(2,1)S(1)}, bf16[3,64,256]{2,1,0:T(8,128)(2,1)S(1)}, u32[]{:S(2)}, u32[]{:S(2)}) collective-permute-start(bf16[3,64,256]{2,1,0:T(8,128)(2,1)S(1)} %get-tuple-element.22), channel_id=1, source_target_pairs={{0,1},{1,0},{2,3},{3,2},{4,8},{5,9},{6,10},{7,11},{8,4},{9,5},{10,... | collective-permute-start | bytes 294920 | tf_op jit(solution)/shard_map/ppermute | solution.py:409
  3.3 2.2 %pool.1 = (f32[48,128]{1,0:T(8,128)S(1)}, f32[48,128]{1,0:T(8,128)S(1)}, bf16[3,16,256]{2,1,0:T(8,128)(2,1)S(1)}, bf16[3,16,256]{2,1,0:T(8,128)(2,1)S(1)}) custom-call(f32[3,16,64,256]{3,2,1,0:T(8,128)S(1)} %get-tuple-element.14.cells.refs_3_.refs_1_, bf16[1024,1024]{1,0:T(8,128)(2,1)S(1)} %get-tuple-element.15.place_hot, ...), custom_call_target="tpu_custom_call" | custom-call | flops 1610612736 | bytes 3145728 | tf_op jit(solution)/shard_map/pool/pallas_call | solution.py:466
  5.4 0.1 collective-permute-start
  5.5 0.5 %collective-permute-start.2 = (bf16[3,16,256]{2,1,0:T(8,128)(2,1)S(1)}, bf16[3,16,256]{2,1,0:T(8,128)(2,1)S(1)}, u32[]{:S(2)}, u32[]{:S(2)}) collective-permute-start(bf16[3,16,256]{2,1,0:T(8,128)(2,1)S(1)} %get-tuple-element.23), channel_id=1, source_target_pairs={{0,1},{2,3},{1,0},{3,2},{4,5},{6,7},{5,4},{7,6},{8,9},{10,11},{9,8... | collective-permute-start | bytes 73736 | tf_op jit(solution)/shard_map/ppermute | solution.py:401
  6.0 2.6 %collective-permute-start.3 = (bf16[3,16,256]{2,1,0:T(8,128)(2,1)S(1)}, bf16[3,16,256]{2,1,0:T(8,128)(2,1)S(1)}, u32[]{:S(2)}, u32[]{:S(2)}) collective-permute-start(bf16[3,16,256]{2,1,0:T(8,128)(2,1)S(1)} %get-tuple-element.24), channel_id=1, source_target_pairs={{1,2},{3,0},{2,1},{0,3},{5,6},{7,4},{6,5},{4,7},{9,10},{11,8},{10,... | collective-permute-start | bytes 73736 | tf_op jit(solution)/shard_map/ppermute | solution.py:401
  8.6 0.0 collective-permute-done.refs_1_
  8.7 4.6 %collective-permute-start.6 = (f32[64,128]{1,0:T(8,128)S(1)}, f32[64,128]{1,0:T(8,128)S(1)}, u32[]{:S(2)}, u32[]{:S(2)}) collective-permute-start(f32[64,128]{1,0:T(8,128)S(1)} %get-tuple-element.21.refs_0_.refs_2_), channel_id=1, source_target_pairs={{0,24},{1,25},{2,26},{3,27},{4,28},{5,29},{6,30},{7,31},{8,16},{9,... | collective-permute-start | bytes 98312 | tf_op jit(solution)/shard_map/ppermute | solution.py:394
  13.3 0.4 %collective-permute-start.4 = (f32[64,128]{1,0:T(8,128)S(1)}, f32[64,128]{1,0:T(8,128)S(1)}, u32[]{:S(2)}, u32[]{:S(2)}) collective-permute-start(f32[64,128]{1,0:T(8,128)S(1)} %get-tuple-element.21.refs_0_.refs_2_), channel_id=1, source_target_pairs={{0,9},{1,8},{2,11},{3,10},{4,13},{5,12},{6,15},{7,14},{8,1},{9,0},... | collective-permute-start | bytes 98312 | tf_op jit(solution)/shard_map/ppermute | solution.py:394
  13.6 0.0 collective-permute-done.3.refs_3_
  13.6 1.9 %collective-permute-start.7 = (bf16[3,64,256]{2,1,0:T(8,128)(2,1)S(1)}, bf16[3,64,256]{2,1,0:T(8,128)(2,1)S(1)}, u32[]{:S(2)}, u32[]{:S(2)}) collective-permute-start(bf16[3,64,256]{2,1,0:T(8,128)(2,1)S(1)} %get-tuple-element.25), channel_id=1, source_target_pairs={{0,4},{1,5},{2,6},{3,7},{4,0},{5,1},{6,2},{7,3},{8,12},{9,13},{10,... | collective-permute-start | bytes 294920 | tf_op jit(solution)/shard_map/ppermute | solution.py:409
  15.5 1.3 %stencil.2.refs_1_.rest_0_ = f32[3,7,64,256]{3,2,1,0:T(8,128)S(1)} custom-call(f32[64,128]{1,0:T(8,128)S(1)} %get-tuple-element.21.refs_0_.refs_2_, f32[3,16,64,256]{3,2,1,0:T(8,128)S(1)} %get-tuple-element.14.cells.refs_3_.refs_1_, bf16[3,16,256]{2,1,0:T(8,128)(2,1)S(1)} %collective-permute-done.2.refs_2_, ...), custom_call_target="tpu_custom_call" | custom-call | flops 344064000 | bytes 2752512 | tf_op jit(solution)/shard_map/stencil/pallas_call | solution.py:488
  16.8 0.0 copy-start.2
  16.8 0.8 %keys.1.refs_0_.key_hot = bf16[1024,512]{1,0:T(8,128)(2,1)S(1)} custom-call(f32[64,128]{1,0:T(8,128)S(1)} %get-tuple-element.21.refs_0_.refs_2_, bf16[3,64,256]{2,1,0:T(8,128)(2,1)S(1)} %collective-permute-done.1.refs_1_.refs_5_, s32[32]{0:T(128)S(1)} %copy-done.6, s32[8,128]{1,0:T(8,128)S(1)} %bitcast.13, s32[8,128]{1,0:T(8,128)S(1)} %bitcast.10), custom_call_target="tpu_custom_call" | custom-call | flops 524288000 | bytes 1048576 | tf_op jit(solution)/shard_map/keys/pallas_call | solution.py:505
  17.7 0.0 collective-permute-done.6.refs_5_
  17.7 0.0 collective-permute-done.5.refs_4_
  17.7 0.0 slice-start
  17.8 0.7 %collective-permute-start.10 = (f32[48,128]{1,0:T(8,128)S(1)}, f32[48,128]{1,0:T(8,128)S(1)}, u32[]{:S(2)}, u32[]{:S(2)}) collective-permute-start(f32[48,128]{1,0:T(8,128)S(1)} %slice.4), channel_id=1, source_target_pairs={{0,6},{1,7},{2,4},{3,5},{4,2},{5,3},{6,0},{7,1},{8,14},{9,15},{10,... | collective-permute-start | bytes 73736 | tf_op jit(solution)/shard_map/ppermute | solution.py:394
  18.5 1.6 %collective-permute-start.9 = (f32[48,128]{1,0:T(8,128)S(1)}, f32[48,128]{1,0:T(8,128)S(1)}, u32[]{:S(2)}, u32[]{:S(2)}) collective-permute-start(f32[48,128]{1,0:T(8,128)S(1)} %slice.4), channel_id=1, source_target_pairs={{0,3},{1,2},{2,1},{3,0},{4,7},{5,6},{6,5},{7,4},{8,11},{9,10},{10,... | collective-permute-start | bytes 73736 | tf_op jit(solution)/shard_map/ppermute | solution.py:394
  20.1 1.0 %collective-permute-start.8 = (f32[112,128]{1,0:T(8,128)S(1)}, f32[112,128]{1,0:T(8,128)S(1)}, u32[]{:S(2)}, u32[]{:S(2)}) collective-permute-start(f32[112,128]{1,0:T(8,128)S(1)} %merge.2.fence_ref.refs_0_.refs_2_), channel_id=1, source_target_pairs={{0,5},{1,4},{2,7},{3,6},{4,1},{5,0},{6,3},{7,2},{8,13},{9,12},{10,... | collective-permute-start | bytes 172040 | tf_op jit(solution)/shard_map/ppermute | solution.py:394
  21.1 0.6 %places.1.refs_0_.place_hot = bf16[1024,1024]{1,0:T(8,128)(2,1)S(1)} custom-call(f32[112,128]{1,0:T(8,128)S(1)} %merge.2.fence_ref.refs_0_.refs_2_, s32[8,128]{1,0:T(8,128)S(1)} %bitcast.7), custom_call_target="tpu_custom_call" | custom-call | flops 1048576000 | bytes 2097152 | tf_op jit(solution)/shard_map/places/pallas_call | solution.py:520
  21.7 0.0 slice-start.1
  21.7 0.0 collective-permute-done.7.refs_4_
  21.7 1.7 %stencil.3.refs_1_.rest_1_ = f32[3,9,64,256]{3,2,1,0:T(8,128)S(1)} custom-call(f32[112,128]{1,0:T(8,128)S(1)} %merge.2.fence_ref.refs_0_.refs_2_, f32[3,16,64,256]{3,2,1,0:T(8,128)S(1)} %get-tuple-element.14.cells.refs_3_.refs_1_, bf16[3,16,256]{2,1,0:T(8,128)(2,1)S(1)} %collective-permute-done.2.refs_2_, ...), custom_call_target="tpu_custom_call" | custom-call | flops 442368000 | bytes 3538944 | tf_op jit(solution)/shard_map/stencil/pallas_call | solution.py:488
  23.4 0.0 copy-start
  23.4 0.0 copy-start.5
  23.4 0.0 collective-permute-done.10.refs_5_
  23.4 0.0 collective-permute-done.9.refs_4_
  23.4 0.2 collective-permute-done.8.refs_3_
  23.7 0.8 %collective-permute-start.11 = (f32[176,128]{1,0:T(8,128)S(1)}, f32[176,128]{1,0:T(8,128)S(1)}, u32[]{:S(2)}, u32[]{:S(2)}) collective-permute-start(f32[176,128]{1,0:T(8,128)S(1)} %merge.3.keep_ref), channel_id=1, source_target_pairs={{0,1},{1,0},{2,3},{3,2},{4,5},{5,4},{6,7},{7,6},{8,9},{9,8},{10,11... | collective-permute-start | bytes 270344 | tf_op jit(solution)/shard_map/ppermute | solution.py:394
  24.5 0.9 %collective-permute-done.11.other_ref = f32[176,128]{1,0:T(8,128)S(1)} collective-permute-done((f32[176,128]{1,0:T(8,128)S(1)}, f32[176,128]{1,0:T(8,128)S(1)}, u32[]{:S(2)}, u32[]{:S(2)}) %collective-permute-start.11) | collective-permute-done | bytes 90144 | tf_op jit(solution)/shard_map/ppermute | solution.py:394
  25.4 3.3 %rotors.1 = (f32[3,16,64,256]{3,2,1,0:T(8,128)}, f32[4,1024]{1,0:T(4,128)}) custom-call(s32[8,128]{1,0:T(8,128)S(1)} %bitcast.8, s32[8,128]{1,0:T(8,128)S(1)} %bitcast.11, bf16[384,1024]{1,0:T(8,128)(2,1)S(1)} %copy-done, bf16[1024,4096]{1,0:T(8,128)(2,1)S(1)} %bitcast.5, f32[1,1024]{1,0:T(1,128)S(1)} %bitcast.14, ...), custom_call_target="tpu_custom_call" | custom-call | flops 1073741824 | bytes 8388608 | tf_op jit(solution)/shard_map/rotors/pallas_call | solution.py:572
  (22 shorter events, 0.1 us)
Async XLA Ops:
  2.8 14.0 %collective-permute-start.1 = (bf16[3,64,256]{2,1,0:T(8,128)(2,1)S(1)}, bf16[3,64,256]{2,1,0:T(8,128)(2,1)S(1)}, u32[]{:S(2)}, u32[]{:S(2)}) collective-permute-start(bf16[3,64,256]{2,1,0:T(8,128)(2,1)S(1)} %get-tuple-element.22), channel_id=1, source_target_pairs={{0,1},{1,0},{2,3},{3,2},{4,8},{5,9},{6,10},{7,11},{8,4},{9,5},{10,... | collective-permute-start | bytes 294920 | tf_op jit(solution)/shard_map/ppermute | solution.py:409
  3.3 5.3 %copy-start.1 = (f32[4,1024]{1,0:T(4,128)S(1)}, f32[4,1024]{1,0:T(4,128)}, u32[]{:S(2)}) copy-start(f32[4,1024]{1,0:T(4,128)} %refs_2_.2) | copy-start | bytes 49156
  5.4 3.2 %collective-permute-start = (f32[48,128]{1,0:T(8,128)S(1)}, f32[48,128]{1,0:T(8,128)S(1)}, u32[]{:S(2)}, u32[]{:S(2)}) collective-permute-start(f32[48,128]{1,0:T(8,128)S(1)} %get-tuple-element.20), channel_id=1, source_target_pairs={{0,1},{1,0},{2,3},{3,2},{4,5},{5,4},{6,7},{7,6},{8,9},{9,8},{10,11... | collective-permute-start | bytes 73736 | tf_op jit(solution)/shard_map/ppermute | solution.py:394
  5.5 7.7 %collective-permute-start.2 = (bf16[3,16,256]{2,1,0:T(8,128)(2,1)S(1)}, bf16[3,16,256]{2,1,0:T(8,128)(2,1)S(1)}, u32[]{:S(2)}, u32[]{:S(2)}) collective-permute-start(bf16[3,16,256]{2,1,0:T(8,128)(2,1)S(1)} %get-tuple-element.23), channel_id=1, source_target_pairs={{0,1},{2,3},{1,0},{3,2},{4,5},{6,7},{5,4},{7,6},{8,9},{10,11},{9,8... | collective-permute-start | bytes 73736 | tf_op jit(solution)/shard_map/ppermute | solution.py:401
  6.0 7.7 %collective-permute-start.3 = (bf16[3,16,256]{2,1,0:T(8,128)(2,1)S(1)}, bf16[3,16,256]{2,1,0:T(8,128)(2,1)S(1)}, u32[]{:S(2)}, u32[]{:S(2)}) collective-permute-start(bf16[3,16,256]{2,1,0:T(8,128)(2,1)S(1)} %get-tuple-element.24), channel_id=1, source_target_pairs={{1,2},{3,0},{2,1},{0,3},{5,6},{7,4},{6,5},{4,7},{9,10},{11,8},{10,... | collective-permute-start | bytes 73736 | tf_op jit(solution)/shard_map/ppermute | solution.py:401
  8.7 9.0 %collective-permute-start.6 = (f32[64,128]{1,0:T(8,128)S(1)}, f32[64,128]{1,0:T(8,128)S(1)}, u32[]{:S(2)}, u32[]{:S(2)}) collective-permute-start(f32[64,128]{1,0:T(8,128)S(1)} %get-tuple-element.21.refs_0_.refs_2_), channel_id=1, source_target_pairs={{0,24},{1,25},{2,26},{3,27},{4,28},{5,29},{6,30},{7,31},{8,16},{9,... | collective-permute-start | bytes 98312 | tf_op jit(solution)/shard_map/ppermute | solution.py:394
  13.3 4.4 %collective-permute-start.5 = (f32[64,128]{1,0:T(8,128)S(1)}, f32[64,128]{1,0:T(8,128)S(1)}, u32[]{:S(2)}, u32[]{:S(2)}) collective-permute-start(f32[64,128]{1,0:T(8,128)S(1)} %get-tuple-element.21.refs_0_.refs_2_), channel_id=1, source_target_pairs={{0,17},{1,16},{2,19},{3,18},{4,21},{5,20},{6,23},{7,22},{8,25},{9,... | collective-permute-start | bytes 98312 | tf_op jit(solution)/shard_map/ppermute | solution.py:394
  13.3 4.4 %collective-permute-start.4 = (f32[64,128]{1,0:T(8,128)S(1)}, f32[64,128]{1,0:T(8,128)S(1)}, u32[]{:S(2)}, u32[]{:S(2)}) collective-permute-start(f32[64,128]{1,0:T(8,128)S(1)} %get-tuple-element.21.refs_0_.refs_2_), channel_id=1, source_target_pairs={{0,9},{1,8},{2,11},{3,10},{4,13},{5,12},{6,15},{7,14},{8,1},{9,0},... | collective-permute-start | bytes 98312 | tf_op jit(solution)/shard_map/ppermute | solution.py:394
  13.6 3.2 %copy-start.3 = (s32[1024]{0:T(1024)S(1)}, s32[1024]{0:T(1024)}, u32[]{:S(2)}) copy-start(s32[1024]{0:T(1024)} %param.19) | copy-start | bytes 12292
  13.6 3.2 %copy-start.4 = (s32[1024,1]{0,1:T(1,128)S(1)}, s32[1024,1]{0,1:T(1,128)}, u32[]{:S(2)}) copy-start(s32[1024,1]{0,1:T(1,128)} %param.17) | copy-start | bytes 12292
  13.6 3.2 %copy-start.6 = (s32[32]{0:T(128)S(1)}, s32[32]{0:T(128)}, u32[]{:S(2)}) copy-start(s32[32]{0:T(128)} %refs_2_.3) | copy-start | bytes 388
  13.6 8.1 %collective-permute-start.7 = (bf16[3,64,256]{2,1,0:T(8,128)(2,1)S(1)}, bf16[3,64,256]{2,1,0:T(8,128)(2,1)S(1)}, u32[]{:S(2)}, u32[]{:S(2)}) collective-permute-start(bf16[3,64,256]{2,1,0:T(8,128)(2,1)S(1)} %get-tuple-element.25), channel_id=1, source_target_pairs={{0,4},{1,5},{2,6},{3,7},{4,0},{5,1},{6,2},{7,3},{8,12},{9,13},{10,... | collective-permute-start | bytes 294920 | tf_op jit(solution)/shard_map/ppermute | solution.py:409
  16.8 4.3 %copy-start.2 = (s32[1024]{0:T(1024)S(1)}, s32[1024]{0:T(1024)}, u32[]{:S(2)}) copy-start(s32[1024]{0:T(1024)} %param.18) | copy-start | bytes 12292
  17.7 7.7 %slice-start = ((s8[8388608]{0:T(1024)(128)(4,1)}), s8[4194304]{0:T(1024)(128)(4,1)S(1)}, s32[]{:S(2)}) async-start(s8[8388608]{0:T(1024)(128)(4,1)} %bitcast.4), calls=%async_computation | async-start | bytes 8388608
  17.8 5.6 %collective-permute-start.10 = (f32[48,128]{1,0:T(8,128)S(1)}, f32[48,128]{1,0:T(8,128)S(1)}, u32[]{:S(2)}, u32[]{:S(2)}) collective-permute-start(f32[48,128]{1,0:T(8,128)S(1)} %slice.4), channel_id=1, source_target_pairs={{0,6},{1,7},{2,4},{3,5},{4,2},{5,3},{6,0},{7,1},{8,14},{9,15},{10,... | collective-permute-start | bytes 73736 | tf_op jit(solution)/shard_map/ppermute | solution.py:394
  18.5 4.9 %collective-permute-start.9 = (f32[48,128]{1,0:T(8,128)S(1)}, f32[48,128]{1,0:T(8,128)S(1)}, u32[]{:S(2)}, u32[]{:S(2)}) collective-permute-start(f32[48,128]{1,0:T(8,128)S(1)} %slice.4), channel_id=1, source_target_pairs={{0,3},{1,2},{2,1},{3,0},{4,7},{5,6},{6,5},{7,4},{8,11},{9,10},{10,... | collective-permute-start | bytes 73736 | tf_op jit(solution)/shard_map/ppermute | solution.py:394
  20.1 3.6 %collective-permute-start.8 = (f32[112,128]{1,0:T(8,128)S(1)}, f32[112,128]{1,0:T(8,128)S(1)}, u32[]{:S(2)}, u32[]{:S(2)}) collective-permute-start(f32[112,128]{1,0:T(8,128)S(1)} %merge.2.fence_ref.refs_0_.refs_2_), channel_id=1, source_target_pairs={{0,5},{1,4},{2,7},{3,6},{4,1},{5,0},{6,3},{7,2},{8,13},{9,12},{10,... | collective-permute-start | bytes 172040 | tf_op jit(solution)/shard_map/ppermute | solution.py:394
  21.7 3.7 %slice-start.1 = ((s8[8388608]{0:T(1024)(128)(4,1)}), s8[4194304]{0:T(1024)(128)(4,1)S(1)}, s32[]{:S(2)}) async-start(s8[8388608]{0:T(1024)(128)(4,1)} %bitcast.4), calls=%async_computation.1 | async-start | bytes 8388608
  23.4 2.0 %copy-start = (bf16[384,1024]{1,0:T(8,128)(2,1)S(1)}, bf16[384,1024]{1,0:T(8,128)(2,1)}, u32[]{:S(2)}) copy-start(bf16[384,1024]{1,0:T(8,128)(2,1)} %w_in_ref.1) | copy-start | bytes 2359300
  23.4 2.0 %copy-start.5 = (f32[1024]{0:T(1024)S(1)}, f32[1024]{0:T(1024)}, u32[]{:S(2)}) copy-start(f32[1024]{0:T(1024)} %param.14) | copy-start | bytes 12292
  23.7 1.7 %collective-permute-start.11 = (f32[176,128]{1,0:T(8,128)S(1)}, f32[176,128]{1,0:T(8,128)S(1)}, u32[]{:S(2)}, u32[]{:S(2)}) collective-permute-start(f32[176,128]{1,0:T(8,128)S(1)} %merge.3.keep_ref), channel_id=1, source_target_pairs={{0,1},{1,0},{2,3},{3,2},{4,5},{5,4},{6,7},{7,6},{8,9},{9,8},{10,11... | collective-permute-start | bytes 270344 | tf_op jit(solution)/shard_map/ppermute | solution.py:394

commit v8 on v7

--- a/solution.py
+++ b/solution.py
@@ -51,6 +51,7 @@
     weight_ref,
     velocity_ref,
     x_odd_ref,
+    slots_ref,
     cells,
     place_hot,
     gains,
@@ -113,6 +114,7 @@
         jnp.concatenate(sub_hot, axis=0), weight_parts, preferred_element_type=F32
     )
     slots = slots_of(rotor_rows[...], slot_table)
+    slots_ref[...] = slots
     slot_hot[...] = jnp.concatenate(
         [hot(slots[g : g + 1, :] == sublanes(rotors)) for g in range(groups)], axis=1
     )
@@ -241,10 +243,9 @@
             )
 
 
-def key_kernel(fences, *refs):
-    slot_ref, rotor_ref, sub_ref, key_ref = refs[fences:]
-    rotors = slot_ref.shape[0]
-    keys = sub_ref[...] // 2 * rotors + slots_of(rotor_ref[...], slot_ref)
+def key_kernel(rotors, fences, *refs):
+    slots_ref, sub_ref, key_ref = refs[fences:]
+    keys = sub_ref[...] // 2 * rotors + slots_ref[...]
     for group in range(keys.shape[0]):
         key = as_column(keys[group : group + 1, :])
         for block in range(key_ref.shape[1] // TILE):
@@ -432,6 +433,7 @@
         load_kernel,
         out_shape=(
             jax.ShapeDtypeStruct((parts, size_y, size_z), BF16),
+            jax.ShapeDtypeStruct((groups, TILE), jnp.int32),
             jax.ShapeDtypeStruct(velocity.shape, F32),
             jax.ShapeDtypeStruct((entries, columns), BF16),
             jax.ShapeDtypeStruct((entries, parts * TILE), F32),
@@ -439,7 +441,7 @@
             jax.ShapeDtypeStruct((rotors, entries), BF16),
         ),
         in_specs=[HBM] * 6,
-        out_specs=tuple(vmem(6)),
+        out_specs=tuple(vmem(7)),
         scratch_shapes=[
             pltpu.VMEM((groups, TILE), jnp.int32),
             pltpu.VMEM((groups, TILE), jnp.int32),
@@ -500,19 +502,19 @@
     )(*fences, velocity, *halos)
 
 
-def key_matrix(fences, slot_of_rotor, rotor, sub, keys):
-    entries = rotor.shape[0] * TILE
+def key_matrix(rotors, fences, slots, sub, keys):
+    entries = slots.shape[0] * TILE
     return pl.pallas_call(
-        functools.partial(key_kernel, len(fences)),
+        functools.partial(key_kernel, rotors, len(fences)),
         out_shape=jax.ShapeDtypeStruct((entries, keys), BF16),
-        in_specs=[ANY] * len(fences) + [SMEM] + vmem(2),
+        in_specs=[ANY] * len(fences) + vmem(2),
         out_specs=vmem(1)[0],
         compiler_params=pltpu.CompilerParams(vmem_limit_bytes=4 << 20),
         cost_estimate=pl.CostEstimate(
             flops=1000 * entries * keys, bytes_accessed=2 * entries * keys, transcendentals=0
         ),
         name="keys",
-    )(*fences, slot_of_rotor, rotor, sub)
+    )(*fences, slots, sub)
 
 
 def place_matrix(fence, tile, columns, halves):
@@ -615,7 +617,7 @@
     sub = entry_sub.reshape(entries // TILE, TILE)
 
     bits = count.bit_length() - 1
-    x_odd, cells, *loaded = load(tile, rotor, sub, slot_of_rotor, shape_weight, velocity)
+    x_odd, slots, cells, *loaded = load(tile, rotor, sub, slot_of_rotor, shape_weight, velocity)
     x_odd = swap_pairs(x_odd, "slab", (slabs, crosses), 1)
     keep, send, y_even, y_odd = pool(bits, cells, *loaded)
     y_even = swap_pairs(y_even, "cross", (slabs, crosses), 0)
@@ -633,8 +635,9 @@
     for step in steps:
         made = []
         if step == steps[0]:
-            keys = w_out.shape[1] // (2 * TILE) * slot_of_rotor.shape[0]
-            key_hot = key_matrix((packed, x_odd), slot_of_rotor, rotor, sub, keys)
+            rotors = slot_of_rotor.shape[0]
+            keys = w_out.shape[1] // (2 * TILE) * rotors
+            key_hot = key_matrix(rotors, (packed, x_odd), slots, sub, keys)
             fields.append(stencil(inner, (packed,), slabs, crosses, cells, (y_even, y_odd)))
             made += [key_hot, fields[-1]]
         if step == steps[-1]:

time: 28.9 us -> 28.9 us (level)
  waiting for transfers between devices: 1.17 us -> 1.86 us
  Pallas kernels: 12 us -> 11.5 us
    ppermute x8, waiting for transfers between devices: 1.16 us -> 1.84 us  [swap(): return lax.ppermute(value, axis, [(i, i ^ offset) for i in range(count)])]
    pallas_call x1, Pallas kernels: 0.83 us -> 0.28 us  [key_matrix(): pl.pallas_call(functools.partial(key_kernel, rotors, len(fences)), out_sh...]
  transfers between devices with their start and end apart: 12 -> 12, of which waited for: 2 -> 3; matrix products, arithmetic and copies ran while one was open for 0% -> 0% of each run, Pallas kernels for 23% -> 21%
where the time goes in v8:
time: 28.9 us; the launch traced here: 28.7 us
  starting transfers between devices  14.5 us (50%)
  Pallas kernels  11.5 us (40%)
  waiting for transfers between devices  1.86 us (6%)
  between operations  0.8 us (3%)
    ppermute x8, starting transfers between devices, swap(): return lax.ppermute(value, axis, [(i, i ^ offset) for i in range(count)])  9.1 us
    pallas_call x1, Pallas kernels, rotors_step(): pl.pallas_call(functools.partial(rotor_kernel, bits, runs), out_shape=(ja...  3.27 us
    ppermute x2, starting transfers between devices, swap_pairs(): return lax.ppermute(value, axis, pairs + [(j, i) for i, j in pairs])  3.1 us
    pallas_call x2, Pallas kernels, stencil(): pl.pallas_call(functools.partial(stencil_kernel, planes, edges, len(fence...  2.96 us
    ppermute x2, starting transfers between devices, swap_pairs(): return lax.ppermute(value, BOTH, pairs)  2.32 us
    pallas_call x1, Pallas kernels, pool(): pl.pallas_call(functools.partial(pool_kernel, bits), out_shape=(part, par...  2.15 us
    pallas_call x1, Pallas kernels, load(): pl.pallas_call(load_kernel, out_shape=(jax.ShapeDtypeStruct((parts, size_...  2.13 us
    ppermute x8, waiting for transfers between devices, swap(): return lax.ppermute(value, axis, [(i, i ^ offset) for i in range(count)])  1.84 us
  transfers between devices with their start and end apart: 12, of which 3 were waited for; matrix products, arithmetic and copies ran while one was open for 0% of the time, Pallas kernels for 21%

profile of v8, /device:TPU:0, one launch (start us, length us, event | category | flops | bytes accessed | tf_op | source)
XLA Modules:
  0.0 28.7 jit_solution(9511694006287179354)
XLA Ops:
  0.6 2.1 %load.1 = (bf16[3,64,256]{2,1,0:T(8,128)(2,1)S(1)}, s32[8,128]{1,0:T(8,128)S(1)}, f32[3,16,64,256]{3,2,1,0:T(8,128)S(1)}, bf16[1024,1024]{1,0:T(8,128)(2,1)S(1)}...) custom-call(s32[8,128]{1,0:T(8,128)} %bitcast.6, s32[8,128]{1,0:T(8,128)} %bitcast.13, ...), custom_call_target="tpu_custom_call" | custom-call | flops 536870912 | bytes 3145728 | tf_op jit(solution)/shard_map/load/pallas_call | solution.py:432
  2.8 0.5 %collective-permute-start.1 = (bf16[3,64,256]{2,1,0:T(8,128)(2,1)S(1)}, bf16[3,64,256]{2,1,0:T(8,128)(2,1)S(1)}, u32[]{:S(2)}, u32[]{:S(2)}) collective-permute-start(bf16[3,64,256]{2,1,0:T(8,128)(2,1)S(1)} %get-tuple-element.23), channel_id=1, source_target_pairs={{0,1},{1,0},{2,3},{3,2},{4,8},{5,9},{6,10},{7,11},{8,4},{9,5},{10,... | collective-permute-start | bytes 294920 | tf_op jit(solution)/shard_map/ppermute | solution.py:410
  3.3 2.1 %pool.1 = (f32[48,128]{1,0:T(8,128)S(1)}, f32[48,128]{1,0:T(8,128)S(1)}, bf16[3,16,256]{2,1,0:T(8,128)(2,1)S(1)}, bf16[3,16,256]{2,1,0:T(8,128)(2,1)S(1)}) custom-call(f32[3,16,64,256]{3,2,1,0:T(8,128)S(1)} %get-tuple-element.15.cells.refs_3_.refs_1_, bf16[1024,1024]{1,0:T(8,128)(2,1)S(1)} %get-tuple-element.16.place_hot, ...), custom_call_target="tpu_custom_call" | custom-call | flops 1610612736 | bytes 3145728 | tf_op jit(solution)/shard_map/pool/pallas_call | solution.py:468
  5.4 0.1 collective-permute-start
  5.5 0.5 %collective-permute-start.2 = (bf16[3,16,256]{2,1,0:T(8,128)(2,1)S(1)}, bf16[3,16,256]{2,1,0:T(8,128)(2,1)S(1)}, u32[]{:S(2)}, u32[]{:S(2)}) collective-permute-start(bf16[3,16,256]{2,1,0:T(8,128)(2,1)S(1)} %get-tuple-element.25), channel_id=1, source_target_pairs={{0,1},{2,3},{1,0},{3,2},{4,5},{6,7},{5,4},{7,6},{8,9},{10,11},{9,8... | collective-permute-start | bytes 73736 | tf_op jit(solution)/shard_map/ppermute | solution.py:402
  6.0 2.6 %collective-permute-start.3 = (bf16[3,16,256]{2,1,0:T(8,128)(2,1)S(1)}, bf16[3,16,256]{2,1,0:T(8,128)(2,1)S(1)}, u32[]{:S(2)}, u32[]{:S(2)}) collective-permute-start(bf16[3,16,256]{2,1,0:T(8,128)(2,1)S(1)} %get-tuple-element.26), channel_id=1, source_target_pairs={{1,2},{3,0},{2,1},{0,3},{5,6},{7,4},{6,5},{4,7},{9,10},{11,8},{10,... | collective-permute-start | bytes 73736 | tf_op jit(solution)/shard_map/ppermute | solution.py:402
  8.6 0.0 collective-permute-done.refs_1_
  8.7 4.6 %collective-permute-start.6 = (f32[64,128]{1,0:T(8,128)S(1)}, f32[64,128]{1,0:T(8,128)S(1)}, u32[]{:S(2)}, u32[]{:S(2)}) collective-permute-start(f32[64,128]{1,0:T(8,128)S(1)} %get-tuple-element.22.refs_0_.refs_2_), channel_id=1, source_target_pairs={{0,24},{1,25},{2,26},{3,27},{4,28},{5,29},{6,30},{7,31},{8,16},{9,... | collective-permute-start | bytes 98312 | tf_op jit(solution)/shard_map/ppermute | solution.py:395
  13.3 0.0 collective-permute-start.5
  13.3 0.0 collective-permute-done.2.refs_2_
  13.3 0.4 %collective-permute-start.4 = (f32[64,128]{1,0:T(8,128)S(1)}, f32[64,128]{1,0:T(8,128)S(1)}, u32[]{:S(2)}, u32[]{:S(2)}) collective-permute-start(f32[64,128]{1,0:T(8,128)S(1)} %get-tuple-element.22.refs_0_.refs_2_), channel_id=1, source_target_pairs={{0,9},{1,8},{2,11},{3,10},{4,13},{5,12},{6,15},{7,14},{8,1},{9,0},... | collective-permute-start | bytes 98312 | tf_op jit(solution)/shard_map/ppermute | solution.py:395
  13.6 0.0 collective-permute-done.3.refs_3_
  13.6 1.8 %collective-permute-start.7 = (bf16[3,64,256]{2,1,0:T(8,128)(2,1)S(1)}, bf16[3,64,256]{2,1,0:T(8,128)(2,1)S(1)}, u32[]{:S(2)}, u32[]{:S(2)}) collective-permute-start(bf16[3,64,256]{2,1,0:T(8,128)(2,1)S(1)} %get-tuple-element.27), channel_id=1, source_target_pairs={{0,4},{1,5},{2,6},{3,7},{4,0},{5,1},{6,2},{7,3},{8,12},{9,13},{10,... | collective-permute-start | bytes 294920 | tf_op jit(solution)/shard_map/ppermute | solution.py:410
  15.4 1.3 %stencil.2.refs_1_.rest_0_ = f32[3,7,64,256]{3,2,1,0:T(8,128)S(1)} custom-call(f32[64,128]{1,0:T(8,128)S(1)} %get-tuple-element.22.refs_0_.refs_2_, f32[3,16,64,256]{3,2,1,0:T(8,128)S(1)} %get-tuple-element.15.cells.refs_3_.refs_1_, bf16[3,16,256]{2,1,0:T(8,128)(2,1)S(1)} %collective-permute-done.2.refs_2_, ...), custom_call_target="tpu_custom_call" | custom-call | flops 344064000 | bytes 2752512 | tf_op jit(solution)/shard_map/stencil/pallas_call | solution.py:490
  16.7 0.0 copy-start.2
  16.7 0.3 keys.1.refs_0_.key_hot
  17.0 0.0 collective-permute-done.6.refs_5_
  17.0 0.5 %collective-permute-done.5.refs_4_ = f32[64,128]{1,0:T(8,128)S(1)} collective-permute-done((f32[64,128]{1,0:T(8,128)S(1)}, f32[64,128]{1,0:T(8,128)S(1)}, u32[]{:S(2)}, u32[]{:S(2)}) %collective-permute-start.5) | collective-permute-done | bytes 32800 | tf_op jit(solution)/shard_map/ppermute | solution.py:395
  17.5 0.9 %collective-permute-start.10 = (f32[48,128]{1,0:T(8,128)S(1)}, f32[48,128]{1,0:T(8,128)S(1)}, u32[]{:S(2)}, u32[]{:S(2)}) collective-permute-start(f32[48,128]{1,0:T(8,128)S(1)} %slice.4), channel_id=1, source_target_pairs={{0,6},{1,7},{2,4},{3,5},{4,2},{5,3},{6,0},{7,1},{8,14},{9,15},{10,... | collective-permute-start | bytes 73736 | tf_op jit(solution)/shard_map/ppermute | solution.py:395
  18.5 1.6 %collective-permute-start.9 = (f32[48,128]{1,0:T(8,128)S(1)}, f32[48,128]{1,0:T(8,128)S(1)}, u32[]{:S(2)}, u32[]{:S(2)}) collective-permute-start(f32[48,128]{1,0:T(8,128)S(1)} %slice.4), channel_id=1, source_target_pairs={{0,3},{1,2},{2,1},{3,0},{4,7},{5,6},{6,5},{7,4},{8,11},{9,10},{10,... | collective-permute-start | bytes 73736 | tf_op jit(solution)/shard_map/ppermute | solution.py:395
  20.1 0.8 %collective-permute-start.8 = (f32[112,128]{1,0:T(8,128)S(1)}, f32[112,128]{1,0:T(8,128)S(1)}, u32[]{:S(2)}, u32[]{:S(2)}) collective-permute-start(f32[112,128]{1,0:T(8,128)S(1)} %merge.2.fence_ref.refs_0_.refs_2_), channel_id=1, source_target_pairs={{0,5},{1,4},{2,7},{3,6},{4,1},{5,0},{6,3},{7,2},{8,13},{9,12},{10,... | collective-permute-start | bytes 172040 | tf_op jit(solution)/shard_map/ppermute | solution.py:395
  20.8 0.6 %places.1.refs_0_.place_hot = bf16[1024,1024]{1,0:T(8,128)(2,1)S(1)} custom-call(f32[112,128]{1,0:T(8,128)S(1)} %merge.2.fence_ref.refs_0_.refs_2_, s32[8,128]{1,0:T(8,128)S(1)} %bitcast.7), custom_call_target="tpu_custom_call" | custom-call | flops 1048576000 | bytes 2097152 | tf_op jit(solution)/shard_map/places/pallas_call | solution.py:522
  21.4 0.0 slice-start.1
  21.5 0.0 collective-permute-done.7.refs_4_
  21.5 1.7 %stencil.3.refs_1_.rest_1_ = f32[3,9,64,256]{3,2,1,0:T(8,128)S(1)} custom-call(f32[112,128]{1,0:T(8,128)S(1)} %merge.2.fence_ref.refs_0_.refs_2_, f32[3,16,64,256]{3,2,1,0:T(8,128)S(1)} %get-tuple-element.15.cells.refs_3_.refs_1_, bf16[3,16,256]{2,1,0:T(8,128)(2,1)S(1)} %collective-permute-done.2.refs_2_, ...), custom_call_target="tpu_custom_call" | custom-call | flops 442368000 | bytes 3538944 | tf_op jit(solution)/shard_map/stencil/pallas_call | solution.py:490
  23.2 0.0 copy-start
  23.2 0.0 copy-start.4
  23.2 0.0 collective-permute-done.9.refs_4_
  23.2 0.4 %collective-permute-done.8.refs_3_ = f32[112,128]{1,0:T(8,128)S(1)} collective-permute-done((f32[112,128]{1,0:T(8,128)S(1)}, f32[112,128]{1,0:T(8,128)S(1)}, u32[]{:S(2)}, u32[]{:S(2)}) %collective-permute-start.8) | collective-permute-done | bytes 57376 | tf_op jit(solution)/shard_map/ppermute | solution.py:395
  23.7 0.8 %collective-permute-start.11 = (f32[176,128]{1,0:T(8,128)S(1)}, f32[176,128]{1,0:T(8,128)S(1)}, u32[]{:S(2)}, u32[]{:S(2)}) collective-permute-start(f32[176,128]{1,0:T(8,128)S(1)} %merge.3.keep_ref), channel_id=1, source_target_pairs={{0,1},{1,0},{2,3},{3,2},{4,5},{5,4},{6,7},{7,6},{8,9},{9,8},{10,11... | collective-permute-start | bytes 270344 | tf_op jit(solution)/shard_map/ppermute | solution.py:395
  24.5 0.9 %collective-permute-done.11.other_ref = f32[176,128]{1,0:T(8,128)S(1)} collective-permute-done((f32[176,128]{1,0:T(8,128)S(1)}, f32[176,128]{1,0:T(8,128)S(1)}, u32[]{:S(2)}, u32[]{:S(2)}) %collective-permute-start.11) | collective-permute-done | bytes 90144 | tf_op jit(solution)/shard_map/ppermute | solution.py:395
  25.4 3.3 %rotors.1 = (f32[3,16,64,256]{3,2,1,0:T(8,128)}, f32[4,1024]{1,0:T(4,128)}) custom-call(s32[8,128]{1,0:T(8,128)S(1)} %bitcast.8, s32[8,128]{1,0:T(8,128)S(1)} %bitcast.11, bf16[384,1024]{1,0:T(8,128)(2,1)S(1)} %copy-done, bf16[1024,4096]{1,0:T(8,128)(2,1)S(1)} %bitcast.5, f32[1,1024]{1,0:T(1,128)S(1)} %bitcast.12, ...), custom_call_target="tpu_custom_call" | custom-call | flops 1073741824 | bytes 8388608 | tf_op jit(solution)/shard_map/rotors/pallas_call | solution.py:574
  (18 shorter events, 0.1 us)
Async XLA Ops:
  2.8 13.9 %collective-permute-start.1 = (bf16[3,64,256]{2,1,0:T(8,128)(2,1)S(1)}, bf16[3,64,256]{2,1,0:T(8,128)(2,1)S(1)}, u32[]{:S(2)}, u32[]{:S(2)}) collective-permute-start(bf16[3,64,256]{2,1,0:T(8,128)(2,1)S(1)} %get-tuple-element.23), channel_id=1, source_target_pairs={{0,1},{1,0},{2,3},{3,2},{4,8},{5,9},{6,10},{7,11},{8,4},{9,5},{10,... | collective-permute-start | bytes 294920 | tf_op jit(solution)/shard_map/ppermute | solution.py:410
  3.3 5.3 %copy-start.1 = (f32[4,1024]{1,0:T(4,128)S(1)}, f32[4,1024]{1,0:T(4,128)}, u32[]{:S(2)}) copy-start(f32[4,1024]{1,0:T(4,128)} %refs_2_.1) | copy-start | bytes 49156
  5.4 3.2 %collective-permute-start = (f32[48,128]{1,0:T(8,128)S(1)}, f32[48,128]{1,0:T(8,128)S(1)}, u32[]{:S(2)}, u32[]{:S(2)}) collective-permute-start(f32[48,128]{1,0:T(8,128)S(1)} %get-tuple-element.21), channel_id=1, source_target_pairs={{0,1},{1,0},{2,3},{3,2},{4,5},{5,4},{6,7},{7,6},{8,9},{9,8},{10,11... | collective-permute-start | bytes 73736 | tf_op jit(solution)/shard_map/ppermute | solution.py:395
  5.5 7.7 %collective-permute-start.2 = (bf16[3,16,256]{2,1,0:T(8,128)(2,1)S(1)}, bf16[3,16,256]{2,1,0:T(8,128)(2,1)S(1)}, u32[]{:S(2)}, u32[]{:S(2)}) collective-permute-start(bf16[3,16,256]{2,1,0:T(8,128)(2,1)S(1)} %get-tuple-element.25), channel_id=1, source_target_pairs={{0,1},{2,3},{1,0},{3,2},{4,5},{6,7},{5,4},{7,6},{8,9},{10,11},{9,8... | collective-permute-start | bytes 73736 | tf_op jit(solution)/shard_map/ppermute | solution.py:402
  6.0 7.7 %collective-permute-start.3 = (bf16[3,16,256]{2,1,0:T(8,128)(2,1)S(1)}, bf16[3,16,256]{2,1,0:T(8,128)(2,1)S(1)}, u32[]{:S(2)}, u32[]{:S(2)}) collective-permute-start(bf16[3,16,256]{2,1,0:T(8,128)(2,1)S(1)} %get-tuple-element.26), channel_id=1, source_target_pairs={{1,2},{3,0},{2,1},{0,3},{5,6},{7,4},{6,5},{4,7},{9,10},{11,8},{10,... | collective-permute-start | bytes 73736 | tf_op jit(solution)/shard_map/ppermute | solution.py:402
  8.7 8.4 %collective-permute-start.6 = (f32[64,128]{1,0:T(8,128)S(1)}, f32[64,128]{1,0:T(8,128)S(1)}, u32[]{:S(2)}, u32[]{:S(2)}) collective-permute-start(f32[64,128]{1,0:T(8,128)S(1)} %get-tuple-element.22.refs_0_.refs_2_), channel_id=1, source_target_pairs={{0,24},{1,25},{2,26},{3,27},{4,28},{5,29},{6,30},{7,31},{8,16},{9,... | collective-permute-start | bytes 98312 | tf_op jit(solution)/shard_map/ppermute | solution.py:395
  13.3 4.2 %collective-permute-start.5 = (f32[64,128]{1,0:T(8,128)S(1)}, f32[64,128]{1,0:T(8,128)S(1)}, u32[]{:S(2)}, u32[]{:S(2)}) collective-permute-start(f32[64,128]{1,0:T(8,128)S(1)} %get-tuple-element.22.refs_0_.refs_2_), channel_id=1, source_target_pairs={{0,17},{1,16},{2,19},{3,18},{4,21},{5,20},{6,23},{7,22},{8,25},{9,... | collective-permute-start | bytes 98312 | tf_op jit(solution)/shard_map/ppermute | solution.py:395
  13.3 4.2 %collective-permute-start.4 = (f32[64,128]{1,0:T(8,128)S(1)}, f32[64,128]{1,0:T(8,128)S(1)}, u32[]{:S(2)}, u32[]{:S(2)}) collective-permute-start(f32[64,128]{1,0:T(8,128)S(1)} %get-tuple-element.22.refs_0_.refs_2_), channel_id=1, source_target_pairs={{0,9},{1,8},{2,11},{3,10},{4,13},{5,12},{6,15},{7,14},{8,1},{9,0},... | collective-permute-start | bytes 98312 | tf_op jit(solution)/shard_map/ppermute | solution.py:395
  13.6 3.1 %copy-start.3 = (s32[1024]{0:T(1024)S(1)}, s32[1024]{0:T(1024)}, u32[]{:S(2)}) copy-start(s32[1024]{0:T(1024)} %param.19) | copy-start | bytes 12292
  13.6 7.8 %collective-permute-start.7 = (bf16[3,64,256]{2,1,0:T(8,128)(2,1)S(1)}, bf16[3,64,256]{2,1,0:T(8,128)(2,1)S(1)}, u32[]{:S(2)}, u32[]{:S(2)}) collective-permute-start(bf16[3,64,256]{2,1,0:T(8,128)(2,1)S(1)} %get-tuple-element.27), channel_id=1, source_target_pairs={{0,4},{1,5},{2,6},{3,7},{4,0},{5,1},{6,2},{7,3},{8,12},{9,13},{10,... | collective-permute-start | bytes 294920 | tf_op jit(solution)/shard_map/ppermute | solution.py:410
  16.7 4.1 %copy-start.2 = (s32[1024]{0:T(1024)S(1)}, s32[1024]{0:T(1024)}, u32[]{:S(2)}) copy-start(s32[1024]{0:T(1024)} %param.18) | copy-start | bytes 12292
  17.5 7.9 %slice-start = ((s8[8388608]{0:T(1024)(128)(4,1)}), s8[4194304]{0:T(1024)(128)(4,1)S(1)}, s32[]{:S(2)}) async-start(s8[8388608]{0:T(1024)(128)(4,1)} %bitcast.4), calls=%async_computation | async-start | bytes 8388608
  17.5 5.6 %collective-permute-start.10 = (f32[48,128]{1,0:T(8,128)S(1)}, f32[48,128]{1,0:T(8,128)S(1)}, u32[]{:S(2)}, u32[]{:S(2)}) collective-permute-start(f32[48,128]{1,0:T(8,128)S(1)} %slice.4), channel_id=1, source_target_pairs={{0,6},{1,7},{2,4},{3,5},{4,2},{5,3},{6,0},{7,1},{8,14},{9,15},{10,... | collective-permute-start | bytes 73736 | tf_op jit(solution)/shard_map/ppermute | solution.py:395
  18.5 4.8 %collective-permute-start.9 = (f32[48,128]{1,0:T(8,128)S(1)}, f32[48,128]{1,0:T(8,128)S(1)}, u32[]{:S(2)}, u32[]{:S(2)}) collective-permute-start(f32[48,128]{1,0:T(8,128)S(1)} %slice.4), channel_id=1, source_target_pairs={{0,3},{1,2},{2,1},{3,0},{4,7},{5,6},{6,5},{7,4},{8,11},{9,10},{10,... | collective-permute-start | bytes 73736 | tf_op jit(solution)/shard_map/ppermute | solution.py:395
  20.1 3.6 %collective-permute-start.8 = (f32[112,128]{1,0:T(8,128)S(1)}, f32[112,128]{1,0:T(8,128)S(1)}, u32[]{:S(2)}, u32[]{:S(2)}) collective-permute-start(f32[112,128]{1,0:T(8,128)S(1)} %merge.2.fence_ref.refs_0_.refs_2_), channel_id=1, source_target_pairs={{0,5},{1,4},{2,7},{3,6},{4,1},{5,0},{6,3},{7,2},{8,13},{9,12},{10,... | collective-permute-start | bytes 172040 | tf_op jit(solution)/shard_map/ppermute | solution.py:395
  21.4 4.0 %slice-start.1 = ((s8[8388608]{0:T(1024)(128)(4,1)}), s8[4194304]{0:T(1024)(128)(4,1)S(1)}, s32[]{:S(2)}) async-start(s8[8388608]{0:T(1024)(128)(4,1)} %bitcast.4), calls=%async_computation.1 | async-start | bytes 8388608
  23.2 2.2 %copy-start = (bf16[384,1024]{1,0:T(8,128)(2,1)S(1)}, bf16[384,1024]{1,0:T(8,128)(2,1)}, u32[]{:S(2)}) copy-start(bf16[384,1024]{1,0:T(8,128)(2,1)} %w_in_ref.1) | copy-start | bytes 2359300
  23.2 2.2 %copy-start.4 = (f32[1024]{0:T(1024)S(1)}, f32[1024]{0:T(1024)}, u32[]{:S(2)}) copy-start(f32[1024]{0:T(1024)} %param.14) | copy-start | bytes 12292
  23.7 1.7 %collective-permute-start.11 = (f32[176,128]{1,0:T(8,128)S(1)}, f32[176,128]{1,0:T(8,128)S(1)}, u32[]{:S(2)}, u32[]{:S(2)}) collective-permute-start(f32[176,128]{1,0:T(8,128)S(1)} %merge.3.keep_ref), channel_id=1, source_target_pairs={{0,1},{1,0},{2,3},{3,2},{4,5},{5,4},{6,7},{7,6},{8,9},{9,8},{10,11... | collective-permute-start | bytes 270344 | tf_op jit(solution)/shard_map/ppermute | solution.py:395

commit v9 on v8

--- a/solution.py
+++ b/solution.py
@@ -50,7 +50,6 @@
     slot_ref,
     weight_ref,
     velocity_ref,
-    x_odd_ref,
     slots_ref,
     cells,
     place_hot,
@@ -118,11 +117,8 @@
     slot_hot[...] = jnp.concatenate(
         [hot(slots[g : g + 1, :] == sublanes(rotors)) for g in range(groups)], axis=1
     )
-    even_x = lax.axis_index("slab") % 2 == 0
-    for c in range(parts):
-        copies[c].wait()
-        first, last = cells[c, 0], cells[c, size_x - 1]
-        x_odd_ref[c] = jnp.where(even_x, first, last).astype(BF16)
+    for copy in copies:
+        copy.wait()
 
 
 def first_half(bits):
@@ -265,11 +261,12 @@
 
 
 def join_kernel(bits, fences, *refs):
-    keep_ref, other_ref, states_ref, cells, out_ref, x_even_ref = refs[fences:]
+    keep_ref, other_ref, states_ref, cells, out_ref, x_even_ref, x_odd_ref = refs[fences:]
     even_x = lax.axis_index("slab") % 2 == 0
     for c in range(cells.shape[0]):
-        face = jnp.where(even_x, cells[c, cells.shape[1] - 1], cells[c, 0])
-        x_even_ref[c] = face.astype(BF16)
+        first, last = cells[c, 0], cells[c, cells.shape[1] - 1]
+        x_even_ref[c] = jnp.where(even_x, last, first).astype(BF16)
+        x_odd_ref[c] = jnp.where(even_x, first, last).astype(BF16)
     rows = keep_ref.shape[0]
     out_ref[:rows, :] = keep_ref[...] + other_ref[...]
     half = states_ref.shape[1] // 2
@@ -432,7 +429,6 @@
     return pl.pallas_call(
         load_kernel,
         out_shape=(
-            jax.ShapeDtypeStruct((parts, size_y, size_z), BF16),
             jax.ShapeDtypeStruct((groups, TILE), jnp.int32),
             jax.ShapeDtypeStruct(velocity.shape, F32),
             jax.ShapeDtypeStruct((entries, columns), BF16),
@@ -441,7 +437,7 @@
             jax.ShapeDtypeStruct((rotors, entries), BF16),
         ),
         in_specs=[HBM] * 6,
-        out_specs=tuple(vmem(7)),
+        out_specs=tuple(vmem(6)),
         scratch_shapes=[
             pltpu.VMEM((groups, TILE), jnp.int32),
             pltpu.VMEM((groups, TILE), jnp.int32),
@@ -540,9 +536,10 @@
         out_shape=(
             jax.ShapeDtypeStruct((rows, TILE), F32),
             jax.ShapeDtypeStruct((parts, size_y, size_z), BF16),
+            jax.ShapeDtypeStruct((parts, size_y, size_z), BF16),
         ),
         in_specs=[ANY] * len(fences) + vmem(4),
-        out_specs=tuple(vmem(2)),
+        out_specs=tuple(vmem(3)),
         compiler_params=pltpu.CompilerParams(vmem_limit_bytes=4 << 20),
         name="join",
     )(*fences, keep, other, states, cells)
@@ -617,8 +614,7 @@
     sub = entry_sub.reshape(entries // TILE, TILE)
 
     bits = count.bit_length() - 1
-    x_odd, slots, cells, *loaded = load(tile, rotor, sub, slot_of_rotor, shape_weight, velocity)
-    x_odd = swap_pairs(x_odd, "slab", (slabs, crosses), 1)
+    slots, cells, *loaded = load(tile, rotor, sub, slot_of_rotor, shape_weight, velocity)
     keep, send, y_even, y_odd = pool(bits, cells, *loaded)
     y_even = swap_pairs(y_even, "cross", (slabs, crosses), 0)
     y_odd = swap_pairs(y_odd, "cross", (slabs, crosses), 1)
@@ -627,8 +623,11 @@
     middle = size_x // 2
     inner, outer = tuple(range(1, middle)), (0,) + tuple(range(middle, size_x))
     runs = ((1, middle - 1, 0, 0), (0, 1, 1, 0), (middle, size_x - middle, 1, 1))
-    packed, x_even = join(bits, (), keep, swap(send, BOTH, count, 1), rotor_states, cells)
+    packed, x_even, x_odd = join(
+        bits, (), keep, swap(send, BOTH, count, 1), rotor_states, cells
+    )
     x_even = swap_pairs(x_even, "slab", (slabs, crosses), 0)
+    x_odd = swap_pairs(x_odd, "slab", (slabs, crosses), 1)
     slab_bit = crosses.bit_length() - 1
     steps = [tuple(range(b, min(b + 2, bits))) for b in range(1, bits, 2)][::-1]
     fields = []
@@ -637,7 +636,7 @@
         if step == steps[0]:
             rotors = slot_of_rotor.shape[0]
             keys = w_out.shape[1] // (2 * TILE) * rotors
-            key_hot = key_matrix(rotors, (packed, x_odd), slots, sub, keys)
+            key_hot = key_matrix(rotors, (packed,), slots, sub, keys)
             fields.append(stencil(inner, (packed,), slabs, crosses, cells, (y_even, y_odd)))
             made += [key_hot, fields[-1]]
         if step == steps[-1]:

time: 28.9 us -> 28.1 us (0.972)
  starting transfers between devices: 14.5 us -> 13.3 us
  waiting for transfers between devices: 1.86 us -> 2.3 us
    ppermute x2, starting transfers between devices: 2.32 us -> 1.57 us  [swap_pairs(): return lax.ppermute(value, BOTH, pairs)]
    ppermute x8, waiting for transfers between devices: 1.84 us -> 2.29 us  [swap(): return lax.ppermute(value, axis, [(i, i ^ offset) for i in range(count)])]
    ppermute x2, starting transfers between devices: 3.1 us -> 2.71 us  [swap_pairs(): return lax.ppermute(value, axis, pairs + [(j, i) for i, j in pairs])]
  transfers between devices with their start and end apart: 12 -> 12, of which waited for: 3 -> 4; matrix products, arithmetic and copies ran while one was open for 0% -> 0% of each run, Pallas kernels for 21% -> 14%
where the time goes in v9:
time: 28.1 us; the launch traced here: 27.9 us
  starting transfers between devices  13.3 us (47%)
  Pallas kernels  11.5 us (41%)
  waiting for transfers between devices  2.3 us (8%)
  between operations  0.81 us (3%)
    ppermute x8, starting transfers between devices, swap(): return lax.ppermute(value, axis, [(i, i ^ offset) for i in range(count)])  9.04 us
    pallas_call x1, Pallas kernels, rotors_step(): pl.pallas_call(functools.partial(rotor_kernel, bits, runs), out_shape=(ja...  3.27 us
    pallas_call x2, Pallas kernels, stencil(): pl.pallas_call(functools.partial(stencil_kernel, planes, edges, len(fence...  2.97 us
    ppermute x2, starting transfers between devices, swap_pairs(): return lax.ppermute(value, axis, pairs + [(j, i) for i, j in pairs])  2.71 us
    ppermute x8, waiting for transfers between devices, swap(): return lax.ppermute(value, axis, [(i, i ^ offset) for i in range(count)])  2.29 us
    pallas_call x1, Pallas kernels, pool(): pl.pallas_call(functools.partial(pool_kernel, bits), out_shape=(part, par...  2.15 us
    pallas_call x1, Pallas kernels, load(): pl.pallas_call(load_kernel, out_shape=(jax.ShapeDtypeStruct((groups, TILE...  2.11 us
    ppermute x2, starting transfers between devices, swap_pairs(): return lax.ppermute(value, BOTH, pairs)  1.57 us
  transfers between devices with their start and end apart: 12, of which 4 were waited for; matrix products, arithmetic and copies ran while one was open for 0% of the time, Pallas kernels for 14%

profile of v9, /device:TPU:0, one launch (start us, length us, event | category | flops | bytes accessed | tf_op | source)
XLA Modules:
  0.0 27.9 jit_solution(8201521181045928042)
XLA Ops:
  0.6 2.1 %load.1 = (s32[8,128]{1,0:T(8,128)S(1)}, f32[3,16,64,256]{3,2,1,0:T(8,128)S(1)}, bf16[1024,1024]{1,0:T(8,128)(2,1)S(1)}, f32[1024,384]{1,0:T(8,128)S(1)}, s32[10...) custom-call(s32[8,128]{1,0:T(8,128)} %bitcast.6, s32[8,128]{1,0:T(8,128)} %bitcast.13, s32[8,128]{1,0:T(8,128)} %bitcast.9, ...), custom_call_target="tpu_custom_call" | custom-call | flops 536870912 | bytes 3145728 | tf_op jit(solution)/shard_map/load/pallas_call | solution.py:429
  2.7 0.0 copy-start.1
  2.8 2.2 %pool.1 = (f32[48,128]{1,0:T(8,128)S(1)}, f32[48,128]{1,0:T(8,128)S(1)}, bf16[3,16,256]{2,1,0:T(8,128)(2,1)S(1)}, bf16[3,16,256]{2,1,0:T(8,128)(2,1)S(1)}) custom-call(f32[3,16,64,256]{3,2,1,0:T(8,128)S(1)} %get-tuple-element.15.cells.refs_3_.refs_1_, bf16[1024,1024]{1,0:T(8,128)(2,1)S(1)} %get-tuple-element.16.place_hot, ...), custom_call_target="tpu_custom_call" | custom-call | flops 1610612736 | bytes 3145728 | tf_op jit(solution)/shard_map/pool/pallas_call | solution.py:464
  4.9 0.0 copy-start.3
  4.9 0.5 %collective-permute-start = (f32[48,128]{1,0:T(8,128)S(1)}, f32[48,128]{1,0:T(8,128)S(1)}, u32[]{:S(2)}, u32[]{:S(2)}) collective-permute-start(f32[48,128]{1,0:T(8,128)S(1)} %get-tuple-element.21), channel_id=1, source_target_pairs={{0,1},{1,0},{2,3},{3,2},{4,5},{5,4},{6,7},{7,6},{8,9},{9,8},{10,11... | collective-permute-start | bytes 73736 | tf_op jit(solution)/shard_map/ppermute | solution.py:392
  5.4 0.1 collective-permute-start.1
  5.5 2.6 %collective-permute-start.2 = (bf16[3,16,256]{2,1,0:T(8,128)(2,1)S(1)}, bf16[3,16,256]{2,1,0:T(8,128)(2,1)S(1)}, u32[]{:S(2)}, u32[]{:S(2)}) collective-permute-start(bf16[3,16,256]{2,1,0:T(8,128)(2,1)S(1)} %get-tuple-element.25), channel_id=1, source_target_pairs={{1,2},{3,0},{2,1},{0,3},{5,6},{7,4},{6,5},{4,7},{9,10},{11,8},{10,... | collective-permute-start | bytes 73736 | tf_op jit(solution)/shard_map/ppermute | solution.py:399
  8.2 0.0 collective-permute-done.refs_1_
  8.2 3.7 %collective-permute-start.5 = (f32[64,128]{1,0:T(8,128)S(1)}, f32[64,128]{1,0:T(8,128)S(1)}, u32[]{:S(2)}, u32[]{:S(2)}) collective-permute-start(f32[64,128]{1,0:T(8,128)S(1)} %get-tuple-element.22.refs_0_.refs_2_), channel_id=1, source_target_pairs={{0,24},{1,25},{2,26},{3,27},{4,28},{5,29},{6,30},{7,31},{8,16},{9,... | collective-permute-start | bytes 98312 | tf_op jit(solution)/shard_map/ppermute | solution.py:392
  11.9 0.0 collective-permute-start.4
  11.9 0.5 %collective-permute-start.3 = (f32[64,128]{1,0:T(8,128)S(1)}, f32[64,128]{1,0:T(8,128)S(1)}, u32[]{:S(2)}, u32[]{:S(2)}) collective-permute-start(f32[64,128]{1,0:T(8,128)S(1)} %get-tuple-element.22.refs_0_.refs_2_), channel_id=1, source_target_pairs={{0,9},{1,8},{2,11},{3,10},{4,13},{5,12},{6,15},{7,14},{8,1},{9,0},... | collective-permute-start | bytes 98312 | tf_op jit(solution)/shard_map/ppermute | solution.py:392
  12.4 0.3 keys.1.refs_0_.key_hot
  12.7 1.6 %collective-permute-start.6 = (bf16[3,64,256]{2,1,0:T(8,128)(2,1)S(1)}, bf16[3,64,256]{2,1,0:T(8,128)(2,1)S(1)}, u32[]{:S(2)}, u32[]{:S(2)}) collective-permute-start(bf16[3,64,256]{2,1,0:T(8,128)(2,1)S(1)} %get-tuple-element.26), channel_id=1, source_target_pairs={{0,4},{1,5},{2,6},{3,7},{4,0},{5,1},{6,2},{7,3},{8,12},{9,13},{10,... | collective-permute-start | bytes 294920 | tf_op jit(solution)/shard_map/ppermute | solution.py:407
  14.2 0.0 collective-permute-start.7
  14.3 1.3 %stencil.2.refs_1_.rest_0_ = f32[3,7,64,256]{3,2,1,0:T(8,128)S(1)} custom-call(f32[64,128]{1,0:T(8,128)S(1)} %get-tuple-element.22.refs_0_.refs_2_, f32[3,16,64,256]{3,2,1,0:T(8,128)S(1)} %get-tuple-element.15.cells.refs_3_.refs_1_, bf16[3,16,256]{2,1,0:T(8,128)(2,1)S(1)} %collective-permute-done.1.refs_2_, ...), custom_call_target="tpu_custom_call" | custom-call | flops 344064000 | bytes 2752512 | tf_op jit(solution)/shard_map/stencil/pallas_call | solution.py:486
  15.5 0.0 copy-start.2
  15.6 0.6 %collective-permute-done.4.refs_4_ = f32[64,128]{1,0:T(8,128)S(1)} collective-permute-done((f32[64,128]{1,0:T(8,128)S(1)}, f32[64,128]{1,0:T(8,128)S(1)}, u32[]{:S(2)}, u32[]{:S(2)}) %collective-permute-start.4) | collective-permute-done | bytes 32800 | tf_op jit(solution)/shard_map/ppermute | solution.py:392
  16.1 0.0 collective-permute-done.3.refs_3_
  16.2 2.4 %collective-permute-start.10 = (f32[48,128]{1,0:T(8,128)S(1)}, f32[48,128]{1,0:T(8,128)S(1)}, u32[]{:S(2)}, u32[]{:S(2)}) collective-permute-start(f32[48,128]{1,0:T(8,128)S(1)} %slice.4), channel_id=1, source_target_pairs={{0,6},{1,7},{2,4},{3,5},{4,2},{5,3},{6,0},{7,1},{8,14},{9,15},{10,... | collective-permute-start | bytes 73736 | tf_op jit(solution)/shard_map/ppermute | solution.py:392
  18.6 0.4 %collective-permute-start.9 = (f32[48,128]{1,0:T(8,128)S(1)}, f32[48,128]{1,0:T(8,128)S(1)}, u32[]{:S(2)}, u32[]{:S(2)}) collective-permute-start(f32[48,128]{1,0:T(8,128)S(1)} %slice.4), channel_id=1, source_target_pairs={{0,3},{1,2},{2,1},{3,0},{4,7},{5,6},{6,5},{7,4},{8,11},{9,10},{10,... | collective-permute-start | bytes 73736 | tf_op jit(solution)/shard_map/ppermute | solution.py:392
  19.0 0.4 %collective-permute-start.8 = (f32[112,128]{1,0:T(8,128)S(1)}, f32[112,128]{1,0:T(8,128)S(1)}, u32[]{:S(2)}, u32[]{:S(2)}) collective-permute-start(f32[112,128]{1,0:T(8,128)S(1)} %merge.2.fence_ref.refs_0_.refs_2_), channel_id=1, source_target_pairs={{0,5},{1,4},{2,7},{3,6},{4,1},{5,0},{6,3},{7,2},{8,13},{9,12},{10,... | collective-permute-start | bytes 172040 | tf_op jit(solution)/shard_map/ppermute | solution.py:392
  19.4 0.6 %places.1.refs_0_.place_hot = bf16[1024,1024]{1,0:T(8,128)(2,1)S(1)} custom-call(f32[112,128]{1,0:T(8,128)S(1)} %merge.2.fence_ref.refs_0_.refs_2_, s32[8,128]{1,0:T(8,128)S(1)} %bitcast.7), custom_call_target="tpu_custom_call" | custom-call | flops 1048576000 | bytes 2097152 | tf_op jit(solution)/shard_map/places/pallas_call | solution.py:518
  20.1 0.0 slice-start.1
  20.1 0.0 collective-permute-done.6.refs_4_
  20.1 1.7 %stencil.3.refs_1_.rest_1_ = f32[3,9,64,256]{3,2,1,0:T(8,128)S(1)} custom-call(f32[112,128]{1,0:T(8,128)S(1)} %merge.2.fence_ref.refs_0_.refs_2_, f32[3,16,64,256]{3,2,1,0:T(8,128)S(1)} %get-tuple-element.15.cells.refs_3_.refs_1_, bf16[3,16,256]{2,1,0:T(8,128)(2,1)S(1)} %collective-permute-done.1.refs_2_, ...), custom_call_target="tpu_custom_call" | custom-call | flops 442368000 | bytes 3538944 | tf_op jit(solution)/shard_map/stencil/pallas_call | solution.py:486
  21.8 0.0 copy-start
  21.8 0.0 copy-start.4
  21.8 0.2 collective-permute-done.9.refs_4_
  22.1 0.5 %collective-permute-done.8.refs_3_ = f32[112,128]{1,0:T(8,128)S(1)} collective-permute-done((f32[112,128]{1,0:T(8,128)S(1)}, f32[112,128]{1,0:T(8,128)S(1)}, u32[]{:S(2)}, u32[]{:S(2)}) %collective-permute-start.8) | collective-permute-done | bytes 57376 | tf_op jit(solution)/shard_map/ppermute | solution.py:392
  22.7 1.1 %collective-permute-start.11 = (f32[176,128]{1,0:T(8,128)S(1)}, f32[176,128]{1,0:T(8,128)S(1)}, u32[]{:S(2)}, u32[]{:S(2)}) collective-permute-start(f32[176,128]{1,0:T(8,128)S(1)} %merge.3.keep_ref), channel_id=1, source_target_pairs={{0,1},{1,0},{2,3},{3,2},{4,5},{5,4},{6,7},{7,6},{8,9},{9,8},{10,11... | collective-permute-start | bytes 270344 | tf_op jit(solution)/shard_map/ppermute | solution.py:392
  23.7 0.9 %collective-permute-done.11.other_ref = f32[176,128]{1,0:T(8,128)S(1)} collective-permute-done((f32[176,128]{1,0:T(8,128)S(1)}, f32[176,128]{1,0:T(8,128)S(1)}, u32[]{:S(2)}, u32[]{:S(2)}) %collective-permute-start.11) | collective-permute-done | bytes 90144 | tf_op jit(solution)/shard_map/ppermute | solution.py:392
  24.7 3.3 %rotors.1 = (f32[3,16,64,256]{3,2,1,0:T(8,128)}, f32[4,1024]{1,0:T(4,128)}) custom-call(s32[8,128]{1,0:T(8,128)S(1)} %bitcast.8, s32[8,128]{1,0:T(8,128)S(1)} %bitcast.11, bf16[384,1024]{1,0:T(8,128)(2,1)S(1)} %copy-done, bf16[1024,4096]{1,0:T(8,128)(2,1)S(1)} %bitcast.5, f32[1,1024]{1,0:T(1,128)S(1)} %bitcast.12, ...), custom_call_target="tpu_custom_call" | custom-call | flops 1073741824 | bytes 8388608 | tf_op jit(solution)/shard_map/rotors/pallas_call | solution.py:571
  (18 shorter events, 0.1 us)
Async XLA Ops:
  2.7 5.4 %copy-start.1 = (f32[4,1024]{1,0:T(4,128)S(1)}, f32[4,1024]{1,0:T(4,128)}, u32[]{:S(2)}) copy-start(f32[4,1024]{1,0:T(4,128)} %refs_2_.1) | copy-start | bytes 49156
  4.9 7.5 %copy-start.3 = (s32[1024]{0:T(1024)S(1)}, s32[1024]{0:T(1024)}, u32[]{:S(2)}) copy-start(s32[1024]{0:T(1024)} %param.19) | copy-start | bytes 12292
  4.9 3.2 %collective-permute-start = (f32[48,128]{1,0:T(8,128)S(1)}, f32[48,128]{1,0:T(8,128)S(1)}, u32[]{:S(2)}, u32[]{:S(2)}) collective-permute-start(f32[48,128]{1,0:T(8,128)S(1)} %get-tuple-element.21), channel_id=1, source_target_pairs={{0,1},{1,0},{2,3},{3,2},{4,5},{5,4},{6,7},{7,6},{8,9},{9,8},{10,11... | collective-permute-start | bytes 73736 | tf_op jit(solution)/shard_map/ppermute | solution.py:392
  5.4 7.2 %collective-permute-start.1 = (bf16[3,16,256]{2,1,0:T(8,128)(2,1)S(1)}, bf16[3,16,256]{2,1,0:T(8,128)(2,1)S(1)}, u32[]{:S(2)}, u32[]{:S(2)}) collective-permute-start(bf16[3,16,256]{2,1,0:T(8,128)(2,1)S(1)} %get-tuple-element.24), channel_id=1, source_target_pairs={{0,1},{2,3},{1,0},{3,2},{4,5},{6,7},{5,4},{7,6},{8,9},{10,11},{9,8... | collective-permute-start | bytes 73736 | tf_op jit(solution)/shard_map/ppermute | solution.py:399
  5.5 8.7 %collective-permute-start.2 = (bf16[3,16,256]{2,1,0:T(8,128)(2,1)S(1)}, bf16[3,16,256]{2,1,0:T(8,128)(2,1)S(1)}, u32[]{:S(2)}, u32[]{:S(2)}) collective-permute-start(bf16[3,16,256]{2,1,0:T(8,128)(2,1)S(1)} %get-tuple-element.25), channel_id=1, source_target_pairs={{1,2},{3,0},{2,1},{0,3},{5,6},{7,4},{6,5},{4,7},{9,10},{11,8},{10,... | collective-permute-start | bytes 73736 | tf_op jit(solution)/shard_map/ppermute | solution.py:399
  8.2 7.3 %collective-permute-start.5 = (f32[64,128]{1,0:T(8,128)S(1)}, f32[64,128]{1,0:T(8,128)S(1)}, u32[]{:S(2)}, u32[]{:S(2)}) collective-permute-start(f32[64,128]{1,0:T(8,128)S(1)} %get-tuple-element.22.refs_0_.refs_2_), channel_id=1, source_target_pairs={{0,24},{1,25},{2,26},{3,27},{4,28},{5,29},{6,30},{7,31},{8,16},{9,... | collective-permute-start | bytes 98312 | tf_op jit(solution)/shard_map/ppermute | solution.py:392
  11.9 4.2 %collective-permute-start.4 = (f32[64,128]{1,0:T(8,128)S(1)}, f32[64,128]{1,0:T(8,128)S(1)}, u32[]{:S(2)}, u32[]{:S(2)}) collective-permute-start(f32[64,128]{1,0:T(8,128)S(1)} %get-tuple-element.22.refs_0_.refs_2_), channel_id=1, source_target_pairs={{0,17},{1,16},{2,19},{3,18},{4,21},{5,20},{6,23},{7,22},{8,25},{9,... | collective-permute-start | bytes 98312 | tf_op jit(solution)/shard_map/ppermute | solution.py:392
  11.9 4.2 %collective-permute-start.3 = (f32[64,128]{1,0:T(8,128)S(1)}, f32[64,128]{1,0:T(8,128)S(1)}, u32[]{:S(2)}, u32[]{:S(2)}) collective-permute-start(f32[64,128]{1,0:T(8,128)S(1)} %get-tuple-element.22.refs_0_.refs_2_), channel_id=1, source_target_pairs={{0,9},{1,8},{2,11},{3,10},{4,13},{5,12},{6,15},{7,14},{8,1},{9,0},... | collective-permute-start | bytes 98312 | tf_op jit(solution)/shard_map/ppermute | solution.py:392
  12.7 7.4 %collective-permute-start.6 = (bf16[3,64,256]{2,1,0:T(8,128)(2,1)S(1)}, bf16[3,64,256]{2,1,0:T(8,128)(2,1)S(1)}, u32[]{:S(2)}, u32[]{:S(2)}) collective-permute-start(bf16[3,64,256]{2,1,0:T(8,128)(2,1)S(1)} %get-tuple-element.26), channel_id=1, source_target_pairs={{0,4},{1,5},{2,6},{3,7},{4,0},{5,1},{6,2},{7,3},{8,12},{9,13},{10,... | collective-permute-start | bytes 294920 | tf_op jit(solution)/shard_map/ppermute | solution.py:407
  14.2 5.8 %collective-permute-start.7 = (bf16[3,64,256]{2,1,0:T(8,128)(2,1)S(1)}, bf16[3,64,256]{2,1,0:T(8,128)(2,1)S(1)}, u32[]{:S(2)}, u32[]{:S(2)}) collective-permute-start(bf16[3,64,256]{2,1,0:T(8,128)(2,1)S(1)} %get-tuple-element.27), channel_id=1, source_target_pairs={{0,1},{1,0},{2,3},{3,2},{4,8},{5,9},{6,10},{7,11},{8,4},{9,5},{10,... | collective-permute-start | bytes 294920 | tf_op jit(solution)/shard_map/ppermute | solution.py:407
  15.5 3.9 %copy-start.2 = (s32[1024]{0:T(1024)S(1)}, s32[1024]{0:T(1024)}, u32[]{:S(2)}) copy-start(s32[1024]{0:T(1024)} %param.18) | copy-start | bytes 12292
  16.1 8.5 %slice-start = ((s8[8388608]{0:T(1024)(128)(4,1)}), s8[4194304]{0:T(1024)(128)(4,1)S(1)}, s32[]{:S(2)}) async-start(s8[8388608]{0:T(1024)(128)(4,1)} %bitcast.4), calls=%async_computation | async-start | bytes 8388608
  16.2 5.7 %collective-permute-start.10 = (f32[48,128]{1,0:T(8,128)S(1)}, f32[48,128]{1,0:T(8,128)S(1)}, u32[]{:S(2)}, u32[]{:S(2)}) collective-permute-start(f32[48,128]{1,0:T(8,128)S(1)} %slice.4), channel_id=1, source_target_pairs={{0,6},{1,7},{2,4},{3,5},{4,2},{5,3},{6,0},{7,1},{8,14},{9,15},{10,... | collective-permute-start | bytes 73736 | tf_op jit(solution)/shard_map/ppermute | solution.py:392
  18.6 3.5 %collective-permute-start.9 = (f32[48,128]{1,0:T(8,128)S(1)}, f32[48,128]{1,0:T(8,128)S(1)}, u32[]{:S(2)}, u32[]{:S(2)}) collective-permute-start(f32[48,128]{1,0:T(8,128)S(1)} %slice.4), channel_id=1, source_target_pairs={{0,3},{1,2},{2,1},{3,0},{4,7},{5,6},{6,5},{7,4},{8,11},{9,10},{10,... | collective-permute-start | bytes 73736 | tf_op jit(solution)/shard_map/ppermute | solution.py:392
  19.0 3.6 %collective-permute-start.8 = (f32[112,128]{1,0:T(8,128)S(1)}, f32[112,128]{1,0:T(8,128)S(1)}, u32[]{:S(2)}, u32[]{:S(2)}) collective-permute-start(f32[112,128]{1,0:T(8,128)S(1)} %merge.2.fence_ref.refs_0_.refs_2_), channel_id=1, source_target_pairs={{0,5},{1,4},{2,7},{3,6},{4,1},{5,0},{6,3},{7,2},{8,13},{9,12},{10,... | collective-permute-start | bytes 172040 | tf_op jit(solution)/shard_map/ppermute | solution.py:392
  20.1 4.6 %slice-start.1 = ((s8[8388608]{0:T(1024)(128)(4,1)}), s8[4194304]{0:T(1024)(128)(4,1)S(1)}, s32[]{:S(2)}) async-start(s8[8388608]{0:T(1024)(128)(4,1)} %bitcast.4), calls=%async_computation.1 | async-start | bytes 8388608
  21.8 2.9 %copy-start = (bf16[384,1024]{1,0:T(8,128)(2,1)S(1)}, bf16[384,1024]{1,0:T(8,128)(2,1)}, u32[]{:S(2)}) copy-start(bf16[384,1024]{1,0:T(8,128)(2,1)} %w_in_ref.1) | copy-start | bytes 2359300
  21.8 2.9 %copy-start.4 = (f32[1024]{0:T(1024)S(1)}, f32[1024]{0:T(1024)}, u32[]{:S(2)}) copy-start(f32[1024]{0:T(1024)} %param.14) | copy-start | bytes 12292
  22.7 2.0 %collective-permute-start.11 = (f32[176,128]{1,0:T(8,128)S(1)}, f32[176,128]{1,0:T(8,128)S(1)}, u32[]{:S(2)}, u32[]{:S(2)}) collective-permute-start(f32[176,128]{1,0:T(8,128)S(1)} %merge.3.keep_ref), channel_id=1, source_target_pairs={{0,1},{1,0},{2,3},{3,2},{4,5},{5,4},{6,7},{7,6},{8,9},{9,8},{10,11... | collective-permute-start | bytes 270344 | tf_op jit(solution)/shard_map/ppermute | solution.py:392

commit v10 on v9

--- a/solution.py
+++ b/solution.py
@@ -620,7 +620,7 @@
     y_odd = swap_pairs(y_odd, "cross", (slabs, crosses), 1)
     pooled_rows = keep.shape[0]
 
-    middle = size_x // 2
+    middle = size_x * 3 // 16
     inner, outer = tuple(range(1, middle)), (0,) + tuple(range(middle, size_x))
     runs = ((1, middle - 1, 0, 0), (0, 1, 1, 0), (middle, size_x - middle, 1, 1))
     packed, x_even, x_odd = join(

time: 28.1 us -> 27.6 us (0.982)
  starting transfers between devices: 13.3 us -> 12.3 us
  waiting for transfers between devices: 2.3 us -> 2.71 us
    ppermute x8, starting transfers between devices: 9.04 us -> 8.13 us  [swap(): return lax.ppermute(value, axis, [(i, i ^ offset) for i in range(count)])]
    ppermute x8, waiting for transfers between devices: 2.29 us -> 2.7 us  [swap(): return lax.ppermute(value, axis, [(i, i ^ offset) for i in range(count)])]
  transfers between devices with their start and end apart: 12 -> 12, of which waited for: 4 -> 2; matrix products, arithmetic and copies ran while one was open for 0% -> 0% of each run, Pallas kernels for 14% -> 14%
where the time goes in v10:
time: 27.6 us; the launch traced here: 27.4 us
  starting transfers between devices  12.3 us (45%)
  Pallas kernels  11.5 us (42%)
  waiting for transfers between devices  2.71 us (10%)
  between operations  0.81 us (3%)
    ppermute x8, starting transfers between devices, swap(): return lax.ppermute(value, axis, [(i, i ^ offset) for i in range(count)])  8.13 us
    pallas_call x1, Pallas kernels, rotors_step(): pl.pallas_call(functools.partial(rotor_kernel, bits, runs), out_shape=(ja...  3.29 us
    pallas_call x2, Pallas kernels, stencil(): pl.pallas_call(functools.partial(stencil_kernel, planes, edges, len(fence...  2.97 us
    ppermute x2, starting transfers between devices, swap_pairs(): return lax.ppermute(value, axis, pairs + [(j, i) for i, j in pairs])  2.71 us
    ppermute x8, waiting for transfers between devices, swap(): return lax.ppermute(value, axis, [(i, i ^ offset) for i in range(count)])  2.7 us
    pallas_call x1, Pallas kernels, pool(): pl.pallas_call(functools.partial(pool_kernel, bits), out_shape=(part, par...  2.15 us
    pallas_call x1, Pallas kernels, load(): pl.pallas_call(load_kernel, out_shape=(jax.ShapeDtypeStruct((groups, TILE...  2.11 us
    ppermute x2, starting transfers between devices, swap_pairs(): return lax.ppermute(value, BOTH, pairs)  1.5 us
  transfers between devices with their start and end apart: 12, of which 2 were waited for; matrix products, arithmetic and copies ran while one was open for 0% of the time, Pallas kernels for 14%

profile of v10, /device:TPU:0, one launch (start us, length us, event | category | flops | bytes accessed | tf_op | source)
XLA Modules:
  0.0 27.4 jit_solution(14173596644036564724)
XLA Ops:
  0.6 2.1 %load.1 = (s32[8,128]{1,0:T(8,128)S(1)}, f32[3,16,64,256]{3,2,1,0:T(8,128)S(1)}, bf16[1024,1024]{1,0:T(8,128)(2,1)S(1)}, f32[1024,384]{1,0:T(8,128)S(1)}, s32[10...) custom-call(s32[8,128]{1,0:T(8,128)} %bitcast.6, s32[8,128]{1,0:T(8,128)} %bitcast.13, s32[8,128]{1,0:T(8,128)} %bitcast.9, ...), custom_call_target="tpu_custom_call" | custom-call | flops 536870912 | bytes 3145728 | tf_op jit(solution)/shard_map/load/pallas_call | solution.py:429
  2.7 0.0 copy-start.1
  2.8 2.2 %pool.1 = (f32[48,128]{1,0:T(8,128)S(1)}, f32[48,128]{1,0:T(8,128)S(1)}, bf16[3,16,256]{2,1,0:T(8,128)(2,1)S(1)}, bf16[3,16,256]{2,1,0:T(8,128)(2,1)S(1)}) custom-call(f32[3,16,64,256]{3,2,1,0:T(8,128)S(1)} %get-tuple-element.15.cells.refs_3_.refs_1_, bf16[1024,1024]{1,0:T(8,128)(2,1)S(1)} %get-tuple-element.16.place_hot, ...), custom_call_target="tpu_custom_call" | custom-call | flops 1610612736 | bytes 3145728 | tf_op jit(solution)/shard_map/pool/pallas_call | solution.py:464
  4.9 0.5 %collective-permute-start = (f32[48,128]{1,0:T(8,128)S(1)}, f32[48,128]{1,0:T(8,128)S(1)}, u32[]{:S(2)}, u32[]{:S(2)}) collective-permute-start(f32[48,128]{1,0:T(8,128)S(1)} %get-tuple-element.21), channel_id=1, source_target_pairs={{0,1},{1,0},{2,3},{3,2},{4,5},{5,4},{6,7},{7,6},{8,9},{9,8},{10,11... | collective-permute-start | bytes 73736 | tf_op jit(solution)/shard_map/ppermute | solution.py:392
  5.4 0.1 collective-permute-start.1
  5.5 2.6 %collective-permute-start.2 = (bf16[3,16,256]{2,1,0:T(8,128)(2,1)S(1)}, bf16[3,16,256]{2,1,0:T(8,128)(2,1)S(1)}, u32[]{:S(2)}, u32[]{:S(2)}) collective-permute-start(bf16[3,16,256]{2,1,0:T(8,128)(2,1)S(1)} %get-tuple-element.25), channel_id=1, source_target_pairs={{1,2},{3,0},{2,1},{0,3},{5,6},{7,4},{6,5},{4,7},{9,10},{11,8},{10,... | collective-permute-start | bytes 73736 | tf_op jit(solution)/shard_map/ppermute | solution.py:399
  8.1 0.0 collective-permute-done.refs_1_
  8.1 3.7 %collective-permute-start.5 = (f32[64,128]{1,0:T(8,128)S(1)}, f32[64,128]{1,0:T(8,128)S(1)}, u32[]{:S(2)}, u32[]{:S(2)}) collective-permute-start(f32[64,128]{1,0:T(8,128)S(1)} %get-tuple-element.22.refs_0_.refs_2_), channel_id=1, source_target_pairs={{0,24},{1,25},{2,26},{3,27},{4,28},{5,29},{6,30},{7,31},{8,16},{9,... | collective-permute-start | bytes 98312 | tf_op jit(solution)/shard_map/ppermute | solution.py:392
  11.8 0.0 collective-permute-start.4
  11.8 0.5 %collective-permute-start.3 = (f32[64,128]{1,0:T(8,128)S(1)}, f32[64,128]{1,0:T(8,128)S(1)}, u32[]{:S(2)}, u32[]{:S(2)}) collective-permute-start(f32[64,128]{1,0:T(8,128)S(1)} %get-tuple-element.22.refs_0_.refs_2_), channel_id=1, source_target_pairs={{0,9},{1,8},{2,11},{3,10},{4,13},{5,12},{6,15},{7,14},{8,1},{9,0},... | collective-permute-start | bytes 98312 | tf_op jit(solution)/shard_map/ppermute | solution.py:392
  12.3 0.0 collective-permute-done.1.refs_2_
  12.3 1.5 %collective-permute-start.6 = (bf16[3,64,256]{2,1,0:T(8,128)(2,1)S(1)}, bf16[3,64,256]{2,1,0:T(8,128)(2,1)S(1)}, u32[]{:S(2)}, u32[]{:S(2)}) collective-permute-start(bf16[3,64,256]{2,1,0:T(8,128)(2,1)S(1)} %get-tuple-element.26), channel_id=1, source_target_pairs={{0,4},{1,5},{2,6},{3,7},{4,0},{5,1},{6,2},{7,3},{8,12},{9,13},{10,... | collective-permute-start | bytes 294920 | tf_op jit(solution)/shard_map/ppermute | solution.py:407
  13.8 0.0 collective-permute-done.2.refs_3_
  13.8 0.0 collective-permute-start.7
  13.8 0.4 %stencil.2.refs_1_.rest_0_ = f32[3,2,64,256]{3,2,1,0:T(8,128)S(1)} custom-call(f32[64,128]{1,0:T(8,128)S(1)} %get-tuple-element.22.refs_0_.refs_2_, f32[3,16,64,256]{3,2,1,0:T(8,128)S(1)} %get-tuple-element.15.cells.refs_3_.refs_1_, bf16[3,16,256]{2,1,0:T(8,128)(2,1)S(1)} %collective-permute-done.1.refs_2_, ...), custom_call_target="tpu_custom_call" | custom-call | flops 98304000 | bytes 786432 | tf_op jit(solution)/shard_map/stencil/pallas_call | solution.py:486
  14.2 0.3 %keys.1.refs_0_.key_hot = bf16[1024,512]{1,0:T(8,128)(2,1)S(1)} custom-call(f32[64,128]{1,0:T(8,128)S(1)} %get-tuple-element.22.refs_0_.refs_2_, s32[8,128]{1,0:T(8,128)S(1)} %get-tuple-element.23.refs_1_, s32[8,128]{1,0:T(8,128)S(1)} %bitcast.10), custom_call_target="tpu_custom_call" | custom-call | flops 524288000 | bytes 1048576 | tf_op jit(solution)/shard_map/keys/pallas_call | solution.py:503
  14.5 0.0 collective-permute-done.5.refs_5_
  14.5 1.5 %collective-permute-done.4.refs_4_ = f32[64,128]{1,0:T(8,128)S(1)} collective-permute-done((f32[64,128]{1,0:T(8,128)S(1)}, f32[64,128]{1,0:T(8,128)S(1)}, u32[]{:S(2)}, u32[]{:S(2)}) %collective-permute-start.4) | collective-permute-done | bytes 32800 | tf_op jit(solution)/shard_map/ppermute | solution.py:392
  16.1 0.0 collective-permute-done.3.refs_3_
  16.1 2.3 %collective-permute-start.10 = (f32[48,128]{1,0:T(8,128)S(1)}, f32[48,128]{1,0:T(8,128)S(1)}, u32[]{:S(2)}, u32[]{:S(2)}) collective-permute-start(f32[48,128]{1,0:T(8,128)S(1)} %slice.4), channel_id=1, source_target_pairs={{0,6},{1,7},{2,4},{3,5},{4,2},{5,3},{6,0},{7,1},{8,14},{9,15},{10,... | collective-permute-start | bytes 73736 | tf_op jit(solution)/shard_map/ppermute | solution.py:392
  18.4 0.2 collective-permute-start.9
  18.6 0.8 %collective-permute-start.8 = (f32[112,128]{1,0:T(8,128)S(1)}, f32[112,128]{1,0:T(8,128)S(1)}, u32[]{:S(2)}, u32[]{:S(2)}) collective-permute-start(f32[112,128]{1,0:T(8,128)S(1)} %merge.2.fence_ref.refs_0_.refs_2_), channel_id=1, source_target_pairs={{0,5},{1,4},{2,7},{3,6},{4,1},{5,0},{6,3},{7,2},{8,13},{9,12},{10,... | collective-permute-start | bytes 172040 | tf_op jit(solution)/shard_map/ppermute | solution.py:392
  19.4 0.6 %places.1.refs_0_.place_hot = bf16[1024,1024]{1,0:T(8,128)(2,1)S(1)} custom-call(f32[112,128]{1,0:T(8,128)S(1)} %merge.2.fence_ref.refs_0_.refs_2_, s32[8,128]{1,0:T(8,128)S(1)} %bitcast.7), custom_call_target="tpu_custom_call" | custom-call | flops 1048576000 | bytes 2097152 | tf_op jit(solution)/shard_map/places/pallas_call | solution.py:518
  20.0 0.0 slice-start.1
  20.0 0.0 collective-permute-done.6.refs_4_
  20.0 2.6 %stencil.3.refs_1_.rest_1_ = f32[3,14,64,256]{3,2,1,0:T(8,128)S(1)} custom-call(f32[112,128]{1,0:T(8,128)S(1)} %merge.2.fence_ref.refs_0_.refs_2_, f32[3,16,64,256]{3,2,1,0:T(8,128)S(1)} %get-tuple-element.15.cells.refs_3_.refs_1_, bf16[3,16,256]{2,1,0:T(8,128)(2,1)S(1)} %collective-permute-done.1.refs_2_, ...), custom_call_target="tpu_custom_call" | custom-call | flops 688128000 | bytes 5505024 | tf_op jit(solution)/shard_map/stencil/pallas_call | solution.py:486
  22.6 0.0 copy-start
  22.7 0.0 copy-start.4
  22.7 0.0 collective-permute-done.10.refs_5_
  22.7 0.2 collective-permute-start.11
  22.9 1.2 %collective-permute-done.11.other_ref = f32[176,128]{1,0:T(8,128)S(1)} collective-permute-done((f32[176,128]{1,0:T(8,128)S(1)}, f32[176,128]{1,0:T(8,128)S(1)}, u32[]{:S(2)}, u32[]{:S(2)}) %collective-permute-start.11) | collective-permute-done | bytes 90144 | tf_op jit(solution)/shard_map/ppermute | solution.py:392
  24.1 3.3 %rotors.1 = (f32[3,16,64,256]{3,2,1,0:T(8,128)}, f32[4,1024]{1,0:T(4,128)}) custom-call(s32[8,128]{1,0:T(8,128)S(1)} %bitcast.8, s32[8,128]{1,0:T(8,128)S(1)} %bitcast.11, bf16[384,1024]{1,0:T(8,128)(2,1)S(1)} %copy-done, bf16[1024,4096]{1,0:T(8,128)(2,1)S(1)} %bitcast.5, f32[1,1024]{1,0:T(1,128)S(1)} %bitcast.12, ...), custom_call_target="tpu_custom_call" | custom-call | flops 1073741824 | bytes 8388608 | tf_op jit(solution)/shard_map/rotors/pallas_call | solution.py:571
  (18 shorter events, 0.1 us)
Async XLA Ops:
  2.7 5.4 %copy-start.1 = (f32[4,1024]{1,0:T(4,128)S(1)}, f32[4,1024]{1,0:T(4,128)}, u32[]{:S(2)}) copy-start(f32[4,1024]{1,0:T(4,128)} %refs_2_.1) | copy-start | bytes 49156
  4.9 3.2 %collective-permute-start = (f32[48,128]{1,0:T(8,128)S(1)}, f32[48,128]{1,0:T(8,128)S(1)}, u32[]{:S(2)}, u32[]{:S(2)}) collective-permute-start(f32[48,128]{1,0:T(8,128)S(1)} %get-tuple-element.21), channel_id=1, source_target_pairs={{0,1},{1,0},{2,3},{3,2},{4,5},{5,4},{6,7},{7,6},{8,9},{9,8},{10,11... | collective-permute-start | bytes 73736 | tf_op jit(solution)/shard_map/ppermute | solution.py:392
  5.4 6.9 %collective-permute-start.1 = (bf16[3,16,256]{2,1,0:T(8,128)(2,1)S(1)}, bf16[3,16,256]{2,1,0:T(8,128)(2,1)S(1)}, u32[]{:S(2)}, u32[]{:S(2)}) collective-permute-start(bf16[3,16,256]{2,1,0:T(8,128)(2,1)S(1)} %get-tuple-element.24), channel_id=1, source_target_pairs={{0,1},{2,3},{1,0},{3,2},{4,5},{6,7},{5,4},{7,6},{8,9},{10,11},{9,8... | collective-permute-start | bytes 73736 | tf_op jit(solution)/shard_map/ppermute | solution.py:399
  5.5 8.4 %collective-permute-start.2 = (bf16[3,16,256]{2,1,0:T(8,128)(2,1)S(1)}, bf16[3,16,256]{2,1,0:T(8,128)(2,1)S(1)}, u32[]{:S(2)}, u32[]{:S(2)}) collective-permute-start(bf16[3,16,256]{2,1,0:T(8,128)(2,1)S(1)} %get-tuple-element.25), channel_id=1, source_target_pairs={{1,2},{3,0},{2,1},{0,3},{5,6},{7,4},{6,5},{4,7},{9,10},{11,8},{10,... | collective-permute-start | bytes 73736 | tf_op jit(solution)/shard_map/ppermute | solution.py:399
  8.1 6.1 %copy-start.3 = (s32[1024]{0:T(1024)S(1)}, s32[1024]{0:T(1024)}, u32[]{:S(2)}) copy-start(s32[1024]{0:T(1024)} %param.19) | copy-start | bytes 12292
  8.1 6.4 %collective-permute-start.5 = (f32[64,128]{1,0:T(8,128)S(1)}, f32[64,128]{1,0:T(8,128)S(1)}, u32[]{:S(2)}, u32[]{:S(2)}) collective-permute-start(f32[64,128]{1,0:T(8,128)S(1)} %get-tuple-element.22.refs_0_.refs_2_), channel_id=1, source_target_pairs={{0,24},{1,25},{2,26},{3,27},{4,28},{5,29},{6,30},{7,31},{8,16},{9,... | collective-permute-start | bytes 98312 | tf_op jit(solution)/shard_map/ppermute | solution.py:392
  11.8 4.2 %collective-permute-start.4 = (f32[64,128]{1,0:T(8,128)S(1)}, f32[64,128]{1,0:T(8,128)S(1)}, u32[]{:S(2)}, u32[]{:S(2)}) collective-permute-start(f32[64,128]{1,0:T(8,128)S(1)} %get-tuple-element.22.refs_0_.refs_2_), channel_id=1, source_target_pairs={{0,17},{1,16},{2,19},{3,18},{4,21},{5,20},{6,23},{7,22},{8,25},{9,... | collective-permute-start | bytes 98312 | tf_op jit(solution)/shard_map/ppermute | solution.py:392
  11.8 4.2 %collective-permute-start.3 = (f32[64,128]{1,0:T(8,128)S(1)}, f32[64,128]{1,0:T(8,128)S(1)}, u32[]{:S(2)}, u32[]{:S(2)}) collective-permute-start(f32[64,128]{1,0:T(8,128)S(1)} %get-tuple-element.22.refs_0_.refs_2_), channel_id=1, source_target_pairs={{0,9},{1,8},{2,11},{3,10},{4,13},{5,12},{6,15},{7,14},{8,1},{9,0},... | collective-permute-start | bytes 98312 | tf_op jit(solution)/shard_map/ppermute | solution.py:392
  12.3 7.7 %collective-permute-start.6 = (bf16[3,64,256]{2,1,0:T(8,128)(2,1)S(1)}, bf16[3,64,256]{2,1,0:T(8,128)(2,1)S(1)}, u32[]{:S(2)}, u32[]{:S(2)}) collective-permute-start(bf16[3,64,256]{2,1,0:T(8,128)(2,1)S(1)} %get-tuple-element.26), channel_id=1, source_target_pairs={{0,4},{1,5},{2,6},{3,7},{4,0},{5,1},{6,2},{7,3},{8,12},{9,13},{10,... | collective-permute-start | bytes 294920 | tf_op jit(solution)/shard_map/ppermute | solution.py:407
  13.8 5.6 %copy-start.2 = (s32[1024]{0:T(1024)S(1)}, s32[1024]{0:T(1024)}, u32[]{:S(2)}) copy-start(s32[1024]{0:T(1024)} %param.18) | copy-start | bytes 12292
  13.8 6.2 %collective-permute-start.7 = (bf16[3,64,256]{2,1,0:T(8,128)(2,1)S(1)}, bf16[3,64,256]{2,1,0:T(8,128)(2,1)S(1)}, u32[]{:S(2)}, u32[]{:S(2)}) collective-permute-start(bf16[3,64,256]{2,1,0:T(8,128)(2,1)S(1)} %get-tuple-element.27), channel_id=1, source_target_pairs={{0,1},{1,0},{2,3},{3,2},{4,8},{5,9},{6,10},{7,11},{8,4},{9,5},{10,... | collective-permute-start | bytes 294920 | tf_op jit(solution)/shard_map/ppermute | solution.py:407
  16.1 6.6 %collective-permute-start.10 = (f32[48,128]{1,0:T(8,128)S(1)}, f32[48,128]{1,0:T(8,128)S(1)}, u32[]{:S(2)}, u32[]{:S(2)}) collective-permute-start(f32[48,128]{1,0:T(8,128)S(1)} %slice.4), channel_id=1, source_target_pairs={{0,6},{1,7},{2,4},{3,5},{4,2},{5,3},{6,0},{7,1},{8,14},{9,15},{10,... | collective-permute-start | bytes 73736 | tf_op jit(solution)/shard_map/ppermute | solution.py:392
  18.4 4.3 %collective-permute-start.9 = (f32[48,128]{1,0:T(8,128)S(1)}, f32[48,128]{1,0:T(8,128)S(1)}, u32[]{:S(2)}, u32[]{:S(2)}) collective-permute-start(f32[48,128]{1,0:T(8,128)S(1)} %slice.4), channel_id=1, source_target_pairs={{0,3},{1,2},{2,1},{3,0},{4,7},{5,6},{6,5},{7,4},{8,11},{9,10},{10,... | collective-permute-start | bytes 73736 | tf_op jit(solution)/shard_map/ppermute | solution.py:392
  18.6 4.1 %collective-permute-start.8 = (f32[112,128]{1,0:T(8,128)S(1)}, f32[112,128]{1,0:T(8,128)S(1)}, u32[]{:S(2)}, u32[]{:S(2)}) collective-permute-start(f32[112,128]{1,0:T(8,128)S(1)} %merge.2.fence_ref.refs_0_.refs_2_), channel_id=1, source_target_pairs={{0,5},{1,4},{2,7},{3,6},{4,1},{5,0},{6,3},{7,2},{8,13},{9,12},{10,... | collective-permute-start | bytes 172040 | tf_op jit(solution)/shard_map/ppermute | solution.py:392
  19.4 4.7 %slice-start = ((s8[8388608]{0:T(1024)(128)(4,1)}), s8[4194304]{0:T(1024)(128)(4,1)S(1)}, s32[]{:S(2)}) async-start(s8[8388608]{0:T(1024)(128)(4,1)} %bitcast.4), calls=%async_computation | async-start | bytes 8388608
  20.0 4.1 %slice-start.1 = ((s8[8388608]{0:T(1024)(128)(4,1)}), s8[4194304]{0:T(1024)(128)(4,1)S(1)}, s32[]{:S(2)}) async-start(s8[8388608]{0:T(1024)(128)(4,1)} %bitcast.4), calls=%async_computation.1 | async-start | bytes 8388608
  22.6 1.5 %copy-start = (bf16[384,1024]{1,0:T(8,128)(2,1)S(1)}, bf16[384,1024]{1,0:T(8,128)(2,1)}, u32[]{:S(2)}) copy-start(bf16[384,1024]{1,0:T(8,128)(2,1)} %w_in_ref.1) | copy-start | bytes 2359300
  22.7 1.4 %copy-start.4 = (f32[1024]{0:T(1024)S(1)}, f32[1024]{0:T(1024)}, u32[]{:S(2)}) copy-start(f32[1024]{0:T(1024)} %param.14) | copy-start | bytes 12292
  22.7 1.4 %collective-permute-start.11 = (f32[176,128]{1,0:T(8,128)S(1)}, f32[176,128]{1,0:T(8,128)S(1)}, u32[]{:S(2)}, u32[]{:S(2)}) collective-permute-start(f32[176,128]{1,0:T(8,128)S(1)} %merge.3.keep_ref), channel_id=1, source_target_pairs={{0,1},{1,0},{2,3},{3,2},{4,5},{5,4},{6,7},{7,6},{8,9},{9,8},{10,11... | collective-permute-start | bytes 270344 | tf_op jit(solution)/shard_map/ppermute | solution.py:392

commit v11 on v10

--- a/solution.py
+++ b/solution.py
@@ -253,10 +253,16 @@
 def place_kernel(halves, fence_ref, tile_ref, place_ref):
     del fence_ref
     places = tile_ref[...] // halves
+    low, high = (places % TILE).astype(F32), (places // TILE).astype(F32)
+    rows = sublanes(TILE).astype(F32).astype(BF16)
+    zeros = jnp.zeros((TILE, TILE), BF16)
     for group in range(places.shape[0]):
+        row = jnp.broadcast_to(low[group : group + 1, :], (TILE, TILE)).astype(BF16)
+        part = jnp.broadcast_to(high[group : group + 1, :], (TILE, TILE)).astype(BF16)
+        found = jnp.where(row == rows, jnp.ones((TILE, TILE), BF16), zeros)
         for block in range(place_ref.shape[0] // TILE):
-            place_ref[pl.ds(block * TILE, TILE), pl.ds(group * TILE, TILE)] = hot(
-                places[group : group + 1, :] == sublanes(TILE) + block * TILE
+            place_ref[pl.ds(block * TILE, TILE), pl.ds(group * TILE, TILE)] = jnp.where(
+                part == jnp.asarray(block, BF16), found, zeros
             )
 
 
@@ -620,7 +626,7 @@
     y_odd = swap_pairs(y_odd, "cross", (slabs, crosses), 1)
     pooled_rows = keep.shape[0]
 
-    middle = size_x * 3 // 16
+    middle = size_x // 4
     inner, outer = tuple(range(1, middle)), (0,) + tuple(range(middle, size_x))
     runs = ((1, middle - 1, 0, 0), (0, 1, 1, 0), (middle, size_x - middle, 1, 1))
     packed, x_even, x_odd = join(

time: 27.6 us -> 27.4 us (level)
  waiting for transfers between devices: 2.71 us -> 2.32 us
  starting transfers between devices: 12.3 us -> 12.6 us
    ppermute x8, waiting for transfers between devices: 2.7 us -> 2.31 us  [swap(): return lax.ppermute(value, axis, [(i, i ^ offset) for i in range(count)])]
where the time goes in v11:
time: 27.4 us; the launch traced here: 27.2 us
  starting transfers between devices  12.6 us (46%)
  Pallas kernels  11.4 us (42%)
  waiting for transfers between devices  2.32 us (8%)
  between operations  0.8 us (3%)
    ppermute x8, starting transfers between devices, swap(): return lax.ppermute(value, axis, [(i, i ^ offset) for i in range(count)])  8.39 us
    pallas_call x1, Pallas kernels, rotors_step(): pl.pallas_call(functools.partial(rotor_kernel, bits, runs), out_shape=(ja...  3.28 us
    pallas_call x2, Pallas kernels, stencil(): pl.pallas_call(functools.partial(stencil_kernel, planes, edges, len(fence...  2.97 us
    ppermute x2, starting transfers between devices, swap_pairs(): return lax.ppermute(value, axis, pairs + [(j, i) for i, j in pairs])  2.71 us
    ppermute x8, waiting for transfers between devices, swap(): return lax.ppermute(value, axis, [(i, i ^ offset) for i in range(count)])  2.31 us
    pallas_call x1, Pallas kernels, pool(): pl.pallas_call(functools.partial(pool_kernel, bits), out_shape=(part, par...  2.15 us
    pallas_call x1, Pallas kernels, load(): pl.pallas_call(load_kernel, out_shape=(jax.ShapeDtypeStruct((groups, TILE...  2.11 us
    ppermute x2, starting transfers between devices, swap_pairs(): return lax.ppermute(value, BOTH, pairs)  1.5 us
  transfers between devices with their start and end apart: 12, of which 2 were waited for; matrix products, arithmetic and copies ran while one was open for 0% of the time, Pallas kernels for 14%

profile of v11, /device:TPU:0, one launch (start us, length us, event | category | flops | bytes accessed | tf_op | source)
XLA Modules:
  0.0 27.2 jit_solution(1247579411031370076)
XLA Ops:
  0.6 2.1 %load.1 = (s32[8,128]{1,0:T(8,128)S(1)}, f32[3,16,64,256]{3,2,1,0:T(8,128)S(1)}, bf16[1024,1024]{1,0:T(8,128)(2,1)S(1)}, f32[1024,384]{1,0:T(8,128)S(1)}, s32[10...) custom-call(s32[8,128]{1,0:T(8,128)} %bitcast.6, s32[8,128]{1,0:T(8,128)} %bitcast.13, s32[8,128]{1,0:T(8,128)} %bitcast.9, ...), custom_call_target="tpu_custom_call" | custom-call | flops 536870912 | bytes 3145728 | tf_op jit(solution)/shard_map/load/pallas_call | solution.py:435
  2.7 0.0 copy-start.1
  2.8 2.2 %pool.1 = (f32[48,128]{1,0:T(8,128)S(1)}, f32[48,128]{1,0:T(8,128)S(1)}, bf16[3,16,256]{2,1,0:T(8,128)(2,1)S(1)}, bf16[3,16,256]{2,1,0:T(8,128)(2,1)S(1)}) custom-call(f32[3,16,64,256]{3,2,1,0:T(8,128)S(1)} %get-tuple-element.15.cells.refs_3_.refs_1_, bf16[1024,1024]{1,0:T(8,128)(2,1)S(1)} %get-tuple-element.16.place_hot, ...), custom_call_target="tpu_custom_call" | custom-call | flops 1610612736 | bytes 3145728 | tf_op jit(solution)/shard_map/pool/pallas_call | solution.py:470
  4.9 0.5 %collective-permute-start = (f32[48,128]{1,0:T(8,128)S(1)}, f32[48,128]{1,0:T(8,128)S(1)}, u32[]{:S(2)}, u32[]{:S(2)}) collective-permute-start(f32[48,128]{1,0:T(8,128)S(1)} %get-tuple-element.21), channel_id=1, source_target_pairs={{0,1},{1,0},{2,3},{3,2},{4,5},{5,4},{6,7},{7,6},{8,9},{9,8},{10,11... | collective-permute-start | bytes 73736 | tf_op jit(solution)/shard_map/ppermute | solution.py:398
  5.4 0.1 collective-permute-start.1
  5.5 2.6 %collective-permute-start.2 = (bf16[3,16,256]{2,1,0:T(8,128)(2,1)S(1)}, bf16[3,16,256]{2,1,0:T(8,128)(2,1)S(1)}, u32[]{:S(2)}, u32[]{:S(2)}) collective-permute-start(bf16[3,16,256]{2,1,0:T(8,128)(2,1)S(1)} %get-tuple-element.25), channel_id=1, source_target_pairs={{1,2},{3,0},{2,1},{0,3},{5,6},{7,4},{6,5},{4,7},{9,10},{11,8},{10,... | collective-permute-start | bytes 73736 | tf_op jit(solution)/shard_map/ppermute | solution.py:405
  8.1 0.0 collective-permute-done.refs_1_
  8.1 3.7 %collective-permute-start.5 = (f32[64,128]{1,0:T(8,128)S(1)}, f32[64,128]{1,0:T(8,128)S(1)}, u32[]{:S(2)}, u32[]{:S(2)}) collective-permute-start(f32[64,128]{1,0:T(8,128)S(1)} %get-tuple-element.22.refs_0_.refs_2_), channel_id=1, source_target_pairs={{0,24},{1,25},{2,26},{3,27},{4,28},{5,29},{6,30},{7,31},{8,16},{9,... | collective-permute-start | bytes 98312 | tf_op jit(solution)/shard_map/ppermute | solution.py:398
  11.8 0.0 collective-permute-start.4
  11.8 0.5 %collective-permute-start.3 = (f32[64,128]{1,0:T(8,128)S(1)}, f32[64,128]{1,0:T(8,128)S(1)}, u32[]{:S(2)}, u32[]{:S(2)}) collective-permute-start(f32[64,128]{1,0:T(8,128)S(1)} %get-tuple-element.22.refs_0_.refs_2_), channel_id=1, source_target_pairs={{0,9},{1,8},{2,11},{3,10},{4,13},{5,12},{6,15},{7,14},{8,1},{9,0},... | collective-permute-start | bytes 98312 | tf_op jit(solution)/shard_map/ppermute | solution.py:398
  12.3 0.0 collective-permute-done.1.refs_2_
  12.3 1.5 %collective-permute-start.6 = (bf16[3,64,256]{2,1,0:T(8,128)(2,1)S(1)}, bf16[3,64,256]{2,1,0:T(8,128)(2,1)S(1)}, u32[]{:S(2)}, u32[]{:S(2)}) collective-permute-start(bf16[3,64,256]{2,1,0:T(8,128)(2,1)S(1)} %get-tuple-element.26), channel_id=1, source_target_pairs={{0,4},{1,5},{2,6},{3,7},{4,0},{5,1},{6,2},{7,3},{8,12},{9,13},{10,... | collective-permute-start | bytes 294920 | tf_op jit(solution)/shard_map/ppermute | solution.py:413
  13.8 0.0 collective-permute-done.2.refs_3_
  13.8 0.0 collective-permute-start.7
  13.8 0.6 %stencil.2.refs_1_.rest_0_ = f32[3,3,64,256]{3,2,1,0:T(8,128)S(1)} custom-call(f32[64,128]{1,0:T(8,128)S(1)} %get-tuple-element.22.refs_0_.refs_2_, f32[3,16,64,256]{3,2,1,0:T(8,128)S(1)} %get-tuple-element.15.cells.refs_3_.refs_1_, bf16[3,16,256]{2,1,0:T(8,128)(2,1)S(1)} %collective-permute-done.1.refs_2_, ...), custom_call_target="tpu_custom_call" | custom-call | flops 147456000 | bytes 1179648 | tf_op jit(solution)/shard_map/stencil/pallas_call | solution.py:492
  14.4 0.3 %keys.1.refs_0_.key_hot = bf16[1024,512]{1,0:T(8,128)(2,1)S(1)} custom-call(f32[64,128]{1,0:T(8,128)S(1)} %get-tuple-element.22.refs_0_.refs_2_, s32[8,128]{1,0:T(8,128)S(1)} %get-tuple-element.23.refs_1_, s32[8,128]{1,0:T(8,128)S(1)} %bitcast.10), custom_call_target="tpu_custom_call" | custom-call | flops 524288000 | bytes 1048576 | tf_op jit(solution)/shard_map/keys/pallas_call | solution.py:509
  14.7 0.0 collective-permute-done.5.refs_5_
  14.7 1.4 %collective-permute-done.4.refs_4_ = f32[64,128]{1,0:T(8,128)S(1)} collective-permute-done((f32[64,128]{1,0:T(8,128)S(1)}, f32[64,128]{1,0:T(8,128)S(1)}, u32[]{:S(2)}, u32[]{:S(2)}) %collective-permute-start.4) | collective-permute-done | bytes 32800 | tf_op jit(solution)/shard_map/ppermute | solution.py:398
  16.1 0.0 collective-permute-done.3.refs_3_
  16.1 2.3 %collective-permute-start.10 = (f32[48,128]{1,0:T(8,128)S(1)}, f32[48,128]{1,0:T(8,128)S(1)}, u32[]{:S(2)}, u32[]{:S(2)}) collective-permute-start(f32[48,128]{1,0:T(8,128)S(1)} %slice.4), channel_id=1, source_target_pairs={{0,6},{1,7},{2,4},{3,5},{4,2},{5,3},{6,0},{7,1},{8,14},{9,15},{10,... | collective-permute-start | bytes 73736 | tf_op jit(solution)/shard_map/ppermute | solution.py:398
  18.4 0.2 collective-permute-start.9
  18.6 0.8 %collective-permute-start.8 = (f32[112,128]{1,0:T(8,128)S(1)}, f32[112,128]{1,0:T(8,128)S(1)}, u32[]{:S(2)}, u32[]{:S(2)}) collective-permute-start(f32[112,128]{1,0:T(8,128)S(1)} %merge.2.fence_ref.refs_0_.refs_2_), channel_id=1, source_target_pairs={{0,5},{1,4},{2,7},{3,6},{4,1},{5,0},{6,3},{7,2},{8,13},{9,12},{10,... | collective-permute-start | bytes 172040 | tf_op jit(solution)/shard_map/ppermute | solution.py:398
  19.4 0.5 %places.1.refs_0_.place_hot = bf16[1024,1024]{1,0:T(8,128)(2,1)S(1)} custom-call(f32[112,128]{1,0:T(8,128)S(1)} %merge.2.fence_ref.refs_0_.refs_2_, s32[8,128]{1,0:T(8,128)S(1)} %bitcast.7), custom_call_target="tpu_custom_call" | custom-call | flops 1048576000 | bytes 2097152 | tf_op jit(solution)/shard_map/places/pallas_call | solution.py:524
  19.9 0.0 slice-start.1
  19.9 0.0 collective-permute-done.6.refs_4_
  20.0 2.4 %stencil.3.refs_1_.rest_1_ = f32[3,13,64,256]{3,2,1,0:T(8,128)S(1)} custom-call(f32[112,128]{1,0:T(8,128)S(1)} %merge.2.fence_ref.refs_0_.refs_2_, f32[3,16,64,256]{3,2,1,0:T(8,128)S(1)} %get-tuple-element.15.cells.refs_3_.refs_1_, bf16[3,16,256]{2,1,0:T(8,128)(2,1)S(1)} %collective-permute-done.1.refs_2_, ...), custom_call_target="tpu_custom_call" | custom-call | flops 638976000 | bytes 5111808 | tf_op jit(solution)/shard_map/stencil/pallas_call | solution.py:492
  22.4 0.0 copy-start
  22.4 0.0 copy-start.4
  22.4 0.0 collective-permute-done.8.refs_3_
  22.5 0.5 %collective-permute-start.11 = (f32[176,128]{1,0:T(8,128)S(1)}, f32[176,128]{1,0:T(8,128)S(1)}, u32[]{:S(2)}, u32[]{:S(2)}) collective-permute-start(f32[176,128]{1,0:T(8,128)S(1)} %merge.3.keep_ref), channel_id=1, source_target_pairs={{0,1},{1,0},{2,3},{3,2},{4,5},{5,4},{6,7},{7,6},{8,9},{9,8},{10,11... | collective-permute-start | bytes 270344 | tf_op jit(solution)/shard_map/ppermute | solution.py:398
  22.9 0.9 %collective-permute-done.11.other_ref = f32[176,128]{1,0:T(8,128)S(1)} collective-permute-done((f32[176,128]{1,0:T(8,128)S(1)}, f32[176,128]{1,0:T(8,128)S(1)}, u32[]{:S(2)}, u32[]{:S(2)}) %collective-permute-start.11) | collective-permute-done | bytes 90144 | tf_op jit(solution)/shard_map/ppermute | solution.py:398
  23.9 3.3 %rotors.1 = (f32[3,16,64,256]{3,2,1,0:T(8,128)}, f32[4,1024]{1,0:T(4,128)}) custom-call(s32[8,128]{1,0:T(8,128)S(1)} %bitcast.8, s32[8,128]{1,0:T(8,128)S(1)} %bitcast.11, bf16[384,1024]{1,0:T(8,128)(2,1)S(1)} %copy-done, bf16[1024,4096]{1,0:T(8,128)(2,1)S(1)} %bitcast.5, f32[1,1024]{1,0:T(1,128)S(1)} %bitcast.12, ...), custom_call_target="tpu_custom_call" | custom-call | flops 1073741824 | bytes 8388608 | tf_op jit(solution)/shard_map/rotors/pallas_call | solution.py:577
  (18 shorter events, 0.1 us)
Async XLA Ops:
  2.7 5.4 %copy-start.1 = (f32[4,1024]{1,0:T(4,128)S(1)}, f32[4,1024]{1,0:T(4,128)}, u32[]{:S(2)}) copy-start(f32[4,1024]{1,0:T(4,128)} %refs_2_.1) | copy-start | bytes 49156
  4.9 3.2 %collective-permute-start = (f32[48,128]{1,0:T(8,128)S(1)}, f32[48,128]{1,0:T(8,128)S(1)}, u32[]{:S(2)}, u32[]{:S(2)}) collective-permute-start(f32[48,128]{1,0:T(8,128)S(1)} %get-tuple-element.21), channel_id=1, source_target_pairs={{0,1},{1,0},{2,3},{3,2},{4,5},{5,4},{6,7},{7,6},{8,9},{9,8},{10,11... | collective-permute-start | bytes 73736 | tf_op jit(solution)/shard_map/ppermute | solution.py:398
  5.4 6.9 %collective-permute-start.1 = (bf16[3,16,256]{2,1,0:T(8,128)(2,1)S(1)}, bf16[3,16,256]{2,1,0:T(8,128)(2,1)S(1)}, u32[]{:S(2)}, u32[]{:S(2)}) collective-permute-start(bf16[3,16,256]{2,1,0:T(8,128)(2,1)S(1)} %get-tuple-element.24), channel_id=1, source_target_pairs={{0,1},{2,3},{1,0},{3,2},{4,5},{6,7},{5,4},{7,6},{8,9},{10,11},{9,8... | collective-permute-start | bytes 73736 | tf_op jit(solution)/shard_map/ppermute | solution.py:405
  5.5 8.4 %collective-permute-start.2 = (bf16[3,16,256]{2,1,0:T(8,128)(2,1)S(1)}, bf16[3,16,256]{2,1,0:T(8,128)(2,1)S(1)}, u32[]{:S(2)}, u32[]{:S(2)}) collective-permute-start(bf16[3,16,256]{2,1,0:T(8,128)(2,1)S(1)} %get-tuple-element.25), channel_id=1, source_target_pairs={{1,2},{3,0},{2,1},{0,3},{5,6},{7,4},{6,5},{4,7},{9,10},{11,8},{10,... | collective-permute-start | bytes 73736 | tf_op jit(solution)/shard_map/ppermute | solution.py:405
  8.1 6.3 %copy-start.3 = (s32[1024]{0:T(1024)S(1)}, s32[1024]{0:T(1024)}, u32[]{:S(2)}) copy-start(s32[1024]{0:T(1024)} %param.19) | copy-start | bytes 12292
  8.1 6.5 %collective-permute-start.5 = (f32[64,128]{1,0:T(8,128)S(1)}, f32[64,128]{1,0:T(8,128)S(1)}, u32[]{:S(2)}, u32[]{:S(2)}) collective-permute-start(f32[64,128]{1,0:T(8,128)S(1)} %get-tuple-element.22.refs_0_.refs_2_), channel_id=1, source_target_pairs={{0,24},{1,25},{2,26},{3,27},{4,28},{5,29},{6,30},{7,31},{8,16},{9,... | collective-permute-start | bytes 98312 | tf_op jit(solution)/shard_map/ppermute | solution.py:398
  11.8 4.2 %collective-permute-start.4 = (f32[64,128]{1,0:T(8,128)S(1)}, f32[64,128]{1,0:T(8,128)S(1)}, u32[]{:S(2)}, u32[]{:S(2)}) collective-permute-start(f32[64,128]{1,0:T(8,128)S(1)} %get-tuple-element.22.refs_0_.refs_2_), channel_id=1, source_target_pairs={{0,17},{1,16},{2,19},{3,18},{4,21},{5,20},{6,23},{7,22},{8,25},{9,... | collective-permute-start | bytes 98312 | tf_op jit(solution)/shard_map/ppermute | solution.py:398
  11.8 4.2 %collective-permute-start.3 = (f32[64,128]{1,0:T(8,128)S(1)}, f32[64,128]{1,0:T(8,128)S(1)}, u32[]{:S(2)}, u32[]{:S(2)}) collective-permute-start(f32[64,128]{1,0:T(8,128)S(1)} %get-tuple-element.22.refs_0_.refs_2_), channel_id=1, source_target_pairs={{0,9},{1,8},{2,11},{3,10},{4,13},{5,12},{6,15},{7,14},{8,1},{9,0},... | collective-permute-start | bytes 98312 | tf_op jit(solution)/shard_map/ppermute | solution.py:398
  12.3 7.6 %collective-permute-start.6 = (bf16[3,64,256]{2,1,0:T(8,128)(2,1)S(1)}, bf16[3,64,256]{2,1,0:T(8,128)(2,1)S(1)}, u32[]{:S(2)}, u32[]{:S(2)}) collective-permute-start(bf16[3,64,256]{2,1,0:T(8,128)(2,1)S(1)} %get-tuple-element.26), channel_id=1, source_target_pairs={{0,4},{1,5},{2,6},{3,7},{4,0},{5,1},{6,2},{7,3},{8,12},{9,13},{10,... | collective-permute-start | bytes 294920 | tf_op jit(solution)/shard_map/ppermute | solution.py:413
  13.8 5.6 %copy-start.2 = (s32[1024]{0:T(1024)S(1)}, s32[1024]{0:T(1024)}, u32[]{:S(2)}) copy-start(s32[1024]{0:T(1024)} %param.18) | copy-start | bytes 12292
  13.8 6.1 %collective-permute-start.7 = (bf16[3,64,256]{2,1,0:T(8,128)(2,1)S(1)}, bf16[3,64,256]{2,1,0:T(8,128)(2,1)S(1)}, u32[]{:S(2)}, u32[]{:S(2)}) collective-permute-start(bf16[3,64,256]{2,1,0:T(8,128)(2,1)S(1)} %get-tuple-element.27), channel_id=1, source_target_pairs={{0,1},{1,0},{2,3},{3,2},{4,8},{5,9},{6,10},{7,11},{8,4},{9,5},{10,... | collective-permute-start | bytes 294920 | tf_op jit(solution)/shard_map/ppermute | solution.py:413
  16.1 7.8 %slice-start = ((s8[8388608]{0:T(1024)(128)(4,1)}), s8[4194304]{0:T(1024)(128)(4,1)S(1)}, s32[]{:S(2)}) async-start(s8[8388608]{0:T(1024)(128)(4,1)} %bitcast.4), calls=%async_computation | async-start | bytes 8388608
  16.1 6.3 %collective-permute-start.10 = (f32[48,128]{1,0:T(8,128)S(1)}, f32[48,128]{1,0:T(8,128)S(1)}, u32[]{:S(2)}, u32[]{:S(2)}) collective-permute-start(f32[48,128]{1,0:T(8,128)S(1)} %slice.4), channel_id=1, source_target_pairs={{0,6},{1,7},{2,4},{3,5},{4,2},{5,3},{6,0},{7,1},{8,14},{9,15},{10,... | collective-permute-start | bytes 73736 | tf_op jit(solution)/shard_map/ppermute | solution.py:398
  18.4 4.0 %collective-permute-start.9 = (f32[48,128]{1,0:T(8,128)S(1)}, f32[48,128]{1,0:T(8,128)S(1)}, u32[]{:S(2)}, u32[]{:S(2)}) collective-permute-start(f32[48,128]{1,0:T(8,128)S(1)} %slice.4), channel_id=1, source_target_pairs={{0,3},{1,2},{2,1},{3,0},{4,7},{5,6},{6,5},{7,4},{8,11},{9,10},{10,... | collective-permute-start | bytes 73736 | tf_op jit(solution)/shard_map/ppermute | solution.py:398
  18.6 3.8 %collective-permute-start.8 = (f32[112,128]{1,0:T(8,128)S(1)}, f32[112,128]{1,0:T(8,128)S(1)}, u32[]{:S(2)}, u32[]{:S(2)}) collective-permute-start(f32[112,128]{1,0:T(8,128)S(1)} %merge.2.fence_ref.refs_0_.refs_2_), channel_id=1, source_target_pairs={{0,5},{1,4},{2,7},{3,6},{4,1},{5,0},{6,3},{7,2},{8,13},{9,12},{10,... | collective-permute-start | bytes 172040 | tf_op jit(solution)/shard_map/ppermute | solution.py:398
  19.9 4.0 %slice-start.1 = ((s8[8388608]{0:T(1024)(128)(4,1)}), s8[4194304]{0:T(1024)(128)(4,1)S(1)}, s32[]{:S(2)}) async-start(s8[8388608]{0:T(1024)(128)(4,1)} %bitcast.4), calls=%async_computation.1 | async-start | bytes 8388608
  22.4 1.5 %copy-start = (bf16[384,1024]{1,0:T(8,128)(2,1)S(1)}, bf16[384,1024]{1,0:T(8,128)(2,1)}, u32[]{:S(2)}) copy-start(bf16[384,1024]{1,0:T(8,128)(2,1)} %w_in_ref.1) | copy-start | bytes 2359300
  22.4 1.5 %copy-start.4 = (f32[1024]{0:T(1024)S(1)}, f32[1024]{0:T(1024)}, u32[]{:S(2)}) copy-start(f32[1024]{0:T(1024)} %param.14) | copy-start | bytes 12292
  22.5 1.4 %collective-permute-start.11 = (f32[176,128]{1,0:T(8,128)S(1)}, f32[176,128]{1,0:T(8,128)S(1)}, u32[]{:S(2)}, u32[]{:S(2)}) collective-permute-start(f32[176,128]{1,0:T(8,128)S(1)} %merge.3.keep_ref), channel_id=1, source_target_pairs={{0,1},{1,0},{2,3},{3,2},{4,5},{5,4},{6,7},{7,6},{8,9},{9,8},{10,11... | collective-permute-start | bytes 270344 | tf_op jit(solution)/shard_map/ppermute | solution.py:398

commit v12 on v11

--- a/solution.py
+++ b/solution.py
@@ -626,7 +626,7 @@
     y_odd = swap_pairs(y_odd, "cross", (slabs, crosses), 1)
     pooled_rows = keep.shape[0]
 
-    middle = size_x // 4
+    middle = size_x * 5 // 16
     inner, outer = tuple(range(1, middle)), (0,) + tuple(range(middle, size_x))
     runs = ((1, middle - 1, 0, 0), (0, 1, 1, 0), (middle, size_x - middle, 1, 1))
     packed, x_even, x_odd = join(

time: 27.4 us -> 27.6 us (level)
  starting transfers between devices: 12.6 us -> 13.1 us
    ppermute x8, starting transfers between devices: 8.39 us -> 8.81 us  [swap(): return lax.ppermute(value, axis, [(i, i ^ offset) for i in range(count)])]
where the time goes in v12:
time: 27.6 us; the launch traced here: 27.4 us
  starting transfers between devices  13.1 us (47%)
  Pallas kernels  11.4 us (41%)
  waiting for transfers between devices  2.06 us (7%)
  between operations  0.82 us (3%)
    ppermute x8, starting transfers between devices, swap(): return lax.ppermute(value, axis, [(i, i ^ offset) for i in range(count)])  8.81 us
    pallas_call x1, Pallas kernels, rotors_step(): pl.pallas_call(functools.partial(rotor_kernel, bits, runs), out_shape=(ja...  3.28 us
    pallas_call x2, Pallas kernels, stencil(): pl.pallas_call(functools.partial(stencil_kernel, planes, edges, len(fence...  2.96 us
    ppermute x2, starting transfers between devices, swap_pairs(): return lax.ppermute(value, axis, pairs + [(j, i) for i, j in pairs])  2.71 us
    pallas_call x1, Pallas kernels, pool(): pl.pallas_call(functools.partial(pool_kernel, bits), out_shape=(part, par...  2.15 us
    pallas_call x1, Pallas kernels, load(): pl.pallas_call(load_kernel, out_shape=(jax.ShapeDtypeStruct((groups, TILE...  2.11 us
    ppermute x8, waiting for transfers between devices, swap(): return lax.ppermute(value, axis, [(i, i ^ offset) for i in range(count)])  2.05 us
    ppermute x2, starting transfers between devices, swap_pairs(): return lax.ppermute(value, BOTH, pairs)  1.57 us
  transfers between devices with their start and end apart: 12, of which 2 were waited for; matrix products, arithmetic and copies ran while one was open for 0% of the time, Pallas kernels for 14%

profile of v12, /device:TPU:0, one launch (start us, length us, event | category | flops | bytes accessed | tf_op | source)
XLA Modules:
  0.0 27.4 jit_solution(14404881614367033461)
XLA Ops:
  0.6 2.1 %load.1 = (s32[8,128]{1,0:T(8,128)S(1)}, f32[3,16,64,256]{3,2,1,0:T(8,128)S(1)}, bf16[1024,1024]{1,0:T(8,128)(2,1)S(1)}, f32[1024,384]{1,0:T(8,128)S(1)}, s32[10...) custom-call(s32[8,128]{1,0:T(8,128)} %bitcast.6, s32[8,128]{1,0:T(8,128)} %bitcast.13, s32[8,128]{1,0:T(8,128)} %bitcast.9, ...), custom_call_target="tpu_custom_call" | custom-call | flops 536870912 | bytes 3145728 | tf_op jit(solution)/shard_map/load/pallas_call | solution.py:435
  2.7 0.0 copy-start.1
  2.8 2.2 %pool.1 = (f32[48,128]{1,0:T(8,128)S(1)}, f32[48,128]{1,0:T(8,128)S(1)}, bf16[3,16,256]{2,1,0:T(8,128)(2,1)S(1)}, bf16[3,16,256]{2,1,0:T(8,128)(2,1)S(1)}) custom-call(f32[3,16,64,256]{3,2,1,0:T(8,128)S(1)} %get-tuple-element.15.cells.refs_3_.refs_1_, bf16[1024,1024]{1,0:T(8,128)(2,1)S(1)} %get-tuple-element.16.place_hot, ...), custom_call_target="tpu_custom_call" | custom-call | flops 1610612736 | bytes 3145728 | tf_op jit(solution)/shard_map/pool/pallas_call | solution.py:470
  4.9 0.0 copy-start.3
  4.9 0.5 %collective-permute-start = (f32[48,128]{1,0:T(8,128)S(1)}, f32[48,128]{1,0:T(8,128)S(1)}, u32[]{:S(2)}, u32[]{:S(2)}) collective-permute-start(f32[48,128]{1,0:T(8,128)S(1)} %get-tuple-element.21), channel_id=1, source_target_pairs={{0,1},{1,0},{2,3},{3,2},{4,5},{5,4},{6,7},{7,6},{8,9},{9,8},{10,11... | collective-permute-start | bytes 73736 | tf_op jit(solution)/shard_map/ppermute | solution.py:398
  5.4 0.1 collective-permute-start.1
  5.5 2.6 %collective-permute-start.2 = (bf16[3,16,256]{2,1,0:T(8,128)(2,1)S(1)}, bf16[3,16,256]{2,1,0:T(8,128)(2,1)S(1)}, u32[]{:S(2)}, u32[]{:S(2)}) collective-permute-start(bf16[3,16,256]{2,1,0:T(8,128)(2,1)S(1)} %get-tuple-element.25), channel_id=1, source_target_pairs={{1,2},{3,0},{2,1},{0,3},{5,6},{7,4},{6,5},{4,7},{9,10},{11,8},{10,... | collective-permute-start | bytes 73736 | tf_op jit(solution)/shard_map/ppermute | solution.py:405
  8.2 0.0 collective-permute-done.refs_1_
  8.2 3.7 %collective-permute-start.5 = (f32[64,128]{1,0:T(8,128)S(1)}, f32[64,128]{1,0:T(8,128)S(1)}, u32[]{:S(2)}, u32[]{:S(2)}) collective-permute-start(f32[64,128]{1,0:T(8,128)S(1)} %get-tuple-element.22.refs_0_.refs_2_), channel_id=1, source_target_pairs={{0,24},{1,25},{2,26},{3,27},{4,28},{5,29},{6,30},{7,31},{8,16},{9,... | collective-permute-start | bytes 98312 | tf_op jit(solution)/shard_map/ppermute | solution.py:398
  11.9 0.5 %collective-permute-start.3 = (f32[64,128]{1,0:T(8,128)S(1)}, f32[64,128]{1,0:T(8,128)S(1)}, u32[]{:S(2)}, u32[]{:S(2)}) collective-permute-start(f32[64,128]{1,0:T(8,128)S(1)} %get-tuple-element.22.refs_0_.refs_2_), channel_id=1, source_target_pairs={{0,9},{1,8},{2,11},{3,10},{4,13},{5,12},{6,15},{7,14},{8,1},{9,0},... | collective-permute-start | bytes 98312 | tf_op jit(solution)/shard_map/ppermute | solution.py:398
  12.4 0.3 %keys.1.refs_0_.key_hot = bf16[1024,512]{1,0:T(8,128)(2,1)S(1)} custom-call(f32[64,128]{1,0:T(8,128)S(1)} %get-tuple-element.22.refs_0_.refs_2_, s32[8,128]{1,0:T(8,128)S(1)} %get-tuple-element.23.refs_1_, s32[8,128]{1,0:T(8,128)S(1)} %bitcast.10), custom_call_target="tpu_custom_call" | custom-call | flops 524288000 | bytes 1048576 | tf_op jit(solution)/shard_map/keys/pallas_call | solution.py:509
  12.7 0.0 copy-start.2
  12.7 0.0 collective-permute-done.1.refs_2_
  12.7 1.6 %collective-permute-start.6 = (bf16[3,64,256]{2,1,0:T(8,128)(2,1)S(1)}, bf16[3,64,256]{2,1,0:T(8,128)(2,1)S(1)}, u32[]{:S(2)}, u32[]{:S(2)}) collective-permute-start(bf16[3,64,256]{2,1,0:T(8,128)(2,1)S(1)} %get-tuple-element.26), channel_id=1, source_target_pairs={{0,4},{1,5},{2,6},{3,7},{4,0},{5,1},{6,2},{7,3},{8,12},{9,13},{10,... | collective-permute-start | bytes 294920 | tf_op jit(solution)/shard_map/ppermute | solution.py:413
  14.3 0.0 collective-permute-done.2.refs_3_
  14.3 0.0 collective-permute-start.7
  14.3 0.7 %stencil.2.refs_1_.rest_0_ = f32[3,4,64,256]{3,2,1,0:T(8,128)S(1)} custom-call(f32[64,128]{1,0:T(8,128)S(1)} %get-tuple-element.22.refs_0_.refs_2_, f32[3,16,64,256]{3,2,1,0:T(8,128)S(1)} %get-tuple-element.15.cells.refs_3_.refs_1_, bf16[3,16,256]{2,1,0:T(8,128)(2,1)S(1)} %collective-permute-done.1.refs_2_, ...), custom_call_target="tpu_custom_call" | custom-call | flops 196608000 | bytes 1572864 | tf_op jit(solution)/shard_map/stencil/pallas_call | solution.py:492
  15.0 0.0 collective-permute-done.5.refs_5_
  15.0 1.1 %collective-permute-done.4.refs_4_ = f32[64,128]{1,0:T(8,128)S(1)} collective-permute-done((f32[64,128]{1,0:T(8,128)S(1)}, f32[64,128]{1,0:T(8,128)S(1)}, u32[]{:S(2)}, u32[]{:S(2)}) %collective-permute-start.4) | collective-permute-done | bytes 32800 | tf_op jit(solution)/shard_map/ppermute | solution.py:398
  16.1 0.0 collective-permute-done.3.refs_3_
  16.2 2.3 %collective-permute-start.10 = (f32[48,128]{1,0:T(8,128)S(1)}, f32[48,128]{1,0:T(8,128)S(1)}, u32[]{:S(2)}, u32[]{:S(2)}) collective-permute-start(f32[48,128]{1,0:T(8,128)S(1)} %slice.4), channel_id=1, source_target_pairs={{0,6},{1,7},{2,4},{3,5},{4,2},{5,3},{6,0},{7,1},{8,14},{9,15},{10,... | collective-permute-start | bytes 73736 | tf_op jit(solution)/shard_map/ppermute | solution.py:398
  18.4 0.2 collective-permute-start.9
  18.7 0.8 %collective-permute-start.8 = (f32[112,128]{1,0:T(8,128)S(1)}, f32[112,128]{1,0:T(8,128)S(1)}, u32[]{:S(2)}, u32[]{:S(2)}) collective-permute-start(f32[112,128]{1,0:T(8,128)S(1)} %merge.2.fence_ref.refs_0_.refs_2_), channel_id=1, source_target_pairs={{0,5},{1,4},{2,7},{3,6},{4,1},{5,0},{6,3},{7,2},{8,13},{9,12},{10,... | collective-permute-start | bytes 172040 | tf_op jit(solution)/shard_map/ppermute | solution.py:398
  19.4 0.5 %places.1.refs_0_.place_hot = bf16[1024,1024]{1,0:T(8,128)(2,1)S(1)} custom-call(f32[112,128]{1,0:T(8,128)S(1)} %merge.2.fence_ref.refs_0_.refs_2_, s32[8,128]{1,0:T(8,128)S(1)} %bitcast.7), custom_call_target="tpu_custom_call" | custom-call | flops 1048576000 | bytes 2097152 | tf_op jit(solution)/shard_map/places/pallas_call | solution.py:524
  20.0 0.0 slice-start.1
  20.0 0.0 collective-permute-done.6.refs_4_
  20.0 2.2 %stencil.3.refs_1_.rest_1_ = f32[3,12,64,256]{3,2,1,0:T(8,128)S(1)} custom-call(f32[112,128]{1,0:T(8,128)S(1)} %merge.2.fence_ref.refs_0_.refs_2_, f32[3,16,64,256]{3,2,1,0:T(8,128)S(1)} %get-tuple-element.15.cells.refs_3_.refs_1_, bf16[3,16,256]{2,1,0:T(8,128)(2,1)S(1)} %collective-permute-done.1.refs_2_, ...), custom_call_target="tpu_custom_call" | custom-call | flops 589824000 | bytes 4718592 | tf_op jit(solution)/shard_map/stencil/pallas_call | solution.py:492
  22.3 0.0 copy-start
  22.3 0.0 copy-start.4
  22.3 0.8 %collective-permute-start.11 = (f32[176,128]{1,0:T(8,128)S(1)}, f32[176,128]{1,0:T(8,128)S(1)}, u32[]{:S(2)}, u32[]{:S(2)}) collective-permute-start(f32[176,128]{1,0:T(8,128)S(1)} %merge.3.keep_ref), channel_id=1, source_target_pairs={{0,1},{1,0},{2,3},{3,2},{4,5},{5,4},{6,7},{7,6},{8,9},{9,8},{10,11... | collective-permute-start | bytes 270344 | tf_op jit(solution)/shard_map/ppermute | solution.py:398
  23.2 0.9 %collective-permute-done.11.other_ref = f32[176,128]{1,0:T(8,128)S(1)} collective-permute-done((f32[176,128]{1,0:T(8,128)S(1)}, f32[176,128]{1,0:T(8,128)S(1)}, u32[]{:S(2)}, u32[]{:S(2)}) %collective-permute-start.11) | collective-permute-done | bytes 90144 | tf_op jit(solution)/shard_map/ppermute | solution.py:398
  24.1 3.3 %rotors.1 = (f32[3,16,64,256]{3,2,1,0:T(8,128)}, f32[4,1024]{1,0:T(4,128)}) custom-call(s32[8,128]{1,0:T(8,128)S(1)} %bitcast.8, s32[8,128]{1,0:T(8,128)S(1)} %bitcast.11, bf16[384,1024]{1,0:T(8,128)(2,1)S(1)} %copy-done, bf16[1024,4096]{1,0:T(8,128)(2,1)S(1)} %bitcast.5, f32[1,1024]{1,0:T(1,128)S(1)} %bitcast.12, ...), custom_call_target="tpu_custom_call" | custom-call | flops 1073741824 | bytes 8388608 | tf_op jit(solution)/shard_map/rotors/pallas_call | solution.py:577
  (18 shorter events, 0.1 us)
Async XLA Ops:
  2.7 5.4 %copy-start.1 = (f32[4,1024]{1,0:T(4,128)S(1)}, f32[4,1024]{1,0:T(4,128)}, u32[]{:S(2)}) copy-start(f32[4,1024]{1,0:T(4,128)} %refs_2_.1) | copy-start | bytes 49156
  4.9 7.5 %copy-start.3 = (s32[1024]{0:T(1024)S(1)}, s32[1024]{0:T(1024)}, u32[]{:S(2)}) copy-start(s32[1024]{0:T(1024)} %param.19) | copy-start | bytes 12292
  4.9 3.2 %collective-permute-start = (f32[48,128]{1,0:T(8,128)S(1)}, f32[48,128]{1,0:T(8,128)S(1)}, u32[]{:S(2)}, u32[]{:S(2)}) collective-permute-start(f32[48,128]{1,0:T(8,128)S(1)} %get-tuple-element.21), channel_id=1, source_target_pairs={{0,1},{1,0},{2,3},{3,2},{4,5},{5,4},{6,7},{7,6},{8,9},{9,8},{10,11... | collective-permute-start | bytes 73736 | tf_op jit(solution)/shard_map/ppermute | solution.py:398
  5.4 7.2 %collective-permute-start.1 = (bf16[3,16,256]{2,1,0:T(8,128)(2,1)S(1)}, bf16[3,16,256]{2,1,0:T(8,128)(2,1)S(1)}, u32[]{:S(2)}, u32[]{:S(2)}) collective-permute-start(bf16[3,16,256]{2,1,0:T(8,128)(2,1)S(1)} %get-tuple-element.24), channel_id=1, source_target_pairs={{0,1},{2,3},{1,0},{3,2},{4,5},{6,7},{5,4},{7,6},{8,9},{10,11},{9,8... | collective-permute-start | bytes 73736 | tf_op jit(solution)/shard_map/ppermute | solution.py:405
  5.5 8.7 %collective-permute-start.2 = (bf16[3,16,256]{2,1,0:T(8,128)(2,1)S(1)}, bf16[3,16,256]{2,1,0:T(8,128)(2,1)S(1)}, u32[]{:S(2)}, u32[]{:S(2)}) collective-permute-start(bf16[3,16,256]{2,1,0:T(8,128)(2,1)S(1)} %get-tuple-element.25), channel_id=1, source_target_pairs={{1,2},{3,0},{2,1},{0,3},{5,6},{7,4},{6,5},{4,7},{9,10},{11,8},{10,... | collective-permute-start | bytes 73736 | tf_op jit(solution)/shard_map/ppermute | solution.py:405
  8.2 6.8 %collective-permute-start.5 = (f32[64,128]{1,0:T(8,128)S(1)}, f32[64,128]{1,0:T(8,128)S(1)}, u32[]{:S(2)}, u32[]{:S(2)}) collective-permute-start(f32[64,128]{1,0:T(8,128)S(1)} %get-tuple-element.22.refs_0_.refs_2_), channel_id=1, source_target_pairs={{0,24},{1,25},{2,26},{3,27},{4,28},{5,29},{6,30},{7,31},{8,16},{9,... | collective-permute-start | bytes 98312 | tf_op jit(solution)/shard_map/ppermute | solution.py:398
  11.9 4.2 %collective-permute-start.4 = (f32[64,128]{1,0:T(8,128)S(1)}, f32[64,128]{1,0:T(8,128)S(1)}, u32[]{:S(2)}, u32[]{:S(2)}) collective-permute-start(f32[64,128]{1,0:T(8,128)S(1)} %get-tuple-element.22.refs_0_.refs_2_), channel_id=1, source_target_pairs={{0,17},{1,16},{2,19},{3,18},{4,21},{5,20},{6,23},{7,22},{8,25},{9,... | collective-permute-start | bytes 98312 | tf_op jit(solution)/shard_map/ppermute | solution.py:398
  11.9 4.2 %collective-permute-start.3 = (f32[64,128]{1,0:T(8,128)S(1)}, f32[64,128]{1,0:T(8,128)S(1)}, u32[]{:S(2)}, u32[]{:S(2)}) collective-permute-start(f32[64,128]{1,0:T(8,128)S(1)} %get-tuple-element.22.refs_0_.refs_2_), channel_id=1, source_target_pairs={{0,9},{1,8},{2,11},{3,10},{4,13},{5,12},{6,15},{7,14},{8,1},{9,0},... | collective-permute-start | bytes 98312 | tf_op jit(solution)/shard_map/ppermute | solution.py:398
  12.7 6.8 %copy-start.2 = (s32[1024]{0:T(1024)S(1)}, s32[1024]{0:T(1024)}, u32[]{:S(2)}) copy-start(s32[1024]{0:T(1024)} %param.18) | copy-start | bytes 12292
  12.7 7.3 %collective-permute-start.6 = (bf16[3,64,256]{2,1,0:T(8,128)(2,1)S(1)}, bf16[3,64,256]{2,1,0:T(8,128)(2,1)S(1)}, u32[]{:S(2)}, u32[]{:S(2)}) collective-permute-start(bf16[3,64,256]{2,1,0:T(8,128)(2,1)S(1)} %get-tuple-element.26), channel_id=1, source_target_pairs={{0,4},{1,5},{2,6},{3,7},{4,0},{5,1},{6,2},{7,3},{8,12},{9,13},{10,... | collective-permute-start | bytes 294920 | tf_op jit(solution)/shard_map/ppermute | solution.py:413
  14.3 5.8 %collective-permute-start.7 = (bf16[3,64,256]{2,1,0:T(8,128)(2,1)S(1)}, bf16[3,64,256]{2,1,0:T(8,128)(2,1)S(1)}, u32[]{:S(2)}, u32[]{:S(2)}) collective-permute-start(bf16[3,64,256]{2,1,0:T(8,128)(2,1)S(1)} %get-tuple-element.27), channel_id=1, source_target_pairs={{0,1},{1,0},{2,3},{3,2},{4,8},{5,9},{6,10},{7,11},{8,4},{9,5},{10,... | collective-permute-start | bytes 294920 | tf_op jit(solution)/shard_map/ppermute | solution.py:413
  16.1 8.0 %slice-start = ((s8[8388608]{0:T(1024)(128)(4,1)}), s8[4194304]{0:T(1024)(128)(4,1)S(1)}, s32[]{:S(2)}) async-start(s8[8388608]{0:T(1024)(128)(4,1)} %bitcast.4), calls=%async_computation | async-start | bytes 8388608
  16.2 6.1 %collective-permute-start.10 = (f32[48,128]{1,0:T(8,128)S(1)}, f32[48,128]{1,0:T(8,128)S(1)}, u32[]{:S(2)}, u32[]{:S(2)}) collective-permute-start(f32[48,128]{1,0:T(8,128)S(1)} %slice.4), channel_id=1, source_target_pairs={{0,6},{1,7},{2,4},{3,5},{4,2},{5,3},{6,0},{7,1},{8,14},{9,15},{10,... | collective-permute-start | bytes 73736 | tf_op jit(solution)/shard_map/ppermute | solution.py:398
  18.4 3.8 %collective-permute-start.9 = (f32[48,128]{1,0:T(8,128)S(1)}, f32[48,128]{1,0:T(8,128)S(1)}, u32[]{:S(2)}, u32[]{:S(2)}) collective-permute-start(f32[48,128]{1,0:T(8,128)S(1)} %slice.4), channel_id=1, source_target_pairs={{0,3},{1,2},{2,1},{3,0},{4,7},{5,6},{6,5},{7,4},{8,11},{9,10},{10,... | collective-permute-start | bytes 73736 | tf_op jit(solution)/shard_map/ppermute | solution.py:398
  18.7 3.6 %collective-permute-start.8 = (f32[112,128]{1,0:T(8,128)S(1)}, f32[112,128]{1,0:T(8,128)S(1)}, u32[]{:S(2)}, u32[]{:S(2)}) collective-permute-start(f32[112,128]{1,0:T(8,128)S(1)} %merge.2.fence_ref.refs_0_.refs_2_), channel_id=1, source_target_pairs={{0,5},{1,4},{2,7},{3,6},{4,1},{5,0},{6,3},{7,2},{8,13},{9,12},{10,... | collective-permute-start | bytes 172040 | tf_op jit(solution)/shard_map/ppermute | solution.py:398
  20.0 4.1 %slice-start.1 = ((s8[8388608]{0:T(1024)(128)(4,1)}), s8[4194304]{0:T(1024)(128)(4,1)S(1)}, s32[]{:S(2)}) async-start(s8[8388608]{0:T(1024)(128)(4,1)} %bitcast.4), calls=%async_computation.1 | async-start | bytes 8388608
  22.3 1.9 %copy-start = (bf16[384,1024]{1,0:T(8,128)(2,1)S(1)}, bf16[384,1024]{1,0:T(8,128)(2,1)}, u32[]{:S(2)}) copy-start(bf16[384,1024]{1,0:T(8,128)(2,1)} %w_in_ref.1) | copy-start | bytes 2359300
  22.3 1.9 %copy-start.4 = (f32[1024]{0:T(1024)S(1)}, f32[1024]{0:T(1024)}, u32[]{:S(2)}) copy-start(f32[1024]{0:T(1024)} %param.14) | copy-start | bytes 12292
  22.3 1.8 %collective-permute-start.11 = (f32[176,128]{1,0:T(8,128)S(1)}, f32[176,128]{1,0:T(8,128)S(1)}, u32[]{:S(2)}, u32[]{:S(2)}) collective-permute-start(f32[176,128]{1,0:T(8,128)S(1)} %merge.3.keep_ref), channel_id=1, source_target_pairs={{0,1},{1,0},{2,3},{3,2},{4,5},{5,4},{6,7},{7,6},{8,9},{9,8},{10,11... | collective-permute-start | bytes 270344 | tf_op jit(solution)/shard_map/ppermute | solution.py:398
